TPU v7x, 32 devices: a whole 2x2x4 slice. The times are simulated.
32 devices in a mesh: batch: 8 (over z, y), gate: 4 (over x, core).
Axes of the slice: x: 2, y: 2, z: 4, core: 2. Of those that a mesh axis runs over, the one named last changes fastest.
Arguments:
- inputs: bfloat16 [2, 384, 20, 512], P(None, 'batch'), may hold values from -6 to 6
- w_in: bfloat16 [2, 512, 4, 4096], P(None, None, None, 'gate'), may hold values from -0.1875 to 0.1875
- w_rec: bfloat16 [2, 512, 4, 4096], P(None, None, None, 'gate'), may hold values from -0.1875 to 0.1875
- bias: bfloat16 [2, 4, 4096], P(None, None, 'gate'), may hold values from -3 to 3
- proj: bfloat16 [2, 4096, 512], P(None, 'gate'), may hold values from -0.375 to 0.375
- state_h: float32 [384, 2, 512], P('batch'), may hold values from -2.9 to 2.9
- state_c: float32 [384, 2, 4096], P('batch', None, 'gate'), may hold values from -2.9 to 2.9
- resets: int32 [384, 20], P('batch'), may hold values from 0 to 1, as said below
- stream_doc: int32 [384], P('batch'), may hold values from 0 to 47, as said below
- cotangent: bfloat16 [2, 384, 20, 512], P(None, 'batch'), may hold values from -6 to 6
Outputs:
- outputs: bfloat16 [2, 384, 20, 512], P(None, 'batch')
- input_grad: bfloat16 [2, 384, 20, 512], P(None, 'batch', None, 'gate')
- grad_w_in: float32 [2, 512, 4, 4096], P(None, 'batch', None, 'gate')
- grad_w_rec: float32 [2, 512, 4, 4096], P(None, 'batch', None, 'gate')
- grad_bias: float32 [2, 4, 4096], P(None, None, ('gate', 'batch'))
- grad_proj: float32 [2, 4096, 512], P(None, 'gate', 'batch')
- final_h: float32 [384, 2, 512], P('batch')
- final_c: float32 [384, 2, 4096], P('batch', None, 'gate')
Inputs may be any that keep to these rules, and one draw needn't show every extreme that they name: `resets`: each stream has at most one reset in the window. `stream_doc`: each aligned block of 48 streams holds a permutation of 0 to 47.
All inputs are finite; a program needn't handle non-finite values.
Results may differ from a plain program's by a relative error of at most 0.025.
Values may be sent and summed in bfloat16 or wider, within the bound.
No kernel may reach another device: no remote copies, remote signals or barrier semaphores. Data moves between devices by JAX's collectives and lax.ppermute only.
A program may use at most 256 MiB of HBM per device.

v0:
```python
import jax
import jax.numpy as jnp
from jax import lax
from jax.sharding import PartitionSpec as P

CLIP_LEVEL = 3.0


def soft_clip(values):
    return CLIP_LEVEL * jnp.tanh(values / CLIP_LEVEL)


def by_direction(stacked):
    return jnp.stack([stacked[0], jnp.flip(stacked[1], axis=1)])


def keep_masks(resets):
    flags = resets.astype(jnp.float32)
    later = jnp.concatenate([flags[:, 1:], jnp.zeros_like(flags[:, :1])], axis=1)
    return jnp.stack([1.0 - flags, 1.0 - jnp.flip(later, axis=1)])


def gate_acts(pre_act):
    return (
        jax.nn.sigmoid(pre_act[:, :, 0]),
        jax.nn.sigmoid(pre_act[:, :, 1]),
        jnp.tanh(pre_act[:, :, 2]),
        jax.nn.sigmoid(pre_act[:, :, 3]),
    )


def body(inputs, w_in, w_rec, bias, proj, state_h, state_c, resets, stream_doc, cotangent):
    steps = inputs.shape[2]
    share_len = inputs.shape[3] // lax.axis_size("gate")
    share_start = lax.axis_index("gate") * share_len
    features = by_direction(inputs)
    upstream = by_direction(cotangent).astype(jnp.float32)
    upstream_t = jnp.moveaxis(upstream, 2, 0)
    keep_mask = jnp.moveaxis(keep_masks(resets), 2, 0)
    start_h = jnp.transpose(state_h[stream_doc], (1, 0, 2)).astype(jnp.bfloat16)
    start_c = jnp.transpose(state_c[stream_doc], (1, 0, 2))
    inflow = jnp.einsum("dstk,dkgc->tdsgc", features, w_in, preferred_element_type=jnp.float32)

    def hidden_from(proj_part):
        summed_share = lax.psum_scatter(proj_part, "gate", scatter_dimension=2, tiled=True)
        clipped = soft_clip(summed_share)
        gathered = lax.all_gather(clipped.astype(jnp.bfloat16), "gate", axis=2, tiled=True)
        return (gathered, 1.0 - (clipped / CLIP_LEVEL) ** 2)

    def forward_step(state_pair, pieces):
        hidden, cell_state = state_pair
        inflow_t, keep_t = pieces
        hidden = hidden * keep_t[:, :, None].astype(jnp.bfloat16)
        cell_state = cell_state * keep_t[:, :, None]
        pre_act = (
            inflow_t
            + jnp.einsum("dsk,dkgc->dsgc", hidden, w_rec, preferred_element_type=jnp.float32)
            + bias[:, None]
        )
        ingate, forget, candidate, outgate = gate_acts(pre_act)
        new_cell = soft_clip(forget * cell_state + ingate * candidate)
        cell_out = (outgate * jnp.tanh(new_cell)).astype(jnp.bfloat16)
        proj_part = jnp.einsum("dsc,dck->dsk", cell_out, proj, preferred_element_type=jnp.float32)
        next_hidden, clip_slope = hidden_from(proj_part)
        return (
            (next_hidden, new_cell),
            (pre_act, cell_state, new_cell, cell_out, hidden, clip_slope, next_hidden),
        )

    (last_h, last_c), saved = lax.scan(forward_step, (start_h, start_c), (inflow, keep_mask))
    pre_all, prev_cell_all, new_cell_all, cell_out_all, hidden_prev_all, slope_all, next_all = saved
    outputs = by_direction(
        features.astype(jnp.float32) + jnp.moveaxis(next_all, 0, 2).astype(jnp.float32)
    ).astype(jnp.bfloat16)
    final_h = (
        jnp.zeros_like(state_h)
        .at[stream_doc]
        .set(jnp.transpose(last_h.astype(jnp.float32), (1, 0, 2)))
    )
    final_c = jnp.zeros_like(state_c).at[stream_doc].set(jnp.transpose(last_c, (1, 0, 2)))

    def backward_step(state_pair, pieces):
        rec_part, cell_grad = state_pair
        pre_act, prev_cell, new_cell, clip_slope, keep_t, up_t = pieces
        summed_share = lax.psum_scatter(
            rec_part.astype(jnp.bfloat16), "gate", scatter_dimension=2, tiled=True
        ).astype(jnp.float32)
        up_share = lax.dynamic_slice_in_dim(up_t, share_start, share_len, 2)
        raw_grad = lax.all_gather(
            ((summed_share + up_share) * clip_slope).astype(jnp.bfloat16),
            "gate",
            axis=2,
            tiled=True,
        )
        mixed_grad = jnp.einsum("dsk,dck->dsc", raw_grad, proj, preferred_element_type=jnp.float32)
        ingate, forget, candidate, outgate = gate_acts(pre_act)
        squash = jnp.tanh(new_cell)
        cell_total = cell_grad + mixed_grad * outgate * (1.0 - squash * squash)
        cell_inner = cell_total * (1.0 - (new_cell / CLIP_LEVEL) ** 2)
        pre_grad = jnp.stack(
            [
                cell_inner * candidate * ingate * (1.0 - ingate),
                cell_inner * prev_cell * forget * (1.0 - forget),
                cell_inner * ingate * (1.0 - candidate * candidate),
                mixed_grad * squash * outgate * (1.0 - outgate),
            ],
            axis=2,
        ).astype(jnp.bfloat16)
        back_rec = (
            jnp.einsum("dsgc,dkgc->dsk", pre_grad, w_rec, preferred_element_type=jnp.float32)
            * keep_t[:, :, None]
        )
        return ((back_rec, cell_inner * forget * keep_t[:, :, None]), (pre_grad, raw_grad))

    def backward_span(state_pair, low_step, high_step):
        pieces = (
            pre_all[low_step:high_step],
            prev_cell_all[low_step:high_step],
            new_cell_all[low_step:high_step],
            slope_all[low_step:high_step],
            keep_mask[low_step:high_step],
            upstream_t[low_step:high_step],
        )
        return lax.scan(backward_step, state_pair, pieces, reverse=True)

    def span_grads(low_step, high_step, pre_grad, raw_grad):
        grad_in = jnp.einsum(
            "dstk,tdsgc->dkgc",
            features[:, :, low_step:high_step],
            pre_grad,
            preferred_element_type=jnp.float32,
        )
        grad_rec = jnp.einsum(
            "tdsk,tdsgc->dkgc",
            hidden_prev_all[low_step:high_step],
            pre_grad,
            preferred_element_type=jnp.float32,
        )
        grad_bias = jnp.sum(pre_grad, axis=(0, 2), dtype=jnp.float32)
        grad_proj = jnp.einsum(
            "tdsc,tdsk->dck",
            cell_out_all[low_step:high_step],
            raw_grad,
            preferred_element_type=jnp.float32,
        )
        return (grad_in, grad_rec, grad_bias, grad_proj)

    zero_pair = (jnp.zeros(start_h.shape, jnp.float32), jnp.zeros(start_c.shape, jnp.float32))
    half_steps = steps // 2
    carried, (late_pre, late_raw) = backward_span(zero_pair, half_steps, steps)
    late_in, late_rec, late_bias, late_proj = span_grads(half_steps, steps, late_pre, late_raw)
    late_sums = (
        lax.psum_scatter(late_in, "batch", scatter_dimension=1, tiled=True),
        lax.psum_scatter(late_rec, "batch", scatter_dimension=1, tiled=True),
        lax.psum_scatter(late_bias, "batch", scatter_dimension=2, tiled=True),
        lax.psum_scatter(late_proj, "batch", scatter_dimension=2, tiled=True),
    )
    carried, (early_pre, early_raw) = backward_span(carried, 0, half_steps)
    early_in, early_rec, early_bias, early_proj = span_grads(0, half_steps, early_pre, early_raw)
    early_sums = (
        lax.psum_scatter(early_in, "batch", scatter_dimension=1, tiled=True),
        lax.psum_scatter(early_rec, "batch", scatter_dimension=1, tiled=True),
        lax.psum_scatter(early_bias, "batch", scatter_dimension=2, tiled=True),
        lax.psum_scatter(early_proj, "batch", scatter_dimension=2, tiled=True),
    )
    grad_w_in = late_sums[0] + early_sums[0]
    grad_w_rec = late_sums[1] + early_sums[1]
    grad_bias = late_sums[2] + early_sums[2]
    grad_proj = late_sums[3] + early_sums[3]
    pre_grad_all = jnp.concatenate([early_pre, late_pre], axis=0)
    input_part = jnp.einsum(
        "tdsgc,dkgc->dstk", pre_grad_all, w_in, preferred_element_type=jnp.float32
    )
    input_share = lax.psum_scatter(
        input_part.astype(jnp.bfloat16), "gate", scatter_dimension=3, tiled=True
    ).astype(jnp.float32)
    up_share_all = lax.dynamic_slice_in_dim(upstream, share_start, share_len, 3)
    input_grad = by_direction(input_share + up_share_all).astype(jnp.bfloat16)
    return (outputs, input_grad, grad_w_in, grad_w_rec, grad_bias, grad_proj, final_h, final_c)


def solution(mesh):
    placed = (
        P(None, "batch", None, None),
        P(None, None, None, "gate"),
        P(None, None, None, "gate"),
        P(None, None, "gate"),
        P(None, "gate", None),
        P("batch", None, None),
        P("batch", None, "gate"),
        P("batch", None),
        P("batch"),
        P(None, "batch", None, None),
    )
    return jax.shard_map(
        body,
        mesh=mesh,
        in_specs=placed,
        out_specs=(
            P(None, "batch", None, None),
            P(None, "batch", None, "gate"),
            P(None, "batch", None, "gate"),
            P(None, "batch", None, "gate"),
            P(None, None, ("gate", "batch")),
            P(None, "gate", "batch"),
            P("batch", None, None),
            P("batch", None, "gate"),
        ),
        check_vma=False,
    )
```

profile of v0, /device:TPU:8, one launch (start us, length us, event | category | flops | bytes accessed | tf_op | source)
XLA Modules:
  0.0 2408.8 jit_solution(15731001401211949656)
XLA Ops:
  33.1 25.6 %convolution_bitcast_fusion.2 = f32[20,2,48,4,1024]{4,2,3,0,1:T(8,128)} fusion(bf16[2,512,4,1024,1]{3,2,1,0,4:T(4,128)(2,1)} %bitcast.528, bf16[1,48,20,512]{3,1,2,0:T(8,128)(2,1)S(1)} %reverse_bitcast_fusion.1, bf16[1,48,20,512]{3,1,2,0:T(8,128)(2,1)S(1)} %get-tuple-element.1191), kind=kOutput, calls=%fused_computation.151 | convolution fusion | flops 8056995840 | bytes 41811968 | tf_op jit(solution)/shard_map/dstk,dkgc->tdsgc/dot_general | solution.py:42
  58.7 726.5 %while.71 = (s32[]{:T(128)}, bf16[2,48,512]{2,1,0:T(8,128)(2,1)S(1)}, f32[2,48,1024]{2,1,0:T(8,128)S(1)}, f32[20,2,48,4,1024]{4,2,1,3,0:T(8,128)}, f32[20,2,48,1...) while((s32[]{:T(128)}, ...), condition=%wide.region_2.3_spmd, body=%wide.region_0.2_spmd.sunk | while | flops 506347616 | bytes 32282168 | solution.py:70
  71.7 16.8 reduce-scatter.31.cloned.1.call-done
  109.1 15.7 reduce-scatter.31.cloned.1.call-done
  399.3 15.7 reduce-scatter.31.cloned.1.call-done
  761.9 15.7 reduce-scatter.31.cloned.1.call-done
  785.3 21.4 fusion.143
  829.8 415.0 %while.73 = (s32[]{:T(128)}, bf16[2,48,512]{2,1,0:T(8,128)(2,1)S(1)}, f32[2,48,1024]{2,1,0:T(8,128)S(1)}, bf16[10,2,48,4,1024]{4,2,1,3,0:T(8,128)(2,1)}, bf16[10...) while((s32[]{:T(128)}, ...), condition=%wide.region_5.6_spmd.clone, body=%wide.region_3.5_spmd.clone.sunk | while | flops 512163840 | bytes 22865680 | solution.py:124
  833.0 20.3 reduce-scatter.35.cloned.1.call-done
  874.7 20.2 reduce-scatter.35.cloned.1.call-done
  916.3 20.3 reduce-scatter.35.cloned.1.call-done
  957.9 19.9 reduce-scatter.35.cloned.1.call-done
  999.2 20.2 reduce-scatter.35.cloned.1.call-done
  1040.9 19.9 reduce-scatter.35.cloned.1.call-done
  1082.1 19.9 reduce-scatter.35.cloned.1.call-done
  1123.4 20.3 reduce-scatter.35.cloned.1.call-done
  1165.1 20.2 reduce-scatter.35.cloned.1.call-done
  1206.7 19.9 reduce-scatter.35.cloned.1.call-done
  1249.9 389.4 %while.72 = (s32[]{:T(128)}, bf16[2,48,512]{2,1,0:T(8,128)(2,1)S(1)}, f32[2,48,1024]{2,1,0:T(8,128)S(1)}, bf16[10,2,48,4,1024]{4,2,1,3,0:T(8,128)(2,1)}, bf16[10...) while((s32[]{:T(128)}, ...), condition=%wide.region_8.9_spmd, body=%wide.region_6.8_spmd.sunk | while | flops 512016384 | bytes 56223520 | solution.py:124
  1253.1 20.4 reduce-scatter.33.cloned.1.call-done
  1292.2 20.4 reduce-scatter.33.cloned.1.call-done
  1331.3 20.1 reduce-scatter.33.cloned.1.call-done
  1370.0 20.4 reduce-scatter.33.cloned.1.call-done
  1409.2 20.4 reduce-scatter.33.cloned.1.call-done
  1448.2 20.1 reduce-scatter.33.cloned.1.call-done
  1486.9 20.1 reduce-scatter.33.cloned.1.call-done
  1525.7 20.4 reduce-scatter.33.cloned.1.call-done
  1564.8 20.1 reduce-scatter.33.cloned.1.call-done
  1603.6 20.4 reduce-scatter.33.cloned.1.call-done
  1760.0 265.9 %reduce-scatter.23.cloned.1.call-done = f32[2,64,4,1024]{3,1,2,0:T(8,128)} async-done(((f32[2,512,4,1024]{3,1,2,0:T(8,128)}), f32[2,64,4,1024]{3,1,2,0:T(8,128)}) %reduce-scatter.23.cloned.1.call-update) | async-done | bytes 2097168 | tf_op jit(solution)/shard_map/reduce_scatter | solution.py:154
  2030.1 278.2 %reduce-scatter.21.cloned.1.call-done = f32[2,64,4,1024]{3,1,2,0:T(8,128)} async-done(((f32[2,512,4,1024]{3,1,2,0:T(8,128)}), f32[2,64,4,1024]{3,1,2,0:T(8,128)}) %reduce-scatter.21.cloned.1.call-update) | async-done | bytes 2097168 | tf_op jit(solution)/shard_map/reduce_scatter | solution.py:153
  2312.6 88.1 %reduce-scatter.25.cloned.1.call-done = f32[2,1024,64]{1,2,0:T(8,128)} async-done(((f32[2,1024,512]{1,2,0:T(8,128)}), f32[2,1024,64]{1,2,0:T(8,128)}) %reduce-scatter.25.cloned.1.call-update) | async-done | bytes 524304 | tf_op jit(solution)/shard_map/reduce_scatter | solution.py:156
  (906 shorter events, 1241.7 us)
Async XLA Ops:
  58.7 29.8 %reduce-scatter.31.cloned.1.call-start = ((), (), s32[]{:S(2)}) async-start(), calls=%async_computation.13 | async-start | bytes 245760 | tf_op jit(solution)/shard_map/while/body/eval_jaxpr/reduce_scatter | solution.py:45
  96.2 28.6 %reduce-scatter.31.cloned.1.call-start = ((), (), s32[]{:S(2)}) async-start(), calls=%async_computation.13 | async-start | bytes 245760 | tf_op jit(solution)/shard_map/while/body/eval_jaxpr/reduce_scatter | solution.py:45
  132.4 28.6 %reduce-scatter.31.cloned.1.call-start = ((), (), s32[]{:S(2)}) async-start(), calls=%async_computation.13 | async-start | bytes 245760 | tf_op jit(solution)/shard_map/while/body/eval_jaxpr/reduce_scatter | solution.py:45
  168.7 28.6 %reduce-scatter.31.cloned.1.call-start = ((), (), s32[]{:S(2)}) async-start(), calls=%async_computation.13 | async-start | bytes 245760 | tf_op jit(solution)/shard_map/while/body/eval_jaxpr/reduce_scatter | solution.py:45
  205.0 28.6 %reduce-scatter.31.cloned.1.call-start = ((), (), s32[]{:S(2)}) async-start(), calls=%async_computation.13 | async-start | bytes 245760 | tf_op jit(solution)/shard_map/while/body/eval_jaxpr/reduce_scatter | solution.py:45
  241.3 28.6 %reduce-scatter.31.cloned.1.call-start = ((), (), s32[]{:S(2)}) async-start(), calls=%async_computation.13 | async-start | bytes 245760 | tf_op jit(solution)/shard_map/while/body/eval_jaxpr/reduce_scatter | solution.py:45
  277.5 28.6 %reduce-scatter.31.cloned.1.call-start = ((), (), s32[]{:S(2)}) async-start(), calls=%async_computation.13 | async-start | bytes 245760 | tf_op jit(solution)/shard_map/while/body/eval_jaxpr/reduce_scatter | solution.py:45
  313.8 28.6 %reduce-scatter.31.cloned.1.call-start = ((), (), s32[]{:S(2)}) async-start(), calls=%async_computation.13 | async-start | bytes 245760 | tf_op jit(solution)/shard_map/while/body/eval_jaxpr/reduce_scatter | solution.py:45
  350.0 28.6 %reduce-scatter.31.cloned.1.call-start = ((), (), s32[]{:S(2)}) async-start(), calls=%async_computation.13 | async-start | bytes 245760 | tf_op jit(solution)/shard_map/while/body/eval_jaxpr/reduce_scatter | solution.py:45
  386.3 28.6 %reduce-scatter.31.cloned.1.call-start = ((), (), s32[]{:S(2)}) async-start(), calls=%async_computation.13 | async-start | bytes 245760 | tf_op jit(solution)/shard_map/while/body/eval_jaxpr/reduce_scatter | solution.py:45
  422.6 28.6 %reduce-scatter.31.cloned.1.call-start = ((), (), s32[]{:S(2)}) async-start(), calls=%async_computation.13 | async-start | bytes 245760 | tf_op jit(solution)/shard_map/while/body/eval_jaxpr/reduce_scatter | solution.py:45
  458.8 28.6 %reduce-scatter.31.cloned.1.call-start = ((), (), s32[]{:S(2)}) async-start(), calls=%async_computation.13 | async-start | bytes 245760 | tf_op jit(solution)/shard_map/while/body/eval_jaxpr/reduce_scatter | solution.py:45
  495.1 28.6 %reduce-scatter.31.cloned.1.call-start = ((), (), s32[]{:S(2)}) async-start(), calls=%async_computation.13 | async-start | bytes 245760 | tf_op jit(solution)/shard_map/while/body/eval_jaxpr/reduce_scatter | solution.py:45
  531.4 28.6 %reduce-scatter.31.cloned.1.call-start = ((), (), s32[]{:S(2)}) async-start(), calls=%async_computation.13 | async-start | bytes 245760 | tf_op jit(solution)/shard_map/while/body/eval_jaxpr/reduce_scatter | solution.py:45
  567.7 28.6 %reduce-scatter.31.cloned.1.call-start = ((), (), s32[]{:S(2)}) async-start(), calls=%async_computation.13 | async-start | bytes 245760 | tf_op jit(solution)/shard_map/while/body/eval_jaxpr/reduce_scatter | solution.py:45
  603.9 28.6 %reduce-scatter.31.cloned.1.call-start = ((), (), s32[]{:S(2)}) async-start(), calls=%async_computation.13 | async-start | bytes 245760 | tf_op jit(solution)/shard_map/while/body/eval_jaxpr/reduce_scatter | solution.py:45
  640.2 28.6 %reduce-scatter.31.cloned.1.call-start = ((), (), s32[]{:S(2)}) async-start(), calls=%async_computation.13 | async-start | bytes 245760 | tf_op jit(solution)/shard_map/while/body/eval_jaxpr/reduce_scatter | solution.py:45
  676.5 28.6 %reduce-scatter.31.cloned.1.call-start = ((), (), s32[]{:S(2)}) async-start(), calls=%async_computation.13 | async-start | bytes 245760 | tf_op jit(solution)/shard_map/while/body/eval_jaxpr/reduce_scatter | solution.py:45
  712.7 28.6 %reduce-scatter.31.cloned.1.call-start = ((), (), s32[]{:S(2)}) async-start(), calls=%async_computation.13 | async-start | bytes 245760 | tf_op jit(solution)/shard_map/while/body/eval_jaxpr/reduce_scatter | solution.py:45
  749.0 28.6 %reduce-scatter.31.cloned.1.call-start = ((), (), s32[]{:S(2)}) async-start(), calls=%async_computation.13 | async-start | bytes 245760 | tf_op jit(solution)/shard_map/while/body/eval_jaxpr/reduce_scatter | solution.py:45
  871.4 23.5 reduce-scatter.35.cloned.1.call-start
  1249.9 23.6 reduce-scatter.33.cloned.1.call-start
  1289.0 23.6 reduce-scatter.33.cloned.1.call-start
  1366.8 23.6 reduce-scatter.33.cloned.1.call-start
  1405.9 23.6 reduce-scatter.33.cloned.1.call-start
  1522.5 23.6 reduce-scatter.33.cloned.1.call-start
  1600.3 23.6 reduce-scatter.33.cloned.1.call-start
  1639.3 112.9 %reduce-scatter.29.cloned.1.call-start = ((), (), s32[]{:S(2)}) async-start(), calls=%async_computation.12 | async-start | bytes 589824
  1649.1 104.8 %reduce-scatter.27.cloned.1.call-start = ((), (), s32[]{:S(2)}) async-start(), calls=%async_computation.11 | async-start | bytes 2457600
  1680.0 345.9 %reduce-scatter.23.cloned.1.call-start = ((), (), s32[]{:S(2)}) async-start(), calls=%async_computation.9 | async-start | bytes 18874368 | tf_op jit(solution)/shard_map/reduce_scatter | solution.py:154
  1705.7 602.6 %reduce-scatter.21.cloned.1.call-start = ((), (), s32[]{:S(2)}) async-start(), calls=%async_computation.8 | async-start | bytes 18874368 | tf_op jit(solution)/shard_map/reduce_scatter | solution.py:153
  1733.5 667.2 %reduce-scatter.25.cloned.1.call-start = ((), (), s32[]{:S(2)}) async-start(), calls=%async_computation.10 | async-start | bytes 4718592 | tf_op jit(solution)/shard_map/reduce_scatter | solution.py:156
  (110 other events, 1604.6 us)
Sparse Core Ops, SparseCore 0:
  67.6 20.9 reduce-scatter.30
  105.0 19.7 reduce-scatter.30
  141.3 19.7 reduce-scatter.30
  177.5 19.7 reduce-scatter.30
  213.8 19.7 reduce-scatter.30
  250.0 19.7 reduce-scatter.30
  286.3 19.7 reduce-scatter.30
  322.6 19.7 reduce-scatter.30
  358.9 19.7 reduce-scatter.30
  395.1 19.7 reduce-scatter.30
  431.4 19.7 reduce-scatter.30
  467.7 19.7 reduce-scatter.30
  503.9 19.7 reduce-scatter.30
  540.2 19.7 reduce-scatter.30
  576.5 19.7 reduce-scatter.30
  612.7 19.7 reduce-scatter.30
  649.0 19.7 reduce-scatter.30
  685.3 19.7 reduce-scatter.30
  721.5 19.7 reduce-scatter.30
  757.8 19.7 reduce-scatter.30
  833.6 19.6 reduce-scatter.34
  916.9 19.6 reduce-scatter.34
  1082.4 19.6 reduce-scatter.34
  1165.6 19.6 reduce-scatter.34
  1207.0 19.6 reduce-scatter.34
  1253.9 19.6 reduce-scatter.32
  1293.0 19.6 reduce-scatter.32
  1331.7 19.6 reduce-scatter.32
  1370.8 19.6 reduce-scatter.32
  1448.7 19.6 reduce-scatter.32
  1487.4 19.6 reduce-scatter.32
  1565.2 19.6 reduce-scatter.32
  (8 shorter events, 156.4 us)
Sparse Core Ops, SparseCore 1:
  1649.2 61.8 reduce-scatter.28
  1714.2 29.7 reduce-scatter.26
  1747.6 278.2 reduce-scatter.22
  2030.1 278.2 reduce-scatter.20
  2312.6 88.1 reduce-scatter.24
where the time goes:
time: 2420 us; the launch traced here: 2410 us
  waiting for transfers between devices  1350 us (56%)
  matrix products  371 us (15%)
  local copies, waits for them, and re-layouts  231 us (10%)
  other arithmetic  219 us (9%)
  blocking collectives  214 us (9%)
    while x60, waiting for transfers between devices  404 us
    reduce_scatter x20, waiting for transfers between devices, hidden_from(): lax.psum_scatter(proj_part, 'gate', scatter_dimension=2, tiled=True)  314 us
    reduce_scatter x1, waiting for transfers between devices, body(): lax.psum_scatter(late_in, 'batch', scatter_dimension=1, tiled=True)  278 us
    reduce_scatter x1, waiting for transfers between devices, body(): lax.psum_scatter(late_rec, 'batch', scatter_dimension=1, tiled=True)  266 us
    dot_general x20, matrix products, forward_step(): jnp.einsum('dsk,dkgc->dsgc', hidden, w_rec, preferred_element_type=jnp.fl...  111 us
    all_gather x20, blocking collectives, backward_step(): lax.all_gather(((summed_share + up_share) * clip_slope).astype(jnp.bfloat...  107 us
    all_gather x20, blocking collectives, hidden_from(): lax.all_gather(clipped.astype(jnp.bfloat16), 'gate', axis=2, tiled=True)  107 us
    dynamic_update_slice x80, other arithmetic, body(): lax.scan(forward_step, (start_h, start_c), (inflow, keep_mask))  99.6 us
  transfers between devices with their start and end apart: 45, of which 43 were waited for; matrix products, arithmetic and copies ran while one was open for 10% of the time, Pallas kernels for 0%

commit v1 on v0

v1 whole, which is shorter than its diff:
```python
import functools

import jax
import jax.numpy as jnp
from jax import lax
from jax.experimental import pallas as pl
from jax.experimental.pallas import tpu as pltpu
from jax.sharding import PartitionSpec as P

CLIP = 3.0
F32, BF16 = jnp.float32, jnp.bfloat16
QUARTERS, HALVES = 2, 2
PIECES = QUARTERS * HALVES
MIB = 2**20

VMEM = pl.BlockSpec(memory_space=pltpu.VMEM)
SMEM = pl.BlockSpec(memory_space=pltpu.SMEM)
ANY = pl.BlockSpec(memory_space=pl.ANY)


def pinned(array):
    return pltpu.with_memory_space_constraint(array, pltpu.VMEM)


def in_hbm(array):
    return pltpu.with_memory_space_constraint(array, pltpu.HBM)


def dot(left, right):
    return jnp.dot(left, right, preferred_element_type=F32)


def place_kernel(count, *refs):
    sources, targets, sems = refs[:count], refs[count : 2 * count], refs[2 * count]
    copies = [pltpu.make_async_copy(a, b, sems.at[i]) for i, (a, b) in enumerate(zip(sources, targets))]
    for copy in copies:
        copy.start()
    for copy in copies:
        copy.wait()


def place(*arrays):
    count = len(arrays)
    return pl.pallas_call(
        functools.partial(place_kernel, count),
        out_shape=tuple(pltpu.VMEM(x.shape, x.dtype) for x in arrays),
        in_specs=[ANY] * count,
        out_specs=[VMEM] * count,
        scratch_shapes=[pltpu.SemaphoreType.DMA((count,))],
        compiler_params=params(1),
        name="place",
    )(*arrays)


def pieces(refs, axis):
    for piece in range(PIECES):
        quarter, half = divmod(piece, HALVES)
        width = refs[0].shape[axis] // HALVES
        yield piece, quarter, width, slice(half * width, (half + 1) * width)


def forward_kernel(
    first, step_ref, p_ref, q_ref, start_ref, keep_ref, cell_ref, inflow_ref, wa_ref, wb_ref, pa_ref, pb_ref,
    part_ref, next_ref, gates_ref, mixed_ref, prev_ref, hidden_ref, slope_ref,
):
    keep = keep_ref[step_ref[1]][:, :1]
    if first:
        hidden = start_ref[...]
    else:
        hidden = clipped(p_ref, q_ref, hidden_ref, slope_ref)
    hidden = hidden * keep.astype(BF16)
    prev_ref[...] = hidden
    part = jnp.zeros(part_ref.shape, F32)
    for piece, quarter, width, cols in pieces((wa_ref, wb_ref), 2):
        w_ref, proj_ref = ((wa_ref, pa_ref), (wb_ref, pb_ref))[quarter]
        acts = []
        for gate in range(4):
            place = slice(gate * width, (gate + 1) * width)
            pre = dot(hidden, w_ref[gate, :, cols]) + inflow_ref[piece, :, place]
            act = jnp.tanh(pre if gate == 2 else 0.5 * pre)
            gates_ref[piece, :, place] = act.astype(BF16)
            acts.append(act if gate == 2 else 0.5 + 0.5 * act)
        ingate, forget, candidate, outgate = acts
        cell = CLIP * jnp.tanh((forget * (keep * cell_ref[piece]) + ingate * candidate) * (1.0 / CLIP))
        next_ref[piece] = cell
        mixed = (outgate * jnp.tanh(cell)).astype(BF16)
        mixed_ref[piece] = mixed
        part = part + dot(mixed, proj_ref[cols, :])
    part_ref[...] = part.astype(BF16)


def clipped(p_ref, q_ref, hidden_ref, slope_ref):
    squash = jnp.tanh((p_ref[...].astype(F32) + q_ref[...].astype(F32)) * (1.0 / CLIP))
    hidden = (CLIP * squash).astype(BF16)
    hidden_ref[...] = hidden
    slope_ref[...] = 1.0 - squash * squash
    return hidden


def between_kernel(
    first, step_ref, feat_ref, bias_ref, wa_ref, wb_ref, cell_ref, gates_ref, mixed_ref, prev_ref, hidden_ref, slope_ref,
    *refs,
):
    out_ref, gates_all, cells_all, mixed_all, prev_all, hidden_all, slope_all, sems = refs if first else refs[6:]
    step, time, time_before, time_after = (step_ref[i] for i in range(4))
    copies = [pltpu.make_async_copy(gates_ref.at[i], gates_all.at[i, step], sems.at[i]) for i in range(PIECES)]
    copies += [
        pltpu.make_async_copy(mixed_ref.at[i], mixed_all.at[i, time], sems.at[PIECES + i]) for i in range(PIECES)
    ]
    copies.append(pltpu.make_async_copy(cell_ref, cells_all.at[step], sems.at[2 * PIECES]))
    copies.append(pltpu.make_async_copy(prev_ref, prev_all.at[time], sems.at[2 * PIECES + 1]))
    if not first:
        copies.append(pltpu.make_async_copy(hidden_ref, hidden_all.at[time_before], sems.at[2 * PIECES + 2]))
        copies.append(pltpu.make_async_copy(slope_ref, slope_all.at[step - 1], sems.at[2 * PIECES + 3]))
    for copy in copies:
        copy.start()
    inflow_into(feat_ref[time_after], bias_ref, wa_ref, wb_ref, out_ref)
    for copy in copies:
        copy.wait()


def inflow_into(feat, bias_ref, wa_ref, wb_ref, out_ref):
    for piece, quarter, width, cols in pieces((wa_ref, wb_ref), 2):
        w_ref = (wa_ref, wb_ref)[quarter]
        for gate in range(4):
            place = slice(gate * width, (gate + 1) * width)
            out_ref[piece, :, place] = dot(feat, w_ref[gate, :, cols]) + bias_ref[piece, :, place]


def inflow_kernel(step_ref, feat_ref, bias_ref, wa_ref, wb_ref, out_ref):
    inflow_into(feat_ref[step_ref[1]], bias_ref, wa_ref, wb_ref, out_ref)


def backward_kernel(
    step_ref, p_ref, q_ref, keep_ref, grad_ref, wa_ref, wb_ref, pa_ref, pb_ref,
    gates_ref, cell_ref, prev_ref, slope_ref, up_ref, start_ref,
    part_ref, next_ref, raw_ref, dz_ref,
):
    step = step_ref[0]
    keep = keep_ref[step_ref[1]][:, :1]
    raw = (up_ref[...].astype(F32) + (p_ref[...].astype(F32) + q_ref[...].astype(F32))) * slope_ref[...]
    raw = raw.astype(BF16)
    raw_ref[...] = raw
    part = jnp.zeros(part_ref.shape, F32)
    for piece, quarter, width, cols in pieces((wa_ref, wb_ref), 1):
        w_ref, proj_ref = ((wa_ref, pa_ref), (wb_ref, pb_ref))[quarter]
        mixed = dot(raw, proj_ref[:, cols])
        acts = [gates_ref[piece, :, gate * width : (gate + 1) * width].astype(F32) for gate in range(4)]
        ingate, forget, outgate = (0.5 + 0.5 * acts[gate] for gate in (0, 1, 3))
        slopes = [1.0 - act * act for act in acts]
        cell = cell_ref[piece]
        prev = keep * jnp.where(step == 0, start_ref[piece], prev_ref[piece])
        squash = jnp.tanh(cell)
        total = grad_ref[piece] + mixed * outgate * (1.0 - squash * squash)
        inner = total * (1.0 - (cell * (1.0 / CLIP)) * (cell * (1.0 / CLIP)))
        next_ref[piece] = keep * inner * forget
        quart = 0.25 * inner
        pre_grads = (
            quart * acts[2] * slopes[0],
            quart * prev * slopes[1],
            inner * ingate * slopes[2],
            0.25 * mixed * squash * slopes[3],
        )
        for gate in range(4):
            low = pre_grads[gate].astype(BF16)
            dz_ref[piece, :, gate * width : (gate + 1) * width] = low
            part = part + dot(low, w_ref[gate, cols, :])
    part_ref[...] = (part * keep).astype(BF16)


def finish_kernel(
    step_ref, p_ref, q_ref, gates_all, cells_all, ups_all, hidden_in, slope_in,
    gates_ref, cell_ref, prev_ref, slope_ref, up_ref, hidden_all, slope_all,
    hidden_buf, sems, hidden_sem,
):
    copies = fetches(
        step_ref[0], step_ref[1], (gates_all, cells_all, ups_all), (gates_ref, cell_ref, prev_ref, up_ref), sems
    )
    for copy in copies:
        copy.start()
    clipped(p_ref, q_ref, hidden_buf, slope_ref)
    hidden_copy = pltpu.make_async_copy(hidden_buf, hidden_all.at[step_ref[1]], hidden_sem)
    hidden_copy.start()
    for copy in copies:
        copy.wait()
    hidden_copy.wait()


def fetches(step, time, sources, targets, sems):
    gates_all, cells_all, ups_all = sources
    gates_ref, cell_ref, prev_ref, up_ref = targets
    before = jnp.maximum(step - 1, 0)
    return [
        pltpu.make_async_copy(gates_all.at[i, step], gates_ref.at[i], sems.at[i]) for i in range(PIECES)
    ] + [
        pltpu.make_async_copy(cells_all.at[step], cell_ref, sems.at[PIECES]),
        pltpu.make_async_copy(cells_all.at[before], prev_ref, sems.at[PIECES + 1]),
        pltpu.make_async_copy(ups_all.at[time], up_ref, sems.at[PIECES + 2]),
    ]


def aside_kernel(
    first, step_ref, dz_ref, raw_ref, wa_ref, wb_ref, gates_all, cells_all, ups_all, slope_all, *refs
):
    gates_ref, cell_ref, prev_ref, slope_ref, up_ref, dz_all, raw_all, dx_all, dx_buf, sems, fetch_sems = (
        refs if first else refs[3:]
    )
    step, time, time_before = (step_ref[i] for i in range(3))
    before = jnp.maximum(step - 1, 0)
    copies = fetches(
        before, time_before, (gates_all, cells_all, ups_all), (gates_ref, cell_ref, prev_ref, up_ref), fetch_sems
    )
    copies.append(pltpu.make_async_copy(slope_all.at[before], slope_ref, fetch_sems.at[PIECES + 3]))
    copies += [pltpu.make_async_copy(dz_ref.at[i], dz_all.at[i, time], sems.at[i]) for i in range(PIECES)]
    copies.append(pltpu.make_async_copy(raw_ref, raw_all.at[time], sems.at[PIECES]))
    for copy in copies:
        copy.start()
    part = jnp.zeros(dx_buf.shape, F32)
    for piece, quarter, width, cols in pieces((wa_ref, wb_ref), 2):
        w_ref = (wa_ref, wb_ref)[quarter]
        for gate in range(4):
            part = part + lax.dot_general(
                dz_ref[piece, :, gate * width : (gate + 1) * width],
                w_ref[gate, :, cols],
                (((1,), (1,)), ((), ())),
                preferred_element_type=F32,
            )
    dx_buf[...] = part
    last = pltpu.make_async_copy(dx_buf, dx_all.at[time], sems.at[PIECES + 1])
    last.start()
    for copy in copies:
        copy.wait()
    last.wait()


def params(mib):
    return pltpu.CompilerParams(vmem_limit_bytes=mib * MIB)


def cost(flops, size):
    return pl.CostEstimate(flops=flops, bytes_accessed=size, transcendentals=0)


def body(inputs, w_in, w_rec, bias, proj, state_h, state_c, resets, stream_doc, cotangent):
    streams, steps, depth = inputs.shape[1:]
    cells = w_in.shape[3]
    width = cells // HALVES
    rank = lax.axis_index("gate")
    own = rank % 2
    gates_size = lax.axis_size("gate")
    swap = [(i, i ^ 1) for i in range(gates_size)]
    across = [(i, i ^ 2) for i in range(gates_size)]

    def pick(stacked, index):
        return lax.dynamic_index_in_dim(stacked, index, 0, keepdims=False)

    def trade(mine, theirs):
        return (mine, lax.ppermute(theirs, "gate", swap))

    def by_gate(stacked, index):
        return jnp.transpose(pick(stacked, index), (1, 0, 2))

    win_a, win_b = trade(by_gate(w_in, own), by_gate(w_in, 1 - own))
    rec_a, rec_b = trade(by_gate(w_rec, own), by_gate(w_rec, 1 - own))
    proj_a, proj_b = trade(pick(proj, own), pick(proj, 1 - own))
    bias_a, bias_b = trade(pick(bias, own), pick(bias, 1 - own))

    def pieces_of(pair):
        split = [x.reshape(4, HALVES, width) for x in pair]
        return jnp.transpose(jnp.stack(split), (0, 2, 1, 3)).reshape(PIECES, 1, 4 * width)

    bias_p = pieces_of((bias_a, bias_b)).astype(F32)

    def cells_to_pieces(pair):
        both = jnp.stack(pair).reshape(QUARTERS, streams, HALVES, width)
        return jnp.transpose(both, (0, 2, 1, 3)).reshape(PIECES, streams, width)

    def by_time(stacked):
        return jnp.transpose(pick(stacked, own), (1, 0, 2))

    feats = by_time(inputs)
    ups = by_time(cotangent)
    flags = resets.astype(F32)
    later = jnp.concatenate([flags[:, 1:], jnp.zeros_like(flags[:, :1])], axis=1)
    keep = 1.0 - jnp.where(own == 0, flags, later)
    keep = jnp.broadcast_to(jnp.transpose(keep)[:, :, None], (steps, streams, 128))

    docs_h = state_h[stream_doc]
    docs_c = state_c[stream_doc]
    start_h = pick(jnp.transpose(docs_h, (1, 0, 2)), own).astype(BF16)
    by_dir_c = jnp.transpose(docs_c, (1, 0, 2))
    start_c = cells_to_pieces(trade(pick(by_dir_c, own), pick(by_dir_c, 1 - own)))

    def at_step(step):
        near = jnp.array([step, step, max(step - 1, 0), min(step + 1, steps - 1)], jnp.int32)
        turned = jnp.array([step] + [steps - 1 - x for x in (step, max(step - 1, 0), min(step + 1, steps - 1))], jnp.int32)
        return jnp.where(own == 0, near, turned)

    def vmem(shape, dtype):
        return pltpu.VMEM(shape, dtype)

    def hbm(shape, dtype):
        return pltpu.HBM(shape, dtype)

    feats_v, keep_v, bias_v, win_av, win_bv = place(feats, keep, bias_p, win_a, win_b)
    rec_av, rec_bv, proj_av, proj_bv, start_hv, start_cv = place(rec_a, rec_b, proj_a, proj_b, start_h, start_c)

    gates_shape, cell_shape = (PIECES, streams, 4 * width), (PIECES, streams, width)
    inflow = pl.pallas_call(
        inflow_kernel,
        out_shape=vmem(gates_shape, F32),
        in_specs=[SMEM] + [VMEM] * 4,
        out_specs=VMEM,
        compiler_params=params(8),
        name="inflow",
    )(at_step(0), pinned(feats_v), pinned(bias_v), pinned(win_av), pinned(win_bv))

    def forward_call(first, step, part, peer, cell, inflow):
        return pl.pallas_call(
            functools.partial(forward_kernel, first),
            out_shape=(
                vmem((streams, depth), BF16),
                vmem(cell_shape, F32),
                vmem(gates_shape, BF16),
                vmem(cell_shape, BF16),
                vmem((streams, depth), BF16),
                vmem((streams, depth), BF16),
                vmem((streams, depth), F32),
            ),
            in_specs=[SMEM] + [VMEM] * 10,
            out_specs=[VMEM] * 7,
            compiler_params=params(8),
            name="forward_step",
        )(
            at_step(step), pinned(part), pinned(peer), pinned(start_hv), pinned(keep_v), pinned(cell), pinned(inflow),
            pinned(rec_av), pinned(rec_bv), pinned(proj_av), pinned(proj_bv),
        )

    def between_call(step, fresh, stacks):
        shapes = (
            hbm((PIECES, steps, streams, 4 * width), BF16),
            hbm((steps,) + cell_shape, F32),
            hbm((PIECES, steps, streams, width), BF16),
            hbm((steps, streams, depth), BF16),
            hbm((steps, streams, depth), BF16),
            hbm((steps, streams, depth), F32),
        )
        inflow, *stacks = pl.pallas_call(
            functools.partial(between_kernel, not stacks),
            out_shape=(vmem(gates_shape, F32),) + shapes,
            in_specs=[SMEM] + [VMEM] * 10 + [ANY] * len(stacks),
            out_specs=[VMEM] + [ANY] * 6,
            scratch_shapes=[pltpu.SemaphoreType.DMA((2 * PIECES + 4,))],
            input_output_aliases={11 + i: 1 + i for i in range(len(stacks))},
            compiler_params=params(8),
            cost_estimate=cost(2 * streams * depth * 8 * cells, 8 * depth * cells * 2),
            name="between",
        )(
            at_step(step), pinned(feats_v), pinned(bias_v), pinned(win_av), pinned(win_bv),
            *(pinned(x) for x in fresh), *(in_hbm(x) for x in stacks),
        )
        return inflow, tuple(stacks)

    def forward_step(step, carry, first=False):
        part, peer, cell, inflow, stacks = carry
        part, cell, *fresh = forward_call(first, step, part, peer, cell, inflow)
        peer = lax.ppermute(part, "gate", across)
        inflow, stacks = between_call(step, (cell, *fresh), stacks)
        return (part, peer, cell, inflow, stacks)

    none = jnp.zeros((streams, depth), BF16)
    carry = forward_step(0, (none, none, start_cv, inflow, ()), True)
    for step in range(1, steps):
        carry = forward_step(step, carry)
    part, peer, cell, _, stacks = carry
    gates_all, cells_all, mixed_all, prev_all, hidden_all, slope_all = stacks

    saved_shapes = (
        vmem(gates_shape, BF16),
        vmem(cell_shape, F32),
        vmem(cell_shape, F32),
        vmem((streams, depth), F32),
        vmem((streams, depth), BF16),
    )
    *saved, hidden_all, slope_all = pl.pallas_call(
        finish_kernel,
        out_shape=saved_shapes + (hbm((steps, streams, depth), BF16), hbm((steps, streams, depth), F32)),
        in_specs=[SMEM, VMEM, VMEM] + [ANY] * 5,
        out_specs=[VMEM] * 5 + [ANY] * 2,
        scratch_shapes=[
            pltpu.VMEM((streams, depth), BF16),
            pltpu.SemaphoreType.DMA((PIECES + 4,)),
            pltpu.SemaphoreType.DMA,
        ],
        input_output_aliases={6: 5, 7: 6},
        compiler_params=params(8),
        name="finish",
    )(
        at_step(steps - 1), pinned(part), pinned(peer), in_hbm(gates_all), in_hbm(cells_all), in_hbm(ups),
        in_hbm(hidden_all), in_hbm(slope_all),
    )

    both_hidden = trade(hidden_all, hidden_all)

    def by_direction(mine, theirs):
        return jnp.stack([jnp.where(own == 0, mine, theirs), jnp.where(own == 0, theirs, mine)])

    hidden_dirs = by_direction(*both_hidden)
    outputs = (inputs.astype(F32) + jnp.transpose(hidden_dirs, (0, 2, 1, 3)).astype(F32)).astype(BF16)
    last_h = jnp.stack([hidden_dirs[0, steps - 1], hidden_dirs[1, 0]], axis=1).astype(F32)
    final_h = jnp.zeros_like(state_h).at[stream_doc].set(last_h)
    last_c = jnp.transpose(cell.reshape(QUARTERS, HALVES, streams, width), (0, 2, 1, 3)).reshape(
        QUARTERS, streams, cells
    )
    last_dirs = by_direction(*trade(last_c[0], last_c[1]))
    final_c = jnp.zeros_like(state_c).at[stream_doc].set(jnp.transpose(last_dirs, (1, 0, 2)))

    rec_at, rec_bt = (jnp.transpose(x, (0, 2, 1)) for x in (rec_a, rec_b))
    proj_at, proj_bt = jnp.transpose(proj_a), jnp.transpose(proj_b)
    rec_atv, rec_btv, proj_atv, proj_btv = place(rec_at, rec_bt, proj_at, proj_bt)

    def backward_call(step, part, peer, grad, saved):
        return pl.pallas_call(
            backward_kernel,
            out_shape=(
                vmem((streams, depth), BF16),
                vmem(cell_shape, F32),
                vmem((streams, depth), BF16),
                vmem(gates_shape, BF16),
            ),
            in_specs=[SMEM] + [VMEM] * 14,
            out_specs=[VMEM] * 4,
            compiler_params=params(8),
            name="backward_step",
        )(
            at_step(step), pinned(part), pinned(peer), pinned(keep_v), pinned(grad),
            pinned(rec_atv), pinned(rec_btv), pinned(proj_atv), pinned(proj_btv),
            *(pinned(x) for x in saved), pinned(start_cv),
        )

    def aside_call(step, dz, raw, stacks):
        shapes = (
            hbm((PIECES, steps, streams, 4 * width), BF16),
            hbm((steps, streams, depth), BF16),
            hbm((steps, streams, depth), F32),
        )
        *outs, dz_all, raw_all, dx_all = pl.pallas_call(
            functools.partial(aside_kernel, not stacks),
            out_shape=saved_shapes + shapes,
            in_specs=[SMEM] + [VMEM] * 4 + [ANY] * (4 + len(stacks)),
            out_specs=[VMEM] * 5 + [ANY] * 3,
            scratch_shapes=[
                pltpu.VMEM((streams, depth), F32),
                pltpu.SemaphoreType.DMA((PIECES + 2,)),
                pltpu.SemaphoreType.DMA((PIECES + 4,)),
            ],
            input_output_aliases={9 + i: 5 + i for i in range(len(stacks))},
            compiler_params=params(8),
            cost_estimate=cost(2 * streams * depth * 8 * cells, 8 * depth * cells * 2),
            name="aside",
        )(
            at_step(step), pinned(dz), pinned(raw), pinned(win_av), pinned(win_bv),
            in_hbm(gates_all), in_hbm(cells_all), in_hbm(ups), in_hbm(slope_all), *(in_hbm(x) for x in stacks),
        )
        return outs, (dz_all, raw_all, dx_all)

    def backward_step(index, carry):
        step = steps - 1 - index
        part, peer, grad, saved, stacks = carry
        part, grad, raw, dz = backward_call(step, part, peer, grad, saved)
        peer = lax.ppermute(part, "gate", across)
        saved, stacks = aside_call(step, dz, raw, stacks)
        return (part, peer, grad, saved, stacks)

    carry = backward_step(0, (none, none, jnp.zeros(cell_shape, F32), saved, ()))
    for index in range(1, steps):
        carry = backward_step(index, carry)
    dz_all, raw_all, dx_all = carry[-1]
    rows = steps * streams
    dz = dz_all.reshape(PIECES, rows, 4 * width)

    def weight_grad(left):
        return jnp.einsum("rk,prn->kpn", left.reshape(rows, depth), dz, preferred_element_type=F32).astype(BF16)

    grad_in = lax.psum_scatter(weight_grad(feats), "batch", scatter_dimension=0, tiled=True)
    grad_rec = lax.psum_scatter(weight_grad(prev_all), "batch", scatter_dimension=0, tiled=True)
    grad_bias = jnp.sum(dz, axis=1, dtype=F32)
    grad_proj = jnp.einsum(
        "ptnc,tnk->kpc", mixed_all, raw_all, preferred_element_type=F32
    ).astype(BF16)
    grad_proj = lax.psum_scatter(grad_proj, "batch", scatter_dimension=0, tiled=True)

    def whole_gates(pieces):
        shaped = pieces.reshape(-1, QUARTERS, HALVES, 4, width)
        return jnp.transpose(shaped, (1, 0, 3, 2, 4)).reshape(QUARTERS, -1, 4, cells)

    def home(quarters):
        return by_direction(*trade(quarters[0], quarters[1])).astype(F32)

    grad_w_in = home(whole_gates(grad_in))
    grad_w_rec = home(whole_gates(grad_rec))
    grad_bias = home(whole_gates(grad_bias[None])[:, 0])
    grad_bias = lax.psum_scatter(grad_bias, "batch", scatter_dimension=2, tiled=True)
    grad_proj = home(jnp.transpose(grad_proj.reshape(-1, QUARTERS, cells), (1, 2, 0)))

    half_cols = depth // 2
    upper = rank // 2
    keep_cols = lax.dynamic_slice_in_dim(dx_all, upper * half_cols, half_cols, 2)
    send_cols = lax.dynamic_slice_in_dim(dx_all, (1 - upper) * half_cols, half_cols, 2).astype(BF16)
    dx_half = keep_cols + lax.ppermute(send_cols, "gate", across).astype(F32)
    up_half = lax.dynamic_slice_in_dim(ups, upper * half_cols, half_cols, 2).astype(F32)
    dx_half = (dx_half + up_half).astype(BF16)
    quarter_cols = half_cols // 2
    mine = lax.dynamic_slice_in_dim(dx_half, own * quarter_cols, quarter_cols, 2)
    theirs = lax.dynamic_slice_in_dim(dx_half, (1 - own) * quarter_cols, quarter_cols, 2)
    dx_dirs = by_direction(*trade(mine, theirs))
    input_grad = jnp.transpose(dx_dirs, (0, 2, 1, 3))
    return (outputs, input_grad, grad_w_in, grad_w_rec, grad_bias, grad_proj, final_h, final_c)


def solution(mesh):
    placed = (
        P(None, "batch", None, None),
        P(None, None, None, "gate"),
        P(None, None, None, "gate"),
        P(None, None, "gate"),
        P(None, "gate", None),
        P("batch", None, None),
        P("batch", None, "gate"),
        P("batch", None),
        P("batch"),
        P(None, "batch", None, None),
    )
    return jax.shard_map(
        body,
        mesh=mesh,
        in_specs=placed,
        out_specs=(
            P(None, "batch", None, None),
            P(None, "batch", None, "gate"),
            P(None, "batch", None, "gate"),
            P(None, "batch", None, "gate"),
            P(None, None, ("gate", "batch")),
            P(None, "gate", "batch"),
            P("batch", None, None),
            P("batch", None, "gate"),
        ),
        check_vma=False,
    )
```

time: 2420 us -> 911 us (0.38)
  waiting for transfers between devices: 1350 us -> 372 us
  matrix products: 371 us -> 39.5 us
  Pallas kernels: 0 us -> 295 us
  blocking collectives: 214 us -> 0 us
  other arithmetic: 219 us -> 23.6 us
  local copies, waits for them, and re-layouts: 231 us -> 105 us
  starting transfers between devices: 2.57 us -> 45.5 us
    reduce_scatter x23 -> x3, waiting for transfers between devices: 946 us -> 362 us  [the longest x1 150 us: body(): lax.psum_scatter(weight_grad(prev_all), 'batch', scatter_dimension=0, til...]
    while x60 -> x0, waiting for transfers between devices: 404 us -> none
    dot_general x88 -> x3, matrix products: 371 us -> 39.5 us  [the longest x2 33.7 us: weight_grad(): jnp.einsum('rk,prn->kpn', left.reshape(rows, depth), dz, preferred_elemen...]
    pallas_call x0 -> x85, Pallas kernels: none -> 295 us  [the longest x20 99.4 us: aside_call(): pl.pallas_call(functools.partial(aside_kernel, not stacks), out_shape=sav...]
    all_gather x40 -> x0, blocking collectives: 214 us -> none  [the longest x20 107 us: backward_step(): lax.all_gather(((summed_share + up_share) * clip_slope).astype(jnp.bfloat...]
    dynamic_update_slice x100 -> x0, other arithmetic: 119 us -> none  [the longest x80 99.6 us: body(): lax.scan(forward_step, (start_h, start_c), (inflow, keep_mask))]
    while x243 -> x0, local copies, waits for them, and re-layouts: 48.7 us -> none
    ppermute x0 -> x52, starting transfers between devices: none -> 45.4 us  [the longest x20 21.9 us: forward_step(): peer = lax.ppermute(part, 'gate', across)]
  transfers between devices with their start and end apart: 45 -> 56, of which waited for: 43 -> 6; matrix products, arithmetic and copies ran while one was open for 10% -> 12% of each run, Pallas kernels for 0% -> 19%
where the time goes in v1:
time: 911 us; the launch traced here: 898 us
  waiting for transfers between devices  372 us (41%)
  Pallas kernels  295 us (32%)
  local copies, waits for them, and re-layouts  105 us (12%)
  starting transfers between devices  45.5 us (5%)
  matrix products  39.5 us (4%)
  other arithmetic  23.6 us (3%)
  between operations  16.7 us (2%)
    reduce_scatter x1, waiting for transfers between devices, body(): lax.psum_scatter(weight_grad(prev_all), 'batch', scatter_dimension=0, til...  150 us
    reduce_scatter x1, waiting for transfers between devices, body(): lax.psum_scatter(weight_grad(feats), 'batch', scatter_dimension=0, tiled=...  147 us
    pallas_call x20, Pallas kernels, aside_call(): pl.pallas_call(functools.partial(aside_kernel, not stacks), out_shape=sav...  99.4 us
    pallas_call x20, Pallas kernels, between_call(): pl.pallas_call(functools.partial(between_kernel, not stacks), out_shape=(...  64.9 us
    reduce_scatter x1, waiting for transfers between devices, body(): lax.psum_scatter(grad_proj, 'batch', scatter_dimension=0, tiled=True)  64.5 us
    pallas_call x20, Pallas kernels, backward_call(): pl.pallas_call(backward_kernel, out_shape=(vmem((streams, depth), BF16),...  62.3 us
    pallas_call x20, Pallas kernels, forward_call(): pl.pallas_call(functools.partial(forward_kernel, first), out_shape=(vmem(...  57.3 us
    dynamic_slice x9, local copies, waits for them, and re-layouts, pick(): return lax.dynamic_index_in_dim(stacked, index, 0, keepdims=False)  41 us
  transfers between devices with their start and end apart: 56, of which 6 were waited for; matrix products, arithmetic and copies ran while one was open for 12% of the time, Pallas kernels for 19%

profile of v1, /device:TPU:8, one launch (start us, length us, event | category | flops | bytes accessed | tf_op | source)
XLA Modules:
  0.0 897.6 jit_solution(17197328118779607116)
XLA Ops:
  7.3 12.7 %constant_dynamic-slice_fusion.1 = (bf16[1,512,4,1024]{3,2,1,0:T(4,128)(2,1)S(1)}, bf16[1,512,4,1024]{3,2,1,0:T(4,128)(2,1)}, bf16[1,512,4,1024]{3,2,1,0:T(4,128)(2,1)}, bf16[1,512,4,1024]{3,2,1,0:T(4,128)(2,1)}) fusion(bf16[2,512,4,1024]{3,2,1,0:T(4,128)(2,1)} %param.175, s32[]{:T(128)S(6)} %select_n.502, s32[]{:T(128)S(6)} %select_n.501, ...), kind=kLoop, calls=%fused_computation.63 | loop fusion | bytes 33554440 | tf_op jit(solution)/shard_map/jit(dynamic_index_in_dim)/dynamic_slice | solution.py:255
  23.3 7.5 copy.434
  39.8 5.7 copy.480
  65.0 6.3 copy.439.refs_1_
  221.6 7.5 copy.433
  259.7 4.9 aside.21
  268.8 4.9 aside.22
  278.0 4.9 aside.23
  287.1 4.9 aside.24
  296.1 4.9 aside.25
  305.3 5.3 aside.26
  314.6 4.9 aside.27
  323.8 4.9 aside.28
  332.8 4.9 aside.29
  342.1 4.9 aside.30
  351.1 4.9 aside.31
  360.3 4.9 aside.32
  369.3 5.1 aside.33
  378.6 4.9 aside.34
  387.6 4.9 aside.35
  396.7 4.9 aside.36
  405.7 5.0 aside.37
  415.0 4.9 aside.38
  423.6 5.9 aside.39
  429.5 6.7 convert_reduce_fusion
  441.6 5.9 bitcast_convert_fusion.2
  447.6 16.7 %bitcast_convert_fusion = bf16[512,4,2048]{2,0,1:T(8,128)(2,1)} fusion(bf16[4,20,48,2048]{3,2,1,0:T(8,128)(2,1)} %get-tuple-element.1072, bf16[20,48,512]{2,1,0:T(8,128)(2,1)S(1)} %copy-done.56), kind=kOutput, calls=%fused_computation.5 | convolution fusion | flops 8057257984 | bytes 25100288 | tf_op jit(solution)/shard_map/rk,prn->kpn/dot_general | solution.py:483
  465.9 16.9 %bitcast_convert_fusion.1 = bf16[512,4,2048]{2,0,1:T(8,128)(2,1)} fusion(bf16[4,20,48,2048]{3,2,1,0:T(8,128)(2,1)} %get-tuple-element.1072, bf16[2,48,20,512]{3,1,2,0:T(8,128)(2,1)S(1)} %copy-done.59, s32[]{:T(128)S(6)} %select_n.501), kind=kOutput, calls=%fused_computation.6 | convolution fusion | flops 8057257984 | bytes 25100292 | tf_op jit(solution)/shard_map/rk,prn->kpn/dot_general | solution.py:483
  495.9 7.2 collective-permute-done.45
  510.6 64.5 %reduce-scatter.11.cloned.1.call-done = bf16[64,4,512]{2,0,1:T(8,128)(2,1)} async-done(((bf16[512,4,512]{2,0,1:T(8,128)(2,1)}), bf16[64,4,512]{2,0,1:T(8,128)(2,1)}) %reduce-scatter.11.cloned.1.call-update) | async-done | bytes 262160 | tf_op jit(solution)/shard_map/reduce_scatter | solution.py:491
  577.0 150.1 %reduce-scatter.9.cloned.1.call-done = bf16[64,4,2048]{2,0,1:T(8,128)(2,1)} async-done(((bf16[512,4,2048]{2,0,1:T(8,128)(2,1)}), bf16[64,4,2048]{2,0,1:T(8,128)(2,1)}) %reduce-scatter.9.cloned.1.call-update) | async-done | bytes 1048592 | tf_op jit(solution)/shard_map/reduce_scatter | solution.py:486
  731.7 147.4 %reduce-scatter.7.cloned.1.call-done = bf16[64,4,2048]{2,0,1:T(8,128)(2,1)} async-done(((bf16[512,4,2048]{2,0,1:T(8,128)(2,1)}), bf16[64,4,2048]{2,0,1:T(8,128)(2,1)}) %reduce-scatter.7.cloned.1.call-update) | async-done | bytes 1048592 | tf_op jit(solution)/shard_map/reduce_scatter | solution.py:485
  (504 shorter events, 331.3 us)
Async XLA Ops:
  7.2 500.9 %reduce-scatter.13.cloned.1.call-start = ((), (), s32[]{:S(2)}) async-start(), calls=%async_computation.7 | async-start | bytes 589824
  23.3 30.9 %collective-permute-start.4 = (bf16[4,512,1024]{2,1,0:T(8,128)(2,1)}, bf16[4,512,1024]{2,1,0:T(8,128)(2,1)}, u32[]{:S(2)}, u32[]{:S(2)}) collective-permute-start(bf16[4,512,1024]{2,1,0:T(8,128)(2,1)} %bitcast.148), channel_id=1, source_target_pairs={{0,1},{1,0},{2,3},{3,2},{4,5},{5,4},{6,7},{7,6},{8,9},{9,8},{10,11... | collective-permute-start | bytes 12582920 | tf_op jit(solution)/shard_map/ppermute | solution.py:258
  30.8 34.2 %collective-permute-start = (bf16[4,512,1024]{1,2,0:T(8,128)(2,1)}, bf16[4,512,1024]{1,2,0:T(8,128)(2,1)}, u32[]{:S(2)}, u32[]{:S(2)}) collective-permute-start(bf16[4,512,1024]{1,2,0:T(8,128)(2,1)} %bitcast.163), channel_id=1, source_target_pairs={{0,1},{1,0},{2,3},{3,2},{4,5},{5,4},{6,7},{7,6},{8,9},{9,8},{10,11... | collective-permute-start | bytes 12582920 | tf_op jit(solution)/shard_map/ppermute | solution.py:258
  31.3 18.2 %collective-permute-start.3 = (bf16[4,1024]{1,0:T(4,128)(2,1)S(1)}, bf16[4,1024]{1,0:T(4,128)(2,1)S(1)}, u32[]{:S(2)}, u32[]{:S(2)}) collective-permute-start(bf16[4,1024]{1,0:T(4,128)(2,1)S(1)} %get-tuple-element.1109), channel_id=1, source_target_pairs={{0,1},{1,0},{2,3},{3,2},{4,5},{5,4},{6,7},{7,6},{8,9},{9,8},{10,11... | collective-permute-start | bytes 24584 | tf_op jit(solution)/shard_map/ppermute | solution.py:258
  34.1 16.2 %collective-permute-start.2 = (f32[48,1024]{1,0:T(8,128)}, f32[48,1024]{1,0:T(8,128)}, u32[]{:S(2)}, u32[]{:S(2)}) collective-permute-start(f32[48,1024]{1,0:T(8,128)} %bitcast.150), channel_id=1, source_target_pairs={{0,1},{1,0},{2,3},{3,2},{4,5},{5,4},{6,7},{7,6},{8,9},{9,8},{10,11... | collective-permute-start | bytes 589832 | tf_op jit(solution)/shard_map/ppermute | solution.py:258
  37.6 15.3 %collective-permute-start.1 = (bf16[1024,512]{0,1:T(8,128)(2,1)}, bf16[1024,512]{0,1:T(8,128)(2,1)S(1)}, u32[]{:S(2)}, u32[]{:S(2)}) collective-permute-start(bf16[1024,512]{0,1:T(8,128)(2,1)} %bitcast.170), channel_id=1, source_target_pairs={{0,1},{1,0},{2,3},{3,2},{4,5},{5,4},{6,7},{7,6},{8,9},{9,8},{10,11... | collective-permute-start | bytes 3145736 | tf_op jit(solution)/shard_map/ppermute | solution.py:258
  219.7 24.6 %collective-permute-start.24 = (bf16[48,512]{1,0:T(8,128)(2,1)S(1)}, bf16[48,512]{1,0:T(8,128)(2,1)S(1)}, u32[]{:S(2)}, u32[]{:S(2)}) collective-permute-start(bf16[48,512]{1,0:T(8,128)(2,1)S(1)} %get-tuple-element.813.p_ref), channel_id=1, source_target_pairs={{0,2},{1,3},{2,0},{3,1},{4,6},{5,7},{6,4},{7,5},{8,10},{9,11},{10,... | collective-permute-start | bytes 147464 | tf_op jit(solution)/shard_map/ppermute | solution.py:367
  249.6 6.0 collective-permute-start.26
  267.6 6.0 collective-permute-start.28
  277.0 5.9 collective-permute-start.29
  286.0 6.1 collective-permute-start.30
  295.1 5.9 collective-permute-start.31
  304.1 6.4 collective-permute-start.32
  313.6 5.9 collective-permute-start.33
  322.6 6.0 collective-permute-start.34
  331.8 5.9 collective-permute-start.35
  341.0 6.1 collective-permute-start.36
  350.1 5.9 collective-permute-start.37
  359.1 6.1 collective-permute-start.38
  368.2 6.1 collective-permute-start.39
  377.4 6.1 collective-permute-start.40
  386.6 5.9 collective-permute-start.41
  395.6 6.1 collective-permute-start.42
  404.7 6.1 collective-permute-start.43
  413.9 6.0 collective-permute-start.44
  441.5 133.6 %reduce-scatter.11.cloned.1.call-start = ((), (), s32[]{:S(2)}) async-start(), calls=%async_computation.6 | async-start | bytes 2359296 | tf_op jit(solution)/shard_map/reduce_scatter | solution.py:491
  447.5 279.6 %reduce-scatter.9.cloned.1.call-start = ((), (), s32[]{:S(2)}) async-start(), calls=%async_computation.5 | async-start | bytes 9437184 | tf_op jit(solution)/shard_map/reduce_scatter | solution.py:486
  464.3 414.7 %reduce-scatter.7.cloned.1.call-start = ((), (), s32[]{:S(2)}) async-start(), calls=%async_computation.4 | async-start | bytes 9437184 | tf_op jit(solution)/shard_map/reduce_scatter | solution.py:485
  482.8 7.6 collective-permute-start.25
  489.5 13.6 %collective-permute-start.45 = (bf16[20,48,256]{2,1,0:T(8,128)(2,1)}, bf16[20,48,256]{2,1,0:T(8,128)(2,1)}, u32[]{:S(2)}, u32[]{:S(2)}) collective-permute-start(bf16[20,48,256]{2,1,0:T(8,128)(2,1)} %dynamic-slice_convert_fusion), channel_id=1, source_target_pairs={{0,2},{1,3},{2,0},{3,1},{4,6},{5,7},{6,4},{7,5},{8,10},{9,11},{10,... | collective-permute-start | bytes 1474568 | tf_op jit(solution)/shard_map/ppermute | solution.py:510
  576.9 154.0 %collective-permute-start.50 = (bf16[1024,64]{0,1:T(8,128)(2,1)S(1)}, bf16[1024,64]{0,1:T(8,128)(2,1)S(1)}, u32[]{:S(2)}, u32[]{:S(2)}) collective-permute-start(bf16[1024,64]{0,1:T(8,128)(2,1)S(1)} %bitcast.176), channel_id=1, source_target_pairs={{0,1},{1,0},{2,3},{3,2},{4,5},{5,4},{6,7},{7,6},{8,9},{9,8},{10,11... | collective-permute-start | bytes 393224 | tf_op jit(solution)/shard_map/ppermute | solution.py:258
  731.0 154.8 %collective-permute-start.48 = (bf16[64,4,1024]{2,1,0:T(4,128)(2,1)}, bf16[64,4,1024]{2,1,0:T(4,128)(2,1)S(1)}, u32[]{:S(2)}, u32[]{:S(2)}) collective-permute-start(bf16[64,4,1024]{2,1,0:T(4,128)(2,1)} %squeeze.82), channel_id=1, source_target_pairs={{0,1},{1,0},{2,3},{3,2},{4,5},{5,4},{6,7},{7,6},{8,9},{9,8},{10,11... | collective-permute-start | bytes 1572872 | tf_op jit(solution)/shard_map/ppermute | solution.py:258
  (136 other events, 762.8 us)
Sparse Core Ops, SparseCore 0:
  441.6 62.4 reduce-scatter.12
  508.7 66.4 reduce-scatter.10
  579.2 147.7 reduce-scatter.8
  730.5 148.4 reduce-scatter.6

commit v2 on v1

--- a/solution.py
+++ b/solution.py
@@ -12,6 +12,7 @@
 QUARTERS, HALVES = 2, 2
 PIECES = QUARTERS * HALVES
 MIB = 2**20
+SHARES = (0.3, 0.3, 0.2, 0.1, 0.1)
 
 VMEM = pl.BlockSpec(memory_space=pltpu.VMEM)
 SMEM = pl.BlockSpec(memory_space=pltpu.SMEM)
@@ -101,14 +102,15 @@
     first, step_ref, feat_ref, bias_ref, wa_ref, wb_ref, cell_ref, gates_ref, mixed_ref, prev_ref, hidden_ref, slope_ref,
     *refs,
 ):
-    out_ref, gates_all, cells_all, mixed_all, prev_all, hidden_all, slope_all, sems = refs if first else refs[6:]
+    out_ref, gates_all, cells_all, mixed_all, prev_all, feat_all, hidden_all, slope_all, sems = refs if first else refs[7:]
     step, time, time_before, time_after = (step_ref[i] for i in range(4))
     copies = [pltpu.make_async_copy(gates_ref.at[i], gates_all.at[i, step], sems.at[i]) for i in range(PIECES)]
     copies += [
-        pltpu.make_async_copy(mixed_ref.at[i], mixed_all.at[i, time], sems.at[PIECES + i]) for i in range(PIECES)
+        pltpu.make_async_copy(mixed_ref.at[i], mixed_all.at[i, step], sems.at[PIECES + i]) for i in range(PIECES)
     ]
     copies.append(pltpu.make_async_copy(cell_ref, cells_all.at[step], sems.at[2 * PIECES]))
-    copies.append(pltpu.make_async_copy(prev_ref, prev_all.at[time], sems.at[2 * PIECES + 1]))
+    copies.append(pltpu.make_async_copy(prev_ref, prev_all.at[step], sems.at[2 * PIECES + 1]))
+    copies.append(pltpu.make_async_copy(feat_ref.at[time], feat_all.at[step], sems.at[2 * PIECES + 4]))
     if not first:
         copies.append(pltpu.make_async_copy(hidden_ref, hidden_all.at[time_before], sems.at[2 * PIECES + 2]))
         copies.append(pltpu.make_async_copy(slope_ref, slope_all.at[step - 1], sems.at[2 * PIECES + 3]))
@@ -200,37 +202,48 @@
 
 
 def aside_kernel(
-    first, step_ref, dz_ref, raw_ref, wa_ref, wb_ref, gates_all, cells_all, ups_all, slope_all, *refs
+    first, opens, step_ref, dz_ref, raw_ref, gates_all, cells_all, ups_all, slope_all, *refs
 ):
-    gates_ref, cell_ref, prev_ref, slope_ref, up_ref, dz_all, raw_all, dx_all, dx_buf, sems, fetch_sems = (
-        refs if first else refs[3:]
-    )
-    step, time, time_before = (step_ref[i] for i in range(3))
+    refs = refs[(0 if first else 4) + (0 if opens else 2) :]
+    gates_ref, cell_ref, prev_ref, slope_ref, up_ref = refs[:5]
+    dz_all, raw_all, near_all, far_all, near_out, far_out, sems, fetch_sems = refs[5:]
+    step, time_before = step_ref[0], step_ref[2]
+    slot, low, high = step_ref[4], step_ref[5], step_ref[6]
     before = jnp.maximum(step - 1, 0)
     copies = fetches(
         before, time_before, (gates_all, cells_all, ups_all), (gates_ref, cell_ref, prev_ref, up_ref), fetch_sems
     )
     copies.append(pltpu.make_async_copy(slope_all.at[before], slope_ref, fetch_sems.at[PIECES + 3]))
-    copies += [pltpu.make_async_copy(dz_ref.at[i], dz_all.at[i, time], sems.at[i]) for i in range(PIECES)]
-    copies.append(pltpu.make_async_copy(raw_ref, raw_all.at[time], sems.at[PIECES]))
+    copies += [pltpu.make_async_copy(dz_ref.at[i], dz_all.at[i, step], sems.at[i]) for i in range(PIECES)]
+    copies.append(pltpu.make_async_copy(raw_ref, raw_all.at[step], sems.at[PIECES]))
+    copies.append(pltpu.make_async_copy(dz_ref.at[low], near_all.at[step], sems.at[PIECES + 1]))
+    copies.append(pltpu.make_async_copy(dz_ref.at[HALVES + high], far_all.at[step], sems.at[PIECES + 2]))
+    copies.append(pltpu.make_async_copy(dz_ref.at[1 - low], near_out.at[slot], sems.at[PIECES + 3]))
+    copies.append(pltpu.make_async_copy(dz_ref.at[HALVES + 1 - high], far_out.at[slot], sems.at[PIECES + 4]))
     for copy in copies:
         copy.start()
-    part = jnp.zeros(dx_buf.shape, F32)
-    for piece, quarter, width, cols in pieces((wa_ref, wb_ref), 2):
-        w_ref = (wa_ref, wb_ref)[quarter]
-        for gate in range(4):
-            part = part + lax.dot_general(
-                dz_ref[piece, :, gate * width : (gate + 1) * width],
-                w_ref[gate, :, cols],
-                (((1,), (1,)), ((), ())),
-                preferred_element_type=F32,
-            )
-    dx_buf[...] = part
-    last = pltpu.make_async_copy(dx_buf, dx_all.at[time], sems.at[PIECES + 1])
-    last.start()
     for copy in copies:
         copy.wait()
-    last.wait()
+
+
+def input_grad_kernel(step_ref, dz_ref, wa_ref, wb_ref, out_ref, acc_ref):
+    piece, gate = pl.program_id(0), pl.program_id(1)
+    steps, streams, width = dz_ref.shape[1:]
+
+    @pl.when((piece == 0) & (gate == 0))
+    def _():
+        acc_ref[...] = jnp.zeros(acc_ref.shape, F32)
+
+    weights = jnp.where(piece < HALVES, wa_ref[0], wb_ref[0])
+    acc_ref[...] += lax.dot_general(
+        dz_ref[0].reshape(steps * streams, width), weights, (((1,), (1,)), ((), ())), preferred_element_type=F32
+    )
+
+    @pl.when((piece == PIECES - 1) & (gate == 3))
+    def _():
+        for step in range(steps):
+            time = step_ref[0] + step_ref[1] * step
+            out_ref[time] = acc_ref[step * streams : (step + 1) * streams, :]
 
 
 def params(mib):
@@ -343,14 +356,15 @@
             hbm((PIECES, steps, streams, width), BF16),
             hbm((steps, streams, depth), BF16),
             hbm((steps, streams, depth), BF16),
+            hbm((steps, streams, depth), BF16),
             hbm((steps, streams, depth), F32),
         )
         inflow, *stacks = pl.pallas_call(
             functools.partial(between_kernel, not stacks),
             out_shape=(vmem(gates_shape, F32),) + shapes,
             in_specs=[SMEM] + [VMEM] * 10 + [ANY] * len(stacks),
-            out_specs=[VMEM] + [ANY] * 6,
-            scratch_shapes=[pltpu.SemaphoreType.DMA((2 * PIECES + 4,))],
+            out_specs=[VMEM] + [ANY] * 7,
+            scratch_shapes=[pltpu.SemaphoreType.DMA((2 * PIECES + 5,))],
             input_output_aliases={11 + i: 1 + i for i in range(len(stacks))},
             compiler_params=params(8),
             cost_estimate=cost(2 * streams * depth * 8 * cells, 8 * depth * cells * 2),
@@ -373,7 +387,7 @@
     for step in range(1, steps):
         carry = forward_step(step, carry)
     part, peer, cell, _, stacks = carry
-    gates_all, cells_all, mixed_all, prev_all, hidden_all, slope_all = stacks
+    gates_all, cells_all, mixed_all, prev_all, feat_all, hidden_all, slope_all = stacks
 
     saved_shapes = (
         vmem(gates_shape, BF16),
@@ -438,70 +452,163 @@
             *(pinned(x) for x in saved), pinned(start_cv),
         )
 
-    def aside_call(step, dz, raw, stacks):
+    n_batch = lax.axis_size("batch")
+    spot = lax.axis_index("batch")
+    low, high = spot % 2, (spot // 2) % 2
+    near_swap = [(i, i ^ 1) for i in range(n_batch)]
+    far_swap = [(i, i ^ 2) for i in range(n_batch)]
+
+    def aside_call(step, slot, slots, dz, raw, stacks, sends):
+        piece_shape = (streams, 4 * width)
         shapes = (
-            hbm((PIECES, steps, streams, 4 * width), BF16),
+            hbm((PIECES, steps) + piece_shape, BF16),
             hbm((steps, streams, depth), BF16),
-            hbm((steps, streams, depth), F32),
+            hbm((steps,) + piece_shape, BF16),
+            hbm((steps,) + piece_shape, BF16),
+            hbm((slots,) + piece_shape, BF16),
+            hbm((slots,) + piece_shape, BF16),
         )
-        *outs, dz_all, raw_all, dx_all = pl.pallas_call(
-            functools.partial(aside_kernel, not stacks),
+        kept = len(stacks)
+        aliases = {7 + i: 5 + i for i in range(kept)}
+        aliases.update({7 + kept + i: 9 + i for i in range(len(sends))})
+        out = pl.pallas_call(
+            functools.partial(aside_kernel, not stacks, not sends),
             out_shape=saved_shapes + shapes,
-            in_specs=[SMEM] + [VMEM] * 4 + [ANY] * (4 + len(stacks)),
-            out_specs=[VMEM] * 5 + [ANY] * 3,
+            in_specs=[SMEM] + [VMEM] * 2 + [ANY] * (4 + kept + len(sends)),
+            out_specs=[VMEM] * 5 + [ANY] * 6,
             scratch_shapes=[
-                pltpu.VMEM((streams, depth), F32),
-                pltpu.SemaphoreType.DMA((PIECES + 2,)),
+                pltpu.SemaphoreType.DMA((PIECES + 5,)),
                 pltpu.SemaphoreType.DMA((PIECES + 4,)),
             ],
-            input_output_aliases={9 + i: 5 + i for i in range(len(stacks))},
+            input_output_aliases=aliases,
             compiler_params=params(8),
-            cost_estimate=cost(2 * streams * depth * 8 * cells, 8 * depth * cells * 2),
+            cost_estimate=cost(0, 8 * MIB),
             name="aside",
         )(
-            at_step(step), pinned(dz), pinned(raw), pinned(win_av), pinned(win_bv),
-            in_hbm(gates_all), in_hbm(cells_all), in_hbm(ups), in_hbm(slope_all), *(in_hbm(x) for x in stacks),
+            jnp.concatenate([at_step(step), jnp.stack([jnp.int32(slot), low, high])]), pinned(dz), pinned(raw),
+            in_hbm(gates_all), in_hbm(cells_all), in_hbm(ups), in_hbm(slope_all), *(in_hbm(x) for x in (*stacks, *sends)),
         )
-        return outs, (dz_all, raw_all, dx_all)
-
-    def backward_step(index, carry):
-        step = steps - 1 - index
-        part, peer, grad, saved, stacks = carry
-        part, grad, raw, dz = backward_call(step, part, peer, grad, saved)
-        peer = lax.ppermute(part, "gate", across)
-        saved, stacks = aside_call(step, dz, raw, stacks)
-        return (part, peer, grad, saved, stacks)
-
-    carry = backward_step(0, (none, none, jnp.zeros(cell_shape, F32), saved, ()))
-    for index in range(1, steps):
-        carry = backward_step(index, carry)
-    dz_all, raw_all, dx_all = carry[-1]
+        return out[:5], tuple(out[5:9]), tuple(out[9:])
+
+    def swapped(array, pairs):
+        return lax.ppermute(array, "batch", pairs)
+
+    carry = (none, none, jnp.zeros(cell_shape, F32), saved, ())
+    top, near_in, far_in = steps, [], []
+    for index, share in enumerate(SHARES):
+        slots = top if index == len(SHARES) - 1 else round(share * steps)
+        sends = ()
+        for step in range(top - 1, top - slots - 1, -1):
+            part, peer, grad, saved, stacks = carry
+            part, grad, raw, dz = backward_call(step, part, peer, grad, saved)
+            peer = lax.ppermute(part, "gate", across)
+            saved, stacks, sends = aside_call(step, step - (top - slots), slots, dz, raw, stacks, sends)
+            carry = (part, peer, grad, saved, stacks)
+        top -= slots
+        near_in.insert(0, swapped(sends[0], near_swap))
+        far_in.insert(0, swapped(sends[1], far_swap))
+    dz_all, raw_all, near_all, far_all = carry[-1]
     rows = steps * streams
-    dz = dz_all.reshape(PIECES, rows, 4 * width)
-
-    def weight_grad(left):
-        return jnp.einsum("rk,prn->kpn", left.reshape(rows, depth), dz, preferred_element_type=F32).astype(BF16)
-
-    grad_in = lax.psum_scatter(weight_grad(feats), "batch", scatter_dimension=0, tiled=True)
-    grad_rec = lax.psum_scatter(weight_grad(prev_all), "batch", scatter_dimension=0, tiled=True)
-    grad_bias = jnp.sum(dz, axis=1, dtype=F32)
-    grad_proj = jnp.einsum(
-        "ptnc,tnk->kpc", mixed_all, raw_all, preferred_element_type=F32
-    ).astype(BF16)
-    grad_proj = lax.psum_scatter(grad_proj, "batch", scatter_dimension=0, tiled=True)
-
-    def whole_gates(pieces):
-        shaped = pieces.reshape(-1, QUARTERS, HALVES, 4, width)
-        return jnp.transpose(shaped, (1, 0, 3, 2, 4)).reshape(QUARTERS, -1, 4, cells)
-
-    def home(quarters):
-        return by_direction(*trade(quarters[0], quarters[1])).astype(F32)
-
-    grad_w_in = home(whole_gates(grad_in))
-    grad_w_rec = home(whole_gates(grad_rec))
-    grad_bias = home(whole_gates(grad_bias[None])[:, 0])
+
+    turn = jnp.where(own == 0, jnp.array([0, 1], jnp.int32), jnp.array([steps - 1, -1], jnp.int32))
+    dx_all = pl.pallas_call(
+        input_grad_kernel,
+        out_shape=jax.ShapeDtypeStruct((steps, streams, depth), F32),
+        grid_spec=pltpu.PrefetchScalarGridSpec(
+            num_scalar_prefetch=1,
+            grid=(PIECES, 4),
+            in_specs=[
+                pl.BlockSpec((1, steps, streams, width), lambda p, g, turn: (p, 0, 0, g)),
+                pl.BlockSpec(
+                    (1, depth, width), lambda p, g, turn: (jnp.where(p < 2, g, 3), 0, jnp.where(p < 2, p, 1))
+                ),
+                pl.BlockSpec(
+                    (1, depth, width), lambda p, g, turn: (jnp.where(p < 2, 0, g), 0, jnp.where(p < 2, 0, p - 2))
+                ),
+            ],
+            out_specs=pl.BlockSpec((steps, streams, depth), lambda p, g, turn: (0, 0, 0)),
+            scratch_shapes=[pltpu.VMEM((rows, depth), F32)],
+        ),
+        compiler_params=params(24),
+        cost_estimate=cost(2 * rows * depth * 8 * cells, 8 * depth * cells * 4),
+        name="input_grad",
+    )(turn, dz_all, win_a, win_b)
+
+    def line_sum(chunks, stride, count):
+        here = (spot // stride) % count
+
+        def chunk(index):
+            return lax.dynamic_index_in_dim(chunks, jnp.clip(index, 0, count - 1), 0, keepdims=False)
+
+        def at(device):
+            return (device // stride) % count
+
+        if count == 2:
+            pairs = [(i, i + stride if at(i) == 0 else i - stride) for i in range(n_batch)]
+            return chunk(here).astype(F32) + swapped(chunk(1 - here), pairs).astype(F32)
+        up, down = None, None
+        for slot in range(1, count):
+            rise, fall = chunk(here + count - slot), chunk(here - count + slot)
+            if slot > 1:
+                rise = (rise.astype(F32) + up.astype(F32)).astype(BF16)
+                fall = (fall.astype(F32) + down.astype(F32)).astype(BF16)
+            up = swapped(rise, [(i, i + stride) for i in range(n_batch) if at(i) < min(slot, count - 1)])
+            down = swapped(fall, [(i, i - stride) for i in range(n_batch) if at(i) > max(count - 1 - slot, 0)])
+        return chunk(here).astype(F32) + up.astype(F32) + down.astype(F32)
+
+    line = n_batch // 2
+    share_rows = depth // n_batch
+
+    def own_half(mine, theirs, index):
+        return jnp.stack([jnp.where(index == 0, mine, theirs), jnp.where(index == 0, theirs, mine)])
+
+    def finish_halves(halves, index, pairs):
+        mine = lax.dynamic_index_in_dim(halves, index, 0, keepdims=False)
+        theirs = lax.dynamic_index_in_dim(halves, 1 - index, 0, keepdims=False)
+        return own_half(mine, swapped(theirs, pairs), index)
+
+    def near_sum(grad):
+        return line_sum(grad.reshape(line, 2, share_rows, -1), 2, line).astype(BF16)
+
+    def far_sum(grad):
+        chunks = jnp.moveaxis(grad.reshape(line, 2, share_rows, -1), 1, 0)
+        mine = line_sum(chunks, 1, 2).astype(BF16)
+        return line_sum(mine.reshape(line // 2, 2, share_rows, -1), 4, line // 2).astype(BF16)
+
+    def rows_of(stacked):
+        return stacked.reshape(rows, -1)
+
+    def product(left, right):
+        return lax.dot_general(rows_of(left), rows_of(right), (((0,), (0,)), ((), ())), preferred_element_type=F32)
+
+    near_in, far_in = jnp.concatenate(near_in, axis=0), jnp.concatenate(far_in, axis=0)
+    near_left = [(x, swapped(x, near_swap)) for x in (feat_all, prev_all)]
+    far_left = [(x, swapped(x, far_swap)) for x in (feat_all, prev_all)]
+    near_sums = [
+        near_sum((product(mine, near_all) + product(theirs, near_in)).astype(BF16)) for mine, theirs in near_left
+    ]
+    far_sums = [far_sum((product(mine, far_all) + product(theirs, far_in)).astype(BF16)) for mine, theirs in far_left]
+    near_sums = [finish_halves(x, low, near_swap) for x in near_sums]
+    far_sums = [finish_halves(x, high, far_swap) for x in far_sums]
+
+    grad_bias = jnp.sum(dz_all, axis=(1, 2), dtype=F32)
+    grad_proj = jnp.einsum("ptnc,tnk->kpc", mixed_all, raw_all, preferred_element_type=F32).astype(BF16)
+    grad_proj = line_sum(jnp.moveaxis(grad_proj.reshape(line, 2, share_rows, -1), 1, 0), 1, 2).astype(BF16)
+    grad_proj = line_sum(grad_proj, 2, line).astype(BF16)
+
+    def gate_rows(halves):
+        shaped = halves.reshape(HALVES, -1, 4, width)
+        return jnp.transpose(shaped, (1, 2, 0, 3)).reshape(-1, 4, cells)
+
+    def home(mine, theirs):
+        return by_direction(*trade(mine, theirs)).astype(F32)
+
+    grad_w_in, grad_w_rec = (home(gate_rows(near), gate_rows(far)) for near, far in zip(near_sums, far_sums))
+    grad_bias = grad_bias.reshape(QUARTERS, HALVES, 1, 4 * width)
+    grad_bias = home(gate_rows(grad_bias[0])[0], gate_rows(grad_bias[1])[0])
     grad_bias = lax.psum_scatter(grad_bias, "batch", scatter_dimension=2, tiled=True)
-    grad_proj = home(jnp.transpose(grad_proj.reshape(-1, QUARTERS, cells), (1, 2, 0)))
+    grad_proj = grad_proj.reshape(share_rows, QUARTERS, cells)
+    grad_proj = home(jnp.transpose(grad_proj[:, 0]), jnp.transpose(grad_proj[:, 1]))
 
     half_cols = depth // 2
     upper = rank // 2

time: 911 us -> 872 us (0.957)
  waiting for transfers between devices: 372 us -> 250 us
  starting transfers between devices: 45.5 us -> 103 us
  local copies, waits for them, and re-layouts: 105 us -> 147 us
  Pallas kernels: 295 us -> 264 us
  other arithmetic: 23.6 us -> 43.9 us
    reduce_scatter x3 -> x0, waiting for transfers between devices: 362 us -> none  [the longest x1 150 us: body(): lax.psum_scatter(weight_grad(prev_all), 'batch', scatter_dimension=0, til...]
    ppermute x19 -> x60, waiting for transfers between devices: 0.05 us -> 191 us  [the longest x41 185 us: swapped(): return lax.ppermute(array, 'batch', pairs)]
    ppermute x19 -> x60, starting transfers between devices: 20.6 us -> 76.7 us  [the longest x41 58.8 us: swapped(): return lax.ppermute(array, 'batch', pairs)]
    unnamed x5 -> x2, waiting for transfers between devices: 0.07 us -> 55.4 us
    unnamed x234 -> x322, local copies, waits for them, and re-layouts: 30 us -> 63 us
    pallas_call x20 -> x21, Pallas kernels: 99.4 us -> 73.6 us  [the longest x20 57.4 us: aside_call(): pl.pallas_call(functools.partial(aside_kernel, not stacks, not sends), ou...]
    convert_element_type x3 -> x20, other arithmetic: 4.81 us -> 17.9 us  [the longest x6 5.36 us: line_sum(): rise = (rise.astype(F32) + up.astype(F32)).astype(BF16)]
    dot_general x2 -> x8, matrix products: 33.7 us -> 30.7 us  [product(): lax.dot_general(rows_of(left), rows_of(right), (((0,), (0,)), ((), ())),...]
  transfers between devices with their start and end apart: 56 -> 94, of which waited for: 6 -> 46; matrix products, arithmetic and copies ran while one was open for 12% -> 18% of each run, Pallas kernels for 19% -> 18%
where the time goes in v2:
time: 872 us; the launch traced here: 859 us
  Pallas kernels  264 us (30%)
  waiting for transfers between devices  250 us (29%)
  local copies, waits for them, and re-layouts  147 us (17%)
  starting transfers between devices  103 us (12%)
  other arithmetic  43.9 us (5%)
  matrix products  33.5 us (4%)
  between operations  17.2 us (2%)
    ppermute x41, waiting for transfers between devices, swapped(): return lax.ppermute(array, 'batch', pairs)  185 us
    unnamed x322, local copies, waits for them, and re-layouts  63 us
    pallas_call x20, Pallas kernels, between_call(): pl.pallas_call(functools.partial(between_kernel, not stacks), out_shape=(...  61.3 us
    pallas_call x20, Pallas kernels, backward_call(): pl.pallas_call(backward_kernel, out_shape=(vmem((streams, depth), BF16),...  60.9 us
    ppermute x41, starting transfers between devices, swapped(): return lax.ppermute(array, 'batch', pairs)  58.8 us
    pallas_call x20, Pallas kernels, aside_call(): pl.pallas_call(functools.partial(aside_kernel, not stacks, not sends), ou...  57.4 us
    pallas_call x20, Pallas kernels, forward_call(): pl.pallas_call(functools.partial(forward_kernel, first), out_shape=(vmem(...  56.8 us
    unnamed x2, waiting for transfers between devices  55.4 us
  transfers between devices with their start and end apart: 94, of which 46 were waited for; matrix products, arithmetic and copies ran while one was open for 18% of the time, Pallas kernels for 18%

profile of v2, /device:TPU:8, one launch (start us, length us, event | category | flops | bytes accessed | tf_op | source)
XLA Modules:
  0.0 858.7 jit_solution(925250780520357361)
XLA Ops:
  7.3 12.8 %constant_dynamic-slice_fusion.1 = (bf16[1,512,4,1024]{3,2,1,0:T(4,128)(2,1)S(1)}, bf16[1,512,4,1024]{3,2,1,0:T(4,128)(2,1)}, bf16[1,512,4,1024]{3,2,1,0:T(4,128)(2,1)}, bf16[1,512,4,1024]{3,2,1,0:T(4,128)(2,1)}) fusion(bf16[2,512,4,1024]{3,2,1,0:T(4,128)(2,1)} %param.177, s32[]{:T(128)S(6)} %select_n.641, s32[]{:T(128)S(6)} %select_n.640, ...), kind=kLoop, calls=%fused_computation.143 | loop fusion | bytes 33554440 | tf_op jit(solution)/shard_map/jit(dynamic_index_in_dim)/dynamic_slice | solution.py:268
  23.4 7.6 copy.500
  44.0 5.7 copy.548
  67.0 6.3 copy.505.refs_1_
  231.9 7.6 copy.499
  248.9 3.8 copy-done.12
  253.3 4.3 between.39
  411.5 3.7 backward_step.39
  415.2 3.9 aside.39
  419.1 6.7 fusion.83
  425.8 4.4 fusion.82
  430.2 4.4 fusion.81
  434.6 4.5 fusion.80
  448.2 7.6 convert_reduce_fusion
  456.9 5.5 copy-done.2
  462.4 16.3 %input_grad.1 = f32[20,48,512]{2,1,0:T(8,128)S(1)} custom-call(s32[2]{0:T(128)S(1)} %broadcast_select_fusion.1.step_ref, bf16[4,20,48,2048]{3,2,1,0:T(8,128)(2,1)S(1)} %copy-done.2, bf16[4,512,1024]{2,1,0:T(8,128)(2,1)S(1)} %bitcast.312, bf16[4,512,1024]{2,1,0:T(8,128)(2,1)} %collective-permute-done.4.refs_4_.wb_ref), custom_call_target="tpu_custom_call" | custom-call | flops 8053063680 | bytes 16777216 | tf_op jit(solution)/shard_map/input_grad/pallas_call | solution.py:514
  492.4 55.4 %reduce-scatter.4.cloned.1.call-done = f32[128,8]{1,0:T(8,128)} async-done(((f32[1024,8]{1,0:T(8,128)}), f32[128,8]{1,0:T(8,128)}) %reduce-scatter.4.cloned.1.call-update) | async-done | bytes 4112
  565.0 10.3 %collective-permute-done.63 = bf16[4,48,2048]{2,1,0:T(8,128)(2,1)S(1)} collective-permute-done((bf16[4,48,2048]{2,1,0:T(8,128)(2,1)}, bf16[4,48,2048]{2,1,0:T(8,128)(2,1)S(1)}, u32[]{:S(2)}, u32[]{:S(2)}) %collective-permute-start.63) | collective-permute-done | bytes 786464 | tf_op jit(solution)/shard_map/ppermute | solution.py:494
  578.4 22.1 %collective-permute-done.64 = bf16[6,48,2048]{2,1,0:T(8,128)(2,1)S(1)} collective-permute-done((bf16[6,48,2048]{2,1,0:T(8,128)(2,1)}, bf16[6,48,2048]{2,1,0:T(8,128)(2,1)S(1)}, u32[]{:S(2)}, u32[]{:S(2)}) %collective-permute-start.64) | collective-permute-done | bytes 1179680 | tf_op jit(solution)/shard_map/ppermute | solution.py:494
  604.8 3.6 fusion
  608.5 64.5 %collective-permute-done.51 = bf16[6,48,2048]{2,1,0:T(8,128)(2,1)S(1)} collective-permute-done((bf16[6,48,2048]{2,1,0:T(8,128)(2,1)S(1)}, bf16[6,48,2048]{2,1,0:T(8,128)(2,1)S(1)}, u32[]{:S(2)}, u32[]{:S(2)}) %collective-permute-start.51) | collective-permute-done | bytes 1179680 | tf_op jit(solution)/shard_map/ppermute | solution.py:494
  684.9 14.2 %collective-permute-done.84 = bf16[4,64,2048]{2,1,0:T(8,128)(2,1)S(1)} collective-permute-done((bf16[4,64,2048]{2,1,0:T(8,128)(2,1)S(1)}, bf16[4,64,2048]{2,1,0:T(8,128)(2,1)S(1)}, u32[]{:S(2)}, u32[]{:S(2)}) %collective-permute-start.84) | collective-permute-done | bytes 1048608 | tf_op jit(solution)/shard_map/ppermute | solution.py:494
  703.2 4.7 collective-permute-done.85
  711.5 5.5 collective-permute-done.86
  720.9 6.0 collective-permute-done.89
  726.9 6.1 collective-permute-start.72
  748.7 28.1 %collective-permute-done.87 = bf16[64,2048]{1,0:T(8,128)(2,1)S(1)} collective-permute-done((bf16[64,2048]{1,0:T(8,128)(2,1)S(1)}, bf16[64,2048]{1,0:T(8,128)(2,1)S(1)}, u32[]{:S(2)}, u32[]{:S(2)}) %collective-permute-start.87) | collective-permute-done | bytes 262176 | tf_op jit(solution)/shard_map/ppermute | solution.py:494
  780.5 5.0 collective-permute-start.73
  797.1 7.9 collective-permute-done.67
  811.8 3.7 collective-permute-done.57
  827.3 3.9 collective-permute-done.76
  834.4 3.7 collective-permute-done.58
  (736 shorter events, 491.9 us)
Async XLA Ops:
  7.2 540.6 %reduce-scatter.4.cloned.1.call-start = ((), (), s32[]{:S(2)}) async-start(), calls=%async_computation.1 | async-start | bytes 589824
  23.4 33.7 %collective-permute-start.4 = (bf16[4,512,1024]{2,1,0:T(8,128)(2,1)}, bf16[4,512,1024]{2,1,0:T(8,128)(2,1)}, u32[]{:S(2)}, u32[]{:S(2)}) collective-permute-start(bf16[4,512,1024]{2,1,0:T(8,128)(2,1)} %bitcast.305), channel_id=1, source_target_pairs={{0,1},{1,0},{2,3},{3,2},{4,5},{5,4},{6,7},{7,6},{8,9},{9,8},{10,11... | collective-permute-start | bytes 12582920 | tf_op jit(solution)/shard_map/ppermute | solution.py:271
  31.0 36.0 %collective-permute-start = (bf16[4,512,1024]{1,2,0:T(8,128)(2,1)}, bf16[4,512,1024]{1,2,0:T(8,128)(2,1)}, u32[]{:S(2)}, u32[]{:S(2)}) collective-permute-start(bf16[4,512,1024]{1,2,0:T(8,128)(2,1)} %bitcast.335), channel_id=1, source_target_pairs={{0,1},{1,0},{2,3},{3,2},{4,5},{5,4},{6,7},{7,6},{8,9},{9,8},{10,11... | collective-permute-start | bytes 12582920 | tf_op jit(solution)/shard_map/ppermute | solution.py:271
  230.8 26.8 %collective-permute-start.24 = (bf16[48,512]{1,0:T(8,128)(2,1)S(1)}, bf16[48,512]{1,0:T(8,128)(2,1)S(1)}, u32[]{:S(2)}, u32[]{:S(2)}) collective-permute-start(bf16[48,512]{1,0:T(8,128)(2,1)S(1)} %get-tuple-element.911.p_ref), channel_id=1, source_target_pairs={{0,2},{1,3},{2,0},{3,1},{4,6},{5,7},{6,4},{7,5},{8,10},{9,11},{10,... | collective-permute-start | bytes 147464 | tf_op jit(solution)/shard_map/ppermute | solution.py:381
  364.8 26.2 %collective-permute-start.92 = (f32[48,1024]{1,0:T(8,128)S(1)}, f32[48,1024]{1,0:T(8,128)S(1)}, u32[]{:S(2)}, u32[]{:S(2)}) collective-permute-start(f32[48,1024]{1,0:T(8,128)S(1)} %bitcast.347), channel_id=1, source_target_pairs={{0,1},{1,0},{2,3},{3,2},{4,5},{5,4},{6,7},{7,6},{8,9},{9,8},{10,11... | collective-permute-start | bytes 589832 | tf_op jit(solution)/shard_map/ppermute | solution.py:271
  380.4 223.7 %collective-permute-start.78 = (bf16[20,48,512]{2,1,0:T(8,128)(2,1)}, bf16[20,48,512]{2,1,0:T(8,128)(2,1)}, u32[]{:S(2)}, u32[]{:S(2)}) collective-permute-start(bf16[20,48,512]{2,1,0:T(8,128)(2,1)} %get-tuple-element.1233), channel_id=1, source_target_pairs={{0,8},{4,12},{8,0},{12,4},{16,24},{20,28},{24,16},{28,20},{1,9},{5... | collective-permute-start | bytes 2949128 | tf_op jit(solution)/shard_map/ppermute | solution.py:494
  380.9 104.3 %collective-permute-start.25 = (bf16[20,48,512]{2,1,0:T(8,128)(2,1)}, bf16[20,48,512]{2,1,0:T(8,128)(2,1)}, u32[]{:S(2)}, u32[]{:S(2)}) collective-permute-start(bf16[20,48,512]{2,1,0:T(8,128)(2,1)} %get-tuple-element.929), channel_id=1, source_target_pairs={{0,1},{1,0},{2,3},{3,2},{4,5},{5,4},{6,7},{7,6},{8,9},{9,8},{10,11... | collective-permute-start | bytes 2949128 | tf_op jit(solution)/shard_map/ppermute | solution.py:271
  403.4 197.8 %collective-permute-start.65 = (bf16[6,48,2048]{2,1,0:T(8,128)(2,1)}, bf16[6,48,2048]{2,1,0:T(8,128)(2,1)}, u32[]{:S(2)}, u32[]{:S(2)}) collective-permute-start(bf16[6,48,2048]{2,1,0:T(8,128)(2,1)} %get-tuple-element.1232), channel_id=1, source_target_pairs={{0,8},{4,12},{8,0},{12,4},{16,24},{20,28},{24,16},{28,20},{1,9},{5... | collective-permute-start | bytes 3538952 | tf_op jit(solution)/shard_map/ppermute | solution.py:494
  405.0 149.4 %collective-permute-start.62 = (bf16[2,48,2048]{2,1,0:T(8,128)(2,1)}, bf16[2,48,2048]{2,1,0:T(8,128)(2,1)}, u32[]{:S(2)}, u32[]{:S(2)}) collective-permute-start(bf16[2,48,2048]{2,1,0:T(8,128)(2,1)} %get-tuple-element.1229), channel_id=1, source_target_pairs={{0,8},{4,12},{8,0},{12,4},{16,24},{20,28},{24,16},{28,20},{1,9},{5... | collective-permute-start | bytes 1179656 | tf_op jit(solution)/shard_map/ppermute | solution.py:494
  479.6 69.8 %collective-permute-start.61 = (bf16[2,48,2048]{2,1,0:T(8,128)(2,1)}, bf16[2,48,2048]{2,1,0:T(8,128)(2,1)}, u32[]{:S(2)}, u32[]{:S(2)}) collective-permute-start(bf16[2,48,2048]{2,1,0:T(8,128)(2,1)} %get-tuple-element.1228), channel_id=1, source_target_pairs={{0,8},{4,12},{8,0},{12,4},{16,24},{20,28},{24,16},{28,20},{1,9},{5... | collective-permute-start | bytes 1179656 | tf_op jit(solution)/shard_map/ppermute | solution.py:494
  485.2 66.7 %collective-permute-start.48 = (bf16[2,48,2048]{2,1,0:T(8,128)(2,1)}, bf16[2,48,2048]{2,1,0:T(8,128)(2,1)}, u32[]{:S(2)}, u32[]{:S(2)}) collective-permute-start(bf16[2,48,2048]{2,1,0:T(8,128)(2,1)} %get-tuple-element.1222), channel_id=1, source_target_pairs={{0,4},{4,0},{8,12},{12,8},{16,20},{20,16},{24,28},{28,24},{1,5},{5... | collective-permute-start | bytes 1179656 | tf_op jit(solution)/shard_map/ppermute | solution.py:494
  562.9 37.6 %collective-permute-start.64 = (bf16[6,48,2048]{2,1,0:T(8,128)(2,1)}, bf16[6,48,2048]{2,1,0:T(8,128)(2,1)S(1)}, u32[]{:S(2)}, u32[]{:S(2)}) collective-permute-start(bf16[6,48,2048]{2,1,0:T(8,128)(2,1)} %get-tuple-element.1231), channel_id=1, source_target_pairs={{0,8},{4,12},{8,0},{12,4},{16,24},{20,28},{24,16},{28,20},{1,9},{5... | collective-permute-start | bytes 3538952 | tf_op jit(solution)/shard_map/ppermute | solution.py:494
  575.4 99.9 %collective-permute-start.70 = (bf16[20,48,512]{2,1,0:T(8,128)(2,1)S(1)}, bf16[20,48,512]{2,1,0:T(8,128)(2,1)S(1)}, u32[]{:S(2)}, u32[]{:S(2)}) collective-permute-start(bf16[20,48,512]{2,1,0:T(8,128)(2,1)S(1)} %copy-done.87), channel_id=1, source_target_pairs={{0,4},{4,0},{8,12},{12,8},{16,20},{20,16},{24,28},{28,24},{1,5},{5... | collective-permute-start | bytes 2949128 | tf_op jit(solution)/shard_map/ppermute | solution.py:494
  577.0 102.2 %collective-permute-start.60 = (bf16[20,48,512]{2,1,0:T(8,128)(2,1)S(1)}, bf16[20,48,512]{2,1,0:T(8,128)(2,1)S(1)}, u32[]{:S(2)}, u32[]{:S(2)}) collective-permute-start(bf16[20,48,512]{2,1,0:T(8,128)(2,1)S(1)} %copy-done.89), channel_id=1, source_target_pairs={{0,8},{4,12},{8,0},{12,4},{16,24},{20,28},{24,16},{28,20},{1,9},{5... | collective-permute-start | bytes 2949128 | tf_op jit(solution)/shard_map/ppermute | solution.py:494
  600.5 81.9 %collective-permute-start.47 = (bf16[20,48,512]{2,1,0:T(8,128)(2,1)S(1)}, bf16[20,48,512]{2,1,0:T(8,128)(2,1)S(1)}, u32[]{:S(2)}, u32[]{:S(2)}) collective-permute-start(bf16[20,48,512]{2,1,0:T(8,128)(2,1)S(1)} %copy-done.89), channel_id=1, source_target_pairs={{0,4},{4,0},{8,12},{12,8},{16,20},{20,16},{24,28},{28,24},{1,5},{5... | collective-permute-start | bytes 2949128 | tf_op jit(solution)/shard_map/ppermute | solution.py:494
  601.2 72.5 %collective-permute-start.52 = (bf16[6,48,2048]{2,1,0:T(8,128)(2,1)S(1)}, bf16[6,48,2048]{2,1,0:T(8,128)(2,1)S(1)}, u32[]{:S(2)}, u32[]{:S(2)}) collective-permute-start(bf16[6,48,2048]{2,1,0:T(8,128)(2,1)S(1)} %copy-done.92), channel_id=1, source_target_pairs={{0,4},{4,0},{8,12},{12,8},{16,20},{20,16},{24,28},{28,24},{1,5},{5... | collective-permute-start | bytes 3538952 | tf_op jit(solution)/shard_map/ppermute | solution.py:494
  604.1 68.9 %collective-permute-start.51 = (bf16[6,48,2048]{2,1,0:T(8,128)(2,1)S(1)}, bf16[6,48,2048]{2,1,0:T(8,128)(2,1)S(1)}, u32[]{:S(2)}, u32[]{:S(2)}) collective-permute-start(bf16[6,48,2048]{2,1,0:T(8,128)(2,1)S(1)} %copy-done.91), channel_id=1, source_target_pairs={{0,4},{4,0},{8,12},{12,8},{16,20},{20,16},{24,28},{28,24},{1,5},{5... | collective-permute-start | bytes 3538952 | tf_op jit(solution)/shard_map/ppermute | solution.py:494
  673.0 26.1 %collective-permute-start.84 = (bf16[4,64,2048]{2,1,0:T(8,128)(2,1)S(1)}, bf16[4,64,2048]{2,1,0:T(8,128)(2,1)S(1)}, u32[]{:S(2)}, u32[]{:S(2)}) collective-permute-start(bf16[4,64,2048]{2,1,0:T(8,128)(2,1)S(1)} %copy-done.108), channel_id=1, source_target_pairs={{0,4},{4,0},{8,12},{12,8},{16,20},{20,16},{24,28},{28,24},{1,5},{5... | collective-permute-start | bytes 3145736 | tf_op jit(solution)/shard_map/ppermute | solution.py:494
  673.7 59.4 %collective-permute-start.79 = (bf16[4,64,2048]{2,1,0:T(8,128)(2,1)S(1)}, bf16[4,64,2048]{2,1,0:T(8,128)(2,1)S(1)}, u32[]{:S(2)}, u32[]{:S(2)}) collective-permute-start(bf16[4,64,2048]{2,1,0:T(8,128)(2,1)S(1)} %dynamic-slice_bitcast_fusion.1), channel_id=1, source_target_pairs={{0,4},{4,0},{8,12},{12,8},{16,20},{20,16},{24,28},{28,24},{1,5},{5... | collective-permute-start | bytes 3145736 | tf_op jit(solution)/shard_map/ppermute | solution.py:494
  677.9 30.9 %collective-permute-start.71 = (bf16[2,64,2048]{2,1,0:T(8,128)(2,1)S(1)}, bf16[2,64,2048]{2,1,0:T(8,128)(2,1)S(1)}, u32[]{:S(2)}, u32[]{:S(2)}) collective-permute-start(bf16[2,64,2048]{2,1,0:T(8,128)(2,1)S(1)} %get-tuple-element.1266), channel_id=1, source_target_pairs={{0,8},{4,12},{1,9},{5,13},{2,10},{6,14},{3,11},{7,15}} | collective-permute-start | bytes 1572872 | tf_op jit(solution)/shard_map/ppermute | solution.py:494
  679.2 64.1 %collective-permute-start.74 = (bf16[2,64,2048]{2,1,0:T(8,128)(2,1)S(1)}, bf16[2,64,2048]{2,1,0:T(8,128)(2,1)S(1)}, u32[]{:S(2)}, u32[]{:S(2)}) collective-permute-start(bf16[2,64,2048]{2,1,0:T(8,128)(2,1)S(1)} %get-tuple-element.1267), channel_id=1, source_target_pairs={{24,16},{28,20},{25,17},{29,21},{26,18},{30,22},{27,19},{31,23}} | collective-permute-start | bytes 1572872 | tf_op jit(solution)/shard_map/ppermute | solution.py:494
  710.8 27.8 %collective-permute-start.66 = (bf16[4,64,2048]{2,1,0:T(8,128)(2,1)S(1)}, bf16[4,64,2048]{2,1,0:T(8,128)(2,1)S(1)}, u32[]{:S(2)}, u32[]{:S(2)}) collective-permute-start(bf16[4,64,2048]{2,1,0:T(8,128)(2,1)S(1)} %dynamic-slice_bitcast_fusion.2), channel_id=1, source_target_pairs={{0,4},{4,0},{8,12},{12,8},{16,20},{20,16},{24,28},{28,24},{1,5},{5... | collective-permute-start | bytes 3145736 | tf_op jit(solution)/shard_map/ppermute | solution.py:494
  717.0 63.5 %collective-permute-start.56 = (bf16[2,64,2048]{2,1,0:T(8,128)(2,1)}, bf16[2,64,2048]{2,1,0:T(8,128)(2,1)}, u32[]{:S(2)}, u32[]{:S(2)}) collective-permute-start(bf16[2,64,2048]{2,1,0:T(8,128)(2,1)} %get-tuple-element.1271), channel_id=1, source_target_pairs={{24,16},{28,20},{25,17},{29,21},{26,18},{30,22},{27,19},{31,23}} | collective-permute-start | bytes 1572872 | tf_op jit(solution)/shard_map/ppermute | solution.py:494
  733.1 52.4 %collective-permute-start.54 = (bf16[2,64,2048]{2,1,0:T(8,128)(2,1)}, bf16[2,64,2048]{2,1,0:T(8,128)(2,1)}, u32[]{:S(2)}, u32[]{:S(2)}) collective-permute-start(bf16[2,64,2048]{2,1,0:T(8,128)(2,1)} %fusion.18), channel_id=1, source_target_pairs={{0,8},{4,12},{8,16},{12,20},{1,9},{5,13},{9,17},{13,21},{2,10},{6,... | collective-permute-start | bytes 1572872 | tf_op jit(solution)/shard_map/ppermute | solution.py:494
  738.6 38.2 %collective-permute-start.87 = (bf16[64,2048]{1,0:T(8,128)(2,1)S(1)}, bf16[64,2048]{1,0:T(8,128)(2,1)S(1)}, u32[]{:S(2)}, u32[]{:S(2)}) collective-permute-start(bf16[64,2048]{1,0:T(8,128)(2,1)S(1)} %get-tuple-element.1276), channel_id=1, source_target_pairs={{0,8},{4,12},{8,16},{12,20},{16,24},{20,28},{1,9},{5,13},{9,17},{1... | collective-permute-start | bytes 786440 | tf_op jit(solution)/shard_map/ppermute | solution.py:494
  743.3 33.5 %collective-permute-start.90 = (bf16[64,2048]{1,0:T(8,128)(2,1)S(1)}, bf16[64,2048]{1,0:T(8,128)(2,1)S(1)}, u32[]{:S(2)}, u32[]{:S(2)}) collective-permute-start(bf16[64,2048]{1,0:T(8,128)(2,1)S(1)} %fusion.26), channel_id=1, source_target_pairs={{8,0},{12,4},{16,8},{20,12},{24,16},{28,20},{9,1},{13,5},{17,9},{2... | collective-permute-start | bytes 786440 | tf_op jit(solution)/shard_map/ppermute | solution.py:494
  746.7 47.1 %collective-permute-start.80 = (bf16[2,64,2048]{2,1,0:T(8,128)(2,1)}, bf16[2,64,2048]{2,1,0:T(8,128)(2,1)}, u32[]{:S(2)}, u32[]{:S(2)}) collective-permute-start(bf16[2,64,2048]{2,1,0:T(8,128)(2,1)} %dynamic-slice_bitcast_fusion.5), channel_id=1, source_target_pairs={{0,16},{4,20},{8,24},{12,28},{16,0},{20,4},{24,8},{28,12},{1,17},{... | collective-permute-start | bytes 1572872 | tf_op jit(solution)/shard_map/ppermute | solution.py:494
  776.8 28.2 %collective-permute-start.67 = (bf16[2,64,2048]{2,1,0:T(8,128)(2,1)}, bf16[2,64,2048]{2,1,0:T(8,128)(2,1)}, u32[]{:S(2)}, u32[]{:S(2)}) collective-permute-start(bf16[2,64,2048]{2,1,0:T(8,128)(2,1)} %dynamic-slice_bitcast_fusion.8), channel_id=1, source_target_pairs={{0,16},{4,20},{8,24},{12,28},{16,0},{20,4},{24,8},{28,12},{1,17},{... | collective-permute-start | bytes 1572872 | tf_op jit(solution)/shard_map/ppermute | solution.py:494
  776.8 32.5 %collective-permute-start.75 = (bf16[2,64,2048]{2,1,0:T(8,128)(2,1)}, bf16[2,64,2048]{2,1,0:T(8,128)(2,1)}, u32[]{:S(2)}, u32[]{:S(2)}) collective-permute-start(bf16[2,64,2048]{2,1,0:T(8,128)(2,1)} %get-tuple-element.1265), channel_id=1, source_target_pairs={{16,8},{20,12},{24,16},{28,20},{17,9},{21,13},{25,17},{29,21},{18,... | collective-permute-start | bytes 1572872 | tf_op jit(solution)/shard_map/ppermute | solution.py:494
  780.5 46.2 %collective-permute-start.73 = (bf16[2,64,2048]{2,1,0:T(8,128)(2,1)}, bf16[2,64,2048]{2,1,0:T(8,128)(2,1)}, u32[]{:S(2)}, u32[]{:S(2)}) collective-permute-start(bf16[2,64,2048]{2,1,0:T(8,128)(2,1)} %get-tuple-element.1264), channel_id=1, source_target_pairs={{0,8},{4,12},{8,16},{12,20},{16,24},{20,28},{1,9},{5,13},{9,17},{1... | collective-permute-start | bytes 1572872 | tf_op jit(solution)/shard_map/ppermute | solution.py:494
  788.3 27.1 %collective-permute-start.57 = (bf16[2,64,2048]{2,1,0:T(8,128)(2,1)S(1)}, bf16[2,64,2048]{2,1,0:T(8,128)(2,1)S(1)}, u32[]{:S(2)}, u32[]{:S(2)}) collective-permute-start(bf16[2,64,2048]{2,1,0:T(8,128)(2,1)S(1)} %get-tuple-element.1269), channel_id=1, source_target_pairs={{16,8},{20,12},{24,16},{28,20},{17,9},{21,13},{25,17},{29,21},{18,... | collective-permute-start | bytes 1572872 | tf_op jit(solution)/shard_map/ppermute | solution.py:494
  793.8 40.6 %collective-permute-start.55 = (bf16[2,64,2048]{2,1,0:T(8,128)(2,1)}, bf16[2,64,2048]{2,1,0:T(8,128)(2,1)}, u32[]{:S(2)}, u32[]{:S(2)}) collective-permute-start(bf16[2,64,2048]{2,1,0:T(8,128)(2,1)} %get-tuple-element.1268), channel_id=1, source_target_pairs={{0,8},{4,12},{8,16},{12,20},{16,24},{20,28},{1,9},{5,13},{9,17},{1... | collective-permute-start | bytes 1572872 | tf_op jit(solution)/shard_map/ppermute | solution.py:494
  (212 other events, 2859.0 us)
Sparse Core Ops, SparseCore 0:
  485.3 62.4 reduce-scatter.3

commit v3 on v2

--- a/solution.py
+++ b/solution.py
@@ -51,6 +51,20 @@
         compiler_params=params(1),
         name="place",
     )(*arrays)
+
+
+def order_kernel(step_ref, feat_ref, out_ref, all_ref, sems, all_sem):
+    steps = feat_ref.shape[0]
+    copies = [
+        pltpu.make_async_copy(feat_ref.at[step_ref[0] + step_ref[1] * i], out_ref.at[i], sems.at[i]) for i in range(steps)
+    ]
+    for copy in copies:
+        copy.start()
+    for copy in copies:
+        copy.wait()
+    whole = pltpu.make_async_copy(out_ref, all_ref, all_sem)
+    whole.start()
+    whole.wait()
 
 
 def pieces(refs, axis):
@@ -99,24 +113,26 @@
 
 
 def between_kernel(
-    first, step_ref, feat_ref, bias_ref, wa_ref, wb_ref, cell_ref, gates_ref, mixed_ref, prev_ref, hidden_ref, slope_ref,
-    *refs,
+    first, passed, step_ref, feat_ref, bias_ref, wa_ref, wb_ref, cell_ref, gates_ref, mixed_ref, prev_ref, hidden_ref,
+    slope_ref, *refs,
 ):
-    out_ref, gates_all, cells_all, mixed_all, prev_all, feat_all, hidden_all, slope_all, sems = refs if first else refs[7:]
-    step, time, time_before, time_after = (step_ref[i] for i in range(4))
+    refs = refs[(0 if first else 6) + passed :]
+    out_ref, gates_all, cells_all, mixed_all, prev_all, hidden_all, slope_all = refs[:7]
+    sems = refs[-1]
+    step, time_before = step_ref[0], step_ref[2]
+    after = jnp.minimum(step + 1, feat_ref.shape[0] - 1)
     copies = [pltpu.make_async_copy(gates_ref.at[i], gates_all.at[i, step], sems.at[i]) for i in range(PIECES)]
     copies += [
         pltpu.make_async_copy(mixed_ref.at[i], mixed_all.at[i, step], sems.at[PIECES + i]) for i in range(PIECES)
     ]
     copies.append(pltpu.make_async_copy(cell_ref, cells_all.at[step], sems.at[2 * PIECES]))
     copies.append(pltpu.make_async_copy(prev_ref, prev_all.at[step], sems.at[2 * PIECES + 1]))
-    copies.append(pltpu.make_async_copy(feat_ref.at[time], feat_all.at[step], sems.at[2 * PIECES + 4]))
     if not first:
         copies.append(pltpu.make_async_copy(hidden_ref, hidden_all.at[time_before], sems.at[2 * PIECES + 2]))
         copies.append(pltpu.make_async_copy(slope_ref, slope_all.at[step - 1], sems.at[2 * PIECES + 3]))
     for copy in copies:
         copy.start()
-    inflow_into(feat_ref[time_after], bias_ref, wa_ref, wb_ref, out_ref)
+    inflow_into(feat_ref[after], bias_ref, wa_ref, wb_ref, out_ref)
     for copy in copies:
         copy.wait()
 
@@ -130,7 +146,7 @@
 
 
 def inflow_kernel(step_ref, feat_ref, bias_ref, wa_ref, wb_ref, out_ref):
-    inflow_into(feat_ref[step_ref[1]], bias_ref, wa_ref, wb_ref, out_ref)
+    inflow_into(feat_ref[0], bias_ref, wa_ref, wb_ref, out_ref)
 
 
 def backward_kernel(
@@ -202,11 +218,12 @@
 
 
 def aside_kernel(
-    first, opens, step_ref, dz_ref, raw_ref, gates_all, cells_all, ups_all, slope_all, *refs
+    first, opens, passed, step_ref, dz_ref, raw_ref, gates_all, cells_all, ups_all, slope_all, *refs
 ):
-    refs = refs[(0 if first else 4) + (0 if opens else 2) :]
+    refs = refs[(0 if first else 4) + (0 if opens else 2) + passed :]
     gates_ref, cell_ref, prev_ref, slope_ref, up_ref = refs[:5]
-    dz_all, raw_all, near_all, far_all, near_out, far_out, sems, fetch_sems = refs[5:]
+    dz_all, raw_all, near_all, far_all, near_out, far_out = refs[5:11]
+    sems, fetch_sems = refs[-2:]
     step, time_before = step_ref[0], step_ref[2]
     slot, low, high = step_ref[4], step_ref[5], step_ref[6]
     before = jnp.maximum(step - 1, 0)
@@ -315,7 +332,27 @@
     def hbm(shape, dtype):
         return pltpu.HBM(shape, dtype)
 
-    feats_v, keep_v, bias_v, win_av, win_bv = place(feats, keep, bias_p, win_a, win_b)
+    n_batch = lax.axis_size("batch")
+    spot = lax.axis_index("batch")
+    low, high = spot % 2, (spot // 2) % 2
+    near_swap = [(i, i ^ 1) for i in range(n_batch)]
+    far_swap = [(i, i ^ 2) for i in range(n_batch)]
+
+    def swapped(array, pairs):
+        return lax.ppermute(array, "batch", pairs)
+
+    turn = jnp.where(own == 0, jnp.array([0, 1], jnp.int32), jnp.array([steps - 1, -1], jnp.int32))
+    feats_v, feat_all = pl.pallas_call(
+        order_kernel,
+        out_shape=(vmem(feats.shape, BF16), hbm(feats.shape, BF16)),
+        in_specs=[SMEM, ANY],
+        out_specs=[VMEM, ANY],
+        scratch_shapes=[pltpu.SemaphoreType.DMA((steps,)), pltpu.SemaphoreType.DMA],
+        compiler_params=params(1),
+        name="order",
+    )(turn, feats)
+    feat_in = (swapped(feat_all, near_swap), swapped(feat_all, far_swap))
+    keep_v, bias_v, win_av, win_bv = place(keep, bias_p, win_a, win_b)
     rec_av, rec_bv, proj_av, proj_bv, start_hv, start_cv = place(rec_a, rec_b, proj_a, proj_b, start_h, start_c)
 
     gates_shape, cell_shape = (PIECES, streams, 4 * width), (PIECES, streams, width)
@@ -326,7 +363,7 @@
         out_specs=VMEM,
         compiler_params=params(8),
         name="inflow",
-    )(at_step(0), pinned(feats_v), pinned(bias_v), pinned(win_av), pinned(win_bv))
+    )(turn, pinned(feats_v), pinned(bias_v), pinned(win_av), pinned(win_bv))
 
     def forward_call(first, step, part, peer, cell, inflow):
         return pl.pallas_call(
@@ -349,45 +386,43 @@
             pinned(rec_av), pinned(rec_bv), pinned(proj_av), pinned(proj_bv),
         )
 
-    def between_call(step, fresh, stacks):
+    def between_call(step, fresh, stacks, passing=()):
         shapes = (
             hbm((PIECES, steps, streams, 4 * width), BF16),
             hbm((steps,) + cell_shape, F32),
             hbm((PIECES, steps, streams, width), BF16),
             hbm((steps, streams, depth), BF16),
             hbm((steps, streams, depth), BF16),
-            hbm((steps, streams, depth), BF16),
             hbm((steps, streams, depth), F32),
         )
-        inflow, *stacks = pl.pallas_call(
-            functools.partial(between_kernel, not stacks),
-            out_shape=(vmem(gates_shape, F32),) + shapes,
-            in_specs=[SMEM] + [VMEM] * 10 + [ANY] * len(stacks),
-            out_specs=[VMEM] + [ANY] * 7,
-            scratch_shapes=[pltpu.SemaphoreType.DMA((2 * PIECES + 5,))],
-            input_output_aliases={11 + i: 1 + i for i in range(len(stacks))},
+        aliases = {11 + i: 1 + i for i in range(len(stacks))}
+        aliases.update({11 + len(stacks) + i: 7 + i for i in range(len(passing))})
+        inflow, *out = pl.pallas_call(
+            functools.partial(between_kernel, not stacks, len(passing)),
+            out_shape=(vmem(gates_shape, F32),) + shapes + tuple(hbm(x.shape, x.dtype) for x in passing),
+            in_specs=[SMEM] + [VMEM] * 10 + [ANY] * (len(stacks) + len(passing)),
+            out_specs=[VMEM] + [ANY] * (6 + len(passing)),
+            scratch_shapes=[pltpu.SemaphoreType.DMA((2 * PIECES + 4,))],
+            input_output_aliases=aliases,
             compiler_params=params(8),
             cost_estimate=cost(2 * streams * depth * 8 * cells, 8 * depth * cells * 2),
             name="between",
         )(
             at_step(step), pinned(feats_v), pinned(bias_v), pinned(win_av), pinned(win_bv),
-            *(pinned(x) for x in fresh), *(in_hbm(x) for x in stacks),
-        )
-        return inflow, tuple(stacks)
-
-    def forward_step(step, carry, first=False):
-        part, peer, cell, inflow, stacks = carry
-        part, cell, *fresh = forward_call(first, step, part, peer, cell, inflow)
+            *(pinned(x) for x in fresh), *(in_hbm(x) for x in (*stacks, *passing)),
+        )
+        return inflow, tuple(out[:6]), tuple(out[6:])
+
+    none = jnp.zeros((streams, depth), BF16)
+    part, peer, cell, stacks = none, none, start_cv, ()
+    for step in range(steps):
+        part, cell, *fresh = forward_call(step == 0, step, part, peer, cell, inflow)
         peer = lax.ppermute(part, "gate", across)
-        inflow, stacks = between_call(step, (cell, *fresh), stacks)
-        return (part, peer, cell, inflow, stacks)
-
-    none = jnp.zeros((streams, depth), BF16)
-    carry = forward_step(0, (none, none, start_cv, inflow, ()), True)
-    for step in range(1, steps):
-        carry = forward_step(step, carry)
-    part, peer, cell, _, stacks = carry
-    gates_all, cells_all, mixed_all, prev_all, feat_all, hidden_all, slope_all = stacks
+        due = step == (2 * steps) // 3
+        inflow, stacks, passed = between_call(step, (cell, *fresh), stacks, feat_in if due else ())
+        feat_in = passed if due else feat_in
+    gates_all, cells_all, mixed_all, prev_all, hidden_all, slope_all = stacks
+    prev_in = (swapped(prev_all, near_swap), swapped(prev_all, far_swap))
 
     saved_shapes = (
         vmem(gates_shape, BF16),
@@ -452,13 +487,7 @@
             *(pinned(x) for x in saved), pinned(start_cv),
         )
 
-    n_batch = lax.axis_size("batch")
-    spot = lax.axis_index("batch")
-    low, high = spot % 2, (spot // 2) % 2
-    near_swap = [(i, i ^ 1) for i in range(n_batch)]
-    far_swap = [(i, i ^ 2) for i in range(n_batch)]
-
-    def aside_call(step, slot, slots, dz, raw, stacks, sends):
+    def aside_call(step, slot, slots, dz, raw, stacks, sends, passing):
         piece_shape = (streams, 4 * width)
         shapes = (
             hbm((PIECES, steps) + piece_shape, BF16),
@@ -471,11 +500,12 @@
         kept = len(stacks)
         aliases = {7 + i: 5 + i for i in range(kept)}
         aliases.update({7 + kept + i: 9 + i for i in range(len(sends))})
+        aliases.update({7 + kept + len(sends) + i: 11 + i for i in range(len(passing))})
         out = pl.pallas_call(
-            functools.partial(aside_kernel, not stacks, not sends),
-            out_shape=saved_shapes + shapes,
-            in_specs=[SMEM] + [VMEM] * 2 + [ANY] * (4 + kept + len(sends)),
-            out_specs=[VMEM] * 5 + [ANY] * 6,
+            functools.partial(aside_kernel, not stacks, not sends, len(passing)),
+            out_shape=saved_shapes + shapes + tuple(hbm(x.shape, x.dtype) for x in passing),
+            in_specs=[SMEM] + [VMEM] * 2 + [ANY] * (4 + kept + len(sends) + len(passing)),
+            out_specs=[VMEM] * 5 + [ANY] * (6 + len(passing)),
             scratch_shapes=[
                 pltpu.SemaphoreType.DMA((PIECES + 5,)),
                 pltpu.SemaphoreType.DMA((PIECES + 4,)),
@@ -486,15 +516,13 @@
             name="aside",
         )(
             jnp.concatenate([at_step(step), jnp.stack([jnp.int32(slot), low, high])]), pinned(dz), pinned(raw),
-            in_hbm(gates_all), in_hbm(cells_all), in_hbm(ups), in_hbm(slope_all), *(in_hbm(x) for x in (*stacks, *sends)),
-        )
-        return out[:5], tuple(out[5:9]), tuple(out[9:])
-
-    def swapped(array, pairs):
-        return lax.ppermute(array, "batch", pairs)
+            in_hbm(gates_all), in_hbm(cells_all), in_hbm(ups), in_hbm(slope_all),
+            *(in_hbm(x) for x in (*stacks, *sends, *passing)),
+        )
+        return out[:5], tuple(out[5:9]), tuple(out[9:11]), tuple(out[11:])
 
     carry = (none, none, jnp.zeros(cell_shape, F32), saved, ())
-    top, near_in, far_in = steps, [], []
+    pending, arrived, top = [(steps - 1 - steps // 3, prev_in)], [], steps
     for index, share in enumerate(SHARES):
         slots = top if index == len(SHARES) - 1 else round(share * steps)
         sends = ()
@@ -502,15 +530,19 @@
             part, peer, grad, saved, stacks = carry
             part, grad, raw, dz = backward_call(step, part, peer, grad, saved)
             peer = lax.ppermute(part, "gate", across)
-            saved, stacks, sends = aside_call(step, step - (top - slots), slots, dz, raw, stacks, sends)
+            passing = pending.pop(0)[1] if pending and pending[0][0] >= step else ()
+            saved, stacks, sends, passed = aside_call(
+                step, step - (top - slots), slots, dz, raw, stacks, sends, passing
+            )
+            arrived += [passed] if passed else []
             carry = (part, peer, grad, saved, stacks)
         top -= slots
-        near_in.insert(0, swapped(sends[0], near_swap))
-        far_in.insert(0, swapped(sends[1], far_swap))
+        pending.append((top - 2 - (2 * slots + 2) // 3, (swapped(sends[0], near_swap), swapped(sends[1], far_swap))))
+    arrived += [arrays for _, arrays in pending]
     dz_all, raw_all, near_all, far_all = carry[-1]
+    prev_in, exchanged = arrived[0], arrived[:0:-1]
     rows = steps * streams
 
-    turn = jnp.where(own == 0, jnp.array([0, 1], jnp.int32), jnp.array([steps - 1, -1], jnp.int32))
     dx_all = pl.pallas_call(
         input_grad_kernel,
         out_shape=jax.ShapeDtypeStruct((steps, streams, depth), F32),
@@ -534,18 +566,18 @@
         name="input_grad",
     )(turn, dz_all, win_a, win_b)
 
-    def line_sum(chunks, stride, count):
+    def line_sum(chunks, axis, stride, count):
         here = (spot // stride) % count
 
         def chunk(index):
-            return lax.dynamic_index_in_dim(chunks, jnp.clip(index, 0, count - 1), 0, keepdims=False)
+            return lax.dynamic_index_in_dim(chunks, jnp.clip(index, 0, count - 1), axis, keepdims=False)
 
         def at(device):
             return (device // stride) % count
 
         if count == 2:
             pairs = [(i, i + stride if at(i) == 0 else i - stride) for i in range(n_batch)]
-            return chunk(here).astype(F32) + swapped(chunk(1 - here), pairs).astype(F32)
+            return (chunk(here).astype(F32) + swapped(chunk(1 - here), pairs).astype(F32)).astype(BF16)
         up, down = None, None
         for slot in range(1, count):
             rise, fall = chunk(here + count - slot), chunk(here - count + slot)
@@ -554,59 +586,57 @@
                 fall = (fall.astype(F32) + down.astype(F32)).astype(BF16)
             up = swapped(rise, [(i, i + stride) for i in range(n_batch) if at(i) < min(slot, count - 1)])
             down = swapped(fall, [(i, i - stride) for i in range(n_batch) if at(i) > max(count - 1 - slot, 0)])
-        return chunk(here).astype(F32) + up.astype(F32) + down.astype(F32)
+        return (chunk(here).astype(F32) + up.astype(F32) + down.astype(F32)).astype(BF16)
 
     line = n_batch // 2
     share_rows = depth // n_batch
 
-    def own_half(mine, theirs, index):
-        return jnp.stack([jnp.where(index == 0, mine, theirs), jnp.where(index == 0, theirs, mine)])
-
     def finish_halves(halves, index, pairs):
-        mine = lax.dynamic_index_in_dim(halves, index, 0, keepdims=False)
-        theirs = lax.dynamic_index_in_dim(halves, 1 - index, 0, keepdims=False)
-        return own_half(mine, swapped(theirs, pairs), index)
-
-    def near_sum(grad):
-        return line_sum(grad.reshape(line, 2, share_rows, -1), 2, line).astype(BF16)
-
-    def far_sum(grad):
-        chunks = jnp.moveaxis(grad.reshape(line, 2, share_rows, -1), 1, 0)
-        mine = line_sum(chunks, 1, 2).astype(BF16)
-        return line_sum(mine.reshape(line // 2, 2, share_rows, -1), 4, line // 2).astype(BF16)
-
-    def rows_of(stacked):
-        return stacked.reshape(rows, -1)
+        mine = lax.dynamic_index_in_dim(halves, index, 1, keepdims=False)
+        theirs = swapped(lax.dynamic_index_in_dim(halves, 1 - index, 1, keepdims=False), pairs)
+        return jnp.stack([jnp.where(index == 0, mine, theirs), jnp.where(index == 0, theirs, mine)], axis=1)
 
     def product(left, right):
-        return lax.dot_general(rows_of(left), rows_of(right), (((0,), (0,)), ((), ())), preferred_element_type=F32)
-
-    near_in, far_in = jnp.concatenate(near_in, axis=0), jnp.concatenate(far_in, axis=0)
-    near_left = [(x, swapped(x, near_swap)) for x in (feat_all, prev_all)]
-    far_left = [(x, swapped(x, far_swap)) for x in (feat_all, prev_all)]
-    near_sums = [
-        near_sum((product(mine, near_all) + product(theirs, near_in)).astype(BF16)) for mine, theirs in near_left
+        return lax.dot_general(
+            left.reshape(rows, -1), right.reshape(rows, -1), (((0,), (0,)), ((), ())), preferred_element_type=F32
+        )
+
+    def both(feat, prev):
+        return jnp.concatenate([feat, prev], axis=2)
+
+    left = both(feat_all, prev_all)
+    sums = [
+        (product(left, kept) + product(both(feat, prev), jnp.concatenate(taken, axis=0)))
+        .astype(BF16)
+        .reshape(2, line, 2, share_rows, 4 * width)
+        for kept, feat, prev, taken in zip((near_all, far_all), feat_in, prev_in, zip(*exchanged))
     ]
-    far_sums = [far_sum((product(mine, far_all) + product(theirs, far_in)).astype(BF16)) for mine, theirs in far_left]
-    near_sums = [finish_halves(x, low, near_swap) for x in near_sums]
-    far_sums = [finish_halves(x, high, far_swap) for x in far_sums]
+    near = finish_halves(line_sum(sums[0], 1, 2, line), low, near_swap)
+    far = line_sum(sums[1], 2, 1, 2).reshape(2, line // 2, 2, share_rows, 4 * width)
+    far = finish_halves(line_sum(far, 1, 4, line // 2), high, far_swap)
+
+    grad_proj = jnp.einsum("ptnc,tnk->kpc", mixed_all, raw_all, preferred_element_type=F32).astype(BF16)
+    grad_proj = line_sum(grad_proj.reshape(line, 2, share_rows, QUARTERS * cells), 1, 1, 2)
+    grad_proj = line_sum(grad_proj, 0, 2, line)
 
     grad_bias = jnp.sum(dz_all, axis=(1, 2), dtype=F32)
-    grad_proj = jnp.einsum("ptnc,tnk->kpc", mixed_all, raw_all, preferred_element_type=F32).astype(BF16)
-    grad_proj = line_sum(jnp.moveaxis(grad_proj.reshape(line, 2, share_rows, -1), 1, 0), 1, 2).astype(BF16)
-    grad_proj = line_sum(grad_proj, 2, line).astype(BF16)
+    stride = 1
+    while stride < n_batch:
+        grad_bias = grad_bias + swapped(grad_bias, [(i, i ^ stride) for i in range(n_batch)])
+        stride *= 2
 
     def gate_rows(halves):
-        shaped = halves.reshape(HALVES, -1, 4, width)
-        return jnp.transpose(shaped, (1, 2, 0, 3)).reshape(-1, 4, cells)
+        shaped = halves.reshape(2, HALVES, -1, 4, width)
+        return jnp.transpose(shaped, (0, 2, 3, 1, 4)).reshape(2, -1, 4, cells)
 
     def home(mine, theirs):
         return by_direction(*trade(mine, theirs)).astype(F32)
 
-    grad_w_in, grad_w_rec = (home(gate_rows(near), gate_rows(far)) for near, far in zip(near_sums, far_sums))
-    grad_bias = grad_bias.reshape(QUARTERS, HALVES, 1, 4 * width)
-    grad_bias = home(gate_rows(grad_bias[0])[0], gate_rows(grad_bias[1])[0])
-    grad_bias = lax.psum_scatter(grad_bias, "batch", scatter_dimension=2, tiled=True)
+    grad_w_in, grad_w_rec = jnp.moveaxis(home(gate_rows(near), gate_rows(far)), 1, 0)
+    shaped = jnp.transpose(grad_bias.reshape(QUARTERS, HALVES, 4, width), (0, 2, 1, 3)).reshape(QUARTERS, 4, cells)
+    own_cells = cells // n_batch
+    shaped = lax.dynamic_slice_in_dim(shaped, spot * own_cells, own_cells, 2)
+    grad_bias = home(shaped[0], shaped[1])
     grad_proj = grad_proj.reshape(share_rows, QUARTERS, cells)
     grad_proj = home(jnp.transpose(grad_proj[:, 0]), jnp.transpose(grad_proj[:, 1]))
 

time: 872 us -> 726 us (0.83)
  waiting for transfers between devices: 250 us -> 112 us
  between operations: 17.2 us -> 4.23 us
  starting transfers between devices: 103 us -> 113 us
    ppermute x41 -> x34, waiting for transfers between devices: 185 us -> 106 us  [swapped(): return lax.ppermute(array, 'batch', pairs)]
    unnamed x2 -> x0, waiting for transfers between devices: 55.4 us -> none
    ppermute x19 -> x39, starting transfers between devices: 17.9 us -> 43.8 us  [body(): peer = lax.ppermute(part, 'gate', across)]
    ppermute x20 -> x0, starting transfers between devices: 22.5 us -> none  [forward_step(): peer = lax.ppermute(part, 'gate', across)]
    ppermute x41 -> x34, starting transfers between devices: 58.8 us -> 66.8 us  [swapped(): return lax.ppermute(array, 'batch', pairs)]
    unnamed x322 -> x341, local copies, waits for them, and re-layouts: 63 us -> 56.8 us
    pallas_call x40 -> x41, Pallas kernels: 119 us -> 122 us  [the longest x20 61.1 us: between_call(): pl.pallas_call(functools.partial(between_kernel, not stacks, len(passing)...]
    dot_general x8 -> x4, matrix products: 30.7 us -> 28.2 us  [product(): lax.dot_general(left.reshape(rows, -1), right.reshape(rows, -1), (((0,),...]
  transfers between devices with their start and end apart: 94 -> 85, of which waited for: 46 -> 27; matrix products, arithmetic and copies ran while one was open for 18% -> 22% of each run, Pallas kernels for 18% -> 35%
where the time goes in v3:
time: 726 us; the launch traced here: 714 us
  Pallas kernels  267 us (37%)
  local copies, waits for them, and re-layouts  152 us (21%)
  starting transfers between devices  113 us (16%)
  waiting for transfers between devices  112 us (15%)
  other arithmetic  35.6 us (5%)
  matrix products  30.6 us (4%)
    ppermute x34, waiting for transfers between devices, swapped(): return lax.ppermute(array, 'batch', pairs)  106 us
    ppermute x34, starting transfers between devices, swapped(): return lax.ppermute(array, 'batch', pairs)  66.8 us
    pallas_call x20, Pallas kernels, between_call(): pl.pallas_call(functools.partial(between_kernel, not stacks, len(passing)...  61.1 us
    pallas_call x20, Pallas kernels, backward_call(): pl.pallas_call(backward_kernel, out_shape=(vmem((streams, depth), BF16),...  60.9 us
    pallas_call x20, Pallas kernels, aside_call(): pl.pallas_call(functools.partial(aside_kernel, not stacks, not sends, len...  57.8 us
    pallas_call x20, Pallas kernels, forward_call(): pl.pallas_call(functools.partial(forward_kernel, first), out_shape=(vmem(...  56.8 us
    unnamed x341, local copies, waits for them, and re-layouts  56.8 us
    ppermute x39, starting transfers between devices, body(): peer = lax.ppermute(part, 'gate', across)  43.8 us
  transfers between devices with their start and end apart: 85, of which 27 were waited for; matrix products, arithmetic and copies ran while one was open for 22% of the time, Pallas kernels for 35%

profile of v3, /device:TPU:8, one launch (start us, length us, event | category | flops | bytes accessed | tf_op | source)
XLA Modules:
  0.0 714.2 jit_solution(3982960034511983623)
XLA Ops:
  0.7 12.8 %constant_dynamic-slice_fusion.5 = (bf16[1,512,4,1024]{3,2,1,0:T(4,128)(2,1)S(1)}, bf16[1,512,4,1024]{3,2,1,0:T(4,128)(2,1)}, bf16[1,512,4,1024]{3,2,1,0:T(4,128)(2,1)}, bf16[1,512,4,1024]{3,2,1,0:T(4,128)(2,1)}) fusion(bf16[2,512,4,1024]{3,2,1,0:T(4,128)(2,1)} %param.175, s32[]{:T(128)S(6)} %select_n.593, s32[]{:T(128)S(6)} %select_n.592, ...), kind=kLoop, calls=%fused_computation.122 | loop fusion | bytes 33554440 | tf_op jit(solution)/shard_map/jit(dynamic_index_in_dim)/dynamic_slice | solution.py:285
  13.5 3.3 copy.537
  16.8 7.7 %copy.481 = bf16[1,512,4,1024]{1,3,2,0:T(8,128)(2,1)} copy(bf16[1,512,4,1024]{3,2,1,0:T(4,128)(2,1)} %get-tuple-element.1273) | data formatting | bytes 8388608 | tf_op jit(solution)/shard_map/jit(dynamic_index_in_dim)/dynamic_slice | solution.py:285
  35.3 5.7 copy.538
  41.1 3.4 copy.536
  62.6 6.3 copy.486.refs_1_
  140.3 3.3 between.28
  184.2 3.2 between.33
  229.0 7.6 %copy.480 = bf16[1,512,4,1024]{1,3,2,0:T(8,128)(2,1)} copy(bf16[1,512,4,1024]{3,2,1,0:T(4,128)(2,1)} %get-tuple-element.1272) | data formatting | bytes 8388608 | tf_op jit(solution)/shard_map/jit(dynamic_index_in_dim)/dynamic_slice | solution.py:285
  246.0 3.8 copy-done.11
  250.4 4.3 between.39
  371.9 5.9 scatter_fusion.1
  420.7 5.9 scatter_fusion
  435.1 3.6 backward_step.39
  438.7 4.0 aside.39
  442.7 7.7 %convert_reduce_fusion = f32[4,2048]{1,0:T(4,128)S(1)} fusion(bf16[4,20,48,2048]{3,2,1,0:T(8,128)(2,1)} %get-tuple-element.1195.dz_ref), kind=kLoop, calls=%fused_computation.4 | loop fusion | flops 15720448 | bytes 15761408 | tf_op jit(solution)/shard_map/reduce_sum | solution.py:622
  452.5 6.8 fusion.80
  459.4 6.9 fusion.79
  470.7 16.3 %input_grad.1 = f32[20,48,512]{2,1,0:T(8,128)S(1)} custom-call(s32[2]{0:T(128)S(1)} %copy-done.84, bf16[4,20,48,2048]{3,2,1,0:T(8,128)(2,1)S(1)} %bitcast.250, bf16[4,512,1024]{2,1,0:T(8,128)(2,1)S(1)} %bitcast.252, bf16[4,512,1024]{2,1,0:T(8,128)(2,1)} %collective-permute-done.4.refs_3_.wb_ref), custom_call_target="tpu_custom_call" | custom-call | flops 8053063680 | bytes 16777216 | tf_op jit(solution)/shard_map/input_grad/pallas_call | solution.py:546
  490.0 4.6 reshape.133
  504.5 8.3 %collective-permute-done.56 = bf16[2,48,2048]{2,1,0:T(8,128)(2,1)S(1)} collective-permute-done((bf16[2,48,2048]{2,1,0:T(8,128)(2,1)S(1)}, bf16[2,48,2048]{2,1,0:T(8,128)(2,1)S(1)}, u32[]{:S(2)}, u32[]{:S(2)}) %collective-permute-start.56) | collective-permute-done | bytes 393248 | tf_op jit(solution)/shard_map/ppermute | solution.py:342
  518.1 7.3 %fusion.1 = bf16[1024,2048]{1,0:T(8,128)(2,1)S(1)} fusion(f32[1024,2048,1]{1,0,2:T(8,128)} %fusion.79, bf16[20,48,2048]{2,1,0:T(8,128)(2,1)S(1)} %constant_dynamic-update-slice_fusion.2, bf16[20,48,512]{2,1,0:T(8,128)(2,1)S(1)} %copy-done.102, bf16[20,48,512]{2,1,0:T(8,128)(2,1)} %get-tuple-element.1197), kind=kOutput, calls=%fused_computation.8 | convolution fusion | flops 4034658304 | bytes 18481152 | tf_op jit(solution)/shard_map/dot_general | solution.py:600
  532.2 7.3 %fusion = bf16[1024,2048]{1,0:T(8,128)(2,1)S(1)} fusion(f32[1024,2048,1]{1,0,2:T(8,128)} %fusion.80, bf16[20,48,2048]{2,1,0:T(8,128)(2,1)S(1)} %constant_dynamic-update-slice_fusion.7, bf16[20,48,512]{2,1,0:T(8,128)(2,1)S(1)} %copy-done.104, bf16[20,48,512]{2,1,0:T(8,128)(2,1)} %get-tuple-element.1205), kind=kOutput, calls=%fused_computation.6 | convolution fusion | flops 4034658304 | bytes 18481152 | tf_op jit(solution)/shard_map/dot_general | solution.py:600
  542.8 10.9 %collective-permute-done.58 = bf16[2,2,64,2048]{3,2,1,0:T(8,128)(2,1)S(1)} collective-permute-done((bf16[2,2,64,2048]{3,2,1,0:T(8,128)(2,1)S(1)}, bf16[2,2,64,2048]{3,2,1,0:T(8,128)(2,1)S(1)}, u32[]{:S(2)}, u32[]{:S(2)}) %collective-permute-start.58) | collective-permute-done | bytes 1048608 | tf_op jit(solution)/shard_map/ppermute | solution.py:342
  562.1 24.1 %collective-permute-done.78 = bf16[64,2048]{1,0:T(8,128)(2,1)S(1)} collective-permute-done((bf16[64,2048]{1,0:T(8,128)(2,1)S(1)}, bf16[64,2048]{1,0:T(8,128)(2,1)S(1)}, u32[]{:S(2)}, u32[]{:S(2)}) %collective-permute-start.78) | collective-permute-done | bytes 262176 | tf_op jit(solution)/shard_map/ppermute | solution.py:342
  592.0 4.8 collective-permute-start.69
  599.7 3.9 collective-permute-start.82
  605.6 36.8 %collective-permute-done.62 = bf16[2,2,64,2048]{3,2,1,0:T(8,128)(2,1)S(1)} collective-permute-done((bf16[2,2,64,2048]{3,2,1,0:T(8,128)(2,1)S(1)}, bf16[2,2,64,2048]{3,2,1,0:T(8,128)(2,1)S(1)}, u32[]{:S(2)}, u32[]{:S(2)}) %collective-permute-start.62) | collective-permute-done | bytes 1048608 | tf_op jit(solution)/shard_map/ppermute | solution.py:342
  646.4 20.5 %collective-permute-start.70 = (bf16[2,64,2048]{2,1,0:T(8,128)(2,1)S(1)}, bf16[2,64,2048]{2,1,0:T(8,128)(2,1)S(1)}, u32[]{:S(2)}, u32[]{:S(2)}) collective-permute-start(bf16[2,64,2048]{2,1,0:T(8,128)(2,1)S(1)} %dynamic-slice_bitcast_fusion.6), channel_id=1, source_target_pairs={{0,8},{4,12},{8,0},{12,4},{16,24},{20,28},{24,16},{28,20},{1,9},{5... | collective-permute-start | bytes 1572872 | tf_op jit(solution)/shard_map/ppermute | solution.py:342
  666.9 3.6 collective-permute-done.82
  672.0 10.5 %collective-permute-done.70 = bf16[2,64,2048]{2,1,0:T(8,128)(2,1)S(1)} collective-permute-done((bf16[2,64,2048]{2,1,0:T(8,128)(2,1)S(1)}, bf16[2,64,2048]{2,1,0:T(8,128)(2,1)S(1)}, u32[]{:S(2)}, u32[]{:S(2)}) %collective-permute-start.70) | collective-permute-done | bytes 524320 | tf_op jit(solution)/shard_map/ppermute | solution.py:342
  683.3 5.9 collective-permute-done.63
  (716 shorter events, 443.1 us)
Async XLA Ops:
  16.8 36.1 %collective-permute-start.4 = (bf16[4,512,1024]{2,1,0:T(8,128)(2,1)}, bf16[4,512,1024]{2,1,0:T(8,128)(2,1)}, u32[]{:S(2)}, u32[]{:S(2)}) collective-permute-start(bf16[4,512,1024]{2,1,0:T(8,128)(2,1)} %bitcast.242), channel_id=1, source_target_pairs={{0,1},{1,0},{2,3},{3,2},{4,5},{5,4},{6,7},{7,6},{8,9},{9,8},{10,11... | collective-permute-start | bytes 12582920 | tf_op jit(solution)/shard_map/ppermute | solution.py:288
  24.5 38.1 %collective-permute-start = (bf16[4,512,1024]{1,2,0:T(8,128)(2,1)}, bf16[4,512,1024]{1,2,0:T(8,128)(2,1)}, u32[]{:S(2)}, u32[]{:S(2)}) collective-permute-start(bf16[4,512,1024]{1,2,0:T(8,128)(2,1)} %bitcast.269), channel_id=1, source_target_pairs={{0,1},{1,0},{2,3},{3,2},{4,5},{5,4},{6,7},{7,6},{8,9},{9,8},{10,11... | collective-permute-start | bytes 12582920 | tf_op jit(solution)/shard_map/ppermute | solution.py:288
  47.5 136.7 %collective-permute-start.19 = (bf16[20,48,512]{2,1,0:T(8,128)(2,1)}, bf16[20,48,512]{2,1,0:T(8,128)(2,1)}, u32[]{:S(2)}, u32[]{:S(2)}) collective-permute-start(bf16[20,48,512]{2,1,0:T(8,128)(2,1)} %get-tuple-element.811), channel_id=1, source_target_pairs={{0,4},{4,0},{8,12},{12,8},{16,20},{20,16},{24,28},{28,24},{1,5},{5... | collective-permute-start | bytes 2949128 | tf_op jit(solution)/shard_map/ppermute | solution.py:342
  49.2 135.1 %collective-permute-start.20 = (bf16[20,48,512]{2,1,0:T(8,128)(2,1)}, bf16[20,48,512]{2,1,0:T(8,128)(2,1)}, u32[]{:S(2)}, u32[]{:S(2)}) collective-permute-start(bf16[20,48,512]{2,1,0:T(8,128)(2,1)} %get-tuple-element.811), channel_id=1, source_target_pairs={{0,8},{4,12},{8,0},{12,4},{16,24},{20,28},{24,16},{28,20},{1,9},{5... | collective-permute-start | bytes 2949128 | tf_op jit(solution)/shard_map/ppermute | solution.py:342
  227.5 29.4 %collective-permute-start.26 = (bf16[48,512]{1,0:T(8,128)(2,1)S(1)}, bf16[48,512]{1,0:T(8,128)(2,1)S(1)}, u32[]{:S(2)}, u32[]{:S(2)}) collective-permute-start(bf16[48,512]{1,0:T(8,128)(2,1)S(1)} %get-tuple-element.883.p_ref), channel_id=1, source_target_pairs={{0,2},{1,3},{2,0},{3,1},{4,6},{5,7},{6,4},{7,5},{8,10},{9,11},{10,... | collective-permute-start | bytes 147464 | tf_op jit(solution)/shard_map/ppermute | solution.py:420
  254.7 57.5 %collective-permute-start.35 = (bf16[20,48,512]{2,1,0:T(8,128)(2,1)}, bf16[20,48,512]{2,1,0:T(8,128)(2,1)S(1)}, u32[]{:S(2)}, u32[]{:S(2)}) collective-permute-start(bf16[20,48,512]{2,1,0:T(8,128)(2,1)} %get-tuple-element.1003), channel_id=1, source_target_pairs={{0,4},{4,0},{8,12},{12,8},{16,20},{20,16},{24,28},{28,24},{1,5},{5... | collective-permute-start | bytes 2949128 | tf_op jit(solution)/shard_map/ppermute | solution.py:342
  255.3 57.0 %collective-permute-start.36 = (bf16[20,48,512]{2,1,0:T(8,128)(2,1)}, bf16[20,48,512]{2,1,0:T(8,128)(2,1)S(1)}, u32[]{:S(2)}, u32[]{:S(2)}) collective-permute-start(bf16[20,48,512]{2,1,0:T(8,128)(2,1)} %get-tuple-element.1003), channel_id=1, source_target_pairs={{0,8},{4,12},{8,0},{12,4},{16,24},{20,28},{24,16},{28,20},{1,9},{5... | collective-permute-start | bytes 2949128 | tf_op jit(solution)/shard_map/ppermute | solution.py:342
  300.7 52.0 %collective-permute-start.42 = (bf16[6,48,2048]{2,1,0:T(8,128)(2,1)}, bf16[6,48,2048]{2,1,0:T(8,128)(2,1)}, u32[]{:S(2)}, u32[]{:S(2)}) collective-permute-start(bf16[6,48,2048]{2,1,0:T(8,128)(2,1)} %get-tuple-element.1079), channel_id=1, source_target_pairs={{0,4},{4,0},{8,12},{12,8},{16,20},{20,16},{24,28},{28,24},{1,5},{5... | collective-permute-start | bytes 3538952 | tf_op jit(solution)/shard_map/ppermute | solution.py:342
  302.3 50.4 %collective-permute-start.43 = (bf16[6,48,2048]{2,1,0:T(8,128)(2,1)}, bf16[6,48,2048]{2,1,0:T(8,128)(2,1)}, u32[]{:S(2)}, u32[]{:S(2)}) collective-permute-start(bf16[6,48,2048]{2,1,0:T(8,128)(2,1)} %get-tuple-element.1080), channel_id=1, source_target_pairs={{0,8},{4,12},{8,0},{12,4},{16,24},{20,28},{24,16},{28,20},{1,9},{5... | collective-permute-start | bytes 3538952 | tf_op jit(solution)/shard_map/ppermute | solution.py:342
  312.2 74.8 %collective-permute-start.27 = (bf16[20,48,512]{2,1,0:T(8,128)(2,1)}, bf16[20,48,512]{2,1,0:T(8,128)(2,1)}, u32[]{:S(2)}, u32[]{:S(2)}) collective-permute-start(bf16[20,48,512]{2,1,0:T(8,128)(2,1)} %get-tuple-element.900), channel_id=1, source_target_pairs={{0,1},{1,0},{2,3},{3,2},{4,5},{5,4},{6,7},{7,6},{8,9},{9,8},{10,11... | collective-permute-start | bytes 2949128 | tf_op jit(solution)/shard_map/ppermute | solution.py:288
  361.1 50.8 %collective-permute-start.50 = (bf16[6,48,2048]{2,1,0:T(8,128)(2,1)}, bf16[6,48,2048]{2,1,0:T(8,128)(2,1)}, u32[]{:S(2)}, u32[]{:S(2)}) collective-permute-start(bf16[6,48,2048]{2,1,0:T(8,128)(2,1)} %get-tuple-element.1167), channel_id=1, source_target_pairs={{0,4},{4,0},{8,12},{12,8},{16,20},{20,16},{24,28},{28,24},{1,5},{5... | collective-permute-start | bytes 3538952 | tf_op jit(solution)/shard_map/ppermute | solution.py:342
  361.6 50.2 %collective-permute-start.51 = (bf16[6,48,2048]{2,1,0:T(8,128)(2,1)}, bf16[6,48,2048]{2,1,0:T(8,128)(2,1)}, u32[]{:S(2)}, u32[]{:S(2)}) collective-permute-start(bf16[6,48,2048]{2,1,0:T(8,128)(2,1)} %get-tuple-element.1168), channel_id=1, source_target_pairs={{0,8},{4,12},{8,0},{12,4},{16,24},{20,28},{24,16},{28,20},{1,9},{5... | collective-permute-start | bytes 3538952 | tf_op jit(solution)/shard_map/ppermute | solution.py:342
  426.6 101.7 %collective-permute-start.67 = (bf16[4,48,2048]{2,1,0:T(8,128)(2,1)}, bf16[4,48,2048]{2,1,0:T(8,128)(2,1)}, u32[]{:S(2)}, u32[]{:S(2)}) collective-permute-start(bf16[4,48,2048]{2,1,0:T(8,128)(2,1)} %get-tuple-element.1209), channel_id=1, source_target_pairs={{0,8},{4,12},{8,0},{12,4},{16,24},{20,28},{24,16},{28,20},{1,9},{5... | collective-permute-start | bytes 2359304 | tf_op jit(solution)/shard_map/ppermute | solution.py:342
  427.1 86.2 %collective-permute-start.57 = (bf16[4,48,2048]{2,1,0:T(8,128)(2,1)}, bf16[4,48,2048]{2,1,0:T(8,128)(2,1)}, u32[]{:S(2)}, u32[]{:S(2)}) collective-permute-start(bf16[4,48,2048]{2,1,0:T(8,128)(2,1)} %get-tuple-element.1201), channel_id=1, source_target_pairs={{0,4},{4,0},{8,12},{12,8},{16,20},{20,16},{24,28},{28,24},{1,5},{5... | collective-permute-start | bytes 2359304 | tf_op jit(solution)/shard_map/ppermute | solution.py:342
  428.6 98.7 %collective-permute-start.66 = (bf16[2,48,2048]{2,1,0:T(8,128)(2,1)}, bf16[2,48,2048]{2,1,0:T(8,128)(2,1)}, u32[]{:S(2)}, u32[]{:S(2)}) collective-permute-start(bf16[2,48,2048]{2,1,0:T(8,128)(2,1)} %get-tuple-element.1208), channel_id=1, source_target_pairs={{0,8},{4,12},{8,0},{12,4},{16,24},{20,28},{24,16},{28,20},{1,9},{5... | collective-permute-start | bytes 1179656 | tf_op jit(solution)/shard_map/ppermute | solution.py:342
  451.0 50.9 %collective-permute-start.55 = (bf16[2,48,2048]{2,1,0:T(8,128)(2,1)}, bf16[2,48,2048]{2,1,0:T(8,128)(2,1)}, u32[]{:S(2)}, u32[]{:S(2)}) collective-permute-start(bf16[2,48,2048]{2,1,0:T(8,128)(2,1)} %get-tuple-element.1199), channel_id=1, source_target_pairs={{0,4},{4,0},{8,12},{12,8},{16,20},{20,16},{24,28},{28,24},{1,5},{5... | collective-permute-start | bytes 1179656 | tf_op jit(solution)/shard_map/ppermute | solution.py:342
  501.9 39.0 %collective-permute-start.76 = (bf16[4,64,2048]{2,1,0:T(8,128)(2,1)S(1)}, bf16[4,64,2048]{2,1,0:T(8,128)(2,1)S(1)}, u32[]{:S(2)}, u32[]{:S(2)}) collective-permute-start(bf16[4,64,2048]{2,1,0:T(8,128)(2,1)S(1)} %dynamic-slice_bitcast_fusion.1), channel_id=1, source_target_pairs={{0,4},{4,0},{8,12},{12,8},{16,20},{20,16},{24,28},{28,24},{1,5},{5... | collective-permute-start | bytes 3145736 | tf_op jit(solution)/shard_map/ppermute | solution.py:342
  513.3 45.3 %collective-permute-start.53 = (bf16[20,48,256]{2,1,0:T(8,128)(2,1)S(1)}, bf16[20,48,256]{2,1,0:T(8,128)(2,1)S(1)}, u32[]{:S(2)}, u32[]{:S(2)}) collective-permute-start(bf16[20,48,256]{2,1,0:T(8,128)(2,1)S(1)} %dynamic-slice_convert_fusion), channel_id=1, source_target_pairs={{0,2},{1,3},{2,0},{3,1},{4,6},{5,7},{6,4},{7,5},{8,10},{9,11},{10,... | collective-permute-start | bytes 1474568 | tf_op jit(solution)/shard_map/ppermute | solution.py:647
  525.7 28.1 %collective-permute-start.58 = (bf16[2,2,64,2048]{3,2,1,0:T(8,128)(2,1)S(1)}, bf16[2,2,64,2048]{3,2,1,0:T(8,128)(2,1)S(1)}, u32[]{:S(2)}, u32[]{:S(2)}) collective-permute-start(bf16[2,2,64,2048]{3,2,1,0:T(8,128)(2,1)S(1)} %get-tuple-element.1238), channel_id=1, source_target_pairs={{0,8},{4,12},{1,9},{5,13},{2,10},{6,14},{3,11},{7,15}} | collective-permute-start | bytes 3145736 | tf_op jit(solution)/shard_map/ppermute | solution.py:342
  539.7 51.1 %collective-permute-start.68 = (bf16[2,4,64,2048]{3,2,1,0:T(8,128)(2,1)S(1)}, bf16[2,4,64,2048]{3,2,1,0:T(8,128)(2,1)S(1)}, u32[]{:S(2)}, u32[]{:S(2)}) collective-permute-start(bf16[2,4,64,2048]{3,2,1,0:T(8,128)(2,1)S(1)} %dynamic-slice_bitcast_fusion), channel_id=1, source_target_pairs={{0,4},{4,0},{8,12},{12,8},{16,20},{20,16},{24,28},{28,24},{1,5},{5... | collective-permute-start | bytes 6291464 | tf_op jit(solution)/shard_map/ppermute | solution.py:342
  540.2 47.4 %collective-permute-start.61 = (bf16[2,2,64,2048]{3,2,1,0:T(8,128)(2,1)S(1)}, bf16[2,2,64,2048]{3,2,1,0:T(8,128)(2,1)S(1)}, u32[]{:S(2)}, u32[]{:S(2)}) collective-permute-start(bf16[2,2,64,2048]{3,2,1,0:T(8,128)(2,1)S(1)} %get-tuple-element.1239), channel_id=1, source_target_pairs={{24,16},{28,20},{25,17},{29,21},{26,18},{30,22},{27,19},{31,23}} | collective-permute-start | bytes 3145736 | tf_op jit(solution)/shard_map/ppermute | solution.py:342
  556.5 31.1 %collective-permute-start.59 = (bf16[2,2,64,2048]{3,2,1,0:T(8,128)(2,1)S(1)}, bf16[2,2,64,2048]{3,2,1,0:T(8,128)(2,1)S(1)}, u32[]{:S(2)}, u32[]{:S(2)}) collective-permute-start(bf16[2,2,64,2048]{3,2,1,0:T(8,128)(2,1)S(1)} %fusion.8), channel_id=1, source_target_pairs={{0,8},{4,12},{8,16},{12,20},{1,9},{5,13},{9,17},{13,21},{2,10},{6,... | collective-permute-start | bytes 3145736 | tf_op jit(solution)/shard_map/ppermute | solution.py:342
  558.6 27.7 %collective-permute-start.78 = (bf16[64,2048]{1,0:T(8,128)(2,1)S(1)}, bf16[64,2048]{1,0:T(8,128)(2,1)S(1)}, u32[]{:S(2)}, u32[]{:S(2)}) collective-permute-start(bf16[64,2048]{1,0:T(8,128)(2,1)S(1)} %fusion.23), channel_id=1, source_target_pairs={{0,8},{4,12},{8,16},{12,20},{1,9},{5,13},{9,17},{13,21},{2,10},{6,... | collective-permute-start | bytes 786440 | tf_op jit(solution)/shard_map/ppermute | solution.py:342
  562.0 34.8 %collective-permute-start.54 = (bf16[20,48,128]{2,1,0:T(8,128)(2,1)S(1)}, bf16[20,48,128]{2,1,0:T(8,128)(2,1)S(1)}, u32[]{:S(2)}, u32[]{:S(2)}) collective-permute-start(bf16[20,48,128]{2,1,0:T(8,128)(2,1)S(1)} %constant_dynamic-slice_fusion.4), channel_id=1, source_target_pairs={{0,1},{1,0},{2,3},{3,2},{4,5},{5,4},{6,7},{7,6},{8,9},{9,8},{10,11... | collective-permute-start | bytes 737288 | tf_op jit(solution)/shard_map/ppermute | solution.py:288
  589.5 52.9 %collective-permute-start.62 = (bf16[2,2,64,2048]{3,2,1,0:T(8,128)(2,1)S(1)}, bf16[2,2,64,2048]{3,2,1,0:T(8,128)(2,1)S(1)}, u32[]{:S(2)}, u32[]{:S(2)}) collective-permute-start(bf16[2,2,64,2048]{3,2,1,0:T(8,128)(2,1)S(1)} %get-tuple-element.1237), channel_id=1, source_target_pairs={{16,8},{20,12},{24,16},{28,20},{17,9},{21,13},{25,17},{29,21},{18,... | collective-permute-start | bytes 3145736 | tf_op jit(solution)/shard_map/ppermute | solution.py:342
  592.0 53.9 %collective-permute-start.69 = (bf16[2,2,64,2048]{3,2,0,1:T(8,128)(2,1)S(1)}, bf16[2,2,64,2048]{3,2,0,1:T(8,128)(2,1)S(1)}, u32[]{:S(2)}, u32[]{:S(2)}) collective-permute-start(bf16[2,2,64,2048]{3,2,0,1:T(8,128)(2,1)S(1)} %bitcast.272), channel_id=1, source_target_pairs={{0,16},{4,20},{8,24},{12,28},{16,0},{20,4},{24,8},{28,12},{1,17},{... | collective-permute-start | bytes 3145736 | tf_op jit(solution)/shard_map/ppermute | solution.py:342
  597.7 69.2 %collective-permute-start.79 = (bf16[64,2048]{1,0:T(8,128)(2,1)S(1)}, bf16[64,2048]{1,0:T(8,128)(2,1)S(1)}, u32[]{:S(2)}, u32[]{:S(2)}) collective-permute-start(bf16[64,2048]{1,0:T(8,128)(2,1)S(1)} %get-tuple-element.1252), channel_id=1, source_target_pairs={{0,8},{4,12},{8,16},{12,20},{16,24},{20,28},{1,9},{5,13},{9,17},{1... | collective-permute-start | bytes 786440 | tf_op jit(solution)/shard_map/ppermute | solution.py:342
  599.7 70.8 %collective-permute-start.82 = (bf16[64,2048]{1,0:T(8,128)(2,1)S(1)}, bf16[64,2048]{1,0:T(8,128)(2,1)S(1)}, u32[]{:S(2)}, u32[]{:S(2)}) collective-permute-start(bf16[64,2048]{1,0:T(8,128)(2,1)S(1)} %fusion.22), channel_id=1, source_target_pairs={{8,0},{12,4},{16,8},{20,12},{24,16},{28,20},{9,1},{13,5},{17,9},{2... | collective-permute-start | bytes 786440 | tf_op jit(solution)/shard_map/ppermute | solution.py:342
  603.6 79.6 %collective-permute-start.60 = (bf16[2,2,64,2048]{3,2,1,0:T(8,128)(2,1)}, bf16[2,2,64,2048]{3,2,1,0:T(8,128)(2,1)}, u32[]{:S(2)}, u32[]{:S(2)}) collective-permute-start(bf16[2,2,64,2048]{3,2,1,0:T(8,128)(2,1)} %get-tuple-element.1236), channel_id=1, source_target_pairs={{0,8},{4,12},{8,16},{12,20},{16,24},{20,28},{1,9},{5,13},{9,17},{1... | collective-permute-start | bytes 3145736 | tf_op jit(solution)/shard_map/ppermute | solution.py:342
  643.7 45.5 %collective-permute-start.63 = (bf16[2,2,64,2048]{3,2,1,0:T(8,128)(2,1)}, bf16[2,2,64,2048]{3,2,1,0:T(8,128)(2,1)}, u32[]{:S(2)}, u32[]{:S(2)}) collective-permute-start(bf16[2,2,64,2048]{3,2,1,0:T(8,128)(2,1)} %fusion.7), channel_id=1, source_target_pairs={{8,0},{12,4},{16,8},{20,12},{24,16},{28,20},{9,1},{13,5},{17,9},{2... | collective-permute-start | bytes 3145736 | tf_op jit(solution)/shard_map/ppermute | solution.py:342
  646.4 36.1 %collective-permute-start.70 = (bf16[2,64,2048]{2,1,0:T(8,128)(2,1)S(1)}, bf16[2,64,2048]{2,1,0:T(8,128)(2,1)S(1)}, u32[]{:S(2)}, u32[]{:S(2)}) collective-permute-start(bf16[2,64,2048]{2,1,0:T(8,128)(2,1)S(1)} %dynamic-slice_bitcast_fusion.6), channel_id=1, source_target_pairs={{0,8},{4,12},{8,0},{12,4},{16,24},{20,28},{24,16},{28,20},{1,9},{5... | collective-permute-start | bytes 1572872 | tf_op jit(solution)/shard_map/ppermute | solution.py:342
  671.9 26.4 %collective-permute-start.83 = (bf16[1024,64]{0,1:T(8,128)(2,1)S(1)}, bf16[1024,64]{0,1:T(8,128)(2,1)}, u32[]{:S(2)}, u32[]{:S(2)}) collective-permute-start(bf16[1024,64]{0,1:T(8,128)(2,1)S(1)} %bitcast.276), channel_id=1, source_target_pairs={{0,1},{1,0},{2,3},{3,2},{4,5},{5,4},{6,7},{7,6},{8,9},{9,8},{10,11... | collective-permute-start | bytes 393224 | tf_op jit(solution)/shard_map/ppermute | solution.py:288
  (215 other events, 2578.4 us)

commit v4 on v3

--- a/solution.py
+++ b/solution.py
@@ -12,7 +12,7 @@
 QUARTERS, HALVES = 2, 2
 PIECES = QUARTERS * HALVES
 MIB = 2**20
-SHARES = (0.3, 0.3, 0.2, 0.1, 0.1)
+SHARES = (0.35, 0.3, 0.2, 0.1, 0.05)
 
 VMEM = pl.BlockSpec(memory_space=pltpu.VMEM)
 SMEM = pl.BlockSpec(memory_space=pltpu.SMEM)
@@ -50,7 +50,62 @@
         scratch_shapes=[pltpu.SemaphoreType.DMA((count,))],
         compiler_params=params(1),
         name="place",
-    )(*arrays)
+    )(*(in_hbm(x) for x in arrays))
+
+
+def layout_kernel(which_ref, w_ref, out_ref, buf, sems):
+    depth, part = w_ref.shape[1], buf.shape[1]
+
+    def fetch(i):
+        return pltpu.make_async_copy(w_ref.at[which_ref[0], pl.ds(i * part, part)], buf.at[i % 3], sems.at[i % 3])
+
+    count = depth // part
+    for i in range(min(2, count)):
+        fetch(i).start()
+    for i in range(count):
+        if i + 2 < count:
+            fetch(i + 2).start()
+        fetch(i).wait()
+        out_ref[:, i * part : (i + 1) * part, :] = jnp.swapaxes(buf[i % 3], 0, 1)
+
+
+def turned_kernel(wa_ref, wb_ref, pa_ref, pb_ref, wat_ref, wbt_ref, pat_ref, pbt_ref):
+    for w_ref, out_ref in ((wa_ref, wat_ref), (wb_ref, wbt_ref)):
+        for gate in range(4):
+            for half in range(HALVES):
+                width = w_ref.shape[2] // HALVES
+                cols = slice(half * width, (half + 1) * width)
+                out_ref[gate, cols, :] = w_ref[gate, :, cols].T
+    pat_ref[...] = pa_ref[...].T
+    pbt_ref[...] = pb_ref[...].T
+
+
+def pass_kernel(*refs):
+    pass
+
+
+def after(token, *arrays):
+    return pl.pallas_call(
+        pass_kernel,
+        out_shape=tuple(pltpu.HBM(x.shape, x.dtype) for x in arrays),
+        in_specs=[ANY] * (1 + len(arrays)),
+        out_specs=[ANY] * len(arrays),
+        input_output_aliases={1 + i: i for i in range(len(arrays))},
+        compiler_params=params(1),
+        name="after",
+    )(token, *(in_hbm(x) for x in arrays))
+
+
+def assemble_kernel(place_ref, near_a, near_b, far_a, far_b, in_ref, rec_ref):
+    own, low, high = place_ref[0], place_ref[1], place_ref[2]
+    width = in_ref.shape[3] // HALVES
+    for direction, mine_ref, theirs_ref, index in ((own, near_a, near_b, low), (1 - own, far_a, far_b, high)):
+        for which, out_ref in ((0, in_ref), (1, rec_ref)):
+            mine, theirs = mine_ref[which].astype(F32), theirs_ref[which].astype(F32)
+            for half in range(HALVES):
+                whole = jnp.where(index == half, mine, theirs)
+                gates = jnp.stack([whole[:, gate * width : (gate + 1) * width] for gate in range(4)])
+                out_ref[direction, :, :, half * width : (half + 1) * width] = jnp.swapaxes(gates, 0, 1)
 
 
 def order_kernel(step_ref, feat_ref, out_ref, all_ref, sems, all_sem):
@@ -113,14 +168,13 @@
 
 
 def between_kernel(
-    first, passed, step_ref, feat_ref, bias_ref, wa_ref, wb_ref, cell_ref, gates_ref, mixed_ref, prev_ref, hidden_ref,
+    first, last, passed, step_ref, feat_ref, bias_ref, wa_ref, wb_ref, cell_ref, gates_ref, mixed_ref, prev_ref, hidden_ref,
     slope_ref, *refs,
 ):
     refs = refs[(0 if first else 6) + passed :]
     out_ref, gates_all, cells_all, mixed_all, prev_all, hidden_all, slope_all = refs[:7]
     sems = refs[-1]
     step, time_before = step_ref[0], step_ref[2]
-    after = jnp.minimum(step + 1, feat_ref.shape[0] - 1)
     copies = [pltpu.make_async_copy(gates_ref.at[i], gates_all.at[i, step], sems.at[i]) for i in range(PIECES)]
     copies += [
         pltpu.make_async_copy(mixed_ref.at[i], mixed_all.at[i, step], sems.at[PIECES + i]) for i in range(PIECES)
@@ -132,7 +186,8 @@
         copies.append(pltpu.make_async_copy(slope_ref, slope_all.at[step - 1], sems.at[2 * PIECES + 3]))
     for copy in copies:
         copy.start()
-    inflow_into(feat_ref[after], bias_ref, wa_ref, wb_ref, out_ref)
+    if not last:
+        inflow_into(feat_ref[step + 1], bias_ref, wa_ref, wb_ref, out_ref)
     for copy in copies:
         copy.wait()
 
@@ -287,11 +342,28 @@
     def trade(mine, theirs):
         return (mine, lax.ppermute(theirs, "gate", swap))
 
-    def by_gate(stacked, index):
-        return jnp.transpose(pick(stacked, index), (1, 0, 2))
-
-    win_a, win_b = trade(by_gate(w_in, own), by_gate(w_in, 1 - own))
-    rec_a, rec_b = trade(by_gate(w_rec, own), by_gate(w_rec, 1 - own))
+    def vmem(shape, dtype):
+        return pltpu.VMEM(shape, dtype)
+
+    def hbm(shape, dtype):
+        return pltpu.HBM(shape, dtype)
+
+    def by_gate(weights, index):
+        shape = (4,) + weights.shape[1:2] + weights.shape[3:]
+        part = weights.shape[1] // 8
+        return pl.pallas_call(
+            layout_kernel,
+            out_shape=vmem(shape, BF16),
+            in_specs=[SMEM, ANY],
+            out_specs=VMEM,
+            scratch_shapes=[pltpu.VMEM((3, part) + weights.shape[2:], BF16), pltpu.SemaphoreType.DMA((3,))],
+            compiler_params=params(8),
+            name="layout",
+        )(jnp.full((1,), index, jnp.int32), in_hbm(weights))
+
+    sent = [by_gate(w, 1 - own) for w in (w_in, w_rec)]
+    win_b, rec_b = (lax.ppermute(x, "gate", swap) for x in sent)
+    win_av, rec_av = by_gate(w_in, own), by_gate(w_rec, own)
     proj_a, proj_b = trade(pick(proj, own), pick(proj, 1 - own))
     bias_a, bias_b = trade(pick(bias, own), pick(bias, 1 - own))
 
@@ -325,12 +397,6 @@
         near = jnp.array([step, step, max(step - 1, 0), min(step + 1, steps - 1)], jnp.int32)
         turned = jnp.array([step] + [steps - 1 - x for x in (step, max(step - 1, 0), min(step + 1, steps - 1))], jnp.int32)
         return jnp.where(own == 0, near, turned)
-
-    def vmem(shape, dtype):
-        return pltpu.VMEM(shape, dtype)
-
-    def hbm(shape, dtype):
-        return pltpu.HBM(shape, dtype)
 
     n_batch = lax.axis_size("batch")
     spot = lax.axis_index("batch")
@@ -352,8 +418,8 @@
         name="order",
     )(turn, feats)
     feat_in = (swapped(feat_all, near_swap), swapped(feat_all, far_swap))
-    keep_v, bias_v, win_av, win_bv = place(keep, bias_p, win_a, win_b)
-    rec_av, rec_bv, proj_av, proj_bv, start_hv, start_cv = place(rec_a, rec_b, proj_a, proj_b, start_h, start_c)
+    keep_v, bias_v, win_bv = place(keep, bias_p, win_b)
+    rec_bv, proj_av, proj_bv, start_hv, start_cv = place(rec_b, proj_a, proj_b, start_h, start_c)
 
     gates_shape, cell_shape = (PIECES, streams, 4 * width), (PIECES, streams, width)
     inflow = pl.pallas_call(
@@ -398,7 +464,7 @@
         aliases = {11 + i: 1 + i for i in range(len(stacks))}
         aliases.update({11 + len(stacks) + i: 7 + i for i in range(len(passing))})
         inflow, *out = pl.pallas_call(
-            functools.partial(between_kernel, not stacks, len(passing)),
+            functools.partial(between_kernel, not stacks, step == steps - 1, len(passing)),
             out_shape=(vmem(gates_shape, F32),) + shapes + tuple(hbm(x.shape, x.dtype) for x in passing),
             in_specs=[SMEM] + [VMEM] * 10 + [ANY] * (len(stacks) + len(passing)),
             out_specs=[VMEM] + [ANY] * (6 + len(passing)),
@@ -449,24 +515,14 @@
         in_hbm(hidden_all), in_hbm(slope_all),
     )
 
-    both_hidden = trade(hidden_all, hidden_all)
-
-    def by_direction(mine, theirs):
-        return jnp.stack([jnp.where(own == 0, mine, theirs), jnp.where(own == 0, theirs, mine)])
-
-    hidden_dirs = by_direction(*both_hidden)
-    outputs = (inputs.astype(F32) + jnp.transpose(hidden_dirs, (0, 2, 1, 3)).astype(F32)).astype(BF16)
-    last_h = jnp.stack([hidden_dirs[0, steps - 1], hidden_dirs[1, 0]], axis=1).astype(F32)
-    final_h = jnp.zeros_like(state_h).at[stream_doc].set(last_h)
-    last_c = jnp.transpose(cell.reshape(QUARTERS, HALVES, streams, width), (0, 2, 1, 3)).reshape(
-        QUARTERS, streams, cells
-    )
-    last_dirs = by_direction(*trade(last_c[0], last_c[1]))
-    final_c = jnp.zeros_like(state_c).at[stream_doc].set(jnp.transpose(last_dirs, (1, 0, 2)))
-
-    rec_at, rec_bt = (jnp.transpose(x, (0, 2, 1)) for x in (rec_a, rec_b))
-    proj_at, proj_bt = jnp.transpose(proj_a), jnp.transpose(proj_b)
-    rec_atv, rec_btv, proj_atv, proj_btv = place(rec_at, rec_bt, proj_at, proj_bt)
+    rec_atv, rec_btv, proj_atv, proj_btv = pl.pallas_call(
+        turned_kernel,
+        out_shape=(vmem((4, cells, depth), BF16),) * 2 + (vmem((depth, cells), BF16),) * 2,
+        in_specs=[VMEM] * 4,
+        out_specs=[VMEM] * 4,
+        compiler_params=params(8),
+        name="turned",
+    )(pinned(rec_av), pinned(rec_bv), pinned(proj_av), pinned(proj_bv))
 
     def backward_call(step, part, peer, grad, saved):
         return pl.pallas_call(
@@ -537,11 +593,110 @@
             arrived += [passed] if passed else []
             carry = (part, peer, grad, saved, stacks)
         top -= slots
-        pending.append((top - 2 - (2 * slots + 2) // 3, (swapped(sends[0], near_swap), swapped(sends[1], far_swap))))
+        due = max(top - 1 - (3 * slots + 3) // 4, 0 if slots > 2 else -1)
+        pending.append((due, (swapped(sends[0], near_swap), swapped(sends[1], far_swap))))
     arrived += [arrays for _, arrays in pending]
     dz_all, raw_all, near_all, far_all = carry[-1]
-    prev_in, exchanged = arrived[0], arrived[:0:-1]
+    prev_in, exchanged = arrived[0], arrived[1:]
     rows = steps * streams
+
+    def by_direction(mine, theirs):
+        return jnp.stack([jnp.where(own == 0, mine, theirs), jnp.where(own == 0, theirs, mine)])
+
+    def line_sum(chunks, axis, stride, count):
+        here = (spot // stride) % count
+
+        def chunk(index):
+            return lax.dynamic_index_in_dim(chunks, jnp.clip(index, 0, count - 1), axis, keepdims=False)
+
+        def at(device):
+            return (device // stride) % count
+
+        if count == 2:
+            pairs = [(i, i + stride if at(i) == 0 else i - stride) for i in range(n_batch)]
+            return (chunk(here).astype(F32) + swapped(chunk(1 - here), pairs).astype(F32)).astype(BF16)
+        up, down = None, None
+        for slot in range(1, count):
+            rise, fall = chunk(here + count - slot), chunk(here - count + slot)
+            if slot > 1:
+                rise = (rise.astype(F32) + up.astype(F32)).astype(BF16)
+                fall = (fall.astype(F32) + down.astype(F32)).astype(BF16)
+            up = swapped(rise, [(i, i + stride) for i in range(n_batch) if at(i) < min(slot, count - 1)])
+            down = swapped(fall, [(i, i - stride) for i in range(n_batch) if at(i) > max(count - 1 - slot, 0)])
+        return (chunk(here).astype(F32) + up.astype(F32) + down.astype(F32)).astype(BF16)
+
+    line = n_batch // 2
+    share_rows = depth // n_batch
+
+    def product(left, right):
+        return lax.dot_general(
+            left.reshape(rows, -1), right.reshape(rows, -1), (((0,), (0,)), ((), ())), preferred_element_type=F32
+        )
+
+    def both(feat, prev):
+        return jnp.concatenate([feat, prev], axis=2)
+
+    left = both(feat_all, prev_all)
+    halves = []
+    for kept, feat, prev, taken in zip((near_all, far_all), feat_in, prev_in, zip(*exchanged)):
+        mine = product(left, kept)
+        *taken, late, latest = taken
+        late, latest = after(mine, late, latest)
+        theirs = product(both(feat, prev), jnp.concatenate([latest, late, *taken[::-1]], axis=0))
+        halves.append((mine + theirs).astype(BF16).reshape(2, line, 2, share_rows, 4 * width))
+    near = line_sum(halves[0], 1, 2, line)
+    far = line_sum(halves[1], 2, 1, 2).reshape(2, line // 2, 2, share_rows, 4 * width)
+    far = line_sum(far, 1, 4, line // 2)
+
+    def halves_of(summed, index, pairs):
+        mine = lax.dynamic_index_in_dim(summed, index, 1, keepdims=False)
+        return mine, swapped(lax.dynamic_index_in_dim(summed, 1 - index, 1, keepdims=False), pairs)
+
+    near_pair = halves_of(near, low, near_swap)
+    far_pair = [lax.ppermute(x, "gate", swap) for x in halves_of(far, high, far_swap)]
+    grad_shape = (2, share_rows, 4, cells)
+    grad_w_in, grad_w_rec = pl.pallas_call(
+        assemble_kernel,
+        out_shape=(jax.ShapeDtypeStruct(grad_shape, F32),) * 2,
+        in_specs=[SMEM] + [VMEM] * 4,
+        out_specs=[VMEM] * 2,
+        compiler_params=params(32),
+        name="assemble",
+    )(jnp.stack([own, low, high]), *near_pair, *far_pair)
+
+    dz_all, mixed_all, hidden_all, cell = after(halves[1], dz_all, mixed_all, hidden_all, cell)
+
+    grad_proj = jnp.einsum("ptnc,tnk->kpc", mixed_all, raw_all, preferred_element_type=F32).astype(BF16)
+    grad_proj = line_sum(grad_proj.reshape(line, 2, share_rows, QUARTERS * cells), 1, 1, 2)
+    grad_proj = line_sum(grad_proj, 0, 2, line)
+
+    grad_bias = jnp.sum(dz_all, axis=(1, 2), dtype=F32)
+    stride = 1
+    while stride < n_batch:
+        grad_bias = grad_bias + swapped(grad_bias, [(i, i ^ stride) for i in range(n_batch)])
+        stride *= 2
+
+    def home(mine, theirs):
+        return by_direction(*trade(mine, theirs)).astype(F32)
+
+    shaped = jnp.transpose(grad_bias.reshape(QUARTERS, HALVES, 4, width), (0, 2, 1, 3)).reshape(QUARTERS, 4, cells)
+    own_cells = cells // n_batch
+    shaped = lax.dynamic_slice_in_dim(shaped, spot * own_cells, own_cells, 2)
+    grad_bias = home(shaped[0], shaped[1])
+    grad_proj = grad_proj.reshape(share_rows, QUARTERS, cells)
+    grad_proj = home(jnp.transpose(grad_proj[:, 0]), jnp.transpose(grad_proj[:, 1]))
+
+    both_hidden = trade(hidden_all, hidden_all)
+
+    hidden_dirs = by_direction(*both_hidden)
+    outputs = (inputs.astype(F32) + jnp.transpose(hidden_dirs, (0, 2, 1, 3)).astype(F32)).astype(BF16)
+    last_h = jnp.stack([hidden_dirs[0, steps - 1], hidden_dirs[1, 0]], axis=1).astype(F32)
+    final_h = jnp.zeros_like(state_h).at[stream_doc].set(last_h)
+    last_c = jnp.transpose(cell.reshape(QUARTERS, HALVES, streams, width), (0, 2, 1, 3)).reshape(
+        QUARTERS, streams, cells
+    )
+    last_dirs = by_direction(*trade(last_c[0], last_c[1]))
+    final_c = jnp.zeros_like(state_c).at[stream_doc].set(jnp.transpose(last_dirs, (1, 0, 2)))
 
     dx_all = pl.pallas_call(
         input_grad_kernel,
@@ -564,81 +719,7 @@
         compiler_params=params(24),
         cost_estimate=cost(2 * rows * depth * 8 * cells, 8 * depth * cells * 4),
         name="input_grad",
-    )(turn, dz_all, win_a, win_b)
-
-    def line_sum(chunks, axis, stride, count):
-        here = (spot // stride) % count
-
-        def chunk(index):
-            return lax.dynamic_index_in_dim(chunks, jnp.clip(index, 0, count - 1), axis, keepdims=False)
-
-        def at(device):
-            return (device // stride) % count
-
-        if count == 2:
-            pairs = [(i, i + stride if at(i) == 0 else i - stride) for i in range(n_batch)]
-            return (chunk(here).astype(F32) + swapped(chunk(1 - here), pairs).astype(F32)).astype(BF16)
-        up, down = None, None
-        for slot in range(1, count):
-            rise, fall = chunk(here + count - slot), chunk(here - count + slot)
-            if slot > 1:
-                rise = (rise.astype(F32) + up.astype(F32)).astype(BF16)
-                fall = (fall.astype(F32) + down.astype(F32)).astype(BF16)
-            up = swapped(rise, [(i, i + stride) for i in range(n_batch) if at(i) < min(slot, count - 1)])
-            down = swapped(fall, [(i, i - stride) for i in range(n_batch) if at(i) > max(count - 1 - slot, 0)])
-        return (chunk(here).astype(F32) + up.astype(F32) + down.astype(F32)).astype(BF16)
-
-    line = n_batch // 2
-    share_rows = depth // n_batch
-
-    def finish_halves(halves, index, pairs):
-        mine = lax.dynamic_index_in_dim(halves, index, 1, keepdims=False)
-        theirs = swapped(lax.dynamic_index_in_dim(halves, 1 - index, 1, keepdims=False), pairs)
-        return jnp.stack([jnp.where(index == 0, mine, theirs), jnp.where(index == 0, theirs, mine)], axis=1)
-
-    def product(left, right):
-        return lax.dot_general(
-            left.reshape(rows, -1), right.reshape(rows, -1), (((0,), (0,)), ((), ())), preferred_element_type=F32
-        )
-
-    def both(feat, prev):
-        return jnp.concatenate([feat, prev], axis=2)
-
-    left = both(feat_all, prev_all)
-    sums = [
-        (product(left, kept) + product(both(feat, prev), jnp.concatenate(taken, axis=0)))
-        .astype(BF16)
-        .reshape(2, line, 2, share_rows, 4 * width)
-        for kept, feat, prev, taken in zip((near_all, far_all), feat_in, prev_in, zip(*exchanged))
-    ]
-    near = finish_halves(line_sum(sums[0], 1, 2, line), low, near_swap)
-    far = line_sum(sums[1], 2, 1, 2).reshape(2, line // 2, 2, share_rows, 4 * width)
-    far = finish_halves(line_sum(far, 1, 4, line // 2), high, far_swap)
-
-    grad_proj = jnp.einsum("ptnc,tnk->kpc", mixed_all, raw_all, preferred_element_type=F32).astype(BF16)
-    grad_proj = line_sum(grad_proj.reshape(line, 2, share_rows, QUARTERS * cells), 1, 1, 2)
-    grad_proj = line_sum(grad_proj, 0, 2, line)
-
-    grad_bias = jnp.sum(dz_all, axis=(1, 2), dtype=F32)
-    stride = 1
-    while stride < n_batch:
-        grad_bias = grad_bias + swapped(grad_bias, [(i, i ^ stride) for i in range(n_batch)])
-        stride *= 2
-
-    def gate_rows(halves):
-        shaped = halves.reshape(2, HALVES, -1, 4, width)
-        return jnp.transpose(shaped, (0, 2, 3, 1, 4)).reshape(2, -1, 4, cells)
-
-    def home(mine, theirs):
-        return by_direction(*trade(mine, theirs)).astype(F32)
-
-    grad_w_in, grad_w_rec = jnp.moveaxis(home(gate_rows(near), gate_rows(far)), 1, 0)
-    shaped = jnp.transpose(grad_bias.reshape(QUARTERS, HALVES, 4, width), (0, 2, 1, 3)).reshape(QUARTERS, 4, cells)
-    own_cells = cells // n_batch
-    shaped = lax.dynamic_slice_in_dim(shaped, spot * own_cells, own_cells, 2)
-    grad_bias = home(shaped[0], shaped[1])
-    grad_proj = grad_proj.reshape(share_rows, QUARTERS, cells)
-    grad_proj = home(jnp.transpose(grad_proj[:, 0]), jnp.transpose(grad_proj[:, 1]))
+    )(turn, dz_all, win_av, win_bv)
 
     half_cols = depth // 2
     upper = rank // 2

time: 726 us -> 653 us (0.90)
  local copies, waits for them, and re-layouts: 152 us -> 80.7 us
  Pallas kernels: 267 us -> 289 us
  starting transfers between devices: 113 us -> 92.6 us
    dynamic_slice x9 -> x1, local copies, waits for them, and re-layouts: 41.3 us -> 0.01 us  [pick(): return lax.dynamic_index_in_dim(stacked, index, 0, keepdims=False)]
    pallas_call x20 -> x29, Pallas kernels: 61.1 us -> 84.9 us  [the longest x20 60 us: between_call(): pl.pallas_call(functools.partial(between_kernel, not stacks, step == step...]
    ppermute x34, starting transfers between devices: 66.8 us -> 43.9 us  [swapped(): return lax.ppermute(array, 'batch', pairs)]
    unnamed x341 -> x317, local copies, waits for them, and re-layouts: 56.8 us -> 36.4 us
    dynamic_slice x2 -> x5, local copies, waits for them, and re-layouts: 0.25 us -> 9.29 us  [chunk(): lax.dynamic_index_in_dim(chunks, jnp.clip(index, 0, count - 1), axis, kee...]
    ppermute x2 -> x0, local copies, waits for them, and re-layouts: 7.58 us -> none  [trade(): return (mine, lax.ppermute(theirs, 'gate', swap))]
  transfers between devices with their start and end apart: 85 -> 86, of which waited for: 27 -> 40; matrix products, arithmetic and copies ran while one was open for 22% -> 16% of each run, Pallas kernels for 35% -> 38%
where the time goes in v4:
time: 653 us; the launch traced here: 646 us
  Pallas kernels  289 us (44%)
  waiting for transfers between devices  109 us (17%)
  starting transfers between devices  92.6 us (14%)
  local copies, waits for them, and re-layouts  80.7 us (12%)
  other arithmetic  39.2 us (6%)
  matrix products  31.6 us (5%)
    ppermute x34, waiting for transfers between devices, swapped(): return lax.ppermute(array, 'batch', pairs)  98.6 us
    pallas_call x20, Pallas kernels, backward_call(): pl.pallas_call(backward_kernel, out_shape=(vmem((streams, depth), BF16),...  61.2 us
    pallas_call x20, Pallas kernels, between_call(): pl.pallas_call(functools.partial(between_kernel, not stacks, step == step...  60 us
    pallas_call x20, Pallas kernels, aside_call(): pl.pallas_call(functools.partial(aside_kernel, not stacks, not sends, len...  57.1 us
    pallas_call x20, Pallas kernels, forward_call(): pl.pallas_call(functools.partial(forward_kernel, first), out_shape=(vmem(...  56.8 us
    ppermute x39, starting transfers between devices, body(): peer = lax.ppermute(part, 'gate', across)  44.9 us
    ppermute x34, starting transfers between devices, swapped(): return lax.ppermute(array, 'batch', pairs)  43.9 us
    unnamed x317, local copies, waits for them, and re-layouts  36.4 us
  transfers between devices with their start and end apart: 86, of which 40 were waited for; matrix products, arithmetic and copies ran while one was open for 16% of the time, Pallas kernels for 38%

profile of v4, /device:TPU:8, one launch (start us, length us, event | category | flops | bytes accessed | tf_op | source)
XLA Modules:
  0.0 645.7 jit_solution(16923002279847579277)
XLA Ops:
  0.7 5.7 layout.4
  6.4 5.7 layout.6
  19.5 3.6 layout.5.wa_ref
  25.3 3.6 layout.7.wa_ref
  31.6 3.3 order.1
  75.9 3.4 between.23
  146.7 3.2 between.33
  168.1 3.3 between.36
  203.9 3.5 finish.1
  308.8 3.4 backward_step.33
  364.4 3.8 backward_step.39
  369.1 3.9 aside.39
  373.8 7.0 %convolution_bitcast_fusion.refs_0_ = f32[1024,2048]{1,0:T(8,128)S(1)} fusion(bf16[20,48,1024]{2,1,0:T(8,128)(2,1)S(1)} %constant_dynamic-update-slice_fusion, bf16[20,48,2048]{2,1,0:T(8,128)(2,1)} %get-tuple-element.1219), kind=kOutput, calls=%fused_computation.9 | convolution fusion | flops 4026531840 | bytes 14286848 | tf_op jit(solution)/shard_map/dot_general | solution.py:632
  380.9 4.6 convolution_bitcast_fusion.1.refs_0_
  399.5 8.3 %fusion.1 = bf16[1024,2048]{1,0:T(8,128)(2,1)S(1)} fusion(f32[1024,2048]{1,0:T(8,128)S(1)} %convolution_bitcast_fusion.1.refs_0_, bf16[20,48,2048]{2,1,0:T(8,128)(2,1)} %copy-done.105, bf16[20,48,512]{2,1,0:T(8,128)(2,1)} %get-tuple-element.1206, bf16[20,48,512]{2,1,0:T(8,128)(2,1)} %get-tuple-element.1205), kind=kOutput, calls=%fused_computation.8 | convolution fusion | flops 4034658304 | bytes 18481152 | tf_op jit(solution)/shard_map/dot_general | solution.py:632
  409.9 9.0 %convert_reduce_fusion = f32[4,2048]{1,0:T(4,128)S(1)} fusion(bf16[4,20,48,2048]{3,2,1,0:T(8,128)(2,1)} %get-tuple-element.1218.dz_ref), kind=kLoop, calls=%fused_computation.4 | loop fusion | flops 15720448 | bytes 15761408 | tf_op jit(solution)/shard_map/reduce_sum | solution.py:673
  422.0 14.6 %input_grad.1 = f32[20,48,512]{2,1,0:T(8,128)S(1)} custom-call(s32[2]{0:T(128)S(1)} %copy-done.63, bf16[4,20,48,2048]{3,2,1,0:T(8,128)(2,1)S(1)} %copy-done.2, bf16[4,512,1024]{2,1,0:T(8,128)(2,1)S(1)} %copy-done.5, bf16[4,512,1024]{2,1,0:T(8,128)(2,1)S(1)} %copy-done.10), custom_call_target="tpu_custom_call" | custom-call | flops 8053063680 | bytes 16777216 | tf_op jit(solution)/shard_map/input_grad/pallas_call | solution.py:701
  444.3 4.4 reshape.115
  450.1 3.6 dynamic-slice_bitcast_fusion
  462.0 9.3 %fusion = bf16[1024,2048]{1,0:T(8,128)(2,1)} fusion(f32[1024,2048]{1,0:T(8,128)} %copy-done.27, bf16[20,48,2048]{2,1,0:T(8,128)(2,1)S(1)} %copy-done.104, bf16[20,48,512]{2,1,0:T(8,128)(2,1)} %get-tuple-element.1221, bf16[20,48,512]{2,1,0:T(8,128)(2,1)} %get-tuple-element.1220), kind=kOutput, calls=%fused_computation.6 | convolution fusion | flops 4034658304 | bytes 18481152 | tf_op jit(solution)/shard_map/dot_general | solution.py:632
  471.5 5.8 constant_dynamic-slice_fusion.10
  488.8 4.0 scatter_fusion.1
  503.9 11.4 %collective-permute-done.78 = bf16[64,2048]{1,0:T(8,128)(2,1)S(1)} collective-permute-done((bf16[64,2048]{1,0:T(8,128)(2,1)S(1)}, bf16[64,2048]{1,0:T(8,128)(2,1)S(1)}, u32[]{:S(2)}, u32[]{:S(2)}) %collective-permute-start.78) | collective-permute-done | bytes 262176 | tf_op jit(solution)/shard_map/ppermute | solution.py:408
  520.9 5.5 collective-permute-done.79
  529.9 5.2 collective-permute-start.80
  540.0 8.9 %collective-permute-done.62 = bf16[2,2,64,2048]{3,2,0,1:T(8,128)(2,1)S(1)} collective-permute-done((bf16[2,2,64,2048]{3,2,0,1:T(8,128)(2,1)S(1)}, bf16[2,2,64,2048]{3,2,0,1:T(8,128)(2,1)S(1)}, u32[]{:S(2)}, u32[]{:S(2)}) %collective-permute-start.62) | collective-permute-done | bytes 1048608 | tf_op jit(solution)/shard_map/ppermute | solution.py:408
  556.0 4.7 collective-permute-done.65
  564.2 24.3 %collective-permute-done.83 = bf16[64,2048]{1,0:T(8,128)(2,1)S(1)} collective-permute-done((bf16[64,2048]{1,0:T(8,128)(2,1)S(1)}, bf16[64,2048]{1,0:T(8,128)(2,1)S(1)}, u32[]{:S(2)}, u32[]{:S(2)}) %collective-permute-start.83) | collective-permute-done | bytes 262176 | tf_op jit(solution)/shard_map/ppermute | solution.py:408
  592.3 26.0 %collective-permute-done.69 = bf16[2,2,64,2048]{3,2,0,1:T(8,128)(2,1)S(1)} collective-permute-done((bf16[2,2,64,2048]{3,2,0,1:T(8,128)(2,1)}, bf16[2,2,64,2048]{3,2,0,1:T(8,128)(2,1)S(1)}, u32[]{:S(2)}, u32[]{:S(2)}) %collective-permute-start.69) | collective-permute-done | bytes 1048608 | tf_op jit(solution)/shard_map/ppermute | solution.py:408
  621.9 7.8 %collective-permute-done.66 = bf16[2,2,64,2048]{3,2,0,1:T(8,128)(2,1)} collective-permute-done((bf16[2,2,64,2048]{3,2,0,1:T(8,128)(2,1)}, bf16[2,2,64,2048]{3,2,0,1:T(8,128)(2,1)}, u32[]{:S(2)}, u32[]{:S(2)}) %collective-permute-start.66) | collective-permute-done | bytes 1048608 | tf_op jit(solution)/shard_map/ppermute | solution.py:408
  638.4 3.6 collective-permute-done.67.near_b
  642.0 3.5 assemble.1
  (679 shorter events, 423.9 us)
Async XLA Ops:
  6.4 34.1 %collective-permute-start.1 = (bf16[4,512,1024]{2,1,0:T(8,128)(2,1)}, bf16[4,512,1024]{2,1,0:T(8,128)(2,1)}, u32[]{:S(2)}, u32[]{:S(2)}) collective-permute-start(bf16[4,512,1024]{2,1,0:T(8,128)(2,1)} %layout.4), channel_id=1, source_target_pairs={{0,1},{1,0},{2,3},{3,2},{4,5},{5,4},{6,7},{7,6},{8,9},{9,8},{10,11... | collective-permute-start | bytes 12582920 | tf_op jit(solution)/shard_map/ppermute | solution.py:365
  12.2 33.9 %collective-permute-start.2 = (bf16[4,512,1024]{2,1,0:T(8,128)(2,1)}, bf16[4,512,1024]{2,1,0:T(8,128)(2,1)}, u32[]{:S(2)}, u32[]{:S(2)}) collective-permute-start(bf16[4,512,1024]{2,1,0:T(8,128)(2,1)} %layout.6), channel_id=1, source_target_pairs={{0,1},{1,0},{2,3},{3,2},{4,5},{5,4},{6,7},{7,6},{8,9},{9,8},{10,11... | collective-permute-start | bytes 12582920 | tf_op jit(solution)/shard_map/ppermute | solution.py:365
  12.7 22.2 %collective-permute-start = (bf16[4,1024]{1,0:T(4,128)(2,1)S(1)}, bf16[4,1024]{1,0:T(4,128)(2,1)S(1)}, u32[]{:S(2)}, u32[]{:S(2)}) collective-permute-start(bf16[4,1024]{1,0:T(4,128)(2,1)S(1)} %get-tuple-element.1270), channel_id=1, source_target_pairs={{0,1},{1,0},{2,3},{3,2},{4,5},{5,4},{6,7},{7,6},{8,9},{9,8},{10,11... | collective-permute-start | bytes 24584 | tf_op jit(solution)/shard_map/ppermute | solution.py:343
  14.9 22.3 %collective-permute-start.4 = (f32[48,1024]{1,0:T(8,128)}, f32[48,1024]{1,0:T(8,128)}, u32[]{:S(2)}, u32[]{:S(2)}) collective-permute-start(f32[48,1024]{1,0:T(8,128)} %bitcast.208), channel_id=1, source_target_pairs={{0,1},{1,0},{2,3},{3,2},{4,5},{5,4},{6,7},{7,6},{8,9},{9,8},{10,11... | collective-permute-start | bytes 589832 | tf_op jit(solution)/shard_map/ppermute | solution.py:343
  18.4 27.6 %collective-permute-start.3 = (bf16[1024,512]{1,0:T(8,128)(2,1)}, bf16[1024,512]{1,0:T(8,128)(2,1)}, u32[]{:S(2)}, u32[]{:S(2)}) collective-permute-start(bf16[1024,512]{1,0:T(8,128)(2,1)} %get-tuple-element.1243), channel_id=1, source_target_pairs={{0,1},{1,0},{2,3},{3,2},{4,5},{5,4},{6,7},{7,6},{8,9},{9,8},{10,11... | collective-permute-start | bytes 3145736 | tf_op jit(solution)/shard_map/ppermute | solution.py:343
  34.9 111.7 %collective-permute-start.19 = (bf16[20,48,512]{2,1,0:T(8,128)(2,1)}, bf16[20,48,512]{2,1,0:T(8,128)(2,1)}, u32[]{:S(2)}, u32[]{:S(2)}) collective-permute-start(bf16[20,48,512]{2,1,0:T(8,128)(2,1)} %get-tuple-element.621), channel_id=1, source_target_pairs={{0,4},{4,0},{8,12},{12,8},{16,20},{20,16},{24,28},{28,24},{1,5},{5... | collective-permute-start | bytes 2949128 | tf_op jit(solution)/shard_map/ppermute | solution.py:408
  37.2 109.4 %collective-permute-start.20 = (bf16[20,48,512]{2,1,0:T(8,128)(2,1)}, bf16[20,48,512]{2,1,0:T(8,128)(2,1)}, u32[]{:S(2)}, u32[]{:S(2)}) collective-permute-start(bf16[20,48,512]{2,1,0:T(8,128)(2,1)} %get-tuple-element.621), channel_id=1, source_target_pairs={{0,8},{4,12},{8,0},{12,4},{16,24},{20,28},{24,16},{28,20},{1,9},{5... | collective-permute-start | bytes 2949128 | tf_op jit(solution)/shard_map/ppermute | solution.py:408
  191.5 62.5 %collective-permute-start.34 = (bf16[20,48,512]{2,1,0:T(8,128)(2,1)}, bf16[20,48,512]{2,1,0:T(8,128)(2,1)}, u32[]{:S(2)}, u32[]{:S(2)}) collective-permute-start(bf16[20,48,512]{2,1,0:T(8,128)(2,1)} %get-tuple-element.903), channel_id=1, source_target_pairs={{0,4},{4,0},{8,12},{12,8},{16,20},{20,16},{24,28},{28,24},{1,5},{5... | collective-permute-start | bytes 2949128 | tf_op jit(solution)/shard_map/ppermute | solution.py:408
  192.1 62.0 %collective-permute-start.35 = (bf16[20,48,512]{2,1,0:T(8,128)(2,1)}, bf16[20,48,512]{2,1,0:T(8,128)(2,1)}, u32[]{:S(2)}, u32[]{:S(2)}) collective-permute-start(bf16[20,48,512]{2,1,0:T(8,128)(2,1)} %get-tuple-element.903), channel_id=1, source_target_pairs={{0,8},{4,12},{8,0},{12,4},{16,24},{20,28},{24,16},{28,20},{1,9},{5... | collective-permute-start | bytes 2949128 | tf_op jit(solution)/shard_map/ppermute | solution.py:408
  256.9 56.7 %collective-permute-start.43 = (bf16[7,48,2048]{2,1,0:T(8,128)(2,1)}, bf16[7,48,2048]{2,1,0:T(8,128)(2,1)S(1)}, u32[]{:S(2)}, u32[]{:S(2)}) collective-permute-start(bf16[7,48,2048]{2,1,0:T(8,128)(2,1)} %get-tuple-element.1114), channel_id=1, source_target_pairs={{0,4},{4,0},{8,12},{12,8},{16,20},{20,16},{24,28},{28,24},{1,5},{5... | collective-permute-start | bytes 4128776 | tf_op jit(solution)/shard_map/ppermute | solution.py:408
  258.0 55.6 %collective-permute-start.44 = (bf16[7,48,2048]{2,1,0:T(8,128)(2,1)}, bf16[7,48,2048]{2,1,0:T(8,128)(2,1)S(1)}, u32[]{:S(2)}, u32[]{:S(2)}) collective-permute-start(bf16[7,48,2048]{2,1,0:T(8,128)(2,1)} %get-tuple-element.1115), channel_id=1, source_target_pairs={{0,8},{4,12},{8,0},{12,4},{16,24},{20,28},{24,16},{28,20},{1,9},{5... | collective-permute-start | bytes 4128776 | tf_op jit(solution)/shard_map/ppermute | solution.py:408
  306.9 52.3 %collective-permute-start.50 = (bf16[6,48,2048]{2,1,0:T(8,128)(2,1)}, bf16[6,48,2048]{2,1,0:T(8,128)(2,1)}, u32[]{:S(2)}, u32[]{:S(2)}) collective-permute-start(bf16[6,48,2048]{2,1,0:T(8,128)(2,1)} %get-tuple-element.1189), channel_id=1, source_target_pairs={{0,4},{4,0},{8,12},{12,8},{16,20},{20,16},{24,28},{28,24},{1,5},{5... | collective-permute-start | bytes 3538952 | tf_op jit(solution)/shard_map/ppermute | solution.py:408
  307.0 52.1 %collective-permute-start.51 = (bf16[6,48,2048]{2,1,0:T(8,128)(2,1)}, bf16[6,48,2048]{2,1,0:T(8,128)(2,1)}, u32[]{:S(2)}, u32[]{:S(2)}) collective-permute-start(bf16[6,48,2048]{2,1,0:T(8,128)(2,1)} %get-tuple-element.1190), channel_id=1, source_target_pairs={{0,8},{4,12},{8,0},{12,4},{16,24},{20,28},{24,16},{28,20},{1,9},{5... | collective-permute-start | bytes 3538952 | tf_op jit(solution)/shard_map/ppermute | solution.py:408
  338.4 29.9 %collective-permute-start.52 = (bf16[4,48,2048]{2,1,0:T(8,128)(2,1)}, bf16[4,48,2048]{2,1,0:T(8,128)(2,1)S(1)}, u32[]{:S(2)}, u32[]{:S(2)}) collective-permute-start(bf16[4,48,2048]{2,1,0:T(8,128)(2,1)} %get-tuple-element.1202), channel_id=1, source_target_pairs={{0,4},{4,0},{8,12},{12,8},{16,20},{20,16},{24,28},{28,24},{1,5},{5... | collective-permute-start | bytes 2359304 | tf_op jit(solution)/shard_map/ppermute | solution.py:408
  339.1 29.1 %collective-permute-start.53 = (bf16[4,48,2048]{2,1,0:T(8,128)(2,1)}, bf16[4,48,2048]{2,1,0:T(8,128)(2,1)}, u32[]{:S(2)}, u32[]{:S(2)}) collective-permute-start(bf16[4,48,2048]{2,1,0:T(8,128)(2,1)} %get-tuple-element.1203), channel_id=1, source_target_pairs={{0,8},{4,12},{8,0},{12,4},{16,24},{20,28},{24,16},{28,20},{1,9},{5... | collective-permute-start | bytes 2359304 | tf_op jit(solution)/shard_map/ppermute | solution.py:408
  362.0 24.6 %collective-permute-start.59 = (bf16[2,48,2048]{2,1,0:T(8,128)(2,1)}, bf16[2,48,2048]{2,1,0:T(8,128)(2,1)S(1)}, u32[]{:S(2)}, u32[]{:S(2)}) collective-permute-start(bf16[2,48,2048]{2,1,0:T(8,128)(2,1)} %get-tuple-element.1222), channel_id=1, source_target_pairs={{0,4},{4,0},{8,12},{12,8},{16,20},{20,16},{24,28},{28,24},{1,5},{5... | collective-permute-start | bytes 1179656 | tf_op jit(solution)/shard_map/ppermute | solution.py:408
  362.4 26.6 %collective-permute-start.54 = (bf16[2,48,2048]{2,1,0:T(8,128)(2,1)}, bf16[2,48,2048]{2,1,0:T(8,128)(2,1)S(1)}, u32[]{:S(2)}, u32[]{:S(2)}) collective-permute-start(bf16[2,48,2048]{2,1,0:T(8,128)(2,1)} %get-tuple-element.1207), channel_id=1, source_target_pairs={{0,8},{4,12},{8,0},{12,4},{16,24},{20,28},{24,16},{28,20},{1,9},{5... | collective-permute-start | bytes 1179656 | tf_op jit(solution)/shard_map/ppermute | solution.py:408
  437.5 48.5 %collective-permute-start.85 = (f32[48,1024]{1,0:T(8,128)}, f32[48,1024]{1,0:T(8,128)}, u32[]{:S(2)}, u32[]{:S(2)}) collective-permute-start(f32[48,1024]{1,0:T(8,128)} %bitcast.105), channel_id=1, source_target_pairs={{0,1},{1,0},{2,3},{3,2},{4,5},{5,4},{6,7},{7,6},{8,9},{9,8},{10,11... | collective-permute-start | bytes 589832 | tf_op jit(solution)/shard_map/ppermute | solution.py:343
  438.4 57.1 %collective-permute-start.56 = (bf16[20,48,512]{2,1,0:T(8,128)(2,1)S(1)}, bf16[20,48,512]{2,1,0:T(8,128)(2,1)}, u32[]{:S(2)}, u32[]{:S(2)}) collective-permute-start(bf16[20,48,512]{2,1,0:T(8,128)(2,1)S(1)} %copy-done.66), channel_id=1, source_target_pairs={{0,1},{1,0},{2,3},{3,2},{4,5},{5,4},{6,7},{7,6},{8,9},{9,8},{10,11... | collective-permute-start | bytes 2949128 | tf_op jit(solution)/shard_map/ppermute | solution.py:343
  454.7 42.3 %collective-permute-start.77 = (bf16[4,64,2048]{2,1,0:T(8,128)(2,1)}, bf16[4,64,2048]{2,1,0:T(8,128)(2,1)}, u32[]{:S(2)}, u32[]{:S(2)}) collective-permute-start(bf16[4,64,2048]{2,1,0:T(8,128)(2,1)} %dynamic-slice_bitcast_fusion.1), channel_id=1, source_target_pairs={{0,4},{4,0},{8,12},{12,8},{16,20},{20,16},{24,28},{28,24},{1,5},{5... | collective-permute-start | bytes 3145736 | tf_op jit(solution)/shard_map/ppermute | solution.py:408
  457.0 24.5 %collective-permute-start.57 = (bf16[20,48,256]{2,1,0:T(8,128)(2,1)}, bf16[20,48,256]{2,1,0:T(8,128)(2,1)S(1)}, u32[]{:S(2)}, u32[]{:S(2)}) collective-permute-start(bf16[20,48,256]{2,1,0:T(8,128)(2,1)} %dynamic-slice_convert_fusion), channel_id=1, source_target_pairs={{0,2},{1,3},{2,0},{3,1},{4,6},{5,7},{6,4},{7,5},{8,10},{9,11},{10,... | collective-permute-start | bytes 1474568 | tf_op jit(solution)/shard_map/ppermute | solution.py:728
  479.4 72.8 %collective-permute-start.68 = (bf16[2,4,64,2048]{3,2,1,0:T(8,128)(2,1)}, bf16[2,4,64,2048]{3,2,1,0:T(8,128)(2,1)}, u32[]{:S(2)}, u32[]{:S(2)}) collective-permute-start(bf16[2,4,64,2048]{3,2,1,0:T(8,128)(2,1)} %dynamic-slice_bitcast_fusion), channel_id=1, source_target_pairs={{0,4},{4,0},{8,12},{12,8},{16,20},{20,16},{24,28},{28,24},{1,5},{5... | collective-permute-start | bytes 6291464 | tf_op jit(solution)/shard_map/ppermute | solution.py:408
  482.3 35.0 %collective-permute-start.61 = (bf16[2,2,64,2048]{3,2,0,1:T(8,128)(2,1)}, bf16[2,2,64,2048]{3,2,0,1:T(8,128)(2,1)}, u32[]{:S(2)}, u32[]{:S(2)}) collective-permute-start(bf16[2,2,64,2048]{3,2,0,1:T(8,128)(2,1)} %bitcast.207), channel_id=1, source_target_pairs={{0,8},{4,12},{1,9},{5,13},{2,10},{6,14},{3,11},{7,15}} | collective-permute-start | bytes 3145736 | tf_op jit(solution)/shard_map/ppermute | solution.py:408
  492.8 35.4 %collective-permute-start.64 = (bf16[2,2,64,2048]{3,2,0,1:T(8,128)(2,1)}, bf16[2,2,64,2048]{3,2,0,1:T(8,128)(2,1)S(1)}, u32[]{:S(2)}, u32[]{:S(2)}) collective-permute-start(bf16[2,2,64,2048]{3,2,0,1:T(8,128)(2,1)} %bitcast.221), channel_id=1, source_target_pairs={{24,16},{28,20},{25,17},{29,21},{26,18},{30,22},{27,19},{31,23}} | collective-permute-start | bytes 3145736 | tf_op jit(solution)/shard_map/ppermute | solution.py:408
  519.0 29.9 %collective-permute-start.62 = (bf16[2,2,64,2048]{3,2,0,1:T(8,128)(2,1)S(1)}, bf16[2,2,64,2048]{3,2,0,1:T(8,128)(2,1)S(1)}, u32[]{:S(2)}, u32[]{:S(2)}) collective-permute-start(bf16[2,2,64,2048]{3,2,0,1:T(8,128)(2,1)S(1)} %fusion.8), channel_id=1, source_target_pairs={{0,8},{4,12},{8,16},{12,20},{1,9},{5,13},{9,17},{13,21},{2,10},{6,... | collective-permute-start | bytes 3145736 | tf_op jit(solution)/shard_map/ppermute | solution.py:408
  528.6 32.0 %collective-permute-start.65 = (bf16[2,2,64,2048]{3,2,0,1:T(8,128)(2,1)S(1)}, bf16[2,2,64,2048]{3,2,0,1:T(8,128)(2,1)S(1)}, u32[]{:S(2)}, u32[]{:S(2)}) collective-permute-start(bf16[2,2,64,2048]{3,2,0,1:T(8,128)(2,1)S(1)} %fusion.6), channel_id=1, source_target_pairs={{16,8},{20,12},{24,16},{28,20},{17,9},{21,13},{25,17},{29,21},{18,... | collective-permute-start | bytes 3145736 | tf_op jit(solution)/shard_map/ppermute | solution.py:408
  529.9 34.3 %collective-permute-start.80 = (bf16[64,2048]{1,0:T(8,128)(2,1)S(1)}, bf16[64,2048]{1,0:T(8,128)(2,1)S(1)}, u32[]{:S(2)}, u32[]{:S(2)}) collective-permute-start(bf16[64,2048]{1,0:T(8,128)(2,1)S(1)} %get-tuple-element.1247), channel_id=1, source_target_pairs={{0,8},{4,12},{8,16},{12,20},{16,24},{20,28},{1,9},{5,13},{9,17},{1... | collective-permute-start | bytes 786440 | tf_op jit(solution)/shard_map/ppermute | solution.py:408
  538.1 50.5 %collective-permute-start.83 = (bf16[64,2048]{1,0:T(8,128)(2,1)S(1)}, bf16[64,2048]{1,0:T(8,128)(2,1)S(1)}, u32[]{:S(2)}, u32[]{:S(2)}) collective-permute-start(bf16[64,2048]{1,0:T(8,128)(2,1)S(1)} %fusion.22), channel_id=1, source_target_pairs={{8,0},{12,4},{16,8},{20,12},{24,16},{28,20},{9,1},{13,5},{17,9},{2... | collective-permute-start | bytes 786440 | tf_op jit(solution)/shard_map/ppermute | solution.py:408
  550.3 71.6 %collective-permute-start.63 = (bf16[2,2,64,2048]{3,2,0,1:T(8,128)(2,1)}, bf16[2,2,64,2048]{3,2,0,1:T(8,128)(2,1)}, u32[]{:S(2)}, u32[]{:S(2)}) collective-permute-start(bf16[2,2,64,2048]{3,2,0,1:T(8,128)(2,1)} %fusion.9), channel_id=1, source_target_pairs={{0,8},{4,12},{8,16},{12,20},{16,24},{20,28},{1,9},{5,13},{9,17},{1... | collective-permute-start | bytes 3145736 | tf_op jit(solution)/shard_map/ppermute | solution.py:408
  556.0 62.4 %collective-permute-start.69 = (bf16[2,2,64,2048]{3,2,0,1:T(8,128)(2,1)}, bf16[2,2,64,2048]{3,2,0,1:T(8,128)(2,1)S(1)}, u32[]{:S(2)}, u32[]{:S(2)}) collective-permute-start(bf16[2,2,64,2048]{3,2,0,1:T(8,128)(2,1)} %bitcast.205), channel_id=1, source_target_pairs={{0,16},{4,20},{8,24},{12,28},{16,0},{20,4},{24,8},{28,12},{1,17},{... | collective-permute-start | bytes 3145736 | tf_op jit(solution)/shard_map/ppermute | solution.py:408
  562.0 67.7 %collective-permute-start.66 = (bf16[2,2,64,2048]{3,2,0,1:T(8,128)(2,1)}, bf16[2,2,64,2048]{3,2,0,1:T(8,128)(2,1)}, u32[]{:S(2)}, u32[]{:S(2)}) collective-permute-start(bf16[2,2,64,2048]{3,2,0,1:T(8,128)(2,1)} %fusion.7), channel_id=1, source_target_pairs={{8,0},{12,4},{16,8},{20,12},{24,16},{28,20},{9,1},{13,5},{17,9},{2... | collective-permute-start | bytes 3145736 | tf_op jit(solution)/shard_map/ppermute | solution.py:408
  592.3 44.2 %collective-permute-start.84 = (bf16[1024,64]{0,1:T(8,128)(2,1)}, bf16[1024,64]{0,1:T(8,128)(2,1)}, u32[]{:S(2)}, u32[]{:S(2)}) collective-permute-start(bf16[1024,64]{0,1:T(8,128)(2,1)} %bitcast.210), channel_id=1, source_target_pairs={{0,1},{1,0},{2,3},{3,2},{4,5},{5,4},{6,7},{7,6},{8,9},{9,8},{10,11... | collective-permute-start | bytes 393224 | tf_op jit(solution)/shard_map/ppermute | solution.py:343
  (205 other events, 2156.8 us)

commit v5 on v4

--- a/solution.py
+++ b/solution.py
@@ -12,7 +12,8 @@
 QUARTERS, HALVES = 2, 2
 PIECES = QUARTERS * HALVES
 MIB = 2**20
-SHARES = (0.35, 0.3, 0.2, 0.1, 0.05)
+LATE = 2
+SHARES = (0.35, 0.3, 0.15, 0.1, 0.1)
 
 VMEM = pl.BlockSpec(memory_space=pltpu.VMEM)
 SMEM = pl.BlockSpec(memory_space=pltpu.SMEM)
@@ -53,11 +54,15 @@
     )(*(in_hbm(x) for x in arrays))
 
 
-def layout_kernel(which_ref, w_ref, out_ref, buf, sems):
+def layout_kernel(which_ref, w_ref, out_ref, all_ref, buf, sems, out_sems):
     depth, part = w_ref.shape[1], buf.shape[1]
 
     def fetch(i):
         return pltpu.make_async_copy(w_ref.at[which_ref[0], pl.ds(i * part, part)], buf.at[i % 3], sems.at[i % 3])
+
+    def store(i):
+        rows = pl.ds(i * part, part)
+        return pltpu.make_async_copy(out_ref.at[:, rows], all_ref.at[:, rows], out_sems.at[i])
 
     count = depth // part
     for i in range(min(2, count)):
@@ -67,17 +72,33 @@
             fetch(i + 2).start()
         fetch(i).wait()
         out_ref[:, i * part : (i + 1) * part, :] = jnp.swapaxes(buf[i % 3], 0, 1)
-
-
-def turned_kernel(wa_ref, wb_ref, pa_ref, pb_ref, wat_ref, wbt_ref, pat_ref, pbt_ref):
-    for w_ref, out_ref in ((wa_ref, wat_ref), (wb_ref, wbt_ref)):
-        for gate in range(4):
-            for half in range(HALVES):
-                width = w_ref.shape[2] // HALVES
-                cols = slice(half * width, (half + 1) * width)
-                out_ref[gate, cols, :] = w_ref[gate, :, cols].T
-    pat_ref[...] = pa_ref[...].T
-    pbt_ref[...] = pb_ref[...].T
+        store(i).start()
+    for i in range(count):
+        store(i).wait()
+
+
+def turned_kernel(wa_ref, wb_ref, pa_ref, pb_ref, wat_ref, wbt_ref, pat_ref, pbt_ref, buf, sems, proj_buf, proj_sems):
+    jobs = [(w_ref, out_ref, gate) for w_ref, out_ref in ((wa_ref, wat_ref), (wb_ref, wbt_ref)) for gate in range(4)]
+
+    def fetch(i):
+        return pltpu.make_async_copy(jobs[i][0].at[jobs[i][2]], buf.at[i % 3], sems.at[i % 3])
+
+    proj_fetches = [pltpu.make_async_copy(x, proj_buf.at[i], proj_sems.at[i]) for i, x in enumerate((pa_ref, pb_ref))]
+    fetch(0).start()
+    fetch(1).start()
+    for copy in proj_fetches:
+        copy.start()
+    for i, (_, out_ref, gate) in enumerate(jobs):
+        if i + 2 < len(jobs):
+            fetch(i + 2).start()
+        fetch(i).wait()
+        for half in range(HALVES):
+            width = buf.shape[2] // HALVES
+            cols = slice(half * width, (half + 1) * width)
+            out_ref[gate, cols, :] = buf[i % 3, :, cols].T
+    for i, out_ref in enumerate((pat_ref, pbt_ref)):
+        proj_fetches[i].wait()
+        out_ref[...] = proj_buf[i].T
 
 
 def pass_kernel(*refs):
@@ -273,7 +294,7 @@
 
 
 def aside_kernel(
-    first, opens, passed, step_ref, dz_ref, raw_ref, gates_all, cells_all, ups_all, slope_all, *refs
+    first, last, opens, passed, step_ref, dz_ref, raw_ref, gates_all, cells_all, ups_all, slope_all, *refs
 ):
     refs = refs[(0 if first else 4) + (0 if opens else 2) + passed :]
     gates_ref, cell_ref, prev_ref, slope_ref, up_ref = refs[:5]
@@ -282,10 +303,12 @@
     step, time_before = step_ref[0], step_ref[2]
     slot, low, high = step_ref[4], step_ref[5], step_ref[6]
     before = jnp.maximum(step - 1, 0)
-    copies = fetches(
-        before, time_before, (gates_all, cells_all, ups_all), (gates_ref, cell_ref, prev_ref, up_ref), fetch_sems
-    )
-    copies.append(pltpu.make_async_copy(slope_all.at[before], slope_ref, fetch_sems.at[PIECES + 3]))
+    copies = []
+    if not last:
+        copies += fetches(
+            before, time_before, (gates_all, cells_all, ups_all), (gates_ref, cell_ref, prev_ref, up_ref), fetch_sems
+        )
+        copies.append(pltpu.make_async_copy(slope_all.at[before], slope_ref, fetch_sems.at[PIECES + 3]))
     copies += [pltpu.make_async_copy(dz_ref.at[i], dz_all.at[i, step], sems.at[i]) for i in range(PIECES)]
     copies.append(pltpu.make_async_copy(raw_ref, raw_all.at[step], sems.at[PIECES]))
     copies.append(pltpu.make_async_copy(dz_ref.at[low], near_all.at[step], sems.at[PIECES + 1]))
@@ -353,17 +376,20 @@
         part = weights.shape[1] // 8
         return pl.pallas_call(
             layout_kernel,
-            out_shape=vmem(shape, BF16),
+            out_shape=(vmem(shape, BF16), hbm(shape, BF16)),
             in_specs=[SMEM, ANY],
-            out_specs=VMEM,
-            scratch_shapes=[pltpu.VMEM((3, part) + weights.shape[2:], BF16), pltpu.SemaphoreType.DMA((3,))],
+            out_specs=[VMEM, ANY],
+            scratch_shapes=[
+                pltpu.VMEM((3, part) + weights.shape[2:], BF16),
+                pltpu.SemaphoreType.DMA((3,)),
+                pltpu.SemaphoreType.DMA((8,)),
+            ],
             compiler_params=params(8),
             name="layout",
         )(jnp.full((1,), index, jnp.int32), in_hbm(weights))
 
-    sent = [by_gate(w, 1 - own) for w in (w_in, w_rec)]
-    win_b, rec_b = (lax.ppermute(x, "gate", swap) for x in sent)
-    win_av, rec_av = by_gate(w_in, own), by_gate(w_rec, own)
+    win_b, rec_b = (lax.ppermute(by_gate(w, 1 - own)[1], "gate", swap) for w in (w_in, w_rec))
+    (win_av, win_a), (rec_av, rec_a) = by_gate(w_in, own), by_gate(w_rec, own)
     proj_a, proj_b = trade(pick(proj, own), pick(proj, 1 - own))
     bias_a, bias_b = trade(pick(bias, own), pick(bias, 1 - own))
 
@@ -518,11 +544,17 @@
     rec_atv, rec_btv, proj_atv, proj_btv = pl.pallas_call(
         turned_kernel,
         out_shape=(vmem((4, cells, depth), BF16),) * 2 + (vmem((depth, cells), BF16),) * 2,
-        in_specs=[VMEM] * 4,
+        in_specs=[ANY] * 4,
         out_specs=[VMEM] * 4,
+        scratch_shapes=[
+            pltpu.VMEM((3, depth, cells), BF16),
+            pltpu.SemaphoreType.DMA((3,)),
+            pltpu.VMEM((2, cells, depth), BF16),
+            pltpu.SemaphoreType.DMA((2,)),
+        ],
         compiler_params=params(8),
         name="turned",
-    )(pinned(rec_av), pinned(rec_bv), pinned(proj_av), pinned(proj_bv))
+    )(*(in_hbm(x) for x in (rec_a, rec_b, proj_a, proj_b)))
 
     def backward_call(step, part, peer, grad, saved):
         return pl.pallas_call(
@@ -558,7 +590,7 @@
         aliases.update({7 + kept + i: 9 + i for i in range(len(sends))})
         aliases.update({7 + kept + len(sends) + i: 11 + i for i in range(len(passing))})
         out = pl.pallas_call(
-            functools.partial(aside_kernel, not stacks, not sends, len(passing)),
+            functools.partial(aside_kernel, not stacks, step == 0, not sends, len(passing)),
             out_shape=saved_shapes + shapes + tuple(hbm(x.shape, x.dtype) for x in passing),
             in_specs=[SMEM] + [VMEM] * 2 + [ANY] * (4 + kept + len(sends) + len(passing)),
             out_specs=[VMEM] * 5 + [ANY] * (6 + len(passing)),
@@ -578,7 +610,7 @@
         return out[:5], tuple(out[5:9]), tuple(out[9:11]), tuple(out[11:])
 
     carry = (none, none, jnp.zeros(cell_shape, F32), saved, ())
-    pending, arrived, top = [(steps - 1 - steps // 3, prev_in)], [], steps
+    pending, arrived, ready, top = [(steps - 1 - steps // 3, prev_in)], [], None, steps
     for index, share in enumerate(SHARES):
         slots = top if index == len(SHARES) - 1 else round(share * steps)
         sends = ()
@@ -586,6 +618,11 @@
             part, peer, grad, saved, stacks = carry
             part, grad, raw, dz = backward_call(step, part, peer, grad, saved)
             peer = lax.ppermute(part, "gate", across)
+            if ready is not None:
+                due, sides = ready
+                sides = after(part, *sides) if step else sides
+                pending.append((due, (swapped(sides[0], near_swap), swapped(sides[1], far_swap))))
+                ready = None
             passing = pending.pop(0)[1] if pending and pending[0][0] >= step else ()
             saved, stacks, sends, passed = aside_call(
                 step, step - (top - slots), slots, dz, raw, stacks, sends, passing
@@ -593,8 +630,8 @@
             arrived += [passed] if passed else []
             carry = (part, peer, grad, saved, stacks)
         top -= slots
-        due = max(top - 1 - (3 * slots + 3) // 4, 0 if slots > 2 else -1)
-        pending.append((due, (swapped(sends[0], near_swap), swapped(sends[1], far_swap))))
+        ready = (max(top - 1 - (3 * slots + 3) // 4, 0 if slots > 2 else -1), sends)
+    pending.append((-1, (swapped(sends[0], near_swap), swapped(sends[1], far_swap))))
     arrived += [arrays for _, arrays in pending]
     dz_all, raw_all, near_all, far_all = carry[-1]
     prev_in, exchanged = arrived[0], arrived[1:]
@@ -603,7 +640,7 @@
     def by_direction(mine, theirs):
         return jnp.stack([jnp.where(own == 0, mine, theirs), jnp.where(own == 0, theirs, mine)])
 
-    def line_sum(chunks, axis, stride, count):
+    def line_sum(chunks, axis, stride, count, first=None):
         here = (spot // stride) % count
 
         def chunk(index):
@@ -615,12 +652,12 @@
         if count == 2:
             pairs = [(i, i + stride if at(i) == 0 else i - stride) for i in range(n_batch)]
             return (chunk(here).astype(F32) + swapped(chunk(1 - here), pairs).astype(F32)).astype(BF16)
-        up, down = None, None
-        for slot in range(1, count):
-            rise, fall = chunk(here + count - slot), chunk(here - count + slot)
-            if slot > 1:
-                rise = (rise.astype(F32) + up.astype(F32)).astype(BF16)
-                fall = (fall.astype(F32) + down.astype(F32)).astype(BF16)
+        ends = [(i, i + stride) for i in range(n_batch) if at(i) == 0]
+        ends += [(i, i - stride) for i in range(n_batch) if at(i) == count - 1]
+        up = down = swapped(chunk(jnp.where(here == 0, count - 1, 0)) if first is None else first, ends)
+        for slot in range(2, count):
+            rise = (chunk(here + count - slot).astype(F32) + up.astype(F32)).astype(BF16)
+            fall = (chunk(here - count + slot).astype(F32) + down.astype(F32)).astype(BF16)
             up = swapped(rise, [(i, i + stride) for i in range(n_batch) if at(i) < min(slot, count - 1)])
             down = swapped(fall, [(i, i - stride) for i in range(n_batch) if at(i) > max(count - 1 - slot, 0)])
         return (chunk(here).astype(F32) + up.astype(F32) + down.astype(F32)).astype(BF16)
@@ -629,23 +666,44 @@
     share_rows = depth // n_batch
 
     def product(left, right):
+        count = left.shape[0] * left.shape[1]
         return lax.dot_general(
-            left.reshape(rows, -1), right.reshape(rows, -1), (((0,), (0,)), ((), ())), preferred_element_type=F32
+            left.reshape(count, -1), right.reshape(count, -1), (((0,), (0,)), ((), ())), preferred_element_type=F32
         )
 
     def both(feat, prev):
         return jnp.concatenate([feat, prev], axis=2)
 
     left = both(feat_all, prev_all)
-    halves = []
-    for kept, feat, prev, taken in zip((near_all, far_all), feat_in, prev_in, zip(*exchanged)):
-        mine = product(left, kept)
-        *taken, late, latest = taken
-        late, latest = after(mine, late, latest)
-        theirs = product(both(feat, prev), jnp.concatenate([latest, late, *taken[::-1]], axis=0))
-        halves.append((mine + theirs).astype(BF16).reshape(2, line, 2, share_rows, 4 * width))
-    near = line_sum(halves[0], 1, 2, line)
-    far = line_sum(halves[1], 2, 1, 2).reshape(2, line // 2, 2, share_rows, 4 * width)
+    early, taken = [], []
+    for kept, feat, prev, parts in zip((near_all, far_all), feat_in, prev_in, zip(*exchanged)):
+        steps_late = sum(x.shape[0] for x in parts[-LATE:])
+        theirs = both(feat, prev)
+        total = product(left, kept) + product(theirs[steps_late:], jnp.concatenate(parts[:-LATE][::-1], axis=0))
+        early.append(total)
+        taken.append((theirs[:steps_late], parts[-LATE:][::-1]))
+    near_late, near_parts = taken[0]
+    near_parts = jnp.concatenate(after(early[0], *near_parts), axis=0)
+    here = spot // 2
+    begin = jnp.where(here == 0, line - 1, 0)
+
+    def line_chunk(array, axis):
+        shape = array.shape[:axis] + (2, line, 2 * share_rows) + array.shape[axis + 1 :]
+        return lax.dynamic_index_in_dim(array.reshape(shape), begin, axis + 1, keepdims=False)
+
+    first = line_chunk(early[0], 0).reshape(4 * share_rows, -1) + product(line_chunk(near_late, 2), near_parts)
+    first = first.astype(BF16)
+    (near_parts,) = after(first, near_parts)
+
+    def rows_first(total):
+        return total.astype(BF16).reshape(2, line, 2, share_rows, 4 * width)
+
+    near = rows_first(early[0] + product(near_late, near_parts))
+    far_parts = jnp.concatenate(after(near, *taken[1][1]), axis=0)
+    far = rows_first(early[1] + product(taken[1][0], far_parts))
+    token = far
+    near = line_sum(near, 1, 2, line, first.reshape(2, 2, share_rows, 4 * width))
+    far = line_sum(far, 2, 1, 2).reshape(2, line // 2, 2, share_rows, 4 * width)
     far = line_sum(far, 1, 4, line // 2)
 
     def halves_of(summed, index, pairs):
@@ -664,7 +722,7 @@
         name="assemble",
     )(jnp.stack([own, low, high]), *near_pair, *far_pair)
 
-    dz_all, mixed_all, hidden_all, cell = after(halves[1], dz_all, mixed_all, hidden_all, cell)
+    dz_all, mixed_all, hidden_all, cell = after(token, dz_all, mixed_all, hidden_all, cell)
 
     grad_proj = jnp.einsum("ptnc,tnk->kpc", mixed_all, raw_all, preferred_element_type=F32).astype(BF16)
     grad_proj = line_sum(grad_proj.reshape(line, 2, share_rows, QUARTERS * cells), 1, 1, 2)
@@ -719,7 +777,7 @@
         compiler_params=params(24),
         cost_estimate=cost(2 * rows * depth * 8 * cells, 8 * depth * cells * 4),
         name="input_grad",
-    )(turn, dz_all, win_av, win_bv)
+    )(turn, dz_all, in_hbm(win_a), in_hbm(win_b))
 
     half_cols = depth // 2
     upper = rank // 2

time: 653 us -> 657 us (level)
  Pallas kernels: 289 us -> 300 us
  local copies, waits for them, and re-layouts: 80.7 us -> 70.2 us
  waiting for transfers between devices: 109 us -> 102 us
    ppermute x34 -> x32, starting transfers between devices: 43.9 us -> 52 us  [swapped(): return lax.ppermute(array, 'batch', pairs)]
    dynamic_slice x5 -> x2, local copies, waits for them, and re-layouts: 9.29 us -> 1.33 us  [chunk(): lax.dynamic_index_in_dim(chunks, jnp.clip(index, 0, count - 1), axis, kee...]
    unnamed x317 -> x282, local copies, waits for them, and re-layouts: 36.4 us -> 28.9 us
    dot_general x4 -> x7, matrix products: 29.2 us -> 35.2 us  [product(): lax.dot_general(left.reshape(count, -1), right.reshape(count, -1), (((0,)...]
    ppermute x34 -> x32, waiting for transfers between devices: 98.6 us -> 93.9 us  [swapped(): return lax.ppermute(array, 'batch', pairs)]
  transfers between devices with their start and end apart: 86 -> 84, of which waited for: 40 -> 38; matrix products, arithmetic and copies ran while one was open for 16% -> 18% of each run, Pallas kernels for 38% -> 41%
where the time goes in v5:
time: 657 us; the launch traced here: 649 us
  Pallas kernels  300 us (46%)
  waiting for transfers between devices  102 us (16%)
  starting transfers between devices  97.4 us (15%)
  local copies, waits for them, and re-layouts  70.2 us (11%)
  other arithmetic  37.6 us (6%)
  matrix products  37.6 us (6%)
    ppermute x32, waiting for transfers between devices, swapped(): return lax.ppermute(array, 'batch', pairs)  93.9 us
    pallas_call x20, Pallas kernels, backward_call(): pl.pallas_call(backward_kernel, out_shape=(vmem((streams, depth), BF16),...  61.1 us
    pallas_call x20, Pallas kernels, between_call(): pl.pallas_call(functools.partial(between_kernel, not stacks, step == step...  59.7 us
    pallas_call x20, Pallas kernels, forward_call(): pl.pallas_call(functools.partial(forward_kernel, first), out_shape=(vmem(...  56.9 us
    pallas_call x20, Pallas kernels, aside_call(): pl.pallas_call(functools.partial(aside_kernel, not stacks, step == 0, not...  56.9 us
    ppermute x32, starting transfers between devices, swapped(): return lax.ppermute(array, 'batch', pairs)  52 us
    ppermute x39, starting transfers between devices, body(): peer = lax.ppermute(part, 'gate', across)  42 us
    dot_general x7, matrix products, product(): lax.dot_general(left.reshape(count, -1), right.reshape(count, -1), (((0,)...  35.2 us
  transfers between devices with their start and end apart: 84, of which 38 were waited for; matrix products, arithmetic and copies ran while one was open for 18% of the time, Pallas kernels for 41%

profile of v5, /device:TPU:8, one launch (start us, length us, event | category | flops | bytes accessed | tf_op | source)
XLA Modules:
  0.0 649.0 jit_solution(10547178584100141614)
XLA Ops:
  0.7 7.3 %layout.4 = (bf16[4,512,1024]{2,1,0:T(8,128)(2,1)}, bf16[4,512,1024]{2,1,0:T(8,128)(2,1)}) custom-call(s32[1]{0:T(128)} %bitcast.7.which_ref, bf16[2,512,4,1024]{3,2,1,0:T(4,128)(2,1)} %w_ref.5), custom_call_target="tpu_custom_call" | custom-call | tf_op jit(solution)/shard_map/layout/pallas_call | solution.py:377
  8.0 7.3 %layout.6 = (bf16[4,512,1024]{2,1,0:T(8,128)(2,1)}, bf16[4,512,1024]{2,1,0:T(8,128)(2,1)}) custom-call(s32[1]{0:T(128)} %bitcast.7.which_ref, bf16[2,512,4,1024]{3,2,1,0:T(4,128)(2,1)} %w_ref.7), custom_call_target="tpu_custom_call" | custom-call | tf_op jit(solution)/shard_map/layout/pallas_call | solution.py:377
  22.7 5.2 layout.5
  29.9 5.2 layout.7
  37.7 3.2 order.1
  112.8 3.2 forward_step.28
  201.2 6.0 turned.1
  207.3 3.5 finish.1
  210.9 3.4 backward_step.20
  358.9 3.4 backward_step.38
  378.7 3.6 backward_step.39
  387.5 7.0 %fusion.90 = f32[1024,2048,1]{1,0,2:T(8,128)S(1)} fusion(bf16[20,48,1024]{2,1,0:T(8,128)(2,1)S(1)} %copy-done.84, bf16[20,48,2048]{2,1,0:T(8,128)(2,1)} %get-tuple-element.1235), kind=kOutput, calls=%fused_computation.220 | convolution fusion | flops 4026531840 | bytes 14286848 | tf_op jit(solution)/shard_map/dot_general | solution.py:670
  394.6 4.9 fusion.89
  399.5 5.7 bitcast_add_fusion.2.refs_0_
  405.2 9.2 %fusion.4 = f32[1024,2048,1]{1,0,2:T(8,128)} fusion(bf16[20,48,1024]{2,1,0:T(8,128)(2,1)} %constant_dynamic-update-slice_fusion.2, bf16[7,48,2048]{2,1,0:T(8,128)(2,1)} %get-tuple-element.1234, bf16[6,48,2048]{2,1,0:T(8,128)(2,1)} %get-tuple-element.1233, bf16[3,48,2048]{2,1,0:T(8,128)(2,1)} %get-tuple-element.1232), kind=kOutput, calls=%fused_computation.16 | convolution fusion | flops 3230662656 | bytes 13500416 | tf_op jit(solution)/shard_map/dot_general | solution.py:670
  423.6 5.4 fusion
  432.8 8.5 %convert_reduce_fusion = f32[4,2048]{1,0:T(4,128)S(1)} fusion(bf16[4,20,48,2048]{3,2,1,0:T(8,128)(2,1)} %get-tuple-element.1255.dz_ref), kind=kLoop, calls=%fused_computation.4 | loop fusion | flops 15720448 | bytes 15761408 | tf_op jit(solution)/shard_map/reduce_sum | solution.py:731
  445.1 16.9 %input_grad.1 = f32[20,48,512]{2,1,0:T(8,128)S(1)} custom-call(s32[2]{0:T(128)S(1)} %copy-done.56, bf16[4,20,48,2048]{3,2,1,0:T(8,128)(2,1)S(1)} %bitcast.224, bf16[4,512,1024]{2,1,0:T(8,128)(2,1)} %get-tuple-element.1256.wa_ref, bf16[4,512,1024]{2,1,0:T(8,128)(2,1)} %collective-permute-done.1.refs_2_.wb_ref), custom_call_target="tpu_custom_call" | custom-call | flops 8053063680 | bytes 16777216 | tf_op jit(solution)/shard_map/input_grad/pallas_call | solution.py:759
  472.5 4.5 reshape.145
  485.1 3.6 collective-permute-done.59
  500.3 8.5 %collective-permute-done.76 = bf16[4,64,2048]{2,1,0:T(8,128)(2,1)} collective-permute-done((bf16[4,64,2048]{2,1,0:T(8,128)(2,1)}, bf16[4,64,2048]{2,1,0:T(8,128)(2,1)}, u32[]{:S(2)}, u32[]{:S(2)}) %collective-permute-start.76) | collective-permute-done | bytes 1048608 | tf_op jit(solution)/shard_map/ppermute | solution.py:434
  513.8 6.1 collective-permute-done.77
  525.8 4.6 collective-permute-start.62
  531.8 4.6 collective-permute-start.79
  538.5 14.8 %collective-permute-done.67 = bf16[2,4,64,2048]{3,2,1,0:T(8,128)(2,1)} collective-permute-done((bf16[2,4,64,2048]{3,2,1,0:T(8,128)(2,1)}, bf16[2,4,64,2048]{3,2,1,0:T(8,128)(2,1)}, u32[]{:S(2)}, u32[]{:S(2)}) %collective-permute-start.67) | collective-permute-done | bytes 2097184 | tf_op jit(solution)/shard_map/ppermute | solution.py:434
  559.8 4.2 collective-permute-start.63
  566.0 15.8 %collective-permute-done.81 = bf16[64,2048]{1,0:T(8,128)(2,1)S(1)} collective-permute-done((bf16[64,2048]{1,0:T(8,128)(2,1)S(1)}, bf16[64,2048]{1,0:T(8,128)(2,1)S(1)}, u32[]{:S(2)}, u32[]{:S(2)}) %collective-permute-start.81) | collective-permute-done | bytes 262176 | tf_op jit(solution)/shard_map/ppermute | solution.py:434
  582.6 20.9 %collective-permute-done.68 = bf16[2,2,64,2048]{3,2,0,1:T(8,128)(2,1)} collective-permute-done((bf16[2,2,64,2048]{3,2,0,1:T(8,128)(2,1)}, bf16[2,2,64,2048]{3,2,0,1:T(8,128)(2,1)}, u32[]{:S(2)}, u32[]{:S(2)}) %collective-permute-start.68) | collective-permute-done | bytes 1048608 | tf_op jit(solution)/shard_map/ppermute | solution.py:434
  606.1 3.5 collective-permute-start.70
  609.6 15.3 %collective-permute-done.63 = bf16[2,2,64,2048]{3,2,1,0:T(8,128)(2,1)S(1)} collective-permute-done((bf16[2,2,64,2048]{3,2,1,0:T(8,128)(2,1)}, bf16[2,2,64,2048]{3,2,1,0:T(8,128)(2,1)S(1)}, u32[]{:S(2)}, u32[]{:S(2)}) %collective-permute-start.63) | collective-permute-done | bytes 1048608 | tf_op jit(solution)/shard_map/ppermute | solution.py:434
  637.2 8.0 %collective-permute-done.66.near_b = bf16[2,64,2048]{2,1,0:T(8,128)(2,1)S(1)} collective-permute-done((bf16[2,64,2048]{2,1,0:T(8,128)(2,1)}, bf16[2,64,2048]{2,1,0:T(8,128)(2,1)S(1)}, u32[]{:S(2)}, u32[]{:S(2)}) %collective-permute-start.66) | collective-permute-done | bytes 524320 | tf_op jit(solution)/shard_map/ppermute | solution.py:434
  645.2 3.5 assemble.1
  (648 shorter events, 418.8 us)
Async XLA Ops:
  8.0 38.4 %collective-permute-start.1 = (bf16[4,512,1024]{2,1,0:T(8,128)(2,1)}, bf16[4,512,1024]{2,1,0:T(8,128)(2,1)}, u32[]{:S(2)}, u32[]{:S(2)}) collective-permute-start(bf16[4,512,1024]{2,1,0:T(8,128)(2,1)} %get-tuple-element.637), channel_id=1, source_target_pairs={{0,1},{1,0},{2,3},{3,2},{4,5},{5,4},{6,7},{7,6},{8,9},{9,8},{10,11... | collective-permute-start | bytes 12582920 | tf_op jit(solution)/shard_map/ppermute | solution.py:391
  15.3 36.6 %collective-permute-start.2 = (bf16[4,512,1024]{2,1,0:T(8,128)(2,1)}, bf16[4,512,1024]{2,1,0:T(8,128)(2,1)}, u32[]{:S(2)}, u32[]{:S(2)}) collective-permute-start(bf16[4,512,1024]{2,1,0:T(8,128)(2,1)} %get-tuple-element.641), channel_id=1, source_target_pairs={{0,1},{1,0},{2,3},{3,2},{4,5},{5,4},{6,7},{7,6},{8,9},{9,8},{10,11... | collective-permute-start | bytes 12582920 | tf_op jit(solution)/shard_map/ppermute | solution.py:391
  18.1 25.1 %collective-permute-start.4 = (f32[48,1024]{1,0:T(8,128)}, f32[48,1024]{1,0:T(8,128)}, u32[]{:S(2)}, u32[]{:S(2)}) collective-permute-start(f32[48,1024]{1,0:T(8,128)} %bitcast.219), channel_id=1, source_target_pairs={{0,1},{1,0},{2,3},{3,2},{4,5},{5,4},{6,7},{7,6},{8,9},{9,8},{10,11... | collective-permute-start | bytes 589832 | tf_op jit(solution)/shard_map/ppermute | solution.py:366
  21.6 30.3 %collective-permute-start.3 = (bf16[1024,512]{1,0:T(8,128)(2,1)}, bf16[1024,512]{1,0:T(8,128)(2,1)}, u32[]{:S(2)}, u32[]{:S(2)}) collective-permute-start(bf16[1024,512]{1,0:T(8,128)(2,1)} %get-tuple-element.1268), channel_id=1, source_target_pairs={{0,1},{1,0},{2,3},{3,2},{4,5},{5,4},{6,7},{7,6},{8,9},{9,8},{10,11... | collective-permute-start | bytes 3145736 | tf_op jit(solution)/shard_map/ppermute | solution.py:366
  40.9 111.3 %collective-permute-start.19 = (bf16[20,48,512]{2,1,0:T(8,128)(2,1)}, bf16[20,48,512]{2,1,0:T(8,128)(2,1)}, u32[]{:S(2)}, u32[]{:S(2)}) collective-permute-start(bf16[20,48,512]{2,1,0:T(8,128)(2,1)} %get-tuple-element.635), channel_id=1, source_target_pairs={{0,4},{4,0},{8,12},{12,8},{16,20},{20,16},{24,28},{28,24},{1,5},{5... | collective-permute-start | bytes 2949128 | tf_op jit(solution)/shard_map/ppermute | solution.py:434
  43.2 109.0 %collective-permute-start.20 = (bf16[20,48,512]{2,1,0:T(8,128)(2,1)}, bf16[20,48,512]{2,1,0:T(8,128)(2,1)}, u32[]{:S(2)}, u32[]{:S(2)}) collective-permute-start(bf16[20,48,512]{2,1,0:T(8,128)(2,1)} %get-tuple-element.635), channel_id=1, source_target_pairs={{0,8},{4,12},{8,0},{12,4},{16,24},{20,28},{24,16},{28,20},{1,9},{5... | collective-permute-start | bytes 2949128 | tf_op jit(solution)/shard_map/ppermute | solution.py:434
  197.0 61.2 %collective-permute-start.34 = (bf16[20,48,512]{2,1,0:T(8,128)(2,1)}, bf16[20,48,512]{2,1,0:T(8,128)(2,1)}, u32[]{:S(2)}, u32[]{:S(2)}) collective-permute-start(bf16[20,48,512]{2,1,0:T(8,128)(2,1)} %get-tuple-element.921), channel_id=1, source_target_pairs={{0,4},{4,0},{8,12},{12,8},{16,20},{20,16},{24,28},{28,24},{1,5},{5... | collective-permute-start | bytes 2949128 | tf_op jit(solution)/shard_map/ppermute | solution.py:434
  197.5 60.7 %collective-permute-start.35 = (bf16[20,48,512]{2,1,0:T(8,128)(2,1)}, bf16[20,48,512]{2,1,0:T(8,128)(2,1)}, u32[]{:S(2)}, u32[]{:S(2)}) collective-permute-start(bf16[20,48,512]{2,1,0:T(8,128)(2,1)} %get-tuple-element.921), channel_id=1, source_target_pairs={{0,8},{4,12},{8,0},{12,4},{16,24},{20,28},{24,16},{28,20},{1,9},{5... | collective-permute-start | bytes 2949128 | tf_op jit(solution)/shard_map/ppermute | solution.py:434
  264.3 50.0 %collective-permute-start.43 = (bf16[7,48,2048]{2,1,0:T(8,128)(2,1)}, bf16[7,48,2048]{2,1,0:T(8,128)(2,1)S(1)}, u32[]{:S(2)}, u32[]{:S(2)}) collective-permute-start(bf16[7,48,2048]{2,1,0:T(8,128)(2,1)} %get-tuple-element.1135), channel_id=1, source_target_pairs={{0,4},{4,0},{8,12},{12,8},{16,20},{20,16},{24,28},{28,24},{1,5},{5... | collective-permute-start | bytes 4128776 | tf_op jit(solution)/shard_map/ppermute | solution.py:434
  265.9 48.4 %collective-permute-start.44 = (bf16[7,48,2048]{2,1,0:T(8,128)(2,1)}, bf16[7,48,2048]{2,1,0:T(8,128)(2,1)S(1)}, u32[]{:S(2)}, u32[]{:S(2)}) collective-permute-start(bf16[7,48,2048]{2,1,0:T(8,128)(2,1)} %get-tuple-element.1136), channel_id=1, source_target_pairs={{0,8},{4,12},{8,0},{12,4},{16,24},{20,28},{24,16},{28,20},{1,9},{5... | collective-permute-start | bytes 4128776 | tf_op jit(solution)/shard_map/ppermute | solution.py:434
  310.1 60.7 %collective-permute-start.50 = (bf16[6,48,2048]{2,1,0:T(8,128)(2,1)}, bf16[6,48,2048]{2,1,0:T(8,128)(2,1)}, u32[]{:S(2)}, u32[]{:S(2)}) collective-permute-start(bf16[6,48,2048]{2,1,0:T(8,128)(2,1)} %get-tuple-element.1210), channel_id=1, source_target_pairs={{0,4},{4,0},{8,12},{12,8},{16,20},{20,16},{24,28},{28,24},{1,5},{5... | collective-permute-start | bytes 3538952 | tf_op jit(solution)/shard_map/ppermute | solution.py:434
  310.7 60.8 %collective-permute-start.51 = (bf16[6,48,2048]{2,1,0:T(8,128)(2,1)}, bf16[6,48,2048]{2,1,0:T(8,128)(2,1)}, u32[]{:S(2)}, u32[]{:S(2)}) collective-permute-start(bf16[6,48,2048]{2,1,0:T(8,128)(2,1)} %get-tuple-element.1211), channel_id=1, source_target_pairs={{0,8},{4,12},{8,0},{12,4},{16,24},{20,28},{24,16},{28,20},{1,9},{5... | collective-permute-start | bytes 3538952 | tf_op jit(solution)/shard_map/ppermute | solution.py:434
  340.7 41.6 %collective-permute-start.52 = (bf16[3,48,2048]{2,1,0:T(8,128)(2,1)}, bf16[3,48,2048]{2,1,0:T(8,128)(2,1)}, u32[]{:S(2)}, u32[]{:S(2)}) collective-permute-start(bf16[3,48,2048]{2,1,0:T(8,128)(2,1)} %get-tuple-element.1227), channel_id=1, source_target_pairs={{0,4},{4,0},{8,12},{12,8},{16,20},{20,16},{24,28},{28,24},{1,5},{5... | collective-permute-start | bytes 1769480 | tf_op jit(solution)/shard_map/ppermute | solution.py:434
  342.4 39.9 %collective-permute-start.53 = (bf16[3,48,2048]{2,1,0:T(8,128)(2,1)}, bf16[3,48,2048]{2,1,0:T(8,128)(2,1)}, u32[]{:S(2)}, u32[]{:S(2)}) collective-permute-start(bf16[3,48,2048]{2,1,0:T(8,128)(2,1)} %get-tuple-element.1228), channel_id=1, source_target_pairs={{0,8},{4,12},{8,0},{12,4},{16,24},{20,28},{24,16},{28,20},{1,9},{5... | collective-permute-start | bytes 1769480 | tf_op jit(solution)/shard_map/ppermute | solution.py:434
  370.9 43.6 %collective-permute-start.55 = (bf16[2,48,2048]{2,1,0:T(8,128)(2,1)}, bf16[2,48,2048]{2,1,0:T(8,128)(2,1)S(1)}, u32[]{:S(2)}, u32[]{:S(2)}) collective-permute-start(bf16[2,48,2048]{2,1,0:T(8,128)(2,1)} %get-tuple-element.1244), channel_id=1, source_target_pairs={{0,4},{4,0},{8,12},{12,8},{16,20},{20,16},{24,28},{28,24},{1,5},{5... | collective-permute-start | bytes 1179656 | tf_op jit(solution)/shard_map/ppermute | solution.py:434
  371.4 50.1 %collective-permute-start.57 = (bf16[2,48,2048]{2,1,0:T(8,128)(2,1)}, bf16[2,48,2048]{2,1,0:T(8,128)(2,1)}, u32[]{:S(2)}, u32[]{:S(2)}) collective-permute-start(bf16[2,48,2048]{2,1,0:T(8,128)(2,1)} %get-tuple-element.1248), channel_id=1, source_target_pairs={{0,8},{4,12},{8,0},{12,4},{16,24},{20,28},{24,16},{28,20},{1,9},{5... | collective-permute-start | bytes 1179656 | tf_op jit(solution)/shard_map/ppermute | solution.py:434
  385.4 29.1 %collective-permute-start.54 = (bf16[2,48,2048]{2,1,0:T(8,128)(2,1)}, bf16[2,48,2048]{2,1,0:T(8,128)(2,1)S(1)}, u32[]{:S(2)}, u32[]{:S(2)}) collective-permute-start(bf16[2,48,2048]{2,1,0:T(8,128)(2,1)} %get-tuple-element.1241), channel_id=1, source_target_pairs={{0,4},{4,0},{8,12},{12,8},{16,20},{20,16},{24,28},{28,24},{1,5},{5... | collective-permute-start | bytes 1179656 | tf_op jit(solution)/shard_map/ppermute | solution.py:434
  387.1 34.4 %collective-permute-start.56 = (bf16[2,48,2048]{2,1,0:T(8,128)(2,1)}, bf16[2,48,2048]{2,1,0:T(8,128)(2,1)S(1)}, u32[]{:S(2)}, u32[]{:S(2)}) collective-permute-start(bf16[2,48,2048]{2,1,0:T(8,128)(2,1)} %get-tuple-element.1247), channel_id=1, source_target_pairs={{0,8},{4,12},{8,0},{12,4},{16,24},{20,28},{24,16},{28,20},{1,9},{5... | collective-permute-start | bytes 1179656 | tf_op jit(solution)/shard_map/ppermute | solution.py:434
  431.4 61.1 %collective-permute-start.83 = (f32[48,1024]{1,0:T(8,128)}, f32[48,1024]{1,0:T(8,128)}, u32[]{:S(2)}, u32[]{:S(2)}) collective-permute-start(f32[48,1024]{1,0:T(8,128)} %bitcast.121), channel_id=1, source_target_pairs={{0,1},{1,0},{2,3},{3,2},{4,5},{5,4},{6,7},{7,6},{8,9},{9,8},{10,11... | collective-permute-start | bytes 589832 | tf_op jit(solution)/shard_map/ppermute | solution.py:366
  432.3 66.5 %collective-permute-start.58 = (bf16[20,48,512]{2,1,0:T(8,128)(2,1)}, bf16[20,48,512]{2,1,0:T(8,128)(2,1)}, u32[]{:S(2)}, u32[]{:S(2)}) collective-permute-start(bf16[20,48,512]{2,1,0:T(8,128)(2,1)} %get-tuple-element.1254), channel_id=1, source_target_pairs={{0,1},{1,0},{2,3},{3,2},{4,5},{5,4},{6,7},{7,6},{8,9},{9,8},{10,11... | collective-permute-start | bytes 2949128 | tf_op jit(solution)/shard_map/ppermute | solution.py:366
  482.5 26.3 %collective-permute-start.76 = (bf16[4,64,2048]{2,1,0:T(8,128)(2,1)}, bf16[4,64,2048]{2,1,0:T(8,128)(2,1)}, u32[]{:S(2)}, u32[]{:S(2)}) collective-permute-start(bf16[4,64,2048]{2,1,0:T(8,128)(2,1)} %dynamic-slice_bitcast_fusion.1), channel_id=1, source_target_pairs={{0,4},{4,0},{8,12},{12,8},{16,20},{20,16},{24,28},{28,24},{1,5},{5... | collective-permute-start | bytes 3145736 | tf_op jit(solution)/shard_map/ppermute | solution.py:434
  484.0 69.3 %collective-permute-start.67 = (bf16[2,4,64,2048]{3,2,1,0:T(8,128)(2,1)}, bf16[2,4,64,2048]{3,2,1,0:T(8,128)(2,1)}, u32[]{:S(2)}, u32[]{:S(2)}) collective-permute-start(bf16[2,4,64,2048]{3,2,1,0:T(8,128)(2,1)} %dynamic-slice_bitcast_fusion), channel_id=1, source_target_pairs={{0,4},{4,0},{8,12},{12,8},{16,20},{20,16},{24,28},{28,24},{1,5},{5... | collective-permute-start | bytes 6291464 | tf_op jit(solution)/shard_map/ppermute | solution.py:434
  489.5 34.3 %collective-permute-start.61 = (bf16[2,2,64,2048]{3,2,1,0:T(8,128)(2,1)S(1)}, bf16[2,2,64,2048]{3,2,1,0:T(8,128)(2,1)}, u32[]{:S(2)}, u32[]{:S(2)}) collective-permute-start(bf16[2,2,64,2048]{3,2,1,0:T(8,128)(2,1)S(1)} %bitcast.233), channel_id=1, source_target_pairs={{0,8},{4,12},{24,16},{28,20},{1,9},{5,13},{25,17},{29,21},{2,10},{... | collective-permute-start | bytes 3145736 | tf_op jit(solution)/shard_map/ppermute | solution.py:434
  525.8 31.6 %collective-permute-start.62 = (bf16[2,2,64,2048]{3,2,1,0:T(8,128)(2,1)S(1)}, bf16[2,2,64,2048]{3,2,1,0:T(8,128)(2,1)S(1)}, u32[]{:S(2)}, u32[]{:S(2)}) collective-permute-start(bf16[2,2,64,2048]{3,2,1,0:T(8,128)(2,1)S(1)} %get-tuple-element.1262), channel_id=1, source_target_pairs={{0,8},{4,12},{8,16},{12,20},{1,9},{5,13},{9,17},{13,21},{2,10},{6,... | collective-permute-start | bytes 3145736 | tf_op jit(solution)/shard_map/ppermute | solution.py:434
  530.3 27.4 %collective-permute-start.64 = (bf16[2,2,64,2048]{3,2,1,0:T(8,128)(2,1)S(1)}, bf16[2,2,64,2048]{3,2,1,0:T(8,128)(2,1)S(1)}, u32[]{:S(2)}, u32[]{:S(2)}) collective-permute-start(bf16[2,2,64,2048]{3,2,1,0:T(8,128)(2,1)S(1)} %get-tuple-element.1263), channel_id=1, source_target_pairs={{16,8},{20,12},{24,16},{28,20},{17,9},{21,13},{25,17},{29,21},{18,... | collective-permute-start | bytes 3145736 | tf_op jit(solution)/shard_map/ppermute | solution.py:434
  531.8 34.2 %collective-permute-start.79 = (bf16[64,2048]{1,0:T(8,128)(2,1)S(1)}, bf16[64,2048]{1,0:T(8,128)(2,1)S(1)}, u32[]{:S(2)}, u32[]{:S(2)}) collective-permute-start(bf16[64,2048]{1,0:T(8,128)(2,1)S(1)} %get-tuple-element.1274), channel_id=1, source_target_pairs={{0,8},{4,12},{8,16},{12,20},{16,24},{20,28},{1,9},{5,13},{9,17},{1... | collective-permute-start | bytes 786440 | tf_op jit(solution)/shard_map/ppermute | solution.py:434
  536.3 45.5 %collective-permute-start.81 = (bf16[64,2048]{1,0:T(8,128)(2,1)S(1)}, bf16[64,2048]{1,0:T(8,128)(2,1)S(1)}, u32[]{:S(2)}, u32[]{:S(2)}) collective-permute-start(bf16[64,2048]{1,0:T(8,128)(2,1)S(1)} %get-tuple-element.1275), channel_id=1, source_target_pairs={{8,0},{12,4},{16,8},{20,12},{24,16},{28,20},{9,1},{13,5},{17,9},{2... | collective-permute-start | bytes 786440 | tf_op jit(solution)/shard_map/ppermute | solution.py:434
  557.0 46.6 %collective-permute-start.68 = (bf16[2,2,64,2048]{3,2,0,1:T(8,128)(2,1)}, bf16[2,2,64,2048]{3,2,0,1:T(8,128)(2,1)}, u32[]{:S(2)}, u32[]{:S(2)}) collective-permute-start(bf16[2,2,64,2048]{3,2,0,1:T(8,128)(2,1)} %bitcast.218), channel_id=1, source_target_pairs={{0,16},{4,20},{8,24},{12,28},{16,0},{20,4},{24,8},{28,12},{1,17},{... | collective-permute-start | bytes 3145736 | tf_op jit(solution)/shard_map/ppermute | solution.py:434
  559.8 65.1 %collective-permute-start.63 = (bf16[2,2,64,2048]{3,2,1,0:T(8,128)(2,1)}, bf16[2,2,64,2048]{3,2,1,0:T(8,128)(2,1)S(1)}, u32[]{:S(2)}, u32[]{:S(2)}) collective-permute-start(bf16[2,2,64,2048]{3,2,1,0:T(8,128)(2,1)} %get-tuple-element.1264), channel_id=1, source_target_pairs={{0,8},{4,12},{8,16},{12,20},{16,24},{20,28},{1,9},{5,13},{9,17},{1... | collective-permute-start | bytes 3145736 | tf_op jit(solution)/shard_map/ppermute | solution.py:434
  564.1 64.0 %collective-permute-start.65 = (bf16[2,2,64,2048]{3,2,1,0:T(8,128)(2,1)}, bf16[2,2,64,2048]{3,2,1,0:T(8,128)(2,1)}, u32[]{:S(2)}, u32[]{:S(2)}) collective-permute-start(bf16[2,2,64,2048]{3,2,1,0:T(8,128)(2,1)} %get-tuple-element.1265), channel_id=1, source_target_pairs={{8,0},{12,4},{16,8},{20,12},{24,16},{28,20},{9,1},{13,5},{17,9},{2... | collective-permute-start | bytes 3145736 | tf_op jit(solution)/shard_map/ppermute | solution.py:434
  582.6 53.7 %collective-permute-start.82 = (bf16[1024,64]{0,1:T(8,128)(2,1)S(1)}, bf16[1024,64]{0,1:T(8,128)(2,1)S(1)}, u32[]{:S(2)}, u32[]{:S(2)}) collective-permute-start(bf16[1024,64]{0,1:T(8,128)(2,1)S(1)} %bitcast.246), channel_id=1, source_target_pairs={{0,1},{1,0},{2,3},{3,2},{4,5},{5,4},{6,7},{7,6},{8,9},{9,8},{10,11... | collective-permute-start | bytes 393224 | tf_op jit(solution)/shard_map/ppermute | solution.py:366
  606.1 26.6 %collective-permute-start.70 = (bf16[2,64,2048]{2,1,0:T(8,128)(2,1)S(1)}, bf16[2,64,2048]{2,1,0:T(8,128)(2,1)}, u32[]{:S(2)}, u32[]{:S(2)}) collective-permute-start(bf16[2,64,2048]{2,1,0:T(8,128)(2,1)S(1)} %get-tuple-element.1276), channel_id=1, source_target_pairs={{0,8},{4,12},{8,0},{12,4},{16,24},{20,28},{24,16},{28,20},{1,9},{5... | collective-permute-start | bytes 1572872 | tf_op jit(solution)/shard_map/ppermute | solution.py:434
  (188 other events, 1414.4 us)

commit v6 on v5

--- a/solution.py
+++ b/solution.py
@@ -54,7 +54,8 @@
     )(*(in_hbm(x) for x in arrays))
 
 
-def layout_kernel(which_ref, w_ref, out_ref, all_ref, buf, sems, out_sems):
+def layout_kernel(keep, which_ref, w_ref, first_ref, second_ref, buf, sems, out_sems):
+    out_ref, all_ref = (first_ref, second_ref) if keep else (second_ref, first_ref)
     depth, part = w_ref.shape[1], buf.shape[1]
 
     def fetch(i):
@@ -105,16 +106,17 @@
     pass
 
 
-def after(token, *arrays):
+def after(tokens, *arrays):
+    count = len(tokens)
     return pl.pallas_call(
         pass_kernel,
-        out_shape=tuple(pltpu.HBM(x.shape, x.dtype) for x in arrays),
-        in_specs=[ANY] * (1 + len(arrays)),
+        out_shape=tuple(jax.ShapeDtypeStruct(x.shape, x.dtype) for x in arrays),
+        in_specs=[ANY] * (count + len(arrays)),
         out_specs=[ANY] * len(arrays),
-        input_output_aliases={1 + i: i for i in range(len(arrays))},
+        input_output_aliases={count + i: i for i in range(len(arrays))},
         compiler_params=params(1),
         name="after",
-    )(token, *(in_hbm(x) for x in arrays))
+    )(*tokens, *arrays)
 
 
 def assemble_kernel(place_ref, near_a, near_b, far_a, far_b, in_ref, rec_ref):
@@ -371,15 +373,17 @@
     def hbm(shape, dtype):
         return pltpu.HBM(shape, dtype)
 
-    def by_gate(weights, index):
+    def by_gate(weights, index, keep=True):
         shape = (4,) + weights.shape[1:2] + weights.shape[3:]
+        kept = (vmem(shape, BF16),) if keep else ()
         part = weights.shape[1] // 8
         return pl.pallas_call(
-            layout_kernel,
-            out_shape=(vmem(shape, BF16), hbm(shape, BF16)),
+            functools.partial(layout_kernel, keep),
+            out_shape=kept + (hbm(shape, BF16),),
             in_specs=[SMEM, ANY],
-            out_specs=[VMEM, ANY],
-            scratch_shapes=[
+            out_specs=[VMEM] * len(kept) + [ANY],
+            scratch_shapes=([] if kept else [pltpu.VMEM(shape, BF16)])
+            + [
                 pltpu.VMEM((3, part) + weights.shape[2:], BF16),
                 pltpu.SemaphoreType.DMA((3,)),
                 pltpu.SemaphoreType.DMA((8,)),
@@ -388,7 +392,7 @@
             name="layout",
         )(jnp.full((1,), index, jnp.int32), in_hbm(weights))
 
-    win_b, rec_b = (lax.ppermute(by_gate(w, 1 - own)[1], "gate", swap) for w in (w_in, w_rec))
+    win_b, rec_b = (lax.ppermute(by_gate(w, 1 - own, False)[0], "gate", swap) for w in (w_in, w_rec))
     (win_av, win_a), (rec_av, rec_a) = by_gate(w_in, own), by_gate(w_rec, own)
     proj_a, proj_b = trade(pick(proj, own), pick(proj, 1 - own))
     bias_a, bias_b = trade(pick(bias, own), pick(bias, 1 - own))
@@ -620,7 +624,7 @@
             peer = lax.ppermute(part, "gate", across)
             if ready is not None:
                 due, sides = ready
-                sides = after(part, *sides) if step else sides
+                sides = after((part,), *sides) if step else sides
                 pending.append((due, (swapped(sides[0], near_swap), swapped(sides[1], far_swap))))
                 ready = None
             passing = pending.pop(0)[1] if pending and pending[0][0] >= step else ()
@@ -640,7 +644,7 @@
     def by_direction(mine, theirs):
         return jnp.stack([jnp.where(own == 0, mine, theirs), jnp.where(own == 0, theirs, mine)])
 
-    def line_sum(chunks, axis, stride, count, first=None):
+    def line_sum(chunks, axis, stride, count, first=None, gates={}):
         here = (spot // stride) % count
 
         def chunk(index):
@@ -656,10 +660,14 @@
         ends += [(i, i - stride) for i in range(n_batch) if at(i) == count - 1]
         up = down = swapped(chunk(jnp.where(here == 0, count - 1, 0)) if first is None else first, ends)
         for slot in range(2, count):
+            if slot in gates:
+                up, down = gates[slot](up, down)
             rise = (chunk(here + count - slot).astype(F32) + up.astype(F32)).astype(BF16)
             fall = (chunk(here - count + slot).astype(F32) + down.astype(F32)).astype(BF16)
             up = swapped(rise, [(i, i + stride) for i in range(n_batch) if at(i) < min(slot, count - 1)])
             down = swapped(fall, [(i, i - stride) for i in range(n_batch) if at(i) > max(count - 1 - slot, 0)])
+        if count in gates:
+            up, down = gates[count](up, down)
         return (chunk(here).astype(F32) + up.astype(F32) + down.astype(F32)).astype(BF16)
 
     line = n_batch // 2
@@ -675,36 +683,92 @@
         return jnp.concatenate([feat, prev], axis=2)
 
     left = both(feat_all, prev_all)
-    early, taken = [], []
-    for kept, feat, prev, parts in zip((near_all, far_all), feat_in, prev_in, zip(*exchanged)):
-        steps_late = sum(x.shape[0] for x in parts[-LATE:])
-        theirs = both(feat, prev)
-        total = product(left, kept) + product(theirs[steps_late:], jnp.concatenate(parts[:-LATE][::-1], axis=0))
-        early.append(total)
-        taken.append((theirs[:steps_late], parts[-LATE:][::-1]))
-    near_late, near_parts = taken[0]
-    near_parts = jnp.concatenate(after(early[0], *near_parts), axis=0)
-    here = spot // 2
-    begin = jnp.where(here == 0, line - 1, 0)
+    def input_grad_of(dz):
+        return pl.pallas_call(
+            input_grad_kernel,
+            out_shape=jax.ShapeDtypeStruct((steps, streams, depth), F32),
+            grid_spec=pltpu.PrefetchScalarGridSpec(
+                num_scalar_prefetch=1,
+                grid=(PIECES, 4),
+                in_specs=[
+                    pl.BlockSpec((1, steps, streams, width), lambda p, g, turn: (p, 0, 0, g)),
+                    pl.BlockSpec(
+                        (1, depth, width), lambda p, g, turn: (jnp.where(p < 2, g, 3), 0, jnp.where(p < 2, p, 1))
+                    ),
+                    pl.BlockSpec(
+                        (1, depth, width), lambda p, g, turn: (jnp.where(p < 2, 0, g), 0, jnp.where(p < 2, 0, p - 2))
+                    ),
+                ],
+                out_specs=pl.BlockSpec((steps, streams, depth), lambda p, g, turn: (0, 0, 0)),
+                scratch_shapes=[pltpu.VMEM((rows, depth), F32)],
+            ),
+            compiler_params=params(16),
+            cost_estimate=cost(2 * rows * depth * 8 * cells, 8 * depth * cells * 4),
+            name="input_grad",
+        )(turn, dz, in_hbm(win_a), in_hbm(win_b))
+
+    grad_proj = jnp.einsum("ptnc,tnk->pkc", mixed_all, raw_all, preferred_element_type=F32).astype(BF16)
+    grad_proj = grad_proj.reshape(PIECES, line, 2, share_rows, width)
+    proj_mine = lax.dynamic_index_in_dim(grad_proj, low, 2, keepdims=False)
+    proj_send = lax.dynamic_index_in_dim(grad_proj, 1 - low, 2, keepdims=False)
+    proj_taken = swapped(proj_send, near_swap)
+
+    def early_sum(kept, theirs, parts):
+        taken = jnp.concatenate(parts[:-LATE][::-1], axis=0)
+        return product(left, kept) + product(theirs[steps - taken.shape[0] :], taken)
+
+    def rows_first(total):
+        return total.astype(BF16).reshape(2, line, 2, share_rows, 4 * width)
+
+    begin = jnp.where(spot // 2 == 0, line - 1, 0)
 
     def line_chunk(array, axis):
         shape = array.shape[:axis] + (2, line, 2 * share_rows) + array.shape[axis + 1 :]
         return lax.dynamic_index_in_dim(array.reshape(shape), begin, axis + 1, keepdims=False)
 
-    first = line_chunk(early[0], 0).reshape(4 * share_rows, -1) + product(line_chunk(near_late, 2), near_parts)
-    first = first.astype(BF16)
-    (near_parts,) = after(first, near_parts)
-
-    def rows_first(total):
-        return total.astype(BF16).reshape(2, line, 2, share_rows, 4 * width)
-
-    near = rows_first(early[0] + product(near_late, near_parts))
-    far_parts = jnp.concatenate(after(near, *taken[1][1]), axis=0)
-    far = rows_first(early[1] + product(taken[1][0], far_parts))
-    token = far
-    near = line_sum(near, 1, 2, line, first.reshape(2, 2, share_rows, 4 * width))
-    far = line_sum(far, 2, 1, 2).reshape(2, line // 2, 2, share_rows, 4 * width)
+    near_parts, far_parts = zip(*exchanged)
+    near_left, far_left = (both(feat, prev) for feat, prev in zip(feat_in, prev_in))
+    late_steps = sum(x.shape[0] for x in near_parts[-LATE:])
+    near_early = early_sum(near_all, near_left, near_parts)
+    near_late = jnp.concatenate(after((near_early, proj_send), *near_parts[-LATE:][::-1]), axis=0)
+    first = line_chunk(near_early, 0).reshape(4 * share_rows, -1)
+    first = (first + product(line_chunk(near_left[:late_steps], 2), near_late)).astype(BF16)
+    (near_late,) = after((first,), near_late)
+    near = rows_first(near_early + product(near_left[:late_steps], near_late))
+
+    far_all, *far_parts = after((first,), far_all, *far_parts)
+    far_early = early_sum(far_all, far_left, far_parts)
+    far_late = jnp.concatenate(after((near, proj_taken), *far_parts[-LATE:][::-1]), axis=0)
+    far = rows_first(far_early + product(far_left[:late_steps], far_late))
+
+    def with_partner(grad):
+        mine = lax.dynamic_index_in_dim(grad, low, 1, keepdims=False)
+        taken = swapped(lax.dynamic_index_in_dim(grad, 1 - low, 1, keepdims=False), near_swap)
+        return taken, (mine.astype(F32) + taken.astype(F32)).astype(BF16)
+
+    (in_taken, far_in), (rec_taken, far_rec) = (with_partner(far[i]) for i in range(2))
+
+    tokens = {}
+
+    def second(up, down):
+        up, down = after((far,), up, down)
+        tokens["dz"], tokens["proj"] = after((up,), dz_all, proj_taken)
+        return up, down
+
+    def third(up, down):
+        tokens["dx"] = input_grad_of(tokens["dz"])
+        tokens["hidden"], tokens["cell"], dz = after((up, tokens["dx"]), hidden_all, cell, tokens["dz"])
+        tokens["bias"] = jnp.sum(dz, axis=(1, 2), dtype=F32)
+        return after((in_taken, tokens["dx"]), up, down)
+
+    def final(up, down):
+        return after((rec_taken, tokens["bias"]), up, down)
+
+    gates = {2: second, 3: third, line: final} if line > 3 else {}
+    near = line_sum(near, 1, 2, line, first.reshape(2, 2, share_rows, 4 * width), gates)
+    far = jnp.stack([far_in, far_rec]).reshape(2, line // 2, 2, share_rows, 4 * width)
     far = line_sum(far, 1, 4, line // 2)
+    dx_all, hidden_all, cell, grad_bias = (tokens[x] for x in ("dx", "hidden", "cell", "bias"))
 
     def halves_of(summed, index, pairs):
         mine = lax.dynamic_index_in_dim(summed, index, 1, keepdims=False)
@@ -718,17 +782,11 @@
         out_shape=(jax.ShapeDtypeStruct(grad_shape, F32),) * 2,
         in_specs=[SMEM] + [VMEM] * 4,
         out_specs=[VMEM] * 2,
-        compiler_params=params(32),
+        compiler_params=params(14),
         name="assemble",
     )(jnp.stack([own, low, high]), *near_pair, *far_pair)
 
-    dz_all, mixed_all, hidden_all, cell = after(token, dz_all, mixed_all, hidden_all, cell)
-
-    grad_proj = jnp.einsum("ptnc,tnk->kpc", mixed_all, raw_all, preferred_element_type=F32).astype(BF16)
-    grad_proj = line_sum(grad_proj.reshape(line, 2, share_rows, QUARTERS * cells), 1, 1, 2)
-    grad_proj = line_sum(grad_proj, 0, 2, line)
-
-    grad_bias = jnp.sum(dz_all, axis=(1, 2), dtype=F32)
+    grad_proj = line_sum((proj_mine.astype(F32) + tokens["proj"].astype(F32)).astype(BF16), 1, 2, line)
     stride = 1
     while stride < n_batch:
         grad_bias = grad_bias + swapped(grad_bias, [(i, i ^ stride) for i in range(n_batch)])
@@ -741,8 +799,9 @@
     own_cells = cells // n_batch
     shaped = lax.dynamic_slice_in_dim(shaped, spot * own_cells, own_cells, 2)
     grad_bias = home(shaped[0], shaped[1])
-    grad_proj = grad_proj.reshape(share_rows, QUARTERS, cells)
-    grad_proj = home(jnp.transpose(grad_proj[:, 0]), jnp.transpose(grad_proj[:, 1]))
+    grad_proj = jnp.transpose(grad_proj.reshape(QUARTERS, HALVES, share_rows, width), (0, 1, 3, 2))
+    grad_proj = grad_proj.reshape(QUARTERS, cells, share_rows)
+    grad_proj = home(grad_proj[0], grad_proj[1])
 
     both_hidden = trade(hidden_all, hidden_all)
 
@@ -755,29 +814,6 @@
     )
     last_dirs = by_direction(*trade(last_c[0], last_c[1]))
     final_c = jnp.zeros_like(state_c).at[stream_doc].set(jnp.transpose(last_dirs, (1, 0, 2)))
-
-    dx_all = pl.pallas_call(
-        input_grad_kernel,
-        out_shape=jax.ShapeDtypeStruct((steps, streams, depth), F32),
-        grid_spec=pltpu.PrefetchScalarGridSpec(
-            num_scalar_prefetch=1,
-            grid=(PIECES, 4),
-            in_specs=[
-                pl.BlockSpec((1, steps, streams, width), lambda p, g, turn: (p, 0, 0, g)),
-                pl.BlockSpec(
-                    (1, depth, width), lambda p, g, turn: (jnp.where(p < 2, g, 3), 0, jnp.where(p < 2, p, 1))
-                ),
-                pl.BlockSpec(
-                    (1, depth, width), lambda p, g, turn: (jnp.where(p < 2, 0, g), 0, jnp.where(p < 2, 0, p - 2))
-                ),
-            ],
-            out_specs=pl.BlockSpec((steps, streams, depth), lambda p, g, turn: (0, 0, 0)),
-            scratch_shapes=[pltpu.VMEM((rows, depth), F32)],
-        ),
-        compiler_params=params(24),
-        cost_estimate=cost(2 * rows * depth * 8 * cells, 8 * depth * cells * 4),
-        name="input_grad",
-    )(turn, dz_all, in_hbm(win_a), in_hbm(win_b))
 
     half_cols = depth // 2
     upper = rank // 2

time: 657 us -> 622 us (0.947)
  waiting for transfers between devices: 102 us -> 83.2 us
  local copies, waits for them, and re-layouts: 70.2 us -> 60.5 us
  other arithmetic: 37.6 us -> 29.9 us
    ppermute x32 -> x33, waiting for transfers between devices: 93.9 us -> 78.2 us  [swapped(): return lax.ppermute(array, 'batch', pairs)]
    ppermute x32 -> x33, starting transfers between devices: 52 us -> 47.5 us  [swapped(): return lax.ppermute(array, 'batch', pairs)]
    pallas_call x13 -> x18, Pallas kernels: 41.9 us -> 37.7 us  [the longest x4 20.8 us: by_gate(): pl.pallas_call(functools.partial(layout_kernel, keep), out_shape=kept + (...]
    unnamed x282 -> x296, local copies, waits for them, and re-layouts: 28.9 us -> 29.1 us
  transfers between devices with their start and end apart: 84 -> 85, of which waited for: 38 -> 34; matrix products, arithmetic and copies ran while one was open for 18% -> 18% of each run, Pallas kernels for 41% -> 43%
where the time goes in v6:
time: 622 us; the launch traced here: 610 us
  Pallas kernels  297 us (48%)
  starting transfers between devices  93.1 us (15%)
  waiting for transfers between devices  83.2 us (13%)
  local copies, waits for them, and re-layouts  60.5 us (10%)
  matrix products  43.1 us (7%)
  other arithmetic  29.9 us (5%)
    ppermute x33, waiting for transfers between devices, swapped(): return lax.ppermute(array, 'batch', pairs)  78.2 us
    pallas_call x20, Pallas kernels, backward_call(): pl.pallas_call(backward_kernel, out_shape=(vmem((streams, depth), BF16),...  60.7 us
    pallas_call x20, Pallas kernels, between_call(): pl.pallas_call(functools.partial(between_kernel, not stacks, step == step...  60.1 us
    pallas_call x20, Pallas kernels, aside_call(): pl.pallas_call(functools.partial(aside_kernel, not stacks, step == 0, not...  56.9 us
    pallas_call x20, Pallas kernels, forward_call(): pl.pallas_call(functools.partial(forward_kernel, first), out_shape=(vmem(...  56.7 us
    ppermute x33, starting transfers between devices, swapped(): return lax.ppermute(array, 'batch', pairs)  47.5 us
    ppermute x39, starting transfers between devices, body(): peer = lax.ppermute(part, 'gate', across)  42.5 us
    dot_general x7, matrix products, product(): lax.dot_general(left.reshape(count, -1), right.reshape(count, -1), (((0,)...  39.3 us
  transfers between devices with their start and end apart: 85, of which 34 were waited for; matrix products, arithmetic and copies ran while one was open for 18% of the time, Pallas kernels for 43%

profile of v6, /device:TPU:8, one launch (start us, length us, event | category | flops | bytes accessed | tf_op | source)
XLA Modules:
  0.0 610.2 jit_solution(2828645114062564261)
XLA Ops:
  0.7 5.2 layout.4
  6.0 5.2 layout.6
  20.7 5.2 layout.5
  27.8 5.2 layout.7
  35.7 3.3 order.1
  80.7 3.3 between.23
  151.2 3.2 between.33
  172.4 3.4 between.36
  200.4 6.0 turned.1
  206.5 3.5 finish.1
  210.1 3.2 backward_step.20
  306.1 3.3 backward_step.33
  378.9 3.6 backward_step.39
  387.5 3.8 bitcast_convert_fusion
  392.6 6.9 %fusion.93 = f32[1024,2048,1]{1,0,2:T(8,128)} fusion(bf16[20,48,1024]{2,1,0:T(8,128)(2,1)S(1)} %copy-done.91, bf16[20,48,2048]{2,1,0:T(8,128)(2,1)S(1)} %copy-done.71), kind=kOutput, calls=%fused_computation.224 | convolution fusion | flops 4026531840 | bytes 14286848 | tf_op jit(solution)/shard_map/dot_general | solution.py:678
  399.5 6.7 %bitcast_add_fusion.3.refs_0_ = f32[1024,2048]{1,0:T(8,128)S(1)} fusion(f32[1024,2048,1]{1,0,2:T(8,128)} %fusion.93, bf16[20,48,1024]{2,1,0:T(8,128)(2,1)S(1)} %copy-done.79, bf16[7,48,2048]{2,1,0:T(8,128)(2,1)S(1)} %copy-done.76, bf16[6,48,2048]{2,1,0:T(8,128)(2,1)} %get-tuple-element.1242, bf16[3,48,2048]{2,1,0:T(8,128)(2,1)} %get-tuple-element.1241), kind=kOutput, calls=%fused_computation.10 | convolution fusion | flops 3232759808 | bytes 21889024 | tf_op jit(solution)/shard_map/dot_general | solution.py:678
  409.0 7.1 %fusion.94 = f32[1024,2048,1]{1,0,2:T(8,128)} fusion(bf16[20,48,1024]{2,1,0:T(8,128)(2,1)S(1)} %copy-done.91, bf16[20,48,2048]{2,1,0:T(8,128)(2,1)S(1)} %get-tuple-element.1258), kind=kOutput, calls=%fused_computation.225 | convolution fusion | flops 4026531840 | bytes 14286848 | tf_op jit(solution)/shard_map/dot_general | solution.py:678
  417.3 8.7 %fusion.8 = f32[1024,2048,1]{1,0,2:T(8,128)} fusion(bf16[20,48,1024]{2,1,0:T(8,128)(2,1)} %constant_dynamic-update-slice_fusion.6, bf16[7,48,2048]{2,1,0:T(8,128)(2,1)S(1)} %get-tuple-element.1263, bf16[6,48,2048]{2,1,0:T(8,128)(2,1)} %get-tuple-element.1262, bf16[3,48,2048]{2,1,0:T(8,128)(2,1)} %get-tuple-element.1261), kind=kOutput, calls=%fused_computation.19 | convolution fusion | flops 3230662656 | bytes 13500416 | tf_op jit(solution)/shard_map/dot_general | solution.py:678
  428.2 8.1 %fusion = bf16[1024,2048]{1,0:T(8,128)(2,1)S(1)} fusion(f32[1024,2048,1]{1,0,2:T(8,128)} %fusion.8, f32[1024,2048,1]{1,0,2:T(8,128)} %fusion.94, bf16[20,48,1024]{2,1,0:T(8,128)(2,1)} %constant_dynamic-update-slice_fusion.6, bf16[2,48,2048]{2,1,0:T(8,128)(2,1)S(1)} %get-tuple-element.1267, bf16[2,48,2048]{2,1,0:T(8,128)(2,1)} %copy-done.25), kind=kOutput, calls=%fused_computation.6 | convolution fusion | flops 813170688 | bytes 23724032 | tf_op jit(solution)/shard_map/dot_general | solution.py:678
  444.6 16.9 %input_grad.1.refs_1_ = f32[20,48,512]{2,1,0:T(8,128)S(1)} custom-call(s32[2]{0:T(128)S(1)} %copy-done.67, bf16[4,20,48,2048]{3,2,1,0:T(8,128)(2,1)S(1)} %get-tuple-element.1270.dz_ref.refs_4_, bf16[4,512,1024]{2,1,0:T(8,128)(2,1)} %get-tuple-element.1271.wa_ref, bf16[4,512,1024]{2,1,0:T(8,128)(2,1)} %collective-permute-done.1.refs_2_.wb_ref), custom_call_target="tpu_custom_call" | custom-call | flops 8053063680 | bytes 16777216 | tf_op jit(solution)/shard_map/input_grad/pallas_call | solution.py:687
  463.4 4.5 collective-permute-start.60
  473.5 9.4 %collective-permute-done.79 = bf16[4,64,512]{2,1,0:T(8,128)(2,1)S(1)} collective-permute-done((bf16[4,64,512]{2,1,0:T(8,128)(2,1)S(1)}, bf16[4,64,512]{2,1,0:T(8,128)(2,1)S(1)}, u32[]{:S(2)}, u32[]{:S(2)}) %collective-permute-start.79) | collective-permute-done | bytes 262176 | tf_op jit(solution)/shard_map/ppermute | solution.py:438
  484.5 5.0 collective-permute-start.80
  493.5 3.5 collective-permute-start.70
  498.0 35.2 %collective-permute-done.82 = bf16[4,64,512]{2,1,0:T(8,128)(2,1)S(1)} collective-permute-done((bf16[4,64,512]{2,1,0:T(8,128)(2,1)S(1)}, bf16[4,64,512]{2,1,0:T(8,128)(2,1)S(1)}, u32[]{:S(2)}, u32[]{:S(2)}) %collective-permute-start.82) | collective-permute-done | bytes 262176 | tf_op jit(solution)/shard_map/ppermute | solution.py:438
  541.6 8.8 %collective-permute-done.75 = f32[4,2048]{1,0:T(4,128)S(1)} collective-permute-done((f32[4,2048]{1,0:T(4,128)S(1)}, f32[4,2048]{1,0:T(4,128)S(1)}, u32[]{:S(2)}, u32[]{:S(2)}) %collective-permute-start.75) | collective-permute-done | bytes 32800 | tf_op jit(solution)/shard_map/ppermute | solution.py:438
  555.5 3.6 fusion.19
  568.2 5.5 scatter_fusion.1
  577.9 9.2 %collective-permute-done.67.refs_2_ = bf16[2,2,64,2048]{3,2,1,0:T(8,128)(2,1)S(1)} collective-permute-done((bf16[2,2,64,2048]{3,2,1,0:T(8,128)(2,1)}, bf16[2,2,64,2048]{3,2,1,0:T(8,128)(2,1)S(1)}, u32[]{:S(2)}, u32[]{:S(2)}) %collective-permute-start.67) | collective-permute-done | bytes 1048608 | tf_op jit(solution)/shard_map/ppermute | solution.py:438
  592.2 7.1 %collective-permute-done.72 = bf16[2,64,2048]{2,1,0:T(8,128)(2,1)} collective-permute-done((bf16[2,64,2048]{2,1,0:T(8,128)(2,1)S(1)}, bf16[2,64,2048]{2,1,0:T(8,128)(2,1)}, u32[]{:S(2)}, u32[]{:S(2)}) %collective-permute-start.72) | collective-permute-done | bytes 524320 | tf_op jit(solution)/shard_map/ppermute | solution.py:438
  601.6 4.2 fusion.2
  605.8 4.0 assemble.1
  (670 shorter events, 394.4 us)
Async XLA Ops:
  5.9 38.5 %collective-permute-start.1 = (bf16[4,512,1024]{2,1,0:T(8,128)(2,1)}, bf16[4,512,1024]{2,1,0:T(8,128)(2,1)}, u32[]{:S(2)}, u32[]{:S(2)}) collective-permute-start(bf16[4,512,1024]{2,1,0:T(8,128)(2,1)} %layout.4), channel_id=1, source_target_pairs={{0,1},{1,0},{2,3},{3,2},{4,5},{5,4},{6,7},{7,6},{8,9},{9,8},{10,11... | collective-permute-start | bytes 12582920 | tf_op jit(solution)/shard_map/ppermute | solution.py:395
  11.2 38.7 %collective-permute-start.2 = (bf16[4,512,1024]{2,1,0:T(8,128)(2,1)}, bf16[4,512,1024]{2,1,0:T(8,128)(2,1)}, u32[]{:S(2)}, u32[]{:S(2)}) collective-permute-start(bf16[4,512,1024]{2,1,0:T(8,128)(2,1)} %layout.6), channel_id=1, source_target_pairs={{0,1},{1,0},{2,3},{3,2},{4,5},{5,4},{6,7},{7,6},{8,9},{9,8},{10,11... | collective-permute-start | bytes 12582920 | tf_op jit(solution)/shard_map/ppermute | solution.py:395
  11.8 27.2 %collective-permute-start = (bf16[4,1024]{1,0:T(4,128)(2,1)S(1)}, bf16[4,1024]{1,0:T(4,128)(2,1)S(1)}, u32[]{:S(2)}, u32[]{:S(2)}) collective-permute-start(bf16[4,1024]{1,0:T(4,128)(2,1)S(1)} %get-tuple-element.1317), channel_id=1, source_target_pairs={{0,1},{1,0},{2,3},{3,2},{4,5},{5,4},{6,7},{7,6},{8,9},{9,8},{10,11... | collective-permute-start | bytes 24584 | tf_op jit(solution)/shard_map/ppermute | solution.py:368
  15.2 26.1 %collective-permute-start.4 = (f32[48,1024]{1,0:T(8,128)}, f32[48,1024]{1,0:T(8,128)}, u32[]{:S(2)}, u32[]{:S(2)}) collective-permute-start(f32[48,1024]{1,0:T(8,128)} %bitcast.249), channel_id=1, source_target_pairs={{0,1},{1,0},{2,3},{3,2},{4,5},{5,4},{6,7},{7,6},{8,9},{9,8},{10,11... | collective-permute-start | bytes 589832 | tf_op jit(solution)/shard_map/ppermute | solution.py:368
  18.6 31.3 %collective-permute-start.3 = (bf16[1024,512]{1,0:T(8,128)(2,1)}, bf16[1024,512]{1,0:T(8,128)(2,1)S(1)}, u32[]{:S(2)}, u32[]{:S(2)}) collective-permute-start(bf16[1024,512]{1,0:T(8,128)(2,1)} %get-tuple-element.1290), channel_id=1, source_target_pairs={{0,1},{1,0},{2,3},{3,2},{4,5},{5,4},{6,7},{7,6},{8,9},{9,8},{10,11... | collective-permute-start | bytes 3145736 | tf_op jit(solution)/shard_map/ppermute | solution.py:368
  39.0 112.2 %collective-permute-start.19 = (bf16[20,48,512]{2,1,0:T(8,128)(2,1)}, bf16[20,48,512]{2,1,0:T(8,128)(2,1)}, u32[]{:S(2)}, u32[]{:S(2)}) collective-permute-start(bf16[20,48,512]{2,1,0:T(8,128)(2,1)} %get-tuple-element.646), channel_id=1, source_target_pairs={{0,4},{4,0},{8,12},{12,8},{16,20},{20,16},{24,28},{28,24},{1,5},{5... | collective-permute-start | bytes 2949128 | tf_op jit(solution)/shard_map/ppermute | solution.py:438
  41.2 110.0 %collective-permute-start.20 = (bf16[20,48,512]{2,1,0:T(8,128)(2,1)}, bf16[20,48,512]{2,1,0:T(8,128)(2,1)}, u32[]{:S(2)}, u32[]{:S(2)}) collective-permute-start(bf16[20,48,512]{2,1,0:T(8,128)(2,1)} %get-tuple-element.646), channel_id=1, source_target_pairs={{0,8},{4,12},{8,0},{12,4},{16,24},{20,28},{24,16},{28,20},{1,9},{5... | collective-permute-start | bytes 2949128 | tf_op jit(solution)/shard_map/ppermute | solution.py:438
  196.1 61.0 %collective-permute-start.34 = (bf16[20,48,512]{2,1,0:T(8,128)(2,1)}, bf16[20,48,512]{2,1,0:T(8,128)(2,1)}, u32[]{:S(2)}, u32[]{:S(2)}) collective-permute-start(bf16[20,48,512]{2,1,0:T(8,128)(2,1)} %get-tuple-element.930), channel_id=1, source_target_pairs={{0,4},{4,0},{8,12},{12,8},{16,20},{20,16},{24,28},{28,24},{1,5},{5... | collective-permute-start | bytes 2949128 | tf_op jit(solution)/shard_map/ppermute | solution.py:438
  196.7 60.4 %collective-permute-start.35 = (bf16[20,48,512]{2,1,0:T(8,128)(2,1)}, bf16[20,48,512]{2,1,0:T(8,128)(2,1)}, u32[]{:S(2)}, u32[]{:S(2)}) collective-permute-start(bf16[20,48,512]{2,1,0:T(8,128)(2,1)} %get-tuple-element.930), channel_id=1, source_target_pairs={{0,8},{4,12},{8,0},{12,4},{16,24},{20,28},{24,16},{28,20},{1,9},{5... | collective-permute-start | bytes 2949128 | tf_op jit(solution)/shard_map/ppermute | solution.py:438
  263.3 50.5 %collective-permute-start.43 = (bf16[7,48,2048]{2,1,0:T(8,128)(2,1)S(1)}, bf16[7,48,2048]{2,1,0:T(8,128)(2,1)S(1)}, u32[]{:S(2)}, u32[]{:S(2)}) collective-permute-start(bf16[7,48,2048]{2,1,0:T(8,128)(2,1)S(1)} %get-tuple-element.1144), channel_id=1, source_target_pairs={{0,4},{4,0},{8,12},{12,8},{16,20},{20,16},{24,28},{28,24},{1,5},{5... | collective-permute-start | bytes 4128776 | tf_op jit(solution)/shard_map/ppermute | solution.py:438
  264.8 48.9 %collective-permute-start.44 = (bf16[7,48,2048]{2,1,0:T(8,128)(2,1)S(1)}, bf16[7,48,2048]{2,1,0:T(8,128)(2,1)S(1)}, u32[]{:S(2)}, u32[]{:S(2)}) collective-permute-start(bf16[7,48,2048]{2,1,0:T(8,128)(2,1)S(1)} %get-tuple-element.1145), channel_id=1, source_target_pairs={{0,8},{4,12},{8,0},{12,4},{16,24},{20,28},{24,16},{28,20},{1,9},{5... | collective-permute-start | bytes 4128776 | tf_op jit(solution)/shard_map/ppermute | solution.py:438
  309.4 61.4 %collective-permute-start.50 = (bf16[6,48,2048]{2,1,0:T(8,128)(2,1)}, bf16[6,48,2048]{2,1,0:T(8,128)(2,1)}, u32[]{:S(2)}, u32[]{:S(2)}) collective-permute-start(bf16[6,48,2048]{2,1,0:T(8,128)(2,1)} %get-tuple-element.1219), channel_id=1, source_target_pairs={{0,4},{4,0},{8,12},{12,8},{16,20},{20,16},{24,28},{28,24},{1,5},{5... | collective-permute-start | bytes 3538952 | tf_op jit(solution)/shard_map/ppermute | solution.py:438
  310.0 61.6 %collective-permute-start.51 = (bf16[6,48,2048]{2,1,0:T(8,128)(2,1)}, bf16[6,48,2048]{2,1,0:T(8,128)(2,1)}, u32[]{:S(2)}, u32[]{:S(2)}) collective-permute-start(bf16[6,48,2048]{2,1,0:T(8,128)(2,1)} %get-tuple-element.1220), channel_id=1, source_target_pairs={{0,8},{4,12},{8,0},{12,4},{16,24},{20,28},{24,16},{28,20},{1,9},{5... | collective-permute-start | bytes 3538952 | tf_op jit(solution)/shard_map/ppermute | solution.py:438
  340.2 42.4 %collective-permute-start.52 = (bf16[3,48,2048]{2,1,0:T(8,128)(2,1)}, bf16[3,48,2048]{2,1,0:T(8,128)(2,1)}, u32[]{:S(2)}, u32[]{:S(2)}) collective-permute-start(bf16[3,48,2048]{2,1,0:T(8,128)(2,1)} %get-tuple-element.1236), channel_id=1, source_target_pairs={{0,4},{4,0},{8,12},{12,8},{16,20},{20,16},{24,28},{28,24},{1,5},{5... | collective-permute-start | bytes 1769480 | tf_op jit(solution)/shard_map/ppermute | solution.py:438
  341.8 40.8 %collective-permute-start.53 = (bf16[3,48,2048]{2,1,0:T(8,128)(2,1)}, bf16[3,48,2048]{2,1,0:T(8,128)(2,1)}, u32[]{:S(2)}, u32[]{:S(2)}) collective-permute-start(bf16[3,48,2048]{2,1,0:T(8,128)(2,1)} %get-tuple-element.1237), channel_id=1, source_target_pairs={{0,8},{4,12},{8,0},{12,4},{16,24},{20,28},{24,16},{28,20},{1,9},{5... | collective-permute-start | bytes 1769480 | tf_op jit(solution)/shard_map/ppermute | solution.py:438
  370.8 35.6 %collective-permute-start.55 = (bf16[2,48,2048]{2,1,0:T(8,128)(2,1)}, bf16[2,48,2048]{2,1,0:T(8,128)(2,1)S(1)}, u32[]{:S(2)}, u32[]{:S(2)}) collective-permute-start(bf16[2,48,2048]{2,1,0:T(8,128)(2,1)} %get-tuple-element.1249), channel_id=1, source_target_pairs={{0,4},{4,0},{8,12},{12,8},{16,20},{20,16},{24,28},{28,24},{1,5},{5... | collective-permute-start | bytes 1179656 | tf_op jit(solution)/shard_map/ppermute | solution.py:438
  371.6 35.5 %collective-permute-start.56 = (bf16[2,48,2048]{2,1,0:T(8,128)(2,1)}, bf16[2,48,2048]{2,1,0:T(8,128)(2,1)S(1)}, u32[]{:S(2)}, u32[]{:S(2)}) collective-permute-start(bf16[2,48,2048]{2,1,0:T(8,128)(2,1)} %copy-done.27), channel_id=1, source_target_pairs={{0,8},{4,12},{8,0},{12,4},{16,24},{20,28},{24,16},{28,20},{1,9},{5... | collective-permute-start | bytes 1179656 | tf_op jit(solution)/shard_map/ppermute | solution.py:438
  385.6 20.8 %collective-permute-start.54 = (bf16[2,48,2048]{2,1,0:T(8,128)(2,1)}, bf16[2,48,2048]{2,1,0:T(8,128)(2,1)S(1)}, u32[]{:S(2)}, u32[]{:S(2)}) collective-permute-start(bf16[2,48,2048]{2,1,0:T(8,128)(2,1)} %get-tuple-element.1246), channel_id=1, source_target_pairs={{0,4},{4,0},{8,12},{12,8},{16,20},{20,16},{24,28},{28,24},{1,5},{5... | collective-permute-start | bytes 1179656 | tf_op jit(solution)/shard_map/ppermute | solution.py:438
  391.4 36.0 %collective-permute-start.58 = (bf16[4,4,64,512]{3,2,1,0:T(8,128)(2,1)S(1)}, bf16[4,4,64,512]{3,2,1,0:T(8,128)(2,1)S(1)}, u32[]{:S(2)}, u32[]{:S(2)}) collective-permute-start(bf16[4,4,64,512]{3,2,1,0:T(8,128)(2,1)S(1)} %dynamic-slice_bitcast_fusion.2.refs_1_), channel_id=1, source_target_pairs={{0,4},{4,0},{8,12},{12,8},{16,20},{20,16},{24,28},{28,24},{1,5},{5... | collective-permute-start | bytes 3145736 | tf_op jit(solution)/shard_map/ppermute | solution.py:438
  416.0 25.1 %collective-permute-start.59 = (bf16[2,2,64,2048]{3,2,1,0:T(8,128)(2,1)S(1)}, bf16[2,2,64,2048]{3,2,1,0:T(8,128)(2,1)S(1)}, u32[]{:S(2)}, u32[]{:S(2)}) collective-permute-start(bf16[2,2,64,2048]{3,2,1,0:T(8,128)(2,1)S(1)} %bitcast.260), channel_id=1, source_target_pairs={{0,8},{4,12},{24,16},{28,20},{1,9},{5,13},{25,17},{29,21},{2,10},{... | collective-permute-start | bytes 3145736 | tf_op jit(solution)/shard_map/ppermute | solution.py:438
  438.0 46.5 %collective-permute-start.64 = (bf16[4,64,2048]{2,1,0:T(8,128)(2,1)}, bf16[4,64,2048]{2,1,0:T(8,128)(2,1)S(1)}, u32[]{:S(2)}, u32[]{:S(2)}) collective-permute-start(bf16[4,64,2048]{2,1,0:T(8,128)(2,1)} %dynamic-slice_bitcast_fusion.1), channel_id=1, source_target_pairs={{0,4},{4,0},{8,12},{12,8},{16,20},{20,16},{24,28},{28,24},{1,5},{5... | collective-permute-start | bytes 3145736 | tf_op jit(solution)/shard_map/ppermute | solution.py:438
  440.0 50.0 %collective-permute-start.65 = (bf16[4,64,2048]{2,1,0:T(8,128)(2,1)}, bf16[4,64,2048]{2,1,0:T(8,128)(2,1)S(1)}, u32[]{:S(2)}, u32[]{:S(2)}) collective-permute-start(bf16[4,64,2048]{2,1,0:T(8,128)(2,1)} %dynamic-slice_bitcast_fusion), channel_id=1, source_target_pairs={{0,4},{4,0},{8,12},{12,8},{16,20},{20,16},{24,28},{28,24},{1,5},{5... | collective-permute-start | bytes 3145736 | tf_op jit(solution)/shard_map/ppermute | solution.py:438
  443.2 24.6 %collective-permute-start.78 = (bf16[4,64,512]{2,1,0:T(8,128)(2,1)S(1)}, bf16[4,64,512]{2,1,0:T(8,128)(2,1)S(1)}, u32[]{:S(2)}, u32[]{:S(2)}) collective-permute-start(bf16[4,64,512]{2,1,0:T(8,128)(2,1)S(1)} %dynamic-slice_bitcast_fusion.11), channel_id=1, source_target_pairs={{0,8},{4,12},{24,16},{28,20},{1,9},{5,13},{25,17},{29,21},{2,10},{... | collective-permute-start | bytes 786440 | tf_op jit(solution)/shard_map/ppermute | solution.py:438
  463.4 70.4 %collective-permute-start.60 = (bf16[2,2,64,2048]{3,2,1,0:T(8,128)(2,1)S(1)}, bf16[2,2,64,2048]{3,2,1,0:T(8,128)(2,1)S(1)}, u32[]{:S(2)}, u32[]{:S(2)}) collective-permute-start(bf16[2,2,64,2048]{3,2,1,0:T(8,128)(2,1)S(1)} %get-tuple-element.1287), channel_id=1, source_target_pairs={{0,8},{4,12},{8,16},{12,20},{1,9},{5,13},{9,17},{13,21},{2,10},{6,... | collective-permute-start | bytes 3145736 | tf_op jit(solution)/shard_map/ppermute | solution.py:438
  483.0 69.2 %collective-permute-start.66 = (bf16[2,2,64,2048]{3,2,1,0:T(8,128)(2,1)S(1)}, bf16[2,2,64,2048]{3,2,1,0:T(8,128)(2,1)S(1)}, u32[]{:S(2)}, u32[]{:S(2)}) collective-permute-start(bf16[2,2,64,2048]{3,2,1,0:T(8,128)(2,1)S(1)} %get-tuple-element.1286), channel_id=1, source_target_pairs={{16,8},{20,12},{24,16},{28,20},{17,9},{21,13},{25,17},{29,21},{18,... | collective-permute-start | bytes 3145736 | tf_op jit(solution)/shard_map/ppermute | solution.py:438
  490.0 43.3 %collective-permute-start.82 = (bf16[4,64,512]{2,1,0:T(8,128)(2,1)S(1)}, bf16[4,64,512]{2,1,0:T(8,128)(2,1)S(1)}, u32[]{:S(2)}, u32[]{:S(2)}) collective-permute-start(bf16[4,64,512]{2,1,0:T(8,128)(2,1)S(1)} %get-tuple-element.1297), channel_id=1, source_target_pairs={{8,0},{12,4},{16,8},{20,12},{24,16},{28,20},{9,1},{13,5},{17,9},{2... | collective-permute-start | bytes 786440 | tf_op jit(solution)/shard_map/ppermute | solution.py:438
  493.5 80.2 %collective-permute-start.70 = (bf16[2,2,64,2048]{3,2,0,1:T(8,128)(2,1)}, bf16[2,2,64,2048]{3,2,0,1:T(8,128)(2,1)}, u32[]{:S(2)}, u32[]{:S(2)}) collective-permute-start(bf16[2,2,64,2048]{3,2,0,1:T(8,128)(2,1)} %fusion.26), channel_id=1, source_target_pairs={{0,16},{4,20},{8,24},{12,28},{16,0},{20,4},{24,8},{28,12},{1,17},{... | collective-permute-start | bytes 3145736 | tf_op jit(solution)/shard_map/ppermute | solution.py:438
  551.6 25.0 %collective-permute-start.61 = (bf16[20,48,512]{2,1,0:T(8,128)(2,1)S(1)}, bf16[20,48,512]{2,1,0:T(8,128)(2,1)}, u32[]{:S(2)}, u32[]{:S(2)}) collective-permute-start(bf16[20,48,512]{2,1,0:T(8,128)(2,1)S(1)} %get-tuple-element.1273), channel_id=1, source_target_pairs={{0,1},{1,0},{2,3},{3,2},{4,5},{5,4},{6,7},{7,6},{8,9},{9,8},{10,11... | collective-permute-start | bytes 2949128 | tf_op jit(solution)/shard_map/ppermute | solution.py:368
  559.1 28.0 %collective-permute-start.67 = (bf16[2,2,64,2048]{3,2,1,0:T(8,128)(2,1)}, bf16[2,2,64,2048]{3,2,1,0:T(8,128)(2,1)S(1)}, u32[]{:S(2)}, u32[]{:S(2)}) collective-permute-start(bf16[2,2,64,2048]{3,2,1,0:T(8,128)(2,1)} %get-tuple-element.1285), channel_id=1, source_target_pairs={{0,8},{4,12},{8,16},{12,20},{16,24},{20,28},{1,9},{5,13},{9,17},{1... | collective-permute-start | bytes 3145736 | tf_op jit(solution)/shard_map/ppermute | solution.py:438
  562.0 27.4 %collective-permute-start.68 = (bf16[2,2,64,2048]{3,2,1,0:T(8,128)(2,1)}, bf16[2,2,64,2048]{3,2,1,0:T(8,128)(2,1)S(1)}, u32[]{:S(2)}, u32[]{:S(2)}) collective-permute-start(bf16[2,2,64,2048]{3,2,1,0:T(8,128)(2,1)} %get-tuple-element.1284), channel_id=1, source_target_pairs={{8,0},{12,4},{16,8},{20,12},{24,16},{28,20},{9,1},{13,5},{17,9},{2... | collective-permute-start | bytes 3145736 | tf_op jit(solution)/shard_map/ppermute | solution.py:438
  576.6 22.7 %collective-permute-start.72 = (bf16[2,64,2048]{2,1,0:T(8,128)(2,1)S(1)}, bf16[2,64,2048]{2,1,0:T(8,128)(2,1)}, u32[]{:S(2)}, u32[]{:S(2)}) collective-permute-start(bf16[2,64,2048]{2,1,0:T(8,128)(2,1)S(1)} %get-tuple-element.1298), channel_id=1, source_target_pairs={{0,8},{4,12},{8,0},{12,4},{16,24},{20,28},{24,16},{28,20},{1,9},{5... | collective-permute-start | bytes 1572872 | tf_op jit(solution)/shard_map/ppermute | solution.py:438
  576.6 29.2 %collective-permute-start.71 = (bf16[2,64,2048]{2,1,0:T(8,128)(2,1)}, bf16[2,64,2048]{2,1,0:T(8,128)(2,1)}, u32[]{:S(2)}, u32[]{:S(2)}) collective-permute-start(bf16[2,64,2048]{2,1,0:T(8,128)(2,1)} %get-tuple-element.1299), channel_id=1, source_target_pairs={{0,1},{1,0},{2,3},{3,2},{4,5},{5,4},{6,7},{7,6},{8,9},{9,8},{10,11... | collective-permute-start | bytes 1572872 | tf_op jit(solution)/shard_map/ppermute | solution.py:778
  (195 other events, 1516.9 us)

commit v7 on v6

--- a/solution.py
+++ b/solution.py
@@ -117,6 +117,71 @@
         compiler_params=params(1),
         name="after",
     )(*tokens, *arrays)
+
+
+def gather_kernel(lows, *refs):
+    (feat_ref, prev_ref, feat_too, prev_too, kept_ref), refs = refs[:5], refs[5:]
+    groups, (left_ref, right_ref, sems) = refs[:-3], refs[-3:]
+    steps, _, depth = feat_ref.shape
+    jobs = [
+        (feat_ref, left_ref.at[:steps, :, :depth]),
+        (prev_ref, left_ref.at[:steps, :, depth:]),
+        (feat_too, left_ref.at[steps:, :, :depth]),
+        (prev_too, left_ref.at[steps:, :, depth:]),
+        (kept_ref, right_ref.at[:steps]),
+    ]
+    jobs += [(x, right_ref.at[steps + low : steps + low + x.shape[0]]) for x, low in zip(groups, lows)]
+    copies = [pltpu.make_async_copy(a, b, sems.at[i]) for i, (a, b) in enumerate(jobs)]
+    for copy in copies:
+        copy.start()
+    for copy in copies:
+        copy.wait()
+
+
+def late_kernel(lows, begin_ref, left_ref, right_in, *refs):
+    groups, (right_ref, first_ref, sems) = refs[:-3], refs[-3:]
+    steps = left_ref.shape[0] // 2
+    copies = [
+        pltpu.make_async_copy(x, right_ref.at[steps + low : steps + low + x.shape[0]], sems.at[i])
+        for i, (x, low) in enumerate(zip(groups, lows))
+    ]
+    for copy in copies:
+        copy.start()
+    for copy in copies:
+        copy.wait()
+    if first_ref.shape[1] % 128:
+        return
+    share, depth = first_ref.shape[1], left_ref.shape[2] // 2
+    rows = left_ref.shape[0] * left_ref.shape[1]
+    left = [
+        left_ref[:, :, pl.ds(pl.multiple_of(i * depth + begin_ref[0] * share, 128), share)].reshape(rows, share)
+        for i in range(2)
+    ]
+    left = jnp.concatenate([x.T for x in left], axis=0)
+    width = right_ref.shape[2] // 4
+
+    def columns(i, _):
+        cols = pl.ds(pl.multiple_of(i * width, width), width)
+        total = dot(left, right_ref[:, :, cols].reshape(rows, width)).astype(BF16)
+        first_ref[0, :, cols] = total[:share]
+        first_ref[1, :, cols] = total[share:]
+        return 0
+
+    lax.fori_loop(0, 4, columns, 0)
+
+
+def product_kernel(left_ref, right_ref, out_ref):
+    rows, depth = left_ref.shape[0] * left_ref.shape[1], left_ref.shape[2] // 2
+    width = right_ref.shape[2] // 4
+    for which in range(2):
+        left = left_ref[:, :, which * depth : (which + 1) * depth].reshape(rows, depth).T
+
+        def columns(i, _):
+            cols = pl.ds(pl.multiple_of(i * width, width), width)
+            out_ref[which, :, cols] = dot(left, right_ref[:, :, cols].reshape(rows, width)).astype(BF16)
+            return 0
+
+        lax.fori_loop(0, 4, columns, 0)
 
 
 def assemble_kernel(place_ref, near_a, near_b, far_a, far_b, in_ref, rec_ref):
@@ -228,9 +293,9 @@
 
 
 def backward_kernel(
-    step_ref, p_ref, q_ref, keep_ref, grad_ref, wa_ref, wb_ref, pa_ref, pb_ref,
+    step_ref, p_ref, q_ref, keep_ref, grad_ref, bias_ref, wa_ref, wb_ref, pa_ref, pb_ref,
     gates_ref, cell_ref, prev_ref, slope_ref, up_ref, start_ref,
-    part_ref, next_ref, raw_ref, dz_ref,
+    part_ref, next_ref, sum_ref, raw_ref, dz_ref,
 ):
     step = step_ref[0]
     keep = keep_ref[step_ref[1]][:, :1]
@@ -259,7 +324,10 @@
         )
         for gate in range(4):
             low = pre_grads[gate].astype(BF16)
-            dz_ref[piece, :, gate * width : (gate + 1) * width] = low
+            place = slice(gate * width, (gate + 1) * width)
+            dz_ref[piece, :, place] = low
+            rows = pre_grads[gate].reshape(-1, 8, width)
+            sum_ref[piece, :, place] = bias_ref[piece, :, place] + jnp.sum(rows, axis=0)
             part = part + dot(low, w_ref[gate, cols, :])
     part_ref[...] = (part * keep).astype(BF16)
 
@@ -452,6 +520,7 @@
     rec_bv, proj_av, proj_bv, start_hv, start_cv = place(rec_b, proj_a, proj_b, start_h, start_c)
 
     gates_shape, cell_shape = (PIECES, streams, 4 * width), (PIECES, streams, width)
+    bias_shape = (PIECES, 8, 4 * width)
     inflow = pl.pallas_call(
         inflow_kernel,
         out_shape=vmem(gates_shape, F32),
@@ -560,21 +629,22 @@
         name="turned",
     )(*(in_hbm(x) for x in (rec_a, rec_b, proj_a, proj_b)))
 
-    def backward_call(step, part, peer, grad, saved):
+    def backward_call(step, part, peer, grad, bias, saved):
         return pl.pallas_call(
             backward_kernel,
             out_shape=(
                 vmem((streams, depth), BF16),
                 vmem(cell_shape, F32),
+                vmem(bias_shape, F32),
                 vmem((streams, depth), BF16),
                 vmem(gates_shape, BF16),
             ),
-            in_specs=[SMEM] + [VMEM] * 14,
-            out_specs=[VMEM] * 4,
+            in_specs=[SMEM] + [VMEM] * 15,
+            out_specs=[VMEM] * 5,
             compiler_params=params(8),
             name="backward_step",
         )(
-            at_step(step), pinned(part), pinned(peer), pinned(keep_v), pinned(grad),
+            at_step(step), pinned(part), pinned(peer), pinned(keep_v), pinned(grad), pinned(bias),
             pinned(rec_atv), pinned(rec_btv), pinned(proj_atv), pinned(proj_btv),
             *(pinned(x) for x in saved), pinned(start_cv),
         )
@@ -613,14 +683,14 @@
         )
         return out[:5], tuple(out[5:9]), tuple(out[9:11]), tuple(out[11:])
 
-    carry = (none, none, jnp.zeros(cell_shape, F32), saved, ())
+    carry = (none, none, jnp.zeros(cell_shape, F32), jnp.zeros(bias_shape, F32), saved, ())
     pending, arrived, ready, top = [(steps - 1 - steps // 3, prev_in)], [], None, steps
     for index, share in enumerate(SHARES):
         slots = top if index == len(SHARES) - 1 else round(share * steps)
         sends = ()
         for step in range(top - 1, top - slots - 1, -1):
-            part, peer, grad, saved, stacks = carry
-            part, grad, raw, dz = backward_call(step, part, peer, grad, saved)
+            part, peer, grad, bias_sum, saved, stacks = carry
+            part, grad, bias_sum, raw, dz = backward_call(step, part, peer, grad, bias_sum, saved)
             peer = lax.ppermute(part, "gate", across)
             if ready is not None:
                 due, sides = ready
@@ -632,12 +702,13 @@
                 step, step - (top - slots), slots, dz, raw, stacks, sends, passing
             )
             arrived += [passed] if passed else []
-            carry = (part, peer, grad, saved, stacks)
+            carry = (part, peer, grad, bias_sum, saved, stacks)
         top -= slots
         ready = (max(top - 1 - (3 * slots + 3) // 4, 0 if slots > 2 else -1), sends)
     pending.append((-1, (swapped(sends[0], near_swap), swapped(sends[1], far_swap))))
     arrived += [arrays for _, arrays in pending]
     dz_all, raw_all, near_all, far_all = carry[-1]
+    bias_sum = carry[3]
     prev_in, exchanged = arrived[0], arrived[1:]
     rows = steps * streams
 
@@ -673,16 +744,6 @@
     line = n_batch // 2
     share_rows = depth // n_batch
 
-    def product(left, right):
-        count = left.shape[0] * left.shape[1]
-        return lax.dot_general(
-            left.reshape(count, -1), right.reshape(count, -1), (((0,), (0,)), ((), ())), preferred_element_type=F32
-        )
-
-    def both(feat, prev):
-        return jnp.concatenate([feat, prev], axis=2)
-
-    left = both(feat_all, prev_all)
     def input_grad_of(dz):
         return pl.pallas_call(
             input_grad_kernel,
@@ -703,79 +764,115 @@
                 scratch_shapes=[pltpu.VMEM((rows, depth), F32)],
             ),
             compiler_params=params(16),
-            cost_estimate=cost(2 * rows * depth * 8 * cells, 8 * depth * cells * 4),
+            cost_estimate=cost(0, 0),
             name="input_grad",
         )(turn, dz, in_hbm(win_a), in_hbm(win_b))
 
     grad_proj = jnp.einsum("ptnc,tnk->pkc", mixed_all, raw_all, preferred_element_type=F32).astype(BF16)
     grad_proj = grad_proj.reshape(PIECES, line, 2, share_rows, width)
-    proj_mine = lax.dynamic_index_in_dim(grad_proj, low, 2, keepdims=False)
-    proj_send = lax.dynamic_index_in_dim(grad_proj, 1 - low, 2, keepdims=False)
-    proj_taken = swapped(proj_send, near_swap)
-
-    def early_sum(kept, theirs, parts):
-        taken = jnp.concatenate(parts[:-LATE][::-1], axis=0)
-        return product(left, kept) + product(theirs[steps - taken.shape[0] :], taken)
-
-    def rows_first(total):
-        return total.astype(BF16).reshape(2, line, 2, share_rows, 4 * width)
-
+    own_cells = cells // n_batch
+    bias_rows = jnp.sum(bias_sum, axis=1).reshape(QUARTERS, HALVES, 4, width)
+    bias_rows = jnp.transpose(bias_rows, (0, 2, 1, 3)).reshape(QUARTERS, 4, line, 2, own_cells)
+    bias_rows = jnp.transpose(bias_rows, (2, 3, 0, 1, 4)).reshape(line, 2, -1)
+    bias_rows = jnp.pad(bias_rows, ((0, 0), (0, 0), (0, PIECES * width - bias_rows.shape[2])))
+    bias_rows = jnp.transpose(bias_rows.reshape(line, 2, PIECES, 1, width), (2, 0, 1, 3, 4)).astype(BF16)
+    grad_proj = jnp.concatenate([grad_proj, bias_rows], axis=3)
+
+    def with_partner(grad):
+        mine = lax.dynamic_index_in_dim(grad, low, grad.ndim - 3, keepdims=False)
+        sent = lax.dynamic_index_in_dim(grad, 1 - low, grad.ndim - 3, keepdims=False)
+        taken = swapped(sent, near_swap)
+        return sent, taken, (mine.astype(F32) + taken.astype(F32)).astype(BF16)
+
+    def across_two(grad):
+        return line_sum(grad.reshape(grad.shape[:-3] + (line // 2, 2) + grad.shape[-2:]), grad.ndim - 3, 4, line // 2)
+
+    proj_sent, proj_taken, proj_y = with_partner(grad_proj)
+
+    lows, count = [], 0
+    for x in exchanged[::-1]:
+        lows.insert(0, count)
+        count += x[0].shape[0]
+
+    def gathered(kept, feat, prev, parts):
+        return pl.pallas_call(
+            functools.partial(gather_kernel, tuple(lows[: len(parts)])),
+            out_shape=(vmem((2 * steps, streams, 2 * depth), BF16), vmem((2 * steps, streams, 4 * width), BF16)),
+            in_specs=[ANY] * (5 + len(parts)),
+            out_specs=[VMEM] * 2,
+            scratch_shapes=[pltpu.SemaphoreType.DMA((5 + len(parts),))],
+            compiler_params=params(1),
+            cost_estimate=cost(0, 0),
+            name="gather",
+        )(*(in_hbm(x) for x in (feat_all, prev_all, feat, prev, kept, *parts)))
+
+    def completed(begin, rows_out, left, right, parts):
+        return pl.pallas_call(
+            functools.partial(late_kernel, tuple(lows[len(lows) - len(parts) :])),
+            out_shape=(vmem(right.shape, BF16), jax.ShapeDtypeStruct((2, max(rows_out, 8), 4 * width), BF16)),
+            in_specs=[SMEM] + [VMEM] * 2 + [ANY] * len(parts),
+            out_specs=[VMEM] * 2,
+            scratch_shapes=[pltpu.SemaphoreType.DMA((len(parts),))],
+            input_output_aliases={2: 0},
+            compiler_params=params(16),
+            cost_estimate=cost(0, 0),
+            name="late",
+        )(begin, pinned(left), pinned(right), *(in_hbm(x) for x in parts))
+
+    def multiplied(left, right):
+        return pl.pallas_call(
+            product_kernel,
+            out_shape=jax.ShapeDtypeStruct((2, depth, 4 * width), BF16),
+            in_specs=[VMEM] * 2,
+            out_specs=VMEM,
+            compiler_params=params(16),
+            cost_estimate=cost(0, 0),
+            name="product",
+        )(pinned(left), pinned(right))
+
+    near_parts, far_parts = zip(*exchanged)
     begin = jnp.where(spot // 2 == 0, line - 1, 0)
-
-    def line_chunk(array, axis):
-        shape = array.shape[:axis] + (2, line, 2 * share_rows) + array.shape[axis + 1 :]
-        return lax.dynamic_index_in_dim(array.reshape(shape), begin, axis + 1, keepdims=False)
-
-    near_parts, far_parts = zip(*exchanged)
-    near_left, far_left = (both(feat, prev) for feat, prev in zip(feat_in, prev_in))
-    late_steps = sum(x.shape[0] for x in near_parts[-LATE:])
-    near_early = early_sum(near_all, near_left, near_parts)
-    near_late = jnp.concatenate(after((near_early, proj_send), *near_parts[-LATE:][::-1]), axis=0)
-    first = line_chunk(near_early, 0).reshape(4 * share_rows, -1)
-    first = (first + product(line_chunk(near_left[:late_steps], 2), near_late)).astype(BF16)
-    (near_late,) = after((first,), near_late)
-    near = rows_first(near_early + product(near_left[:late_steps], near_late))
-
+    chunk_rows = 2 * share_rows if 2 * share_rows % 128 == 0 else 0
+    near_left, near_right = gathered(near_all, feat_in[0], prev_in[0], near_parts[:-LATE])
+    near_late = after((near_left, proj_sent), *near_parts[-LATE:])
+    near_right, first = completed(jnp.full((1,), begin, jnp.int32), chunk_rows, near_left, near_right, near_late)
     far_all, *far_parts = after((first,), far_all, *far_parts)
-    far_early = early_sum(far_all, far_left, far_parts)
-    far_late = jnp.concatenate(after((near, proj_taken), *far_parts[-LATE:][::-1]), axis=0)
-    far = rows_first(far_early + product(far_left[:late_steps], far_late))
-
-    def with_partner(grad):
-        mine = lax.dynamic_index_in_dim(grad, low, 1, keepdims=False)
-        taken = swapped(lax.dynamic_index_in_dim(grad, 1 - low, 1, keepdims=False), near_swap)
-        return taken, (mine.astype(F32) + taken.astype(F32)).astype(BF16)
-
-    (in_taken, far_in), (rec_taken, far_rec) = (with_partner(far[i]) for i in range(2))
+    far_left, far_right = gathered(far_all, feat_in[1], prev_in[1], far_parts[:-LATE])
+    far_right, _ = completed(jnp.zeros((1,), jnp.int32), 0, far_left, far_right, far_parts[-LATE:])
+    far = multiplied(far_left, far_right).reshape(2, line, 2, share_rows, 4 * width)
+    near = multiplied(near_left, near_right).reshape(2, line, 2, share_rows, 4 * width)
+    (_, in_taken, far_in), (_, rec_taken, far_rec) = (with_partner(far[i]) for i in range(2))
+    proj_two = across_two(proj_y)
+    in_two, rec_two = across_two(far_in), across_two(far_rec)
 
     tokens = {}
 
     def second(up, down):
-        up, down = after((far,), up, down)
-        tokens["dz"], tokens["proj"] = after((up,), dz_all, proj_taken)
-        return up, down
+        (tokens["dz"],) = after((up,), dz_all)
+        return after((far, proj_taken), up, down)
 
     def third(up, down):
         tokens["dx"] = input_grad_of(tokens["dz"])
-        tokens["hidden"], tokens["cell"], dz = after((up, tokens["dx"]), hidden_all, cell, tokens["dz"])
-        tokens["bias"] = jnp.sum(dz, axis=(1, 2), dtype=F32)
-        return after((in_taken, tokens["dx"]), up, down)
+        tokens["hidden"], tokens["cell"] = after((up, tokens["dx"]), hidden_all, cell)
+        return after((in_taken, proj_two, tokens["dx"]), up, down)
 
     def final(up, down):
-        return after((rec_taken, tokens["bias"]), up, down)
+        return after((rec_taken, in_two), up, down)
 
     gates = {2: second, 3: third, line: final} if line > 3 else {}
-    near = line_sum(near, 1, 2, line, first.reshape(2, 2, share_rows, 4 * width), gates)
-    far = jnp.stack([far_in, far_rec]).reshape(2, line // 2, 2, share_rows, 4 * width)
-    far = line_sum(far, 1, 4, line // 2)
-    dx_all, hidden_all, cell, grad_bias = (tokens[x] for x in ("dx", "hidden", "cell", "bias"))
+    first = first.reshape(2, 2, share_rows, 4 * width) if chunk_rows else None
+    near = line_sum(near, 1, 2, line, first, gates)
+    dx_all, hidden_all, cell = (tokens[x] for x in ("dx", "hidden", "cell"))
 
     def halves_of(summed, index, pairs):
         mine = lax.dynamic_index_in_dim(summed, index, 1, keepdims=False)
         return mine, swapped(lax.dynamic_index_in_dim(summed, 1 - index, 1, keepdims=False), pairs)
 
     near_pair = halves_of(near, low, near_swap)
-    far_pair = [lax.ppermute(x, "gate", swap) for x in halves_of(far, high, far_swap)]
+    far_pair = halves_of(jnp.stack([in_two, rec_two]), high, far_swap)
+    far_pair = [lax.ppermute(x, "gate", swap) for x in far_pair]
+    proj_mine, proj_theirs = halves_of(proj_two, high, far_swap)
+    grad_proj = proj_mine.astype(F32) + proj_theirs.astype(F32)
     grad_shape = (2, share_rows, 4, cells)
     grad_w_in, grad_w_rec = pl.pallas_call(
         assemble_kernel,
@@ -786,21 +883,13 @@
         name="assemble",
     )(jnp.stack([own, low, high]), *near_pair, *far_pair)
 
-    grad_proj = line_sum((proj_mine.astype(F32) + tokens["proj"].astype(F32)).astype(BF16), 1, 2, line)
-    stride = 1
-    while stride < n_batch:
-        grad_bias = grad_bias + swapped(grad_bias, [(i, i ^ stride) for i in range(n_batch)])
-        stride *= 2
-
     def home(mine, theirs):
         return by_direction(*trade(mine, theirs)).astype(F32)
 
-    shaped = jnp.transpose(grad_bias.reshape(QUARTERS, HALVES, 4, width), (0, 2, 1, 3)).reshape(QUARTERS, 4, cells)
-    own_cells = cells // n_batch
-    shaped = lax.dynamic_slice_in_dim(shaped, spot * own_cells, own_cells, 2)
+    shaped = grad_proj[:, share_rows].reshape(-1)[: QUARTERS * 4 * own_cells].reshape(QUARTERS, 4, own_cells)
     grad_bias = home(shaped[0], shaped[1])
-    grad_proj = jnp.transpose(grad_proj.reshape(QUARTERS, HALVES, share_rows, width), (0, 1, 3, 2))
-    grad_proj = grad_proj.reshape(QUARTERS, cells, share_rows)
+    grad_proj = grad_proj[:, :share_rows].reshape(QUARTERS, HALVES, share_rows, width)
+    grad_proj = jnp.transpose(grad_proj, (0, 1, 3, 2)).reshape(QUARTERS, cells, share_rows).astype(BF16)
     grad_proj = home(grad_proj[0], grad_proj[1])
 
     both_hidden = trade(hidden_all, hidden_all)

time: 622 us -> 579 us (0.931)
  matrix products: 43.1 us -> 3.57 us
  Pallas kernels: 297 us -> 335 us
  waiting for transfers between devices: 83.2 us -> 61.1 us
  local copies, waits for them, and re-layouts: 60.5 us -> 48.9 us
    dot_general x7 -> x0, matrix products: 39.3 us -> none  [product(): lax.dot_general(left.reshape(count, -1), right.reshape(count, -1), (((0,)...]
    pallas_call x0 -> x6, Pallas kernels: none -> 37.4 us  [the longest x2 22.8 us: multiplied(): pl.pallas_call(product_kernel, out_shape=jax.ShapeDtypeStruct((2, depth,...]
    ppermute x33 -> x28, waiting for transfers between devices: 78.2 us -> 47.8 us  [swapped(): return lax.ppermute(array, 'batch', pairs)]
    unnamed x296 -> x276, local copies, waits for them, and re-layouts: 29.1 us -> 23.3 us
    ppermute x33 -> x28, starting transfers between devices: 47.5 us -> 45.3 us  [swapped(): return lax.ppermute(array, 'batch', pairs)]
  transfers between devices with their start and end apart: 85 -> 80, of which waited for: 34 -> 41; matrix products, arithmetic and copies ran while one was open for 18% -> 10% of each run, Pallas kernels for 43% -> 53%
where the time goes in v7:
time: 579 us; the launch traced here: 568 us
  Pallas kernels  335 us (58%)
  starting transfers between devices  89.7 us (15%)
  waiting for transfers between devices  61.1 us (11%)
  local copies, waits for them, and re-layouts  48.9 us (8%)
  other arithmetic  25.7 us (4%)
    pallas_call x20, Pallas kernels, backward_call(): pl.pallas_call(backward_kernel, out_shape=(vmem((streams, depth), BF16),...  62.7 us
    pallas_call x20, Pallas kernels, between_call(): pl.pallas_call(functools.partial(between_kernel, not stacks, step == step...  59.6 us
    pallas_call x20, Pallas kernels, forward_call(): pl.pallas_call(functools.partial(forward_kernel, first), out_shape=(vmem(...  56.9 us
    pallas_call x20, Pallas kernels, aside_call(): pl.pallas_call(functools.partial(aside_kernel, not stacks, step == 0, not...  56.2 us
    ppermute x28, waiting for transfers between devices, swapped(): return lax.ppermute(array, 'batch', pairs)  47.8 us
    ppermute x28, starting transfers between devices, swapped(): return lax.ppermute(array, 'batch', pairs)  45.3 us
    ppermute x39, starting transfers between devices, body(): peer = lax.ppermute(part, 'gate', across)  40.9 us
    unnamed x276, local copies, waits for them, and re-layouts  23.3 us
  transfers between devices with their start and end apart: 80, of which 41 were waited for; matrix products, arithmetic and copies ran while one was open for 10% of the time, Pallas kernels for 53%

profile of v7, /device:TPU:8, one launch (start us, length us, event | category | flops | bytes accessed | tf_op | source)
XLA Modules:
  0.0 567.9 jit_solution(7284032712997593210)
XLA Ops:
  0.7 5.2 layout.4
  6.0 5.2 layout.6
  18.6 5.2 layout.5
  25.8 5.2 layout.7
  33.7 3.6 order.1
  138.3 3.2 forward_step.32
  149.6 3.2 between.33
  198.5 6.0 %turned.1 = (bf16[4,1024,512]{2,1,0:T(8,128)(2,1)S(1)}, bf16[4,1024,512]{2,1,0:T(8,128)(2,1)S(1)}, bf16[512,1024]{1,0:T(8,128)(2,1)S(1)}, bf16[512,1024]{1,0:T(8,128)(2,1)S(1)}) custom-call(bf16[4,512,1024]{2,1,0:T(8,128)(2,1)} %get-tuple-element.954.wa_ref, bf16[4,512,1024]{2,1,0:T(8,128)(2,1)} %collective-permute-done.2.refs_0_.wb_ref, ...), custom_call_target="tpu_custom_call" | custom-call | tf_op jit(solution)/shard_map/turned/pallas_call | solution.py:617
  204.6 3.5 finish.1
  208.2 3.3 backward_step.20
  251.9 3.5 backward_step.26
  364.2 3.6 backward_step.39
  376.9 3.6 bitcast_convert_fusion
  382.7 4.2 gather.14
  387.7 4.5 late.2
  395.2 4.2 gather.15
  401.2 11.2 %product.3 = bf16[2,512,2048]{2,1,0:T(8,128)(2,1)S(1)} custom-call(bf16[40,48,1024]{2,1,0:T(8,128)(2,1)S(1)} %get-tuple-element.1310.left_ref, bf16[40,48,2048]{2,1,0:T(8,128)(2,1)S(1)} %get-tuple-element.1314.right_ref), custom_call_target="tpu_custom_call" | custom-call | tf_op jit(solution)/shard_map/product/pallas_call | solution.py:823
  418.1 11.7 %product.2 = bf16[2,512,2048]{2,1,0:T(8,128)(2,1)S(1)} custom-call(bf16[40,48,1024]{2,1,0:T(8,128)(2,1)S(1)} %get-tuple-element.1285.refs_0_.left_ref, bf16[40,48,2048]{2,1,0:T(8,128)(2,1)S(1)} %get-tuple-element.1296.right_ref), custom_call_target="tpu_custom_call" | custom-call | tf_op jit(solution)/shard_map/product/pallas_call | solution.py:823
  434.0 4.8 collective-permute-start.67
  441.3 4.6 collective-permute-start.60
  448.1 13.2 %collective-permute-done.67 = bf16[4,2,65,512]{3,0,2,1:T(4,128)(2,1)S(1)} collective-permute-done((bf16[4,2,65,512]{3,0,2,1:T(4,128)(2,1)S(1)}, bf16[4,2,65,512]{3,0,2,1:T(4,128)(2,1)S(1)}, u32[]{:S(2)}, u32[]{:S(2)}) %collective-permute-start.67) | collective-permute-done | bytes 532512 | tf_op jit(solution)/shard_map/ppermute | solution.py:506
  461.5 9.4 %collective-permute-start.76 = (bf16[4,65,512]{2,1,0:T(8,128)(2,1)S(1)}, bf16[4,65,512]{2,1,0:T(8,128)(2,1)S(1)}, u32[]{:S(2)}, u32[]{:S(2)}) collective-permute-start(bf16[4,65,512]{2,1,0:T(8,128)(2,1)S(1)} %dynamic-slice_bitcast_fusion.11), channel_id=1, source_target_pairs={{0,8},{4,12},{8,0},{12,4},{16,24},{20,28},{24,16},{28,20},{1,9},{5... | collective-permute-start | bytes 798728 | tf_op jit(solution)/shard_map/ppermute | solution.py:506
  471.0 16.9 %input_grad.1.refs_1_.refs_2_ = f32[20,48,512]{2,1,0:T(8,128)S(1)} custom-call(s32[2]{0:T(128)S(1)} %copy-done.70, bf16[4,20,48,2048]{3,2,1,0:T(8,128)(2,1)S(1)} %after.18.dz_ref, bf16[4,512,1024]{2,1,0:T(8,128)(2,1)} %get-tuple-element.1317.wa_ref, bf16[4,512,1024]{2,1,0:T(8,128)(2,1)} %collective-permute-done.1.refs_2_.wb_ref), custom_call_target="tpu_custom_call" | custom-call | tf_op jit(solution)/shard_map/input_grad/pallas_call | solution.py:748
  492.3 4.6 collective-permute-done.62
  498.4 4.3 collective-permute-done.72
  502.9 5.5 collective-permute-done.66
  511.1 6.3 %collective-permute-done.68.refs_4_ = bf16[2,2,64,2048]{3,2,1,0:T(8,128)(2,1)S(1)} collective-permute-done((bf16[2,2,64,2048]{3,2,1,0:T(8,128)(2,1)S(1)}, bf16[2,2,64,2048]{3,2,1,0:T(8,128)(2,1)S(1)}, u32[]{:S(2)}, u32[]{:S(2)}) %collective-permute-start.68) | collective-permute-done | bytes 1048608 | tf_op jit(solution)/shard_map/ppermute | solution.py:506
  519.6 4.1 collective-permute-start.69
  531.9 14.3 %collective-permute-done.69.refs_2_ = bf16[2,2,64,2048]{3,2,1,0:T(8,128)(2,1)S(1)} collective-permute-done((bf16[2,2,64,2048]{3,2,1,0:T(8,128)(2,1)}, bf16[2,2,64,2048]{3,2,1,0:T(8,128)(2,1)S(1)}, u32[]{:S(2)}, u32[]{:S(2)}) %collective-permute-start.69) | collective-permute-done | bytes 1048608 | tf_op jit(solution)/shard_map/ppermute | solution.py:506
  553.7 5.3 scatter_fusion
  559.0 3.5 fusion
  563.7 4.0 assemble.1
  (640 shorter events, 373.6 us)
Async XLA Ops:
  5.9 36.7 %collective-permute-start.1 = (bf16[4,512,1024]{2,1,0:T(8,128)(2,1)}, bf16[4,512,1024]{2,1,0:T(8,128)(2,1)}, u32[]{:S(2)}, u32[]{:S(2)}) collective-permute-start(bf16[4,512,1024]{2,1,0:T(8,128)(2,1)} %layout.4), channel_id=1, source_target_pairs={{0,1},{1,0},{2,3},{3,2},{4,5},{5,4},{6,7},{7,6},{8,9},{9,8},{10,11... | collective-permute-start | bytes 12582920 | tf_op jit(solution)/shard_map/ppermute | solution.py:463
  11.2 38.2 %collective-permute-start.2 = (bf16[4,512,1024]{2,1,0:T(8,128)(2,1)}, bf16[4,512,1024]{2,1,0:T(8,128)(2,1)}, u32[]{:S(2)}, u32[]{:S(2)}) collective-permute-start(bf16[4,512,1024]{2,1,0:T(8,128)(2,1)} %layout.6), channel_id=1, source_target_pairs={{0,1},{1,0},{2,3},{3,2},{4,5},{5,4},{6,7},{7,6},{8,9},{9,8},{10,11... | collective-permute-start | bytes 12582920 | tf_op jit(solution)/shard_map/ppermute | solution.py:463
  11.8 25.6 %collective-permute-start = (bf16[4,1024]{1,0:T(4,128)(2,1)S(1)}, bf16[4,1024]{1,0:T(4,128)(2,1)S(1)}, u32[]{:S(2)}, u32[]{:S(2)}) collective-permute-start(bf16[4,1024]{1,0:T(4,128)(2,1)S(1)} %get-tuple-element.1359), channel_id=1, source_target_pairs={{0,1},{1,0},{2,3},{3,2},{4,5},{5,4},{6,7},{7,6},{8,9},{9,8},{10,11... | collective-permute-start | bytes 24584 | tf_op jit(solution)/shard_map/ppermute | solution.py:436
  14.0 25.6 %collective-permute-start.4 = (f32[48,1024]{1,0:T(8,128)}, f32[48,1024]{1,0:T(8,128)}, u32[]{:S(2)}, u32[]{:S(2)}) collective-permute-start(f32[48,1024]{1,0:T(8,128)} %bitcast.197), channel_id=1, source_target_pairs={{0,1},{1,0},{2,3},{3,2},{4,5},{5,4},{6,7},{7,6},{8,9},{9,8},{10,11... | collective-permute-start | bytes 589832 | tf_op jit(solution)/shard_map/ppermute | solution.py:436
  17.5 31.9 %collective-permute-start.3 = (bf16[1024,512]{1,0:T(8,128)(2,1)}, bf16[1024,512]{1,0:T(8,128)(2,1)}, u32[]{:S(2)}, u32[]{:S(2)}) collective-permute-start(bf16[1024,512]{1,0:T(8,128)(2,1)} %get-tuple-element.1334), channel_id=1, source_target_pairs={{0,1},{1,0},{2,3},{3,2},{4,5},{5,4},{6,7},{7,6},{8,9},{9,8},{10,11... | collective-permute-start | bytes 3145736 | tf_op jit(solution)/shard_map/ppermute | solution.py:436
  37.3 112.2 %collective-permute-start.19 = (bf16[20,48,512]{2,1,0:T(8,128)(2,1)}, bf16[20,48,512]{2,1,0:T(8,128)(2,1)}, u32[]{:S(2)}, u32[]{:S(2)}) collective-permute-start(bf16[20,48,512]{2,1,0:T(8,128)(2,1)} %get-tuple-element.668.refs_0_), channel_id=1, source_target_pairs={{0,4},{4,0},{8,12},{12,8},{16,20},{20,16},{24,28},{28,24},{1,5},{5... | collective-permute-start | bytes 2949128 | tf_op jit(solution)/shard_map/ppermute | solution.py:506
  39.6 110.0 %collective-permute-start.20 = (bf16[20,48,512]{2,1,0:T(8,128)(2,1)}, bf16[20,48,512]{2,1,0:T(8,128)(2,1)}, u32[]{:S(2)}, u32[]{:S(2)}) collective-permute-start(bf16[20,48,512]{2,1,0:T(8,128)(2,1)} %get-tuple-element.668.refs_0_), channel_id=1, source_target_pairs={{0,8},{4,12},{8,0},{12,4},{16,24},{20,28},{24,16},{28,20},{1,9},{5... | collective-permute-start | bytes 2949128 | tf_op jit(solution)/shard_map/ppermute | solution.py:506
  194.2 62.2 %collective-permute-start.33 = (bf16[20,48,512]{2,1,0:T(8,128)(2,1)}, bf16[20,48,512]{2,1,0:T(8,128)(2,1)}, u32[]{:S(2)}, u32[]{:S(2)}) collective-permute-start(bf16[20,48,512]{2,1,0:T(8,128)(2,1)} %get-tuple-element.952.refs_1_), channel_id=1, source_target_pairs={{0,4},{4,0},{8,12},{12,8},{16,20},{20,16},{24,28},{28,24},{1,5},{5... | collective-permute-start | bytes 2949128 | tf_op jit(solution)/shard_map/ppermute | solution.py:506
  194.8 61.7 %collective-permute-start.34 = (bf16[20,48,512]{2,1,0:T(8,128)(2,1)}, bf16[20,48,512]{2,1,0:T(8,128)(2,1)}, u32[]{:S(2)}, u32[]{:S(2)}) collective-permute-start(bf16[20,48,512]{2,1,0:T(8,128)(2,1)} %get-tuple-element.952.refs_1_), channel_id=1, source_target_pairs={{0,8},{4,12},{8,0},{12,4},{16,24},{20,28},{24,16},{28,20},{1,9},{5... | collective-permute-start | bytes 2949128 | tf_op jit(solution)/shard_map/ppermute | solution.py:506
  262.6 49.5 %collective-permute-start.43 = (bf16[7,48,2048]{2,1,0:T(8,128)(2,1)S(1)}, bf16[7,48,2048]{2,1,0:T(8,128)(2,1)S(1)}, u32[]{:S(2)}, u32[]{:S(2)}) collective-permute-start(bf16[7,48,2048]{2,1,0:T(8,128)(2,1)S(1)} %get-tuple-element.1182), channel_id=1, source_target_pairs={{0,4},{4,0},{8,12},{12,8},{16,20},{20,16},{24,28},{28,24},{1,5},{5... | collective-permute-start | bytes 4128776 | tf_op jit(solution)/shard_map/ppermute | solution.py:506
  264.2 47.9 %collective-permute-start.44 = (bf16[7,48,2048]{2,1,0:T(8,128)(2,1)S(1)}, bf16[7,48,2048]{2,1,0:T(8,128)(2,1)S(1)}, u32[]{:S(2)}, u32[]{:S(2)}) collective-permute-start(bf16[7,48,2048]{2,1,0:T(8,128)(2,1)S(1)} %get-tuple-element.1183), channel_id=1, source_target_pairs={{0,8},{4,12},{8,0},{12,4},{16,24},{20,28},{24,16},{28,20},{1,9},{5... | collective-permute-start | bytes 4128776 | tf_op jit(solution)/shard_map/ppermute | solution.py:506
  309.0 47.3 %collective-permute-start.50 = (bf16[6,48,2048]{2,1,0:T(8,128)(2,1)}, bf16[6,48,2048]{2,1,0:T(8,128)(2,1)}, u32[]{:S(2)}, u32[]{:S(2)}) collective-permute-start(bf16[6,48,2048]{2,1,0:T(8,128)(2,1)} %get-tuple-element.1262), channel_id=1, source_target_pairs={{0,4},{4,0},{8,12},{12,8},{16,20},{20,16},{24,28},{28,24},{1,5},{5... | collective-permute-start | bytes 3538952 | tf_op jit(solution)/shard_map/ppermute | solution.py:506
  309.3 47.5 %collective-permute-start.51 = (bf16[6,48,2048]{2,1,0:T(8,128)(2,1)}, bf16[6,48,2048]{2,1,0:T(8,128)(2,1)}, u32[]{:S(2)}, u32[]{:S(2)}) collective-permute-start(bf16[6,48,2048]{2,1,0:T(8,128)(2,1)} %get-tuple-element.1263), channel_id=1, source_target_pairs={{0,8},{4,12},{8,0},{12,4},{16,24},{20,28},{24,16},{28,20},{1,9},{5... | collective-permute-start | bytes 3538952 | tf_op jit(solution)/shard_map/ppermute | solution.py:506
  334.1 36.6 %collective-permute-start.52 = (bf16[3,48,2048]{2,1,0:T(8,128)(2,1)}, bf16[3,48,2048]{2,1,0:T(8,128)(2,1)}, u32[]{:S(2)}, u32[]{:S(2)}) collective-permute-start(bf16[3,48,2048]{2,1,0:T(8,128)(2,1)} %get-tuple-element.1279), channel_id=1, source_target_pairs={{0,4},{4,0},{8,12},{12,8},{16,20},{20,16},{24,28},{28,24},{1,5},{5... | collective-permute-start | bytes 1769480 | tf_op jit(solution)/shard_map/ppermute | solution.py:506
  335.6 35.1 %collective-permute-start.53 = (bf16[3,48,2048]{2,1,0:T(8,128)(2,1)}, bf16[3,48,2048]{2,1,0:T(8,128)(2,1)}, u32[]{:S(2)}, u32[]{:S(2)}) collective-permute-start(bf16[3,48,2048]{2,1,0:T(8,128)(2,1)} %get-tuple-element.1280), channel_id=1, source_target_pairs={{0,8},{4,12},{8,0},{12,4},{16,24},{20,28},{24,16},{28,20},{1,9},{5... | collective-permute-start | bytes 1769480 | tf_op jit(solution)/shard_map/ppermute | solution.py:506
  356.3 30.6 %collective-permute-start.54 = (bf16[2,48,2048]{2,1,0:T(8,128)(2,1)S(1)}, bf16[2,48,2048]{2,1,0:T(8,128)(2,1)}, u32[]{:S(2)}, u32[]{:S(2)}) collective-permute-start(bf16[2,48,2048]{2,1,0:T(8,128)(2,1)S(1)} %get-tuple-element.1292), channel_id=1, source_target_pairs={{0,4},{4,0},{8,12},{12,8},{16,20},{20,16},{24,28},{28,24},{1,5},{5... | collective-permute-start | bytes 1179656 | tf_op jit(solution)/shard_map/ppermute | solution.py:506
  356.8 35.3 %collective-permute-start.56 = (bf16[2,48,2048]{2,1,0:T(8,128)(2,1)}, bf16[2,48,2048]{2,1,0:T(8,128)(2,1)}, u32[]{:S(2)}, u32[]{:S(2)}) collective-permute-start(bf16[2,48,2048]{2,1,0:T(8,128)(2,1)} %copy-done.25), channel_id=1, source_target_pairs={{0,8},{4,12},{8,0},{12,4},{16,24},{20,28},{24,16},{28,20},{1,9},{5... | collective-permute-start | bytes 1179656 | tf_op jit(solution)/shard_map/ppermute | solution.py:506
  382.2 48.2 %collective-permute-start.58 = (bf16[4,4,65,512]{3,1,2,0:T(4,128)(2,1)}, bf16[4,4,65,512]{3,1,2,0:T(4,128)(2,1)}, u32[]{:S(2)}, u32[]{:S(2)}) collective-permute-start(bf16[4,4,65,512]{3,1,2,0:T(4,128)(2,1)} %copy.492), channel_id=1, source_target_pairs={{0,4},{4,0},{8,12},{12,8},{16,20},{20,16},{24,28},{28,24},{1,5},{5... | collective-permute-start | bytes 3194888 | tf_op jit(solution)/shard_map/ppermute | solution.py:506
  412.4 27.9 %collective-permute-start.59 = (bf16[2,2,64,2048]{3,2,1,0:T(8,128)(2,1)S(1)}, bf16[2,2,64,2048]{3,2,1,0:T(8,128)(2,1)S(1)}, u32[]{:S(2)}, u32[]{:S(2)}) collective-permute-start(bf16[2,2,64,2048]{3,2,1,0:T(8,128)(2,1)S(1)} %bitcast.209), channel_id=1, source_target_pairs={{0,8},{4,12},{24,16},{28,20},{1,9},{5,13},{25,17},{29,21},{2,10},{... | collective-permute-start | bytes 3145736 | tf_op jit(solution)/shard_map/ppermute | solution.py:506
  415.4 30.4 %collective-permute-start.64 = (bf16[4,64,2048]{2,1,0:T(8,128)(2,1)}, bf16[4,64,2048]{2,1,0:T(8,128)(2,1)}, u32[]{:S(2)}, u32[]{:S(2)}) collective-permute-start(bf16[4,64,2048]{2,1,0:T(8,128)(2,1)} %dynamic-slice_bitcast_fusion.1), channel_id=1, source_target_pairs={{0,4},{4,0},{8,12},{12,8},{16,20},{20,16},{24,28},{28,24},{1,5},{5... | collective-permute-start | bytes 3145736 | tf_op jit(solution)/shard_map/ppermute | solution.py:506
  434.0 27.2 %collective-permute-start.67 = (bf16[4,2,65,512]{3,0,2,1:T(4,128)(2,1)S(1)}, bf16[4,2,65,512]{3,0,2,1:T(4,128)(2,1)S(1)}, u32[]{:S(2)}, u32[]{:S(2)}) collective-permute-start(bf16[4,2,65,512]{3,0,2,1:T(4,128)(2,1)S(1)} %get-tuple-element.1338), channel_id=1, source_target_pairs={{0,16},{4,20},{8,24},{12,28},{16,0},{20,4},{24,8},{28,12},{1,17},{... | collective-permute-start | bytes 1597448 | tf_op jit(solution)/shard_map/ppermute | solution.py:506
  441.3 69.0 %collective-permute-start.60 = (bf16[2,2,64,2048]{3,2,1,0:T(8,128)(2,1)S(1)}, bf16[2,2,64,2048]{3,2,1,0:T(8,128)(2,1)S(1)}, u32[]{:S(2)}, u32[]{:S(2)}) collective-permute-start(bf16[2,2,64,2048]{3,2,1,0:T(8,128)(2,1)S(1)} %get-tuple-element.1331), channel_id=1, source_target_pairs={{0,8},{4,12},{8,16},{12,20},{1,9},{5,13},{9,17},{13,21},{2,10},{6,... | collective-permute-start | bytes 3145736 | tf_op jit(solution)/shard_map/ppermute | solution.py:506
  447.6 55.2 %collective-permute-start.72 = (bf16[2,64,2048]{2,1,0:T(8,128)(2,1)S(1)}, bf16[2,64,2048]{2,1,0:T(8,128)(2,1)S(1)}, u32[]{:S(2)}, u32[]{:S(2)}) collective-permute-start(bf16[2,64,2048]{2,1,0:T(8,128)(2,1)S(1)} %dynamic-slice_bitcast_fusion.7), channel_id=1, source_target_pairs={{0,16},{4,20},{8,24},{12,28},{16,0},{20,4},{24,8},{28,12},{1,17},{... | collective-permute-start | bytes 1572872 | tf_op jit(solution)/shard_map/ppermute | solution.py:506
  461.5 27.5 %collective-permute-start.76 = (bf16[4,65,512]{2,1,0:T(8,128)(2,1)S(1)}, bf16[4,65,512]{2,1,0:T(8,128)(2,1)S(1)}, u32[]{:S(2)}, u32[]{:S(2)}) collective-permute-start(bf16[4,65,512]{2,1,0:T(8,128)(2,1)S(1)} %dynamic-slice_bitcast_fusion.11), channel_id=1, source_target_pairs={{0,8},{4,12},{8,0},{12,4},{16,24},{20,28},{24,16},{28,20},{1,9},{5... | collective-permute-start | bytes 798728 | tf_op jit(solution)/shard_map/ppermute | solution.py:506
  470.9 37.5 %collective-permute-start.66 = (bf16[2,64,2048]{2,1,0:T(8,128)(2,1)S(1)}, bf16[2,64,2048]{2,1,0:T(8,128)(2,1)S(1)}, u32[]{:S(2)}, u32[]{:S(2)}) collective-permute-start(bf16[2,64,2048]{2,1,0:T(8,128)(2,1)S(1)} %dynamic-slice_bitcast_fusion.10), channel_id=1, source_target_pairs={{0,16},{4,20},{8,24},{12,28},{16,0},{20,4},{24,8},{28,12},{1,17},{... | collective-permute-start | bytes 1572872 | tf_op jit(solution)/shard_map/ppermute | solution.py:506
  490.4 27.1 %collective-permute-start.68 = (bf16[2,2,64,2048]{3,2,1,0:T(8,128)(2,1)S(1)}, bf16[2,2,64,2048]{3,2,1,0:T(8,128)(2,1)S(1)}, u32[]{:S(2)}, u32[]{:S(2)}) collective-permute-start(bf16[2,2,64,2048]{3,2,1,0:T(8,128)(2,1)S(1)} %get-tuple-element.1330), channel_id=1, source_target_pairs={{16,8},{20,12},{24,16},{28,20},{17,9},{21,13},{25,17},{29,21},{18,... | collective-permute-start | bytes 3145736 | tf_op jit(solution)/shard_map/ppermute | solution.py:506
  502.7 21.0 %collective-permute-start.63 = (bf16[20,48,128]{2,1,0:T(8,128)(2,1)S(1)}, bf16[20,48,128]{2,1,0:T(8,128)(2,1)S(1)}, u32[]{:S(2)}, u32[]{:S(2)}) collective-permute-start(bf16[20,48,128]{2,1,0:T(8,128)(2,1)S(1)} %constant_dynamic-slice_fusion.1), channel_id=1, source_target_pairs={{0,1},{1,0},{2,3},{3,2},{4,5},{5,4},{6,7},{7,6},{8,9},{9,8},{10,11... | collective-permute-start | bytes 737288 | tf_op jit(solution)/shard_map/ppermute | solution.py:436
  510.6 19.8 %collective-permute-start.61 = (bf16[20,48,512]{2,1,0:T(8,128)(2,1)S(1)}, bf16[20,48,512]{2,1,0:T(8,128)(2,1)}, u32[]{:S(2)}, u32[]{:S(2)}) collective-permute-start(bf16[20,48,512]{2,1,0:T(8,128)(2,1)S(1)} %get-tuple-element.1319), channel_id=1, source_target_pairs={{0,1},{1,0},{2,3},{3,2},{4,5},{5,4},{6,7},{7,6},{8,9},{9,8},{10,11... | collective-permute-start | bytes 2949128 | tf_op jit(solution)/shard_map/ppermute | solution.py:436
  519.6 26.6 %collective-permute-start.69 = (bf16[2,2,64,2048]{3,2,1,0:T(8,128)(2,1)}, bf16[2,2,64,2048]{3,2,1,0:T(8,128)(2,1)S(1)}, u32[]{:S(2)}, u32[]{:S(2)}) collective-permute-start(bf16[2,2,64,2048]{3,2,1,0:T(8,128)(2,1)} %get-tuple-element.1329), channel_id=1, source_target_pairs={{0,8},{4,12},{8,16},{12,20},{16,24},{20,28},{1,9},{5,13},{9,17},{1... | collective-permute-start | bytes 3145736 | tf_op jit(solution)/shard_map/ppermute | solution.py:506
  523.7 25.6 %collective-permute-start.70 = (bf16[2,2,64,2048]{3,2,1,0:T(8,128)(2,1)}, bf16[2,2,64,2048]{3,2,1,0:T(8,128)(2,1)}, u32[]{:S(2)}, u32[]{:S(2)}) collective-permute-start(bf16[2,2,64,2048]{3,2,1,0:T(8,128)(2,1)} %get-tuple-element.1328), channel_id=1, source_target_pairs={{8,0},{12,4},{16,8},{20,12},{24,16},{28,20},{9,1},{13,5},{17,9},{2... | collective-permute-start | bytes 3145736 | tf_op jit(solution)/shard_map/ppermute | solution.py:506
  527.0 35.5 %collective-permute-start.73 = (bf16[2,64,2048]{2,1,0:T(8,128)(2,1)}, bf16[2,64,2048]{2,1,0:T(8,128)(2,1)}, u32[]{:S(2)}, u32[]{:S(2)}) collective-permute-start(bf16[2,64,2048]{2,1,0:T(8,128)(2,1)} %get-tuple-element.1341), channel_id=1, source_target_pairs={{0,1},{1,0},{2,3},{3,2},{4,5},{5,4},{6,7},{7,6},{8,9},{9,8},{10,11... | collective-permute-start | bytes 1572872 | tf_op jit(solution)/shard_map/ppermute | solution.py:873
  527.1 35.4 %collective-permute-start.75 = (bf16[2,64,2048]{2,1,0:T(8,128)(2,1)}, bf16[2,64,2048]{2,1,0:T(8,128)(2,1)}, u32[]{:S(2)}, u32[]{:S(2)}) collective-permute-start(bf16[2,64,2048]{2,1,0:T(8,128)(2,1)} %collective-permute-done.74), channel_id=1, source_target_pairs={{0,1},{1,0},{2,3},{3,2},{4,5},{5,4},{6,7},{7,6},{8,9},{9,8},{10,11... | collective-permute-start | bytes 1572872 | tf_op jit(solution)/shard_map/ppermute | solution.py:873
  (182 other events, 1400.4 us)

commit v8 on v7

--- a/solution.py
+++ b/solution.py
@@ -834,35 +834,55 @@
     begin = jnp.where(spot // 2 == 0, line - 1, 0)
     chunk_rows = 2 * share_rows if 2 * share_rows % 128 == 0 else 0
     near_left, near_right = gathered(near_all, feat_in[0], prev_in[0], near_parts[:-LATE])
-    near_late = after((near_left, proj_sent), *near_parts[-LATE:])
+    near_late = after((near_left, proj_sent, *far_parts[-LATE:]), *near_parts[-LATE:])
     near_right, first = completed(jnp.full((1,), begin, jnp.int32), chunk_rows, near_left, near_right, near_late)
     far_all, *far_parts = after((first,), far_all, *far_parts)
     far_left, far_right = gathered(far_all, feat_in[1], prev_in[1], far_parts[:-LATE])
     far_right, _ = completed(jnp.zeros((1,), jnp.int32), 0, far_left, far_right, far_parts[-LATE:])
     far = multiplied(far_left, far_right).reshape(2, line, 2, share_rows, 4 * width)
     near = multiplied(near_left, near_right).reshape(2, line, 2, share_rows, 4 * width)
-    (_, in_taken, far_in), (_, rec_taken, far_rec) = (with_partner(far[i]) for i in range(2))
-    proj_two = across_two(proj_y)
-    in_two, rec_two = across_two(far_in), across_two(far_rec)
+
+    def states_of(hidden, cell):
+        both_hidden = trade(hidden, hidden)
+
+        hidden_dirs = by_direction(*both_hidden)
+        outputs = (inputs.astype(F32) + jnp.transpose(hidden_dirs, (0, 2, 1, 3)).astype(F32)).astype(BF16)
+        last_h = jnp.stack([hidden_dirs[0, steps - 1], hidden_dirs[1, 0]], axis=1).astype(F32)
+        final_h = jnp.zeros_like(state_h).at[stream_doc].set(last_h)
+        last_c = jnp.transpose(cell.reshape(QUARTERS, HALVES, streams, width), (0, 2, 1, 3)).reshape(
+            QUARTERS, streams, cells
+        )
+        last_dirs = by_direction(*trade(last_c[0], last_c[1]))
+        final_c = jnp.zeros_like(state_c).at[stream_doc].set(jnp.transpose(last_dirs, (1, 0, 2)))
+        return outputs, final_h, final_c
 
     tokens = {}
 
     def second(up, down):
-        (tokens["dz"],) = after((up,), dz_all)
-        return after((far, proj_taken), up, down)
+        up, sent, tokens["dz"], proj_sum = after((), up, far, dz_all, proj_y)
+        tokens["in"], tokens["rec"] = (with_partner(sent[i])[2] for i in range(2))
+        tokens["proj"] = across_two(proj_sum)
+        return up, up
 
     def third(up, down):
-        tokens["dx"] = input_grad_of(tokens["dz"])
-        tokens["hidden"], tokens["cell"] = after((up, tokens["dx"]), hidden_all, cell)
-        return after((in_taken, proj_two, tokens["dx"]), up, down)
+        dx = input_grad_of(tokens["dz"])
+        up, down, tokens["dx"], in_sum, tokens["proj"], hidden, last_cell = after(
+            (), up, down, dx, tokens["in"], tokens["proj"], hidden_all, cell
+        )
+        tokens["in"] = across_two(in_sum)
+        tokens["states"] = states_of(hidden, last_cell)
+        return up, down
 
     def final(up, down):
-        return after((rec_taken, in_two), up, down)
+        up, down, tokens["in"], rec_sum = after(tokens["states"], up, down, tokens["in"], tokens["rec"])
+        tokens["rec"] = across_two(rec_sum)
+        return up, down
 
     gates = {2: second, 3: third, line: final} if line > 3 else {}
     first = first.reshape(2, 2, share_rows, 4 * width) if chunk_rows else None
     near = line_sum(near, 1, 2, line, first, gates)
-    dx_all, hidden_all, cell = (tokens[x] for x in ("dx", "hidden", "cell"))
+    dx_all, (outputs, final_h, final_c) = tokens["dx"], tokens["states"]
+    in_two, rec_two, proj_two = tokens["in"], tokens["rec"], tokens["proj"]
 
     def halves_of(summed, index, pairs):
         mine = lax.dynamic_index_in_dim(summed, index, 1, keepdims=False)
@@ -891,18 +911,6 @@
     grad_proj = grad_proj[:, :share_rows].reshape(QUARTERS, HALVES, share_rows, width)
     grad_proj = jnp.transpose(grad_proj, (0, 1, 3, 2)).reshape(QUARTERS, cells, share_rows).astype(BF16)
     grad_proj = home(grad_proj[0], grad_proj[1])
-
-    both_hidden = trade(hidden_all, hidden_all)
-
-    hidden_dirs = by_direction(*both_hidden)
-    outputs = (inputs.astype(F32) + jnp.transpose(hidden_dirs, (0, 2, 1, 3)).astype(F32)).astype(BF16)
-    last_h = jnp.stack([hidden_dirs[0, steps - 1], hidden_dirs[1, 0]], axis=1).astype(F32)
-    final_h = jnp.zeros_like(state_h).at[stream_doc].set(last_h)
-    last_c = jnp.transpose(cell.reshape(QUARTERS, HALVES, streams, width), (0, 2, 1, 3)).reshape(
-        QUARTERS, streams, cells
-    )
-    last_dirs = by_direction(*trade(last_c[0], last_c[1]))
-    final_c = jnp.zeros_like(state_c).at[stream_doc].set(jnp.transpose(last_dirs, (1, 0, 2)))
 
     half_cols = depth // 2
     upper = rank // 2

time: 579 us -> 587 us (1.014)
  local copies, waits for them, and re-layouts: 48.9 us -> 77.8 us
  waiting for transfers between devices: 61.1 us -> 34.1 us
  other arithmetic: 25.7 us -> 34.6 us
    unnamed x276 -> x312, local copies, waits for them, and re-layouts: 23.3 us -> 48.8 us
    ppermute x28, waiting for transfers between devices: 47.8 us -> 27.1 us  [swapped(): return lax.ppermute(array, 'batch', pairs)]
  transfers between devices with their start and end apart: 80 -> 80, of which waited for: 41 -> 34; matrix products, arithmetic and copies ran while one was open for 10% -> 12% of each run, Pallas kernels for 53% -> 53%
where the time goes in v8:
time: 587 us; the launch traced here: 578 us
  Pallas kernels  336 us (57%)
  starting transfers between devices  88.2 us (15%)
  local copies, waits for them, and re-layouts  77.8 us (13%)
  other arithmetic  34.6 us (6%)
  waiting for transfers between devices  34.1 us (6%)
    pallas_call x20, Pallas kernels, backward_call(): pl.pallas_call(backward_kernel, out_shape=(vmem((streams, depth), BF16),...  62.8 us
    pallas_call x20, Pallas kernels, between_call(): pl.pallas_call(functools.partial(between_kernel, not stacks, step == step...  59.6 us
    pallas_call x20, Pallas kernels, forward_call(): pl.pallas_call(functools.partial(forward_kernel, first), out_shape=(vmem(...  56.9 us
    pallas_call x20, Pallas kernels, aside_call(): pl.pallas_call(functools.partial(aside_kernel, not stacks, step == 0, not...  56.2 us
    unnamed x312, local copies, waits for them, and re-layouts  48.8 us
    ppermute x28, starting transfers between devices, swapped(): return lax.ppermute(array, 'batch', pairs)  43.2 us
    ppermute x39, starting transfers between devices, body(): peer = lax.ppermute(part, 'gate', across)  41.5 us
    ppermute x28, waiting for transfers between devices, swapped(): return lax.ppermute(array, 'batch', pairs)  27.1 us
  transfers between devices with their start and end apart: 80, of which 34 were waited for; matrix products, arithmetic and copies ran while one was open for 12% of the time, Pallas kernels for 53%

profile of v8, /device:TPU:8, one launch (start us, length us, event | category | flops | bytes accessed | tf_op | source)
XLA Modules:
  0.0 577.5 jit_solution(10530414639623431790)
XLA Ops:
  0.7 5.2 layout.4
  6.0 5.2 layout.6
  19.1 5.2 layout.5
  26.4 5.2 layout.7
  34.3 3.2 order.1
  79.3 3.1 between.23
  110.4 3.2 forward_step.28
  149.8 3.2 between.33
  198.8 6.0 %turned.1 = (bf16[4,1024,512]{2,1,0:T(8,128)(2,1)S(1)}, bf16[4,1024,512]{2,1,0:T(8,128)(2,1)S(1)}, bf16[512,1024]{1,0:T(8,128)(2,1)S(1)}, bf16[512,1024]{1,0:T(8,128)(2,1)S(1)}) custom-call(bf16[4,512,1024]{2,1,0:T(8,128)(2,1)} %get-tuple-element.961.wa_ref, bf16[4,512,1024]{2,1,0:T(8,128)(2,1)} %collective-permute-done.2.refs_0_.wb_ref, ...), custom_call_target="tpu_custom_call" | custom-call | tf_op jit(solution)/shard_map/turned/pallas_call | solution.py:617
  204.9 3.5 finish.1
  208.5 3.5 backward_step.20
  252.4 3.2 backward_step.26
  364.8 3.7 backward_step.39
  377.6 3.6 bitcast_convert_fusion
  384.0 4.2 gather.14
  390.1 5.4 late.2
  395.5 3.1 copy-done.21
  405.1 4.3 gather.15
  411.4 11.3 %product.3 = bf16[2,512,2048]{2,1,0:T(8,128)(2,1)S(1)} custom-call(bf16[40,48,1024]{2,1,0:T(8,128)(2,1)S(1)} %get-tuple-element.1317.left_ref, bf16[40,48,2048]{2,1,0:T(8,128)(2,1)S(1)} %get-tuple-element.1321.right_ref), custom_call_target="tpu_custom_call" | custom-call | tf_op jit(solution)/shard_map/product/pallas_call | solution.py:823
  422.8 11.2 %product.2 = bf16[2,512,2048]{2,1,0:T(8,128)(2,1)S(1)} custom-call(bf16[40,48,1024]{2,1,0:T(8,128)(2,1)S(1)} %copy-done.20, bf16[40,48,2048]{2,1,0:T(8,128)(2,1)S(1)} %bitcast.199), custom_call_target="tpu_custom_call" | custom-call | tf_op jit(solution)/shard_map/product/pallas_call | solution.py:823
  437.7 5.4 copy-done.2
  445.1 4.3 collective-permute-start.63
  461.2 5.5 copy-done.3
  466.7 17.1 %input_grad.1.refs_2_ = f32[20,48,512]{2,1,0:T(8,128)S(1)} custom-call(s32[2]{0:T(128)S(1)} %copy-done.84, bf16[4,20,48,2048]{3,2,1,0:T(8,128)(2,1)S(1)} %copy-done.3, bf16[4,512,1024]{2,1,0:T(8,128)(2,1)} %get-tuple-element.1325.wa_ref, bf16[4,512,1024]{2,1,0:T(8,128)(2,1)} %collective-permute-done.1.refs_2_.wb_ref), custom_call_target="tpu_custom_call" | custom-call | tf_op jit(solution)/shard_map/input_grad/pallas_call | solution.py:748
  488.4 3.4 collective-permute-start.77
  493.3 3.9 fusion.5
  500.2 4.1 collective-permute-start.69
  509.9 6.1 %scatter_fusion.1 = f32[48,2,1024]{2,1,0:T(2,128)} fusion(f32[48,2,1024]{2,1,0:T(2,128)} %broadcast_in_dim.48, s32[48]{0:T(128)S(1)} %copy-done.103, f32[48,2,1024]{2,1,0:T(2,128)} %maximum_bitcast_fusion.1), kind=kCustom, calls=%fused_computation.3 | custom fusion | bytes 1179840 | tf_op jit(solution)/shard_map/scatter | solution.py:856
  527.4 3.8 fusion.refs_0_
  535.9 19.0 %collective-permute-done.73 = bf16[2,64,2048]{2,1,0:T(8,128)(2,1)S(1)} collective-permute-done((bf16[2,64,2048]{2,1,0:T(8,128)(2,1)S(1)}, bf16[2,64,2048]{2,1,0:T(8,128)(2,1)S(1)}, u32[]{:S(2)}, u32[]{:S(2)}) %collective-permute-start.73) | collective-permute-done | bytes 524320 | tf_op jit(solution)/shard_map/ppermute | solution.py:506
  561.1 8.0 %collective-permute-done.75 = bf16[2,64,2048]{2,1,0:T(8,128)(2,1)S(1)} collective-permute-done((bf16[2,64,2048]{2,1,0:T(8,128)(2,1)S(1)}, bf16[2,64,2048]{2,1,0:T(8,128)(2,1)S(1)}, u32[]{:S(2)}, u32[]{:S(2)}) %collective-permute-start.75) | collective-permute-done | bytes 524320 | tf_op jit(solution)/shard_map/ppermute | solution.py:506
  573.8 3.5 assemble.1
  (673 shorter events, 393.2 us)
Async XLA Ops:
  5.9 36.9 %collective-permute-start.1 = (bf16[4,512,1024]{2,1,0:T(8,128)(2,1)}, bf16[4,512,1024]{2,1,0:T(8,128)(2,1)}, u32[]{:S(2)}, u32[]{:S(2)}) collective-permute-start(bf16[4,512,1024]{2,1,0:T(8,128)(2,1)} %layout.4), channel_id=1, source_target_pairs={{0,1},{1,0},{2,3},{3,2},{4,5},{5,4},{6,7},{7,6},{8,9},{9,8},{10,11... | collective-permute-start | bytes 12582920 | tf_op jit(solution)/shard_map/ppermute | solution.py:463
  11.2 38.3 %collective-permute-start.2 = (bf16[4,512,1024]{2,1,0:T(8,128)(2,1)}, bf16[4,512,1024]{2,1,0:T(8,128)(2,1)}, u32[]{:S(2)}, u32[]{:S(2)}) collective-permute-start(bf16[4,512,1024]{2,1,0:T(8,128)(2,1)} %layout.6), channel_id=1, source_target_pairs={{0,1},{1,0},{2,3},{3,2},{4,5},{5,4},{6,7},{7,6},{8,9},{9,8},{10,11... | collective-permute-start | bytes 12582920 | tf_op jit(solution)/shard_map/ppermute | solution.py:463
  11.8 25.7 %collective-permute-start = (bf16[4,1024]{1,0:T(4,128)(2,1)S(1)}, bf16[4,1024]{1,0:T(4,128)(2,1)S(1)}, u32[]{:S(2)}, u32[]{:S(2)}) collective-permute-start(bf16[4,1024]{1,0:T(4,128)(2,1)S(1)} %get-tuple-element.1389), channel_id=1, source_target_pairs={{0,1},{1,0},{2,3},{3,2},{4,5},{5,4},{6,7},{7,6},{8,9},{9,8},{10,11... | collective-permute-start | bytes 24584 | tf_op jit(solution)/shard_map/ppermute | solution.py:436
  14.6 25.2 %collective-permute-start.4 = (f32[48,1024]{1,0:T(8,128)}, f32[48,1024]{1,0:T(8,128)}, u32[]{:S(2)}, u32[]{:S(2)}) collective-permute-start(f32[48,1024]{1,0:T(8,128)} %bitcast.191), channel_id=1, source_target_pairs={{0,1},{1,0},{2,3},{3,2},{4,5},{5,4},{6,7},{7,6},{8,9},{9,8},{10,11... | collective-permute-start | bytes 589832 | tf_op jit(solution)/shard_map/ppermute | solution.py:436
  18.0 31.5 %collective-permute-start.3 = (bf16[1024,512]{1,0:T(8,128)(2,1)}, bf16[1024,512]{1,0:T(8,128)(2,1)}, u32[]{:S(2)}, u32[]{:S(2)}) collective-permute-start(bf16[1024,512]{1,0:T(8,128)(2,1)} %get-tuple-element.1364), channel_id=1, source_target_pairs={{0,1},{1,0},{2,3},{3,2},{4,5},{5,4},{6,7},{7,6},{8,9},{9,8},{10,11... | collective-permute-start | bytes 3145736 | tf_op jit(solution)/shard_map/ppermute | solution.py:436
  37.5 112.3 %collective-permute-start.19 = (bf16[20,48,512]{2,1,0:T(8,128)(2,1)}, bf16[20,48,512]{2,1,0:T(8,128)(2,1)}, u32[]{:S(2)}, u32[]{:S(2)}) collective-permute-start(bf16[20,48,512]{2,1,0:T(8,128)(2,1)} %get-tuple-element.675.refs_0_), channel_id=1, source_target_pairs={{0,4},{4,0},{8,12},{12,8},{16,20},{20,16},{24,28},{28,24},{1,5},{5... | collective-permute-start | bytes 2949128 | tf_op jit(solution)/shard_map/ppermute | solution.py:506
  39.8 110.0 %collective-permute-start.20 = (bf16[20,48,512]{2,1,0:T(8,128)(2,1)}, bf16[20,48,512]{2,1,0:T(8,128)(2,1)}, u32[]{:S(2)}, u32[]{:S(2)}) collective-permute-start(bf16[20,48,512]{2,1,0:T(8,128)(2,1)} %get-tuple-element.675.refs_0_), channel_id=1, source_target_pairs={{0,8},{4,12},{8,0},{12,4},{16,24},{20,28},{24,16},{28,20},{1,9},{5... | collective-permute-start | bytes 2949128 | tf_op jit(solution)/shard_map/ppermute | solution.py:506
  194.5 62.2 %collective-permute-start.33 = (bf16[20,48,512]{2,1,0:T(8,128)(2,1)}, bf16[20,48,512]{2,1,0:T(8,128)(2,1)}, u32[]{:S(2)}, u32[]{:S(2)}) collective-permute-start(bf16[20,48,512]{2,1,0:T(8,128)(2,1)} %get-tuple-element.959.refs_1_), channel_id=1, source_target_pairs={{0,4},{4,0},{8,12},{12,8},{16,20},{20,16},{24,28},{28,24},{1,5},{5... | collective-permute-start | bytes 2949128 | tf_op jit(solution)/shard_map/ppermute | solution.py:506
  195.1 61.6 %collective-permute-start.34 = (bf16[20,48,512]{2,1,0:T(8,128)(2,1)}, bf16[20,48,512]{2,1,0:T(8,128)(2,1)}, u32[]{:S(2)}, u32[]{:S(2)}) collective-permute-start(bf16[20,48,512]{2,1,0:T(8,128)(2,1)} %get-tuple-element.959.refs_1_), channel_id=1, source_target_pairs={{0,8},{4,12},{8,0},{12,4},{16,24},{20,28},{24,16},{28,20},{1,9},{5... | collective-permute-start | bytes 2949128 | tf_op jit(solution)/shard_map/ppermute | solution.py:506
  262.9 49.1 %collective-permute-start.43 = (bf16[7,48,2048]{2,1,0:T(8,128)(2,1)S(1)}, bf16[7,48,2048]{2,1,0:T(8,128)(2,1)S(1)}, u32[]{:S(2)}, u32[]{:S(2)}) collective-permute-start(bf16[7,48,2048]{2,1,0:T(8,128)(2,1)S(1)} %get-tuple-element.1189), channel_id=1, source_target_pairs={{0,4},{4,0},{8,12},{12,8},{16,20},{20,16},{24,28},{28,24},{1,5},{5... | collective-permute-start | bytes 4128776 | tf_op jit(solution)/shard_map/ppermute | solution.py:506
  264.5 47.5 %collective-permute-start.44 = (bf16[7,48,2048]{2,1,0:T(8,128)(2,1)S(1)}, bf16[7,48,2048]{2,1,0:T(8,128)(2,1)S(1)}, u32[]{:S(2)}, u32[]{:S(2)}) collective-permute-start(bf16[7,48,2048]{2,1,0:T(8,128)(2,1)S(1)} %get-tuple-element.1190), channel_id=1, source_target_pairs={{0,8},{4,12},{8,0},{12,4},{16,24},{20,28},{24,16},{28,20},{1,9},{5... | collective-permute-start | bytes 4128776 | tf_op jit(solution)/shard_map/ppermute | solution.py:506
  308.8 47.4 %collective-permute-start.50 = (bf16[6,48,2048]{2,1,0:T(8,128)(2,1)}, bf16[6,48,2048]{2,1,0:T(8,128)(2,1)}, u32[]{:S(2)}, u32[]{:S(2)}) collective-permute-start(bf16[6,48,2048]{2,1,0:T(8,128)(2,1)} %get-tuple-element.1269), channel_id=1, source_target_pairs={{0,4},{4,0},{8,12},{12,8},{16,20},{20,16},{24,28},{28,24},{1,5},{5... | collective-permute-start | bytes 3538952 | tf_op jit(solution)/shard_map/ppermute | solution.py:506
  309.3 49.2 %collective-permute-start.51 = (bf16[6,48,2048]{2,1,0:T(8,128)(2,1)}, bf16[6,48,2048]{2,1,0:T(8,128)(2,1)}, u32[]{:S(2)}, u32[]{:S(2)}) collective-permute-start(bf16[6,48,2048]{2,1,0:T(8,128)(2,1)} %get-tuple-element.1270), channel_id=1, source_target_pairs={{0,8},{4,12},{8,0},{12,4},{16,24},{20,28},{24,16},{28,20},{1,9},{5... | collective-permute-start | bytes 3538952 | tf_op jit(solution)/shard_map/ppermute | solution.py:506
  334.0 37.4 %collective-permute-start.52 = (bf16[3,48,2048]{2,1,0:T(8,128)(2,1)}, bf16[3,48,2048]{2,1,0:T(8,128)(2,1)}, u32[]{:S(2)}, u32[]{:S(2)}) collective-permute-start(bf16[3,48,2048]{2,1,0:T(8,128)(2,1)} %get-tuple-element.1286), channel_id=1, source_target_pairs={{0,4},{4,0},{8,12},{12,8},{16,20},{20,16},{24,28},{28,24},{1,5},{5... | collective-permute-start | bytes 1769480 | tf_op jit(solution)/shard_map/ppermute | solution.py:506
  335.6 35.7 %collective-permute-start.53 = (bf16[3,48,2048]{2,1,0:T(8,128)(2,1)}, bf16[3,48,2048]{2,1,0:T(8,128)(2,1)}, u32[]{:S(2)}, u32[]{:S(2)}) collective-permute-start(bf16[3,48,2048]{2,1,0:T(8,128)(2,1)} %get-tuple-element.1287), channel_id=1, source_target_pairs={{0,8},{4,12},{8,0},{12,4},{16,24},{20,28},{24,16},{28,20},{1,9},{5... | collective-permute-start | bytes 1769480 | tf_op jit(solution)/shard_map/ppermute | solution.py:506
  356.9 31.3 %collective-permute-start.54 = (bf16[2,48,2048]{2,1,0:T(8,128)(2,1)}, bf16[2,48,2048]{2,1,0:T(8,128)(2,1)S(1)}, u32[]{:S(2)}, u32[]{:S(2)}) collective-permute-start(bf16[2,48,2048]{2,1,0:T(8,128)(2,1)} %copy-done.40), channel_id=1, source_target_pairs={{0,8},{4,12},{8,0},{12,4},{16,24},{20,28},{24,16},{28,20},{1,9},{5... | collective-permute-start | bytes 1179656 | tf_op jit(solution)/shard_map/ppermute | solution.py:506
  358.5 29.7 %collective-permute-start.56 = (bf16[2,48,2048]{2,1,0:T(8,128)(2,1)}, bf16[2,48,2048]{2,1,0:T(8,128)(2,1)}, u32[]{:S(2)}, u32[]{:S(2)}) collective-permute-start(bf16[2,48,2048]{2,1,0:T(8,128)(2,1)} %copy-done.38), channel_id=1, source_target_pairs={{0,4},{4,0},{8,12},{12,8},{16,20},{20,16},{24,28},{28,24},{1,5},{5... | collective-permute-start | bytes 1179656 | tf_op jit(solution)/shard_map/ppermute | solution.py:506
  382.9 53.0 %collective-permute-start.59 = (bf16[4,4,65,512]{3,1,2,0:T(4,128)(2,1)}, bf16[4,4,65,512]{3,1,2,0:T(4,128)(2,1)}, u32[]{:S(2)}, u32[]{:S(2)}) collective-permute-start(bf16[4,4,65,512]{3,1,2,0:T(4,128)(2,1)} %copy.511), channel_id=1, source_target_pairs={{0,4},{4,0},{8,12},{12,8},{16,20},{20,16},{24,28},{28,24},{1,5},{5... | collective-permute-start | bytes 3194888 | tf_op jit(solution)/shard_map/ppermute | solution.py:506
  398.7 38.9 %collective-permute-start.58 = (bf16[2,2,64,2048]{3,2,1,0:T(8,128)(2,1)}, bf16[2,2,64,2048]{3,2,1,0:T(8,128)(2,1)S(1)}, u32[]{:S(2)}, u32[]{:S(2)}) collective-permute-start(bf16[2,2,64,2048]{3,2,1,0:T(8,128)(2,1)} %bitcast.31), channel_id=1, source_target_pairs={{0,8},{4,12},{24,16},{28,20},{1,9},{5,13},{25,17},{29,21},{2,10},{... | collective-permute-start | bytes 3145736 | tf_op jit(solution)/shard_map/ppermute | solution.py:506
  445.1 38.7 %collective-permute-start.63 = (bf16[4,2,65,512]{3,0,2,1:T(4,128)(2,1)S(1)}, bf16[4,2,65,512]{3,0,2,1:T(4,128)(2,1)S(1)}, u32[]{:S(2)}, u32[]{:S(2)}) collective-permute-start(bf16[4,2,65,512]{3,0,2,1:T(4,128)(2,1)S(1)} %get-tuple-element.1368), channel_id=1, source_target_pairs={{0,16},{4,20},{8,24},{12,28},{16,0},{20,4},{24,8},{28,12},{1,17},{... | collective-permute-start | bytes 1597448 | tf_op jit(solution)/shard_map/ppermute | solution.py:506
  452.5 33.5 %collective-permute-start.62 = (bf16[4,64,2048]{2,1,0:T(8,128)(2,1)}, bf16[4,64,2048]{2,1,0:T(8,128)(2,1)}, u32[]{:S(2)}, u32[]{:S(2)}) collective-permute-start(bf16[4,64,2048]{2,1,0:T(8,128)(2,1)} %dynamic-slice_bitcast_fusion.1), channel_id=1, source_target_pairs={{0,4},{4,0},{8,12},{12,8},{16,20},{20,16},{24,28},{28,24},{1,5},{5... | collective-permute-start | bytes 3145736 | tf_op jit(solution)/shard_map/ppermute | solution.py:506
  456.1 31.5 %collective-permute-start.60 = (bf16[2,2,64,2048]{3,2,1,0:T(8,128)(2,1)}, bf16[2,2,64,2048]{3,2,1,0:T(8,128)(2,1)}, u32[]{:S(2)}, u32[]{:S(2)}) collective-permute-start(bf16[2,2,64,2048]{3,2,1,0:T(8,128)(2,1)} %get-tuple-element.1359), channel_id=1, source_target_pairs={{0,8},{4,12},{8,16},{12,20},{1,9},{5,13},{9,17},{13,21},{2,10},{6,... | collective-permute-start | bytes 3145736 | tf_op jit(solution)/shard_map/ppermute | solution.py:506
  458.0 29.6 %collective-permute-start.61 = (bf16[2,2,64,2048]{3,2,1,0:T(8,128)(2,1)}, bf16[2,2,64,2048]{3,2,1,0:T(8,128)(2,1)}, u32[]{:S(2)}, u32[]{:S(2)}) collective-permute-start(bf16[2,2,64,2048]{3,2,1,0:T(8,128)(2,1)} %get-tuple-element.1358), channel_id=1, source_target_pairs={{16,8},{20,12},{24,16},{28,20},{17,9},{21,13},{25,17},{29,21},{18,... | collective-permute-start | bytes 3145736 | tf_op jit(solution)/shard_map/ppermute | solution.py:506
  460.7 43.8 %collective-permute-start.71 = (bf16[4,64,2048]{2,1,0:T(8,128)(2,1)S(1)}, bf16[4,64,2048]{2,1,0:T(8,128)(2,1)S(1)}, u32[]{:S(2)}, u32[]{:S(2)}) collective-permute-start(bf16[4,64,2048]{2,1,0:T(8,128)(2,1)S(1)} %dynamic-slice_bitcast_fusion), channel_id=1, source_target_pairs={{0,4},{4,0},{8,12},{12,8},{16,20},{20,16},{24,28},{28,24},{1,5},{5... | collective-permute-start | bytes 3145736 | tf_op jit(solution)/shard_map/ppermute | solution.py:506
  488.4 27.7 %collective-permute-start.77 = (bf16[4,65,512]{2,1,0:T(8,128)(2,1)}, bf16[4,65,512]{2,1,0:T(8,128)(2,1)}, u32[]{:S(2)}, u32[]{:S(2)}) collective-permute-start(bf16[4,65,512]{2,1,0:T(8,128)(2,1)} %dynamic-slice_bitcast_fusion.11), channel_id=1, source_target_pairs={{0,8},{4,12},{8,0},{12,4},{16,24},{20,28},{24,16},{28,20},{1,9},{5... | collective-permute-start | bytes 798728 | tf_op jit(solution)/shard_map/ppermute | solution.py:506
  492.6 27.3 %collective-permute-start.70 = (bf16[2,64,2048]{2,1,0:T(8,128)(2,1)}, bf16[2,64,2048]{2,1,0:T(8,128)(2,1)}, u32[]{:S(2)}, u32[]{:S(2)}) collective-permute-start(bf16[2,64,2048]{2,1,0:T(8,128)(2,1)} %dynamic-slice_bitcast_fusion.10), channel_id=1, source_target_pairs={{0,16},{4,20},{8,24},{12,28},{16,0},{20,4},{24,8},{28,12},{1,17},{... | collective-permute-start | bytes 1572872 | tf_op jit(solution)/shard_map/ppermute | solution.py:506
  497.2 33.9 %collective-permute-start.68 = (bf16[2,2,64,2048]{3,2,1,0:T(8,128)(2,1)}, bf16[2,2,64,2048]{3,2,1,0:T(8,128)(2,1)}, u32[]{:S(2)}, u32[]{:S(2)}) collective-permute-start(bf16[2,2,64,2048]{3,2,1,0:T(8,128)(2,1)} %get-tuple-element.1363), channel_id=1, source_target_pairs={{0,8},{4,12},{8,16},{12,20},{16,24},{20,28},{1,9},{5,13},{9,17},{1... | collective-permute-start | bytes 3145736 | tf_op jit(solution)/shard_map/ppermute | solution.py:506
  500.2 31.0 %collective-permute-start.69 = (bf16[2,2,64,2048]{3,2,1,0:T(8,128)(2,1)}, bf16[2,2,64,2048]{3,2,1,0:T(8,128)(2,1)}, u32[]{:S(2)}, u32[]{:S(2)}) collective-permute-start(bf16[2,2,64,2048]{3,2,1,0:T(8,128)(2,1)} %get-tuple-element.1362), channel_id=1, source_target_pairs={{8,0},{12,4},{16,8},{20,12},{24,16},{28,20},{9,1},{13,5},{17,9},{2... | collective-permute-start | bytes 3145736 | tf_op jit(solution)/shard_map/ppermute | solution.py:506
  516.1 18.1 %collective-permute-start.65 = (bf16[20,48,256]{2,1,0:T(8,128)(2,1)}, bf16[20,48,256]{2,1,0:T(8,128)(2,1)}, u32[]{:S(2)}, u32[]{:S(2)}) collective-permute-start(bf16[20,48,256]{2,1,0:T(8,128)(2,1)} %dynamic-slice_convert_fusion), channel_id=1, source_target_pairs={{0,2},{1,3},{2,0},{3,1},{4,6},{5,7},{6,4},{7,5},{8,10},{9,11},{10,... | collective-permute-start | bytes 1474568 | tf_op jit(solution)/shard_map/ppermute | solution.py:919
  519.9 49.2 %collective-permute-start.79 = (bf16[1024,64]{0,1:T(8,128)(2,1)}, bf16[1024,64]{0,1:T(8,128)(2,1)}, u32[]{:S(2)}, u32[]{:S(2)}) collective-permute-start(bf16[1024,64]{0,1:T(8,128)(2,1)} %bitcast.125), channel_id=1, source_target_pairs={{0,1},{1,0},{2,3},{3,2},{4,5},{5,4},{6,7},{7,6},{8,9},{9,8},{10,11... | collective-permute-start | bytes 393224 | tf_op jit(solution)/shard_map/ppermute | solution.py:436
  531.2 23.7 %collective-permute-start.73 = (bf16[2,64,2048]{2,1,0:T(8,128)(2,1)S(1)}, bf16[2,64,2048]{2,1,0:T(8,128)(2,1)S(1)}, u32[]{:S(2)}, u32[]{:S(2)}) collective-permute-start(bf16[2,64,2048]{2,1,0:T(8,128)(2,1)S(1)} %dynamic-slice_bitcast_fusion.7), channel_id=1, source_target_pairs={{0,16},{4,20},{8,24},{12,28},{16,0},{20,4},{24,8},{28,12},{1,17},{... | collective-permute-start | bytes 1572872 | tf_op jit(solution)/shard_map/ppermute | solution.py:506
  535.8 35.1 %collective-permute-start.66 = (bf16[20,48,128]{2,1,0:T(8,128)(2,1)S(1)}, bf16[20,48,128]{2,1,0:T(8,128)(2,1)S(1)}, u32[]{:S(2)}, u32[]{:S(2)}) collective-permute-start(bf16[20,48,128]{2,1,0:T(8,128)(2,1)S(1)} %constant_dynamic-slice_fusion), channel_id=1, source_target_pairs={{0,1},{1,0},{2,3},{3,2},{4,5},{5,4},{6,7},{7,6},{8,9},{9,8},{10,11... | collective-permute-start | bytes 737288 | tf_op jit(solution)/shard_map/ppermute | solution.py:436
  (200 other events, 1370.0 us)

commit v9 on v8

--- a/solution.py
+++ b/solution.py
@@ -106,7 +106,7 @@
     pass
 
 
-def after(tokens, *arrays):
+def after(tokens, *arrays, free=0):
     count = len(tokens)
     return pl.pallas_call(
         pass_kernel,
@@ -116,7 +116,7 @@
         input_output_aliases={count + i: i for i in range(len(arrays))},
         compiler_params=params(1),
         name="after",
-    )(*tokens, *arrays)
+    )(*tokens, *(in_hbm(x) if x.size * x.dtype.itemsize > free else x for x in arrays))
 
 
 def gather_kernel(lows, *refs):
@@ -196,18 +196,30 @@
                 out_ref[direction, :, :, half * width : (half + 1) * width] = jnp.swapaxes(gates, 0, 1)
 
 
-def order_kernel(step_ref, feat_ref, out_ref, all_ref, sems, all_sem):
-    steps = feat_ref.shape[0]
-    copies = [
-        pltpu.make_async_copy(feat_ref.at[step_ref[0] + step_ref[1] * i], out_ref.at[i], sems.at[i]) for i in range(steps)
-    ]
+def order_kernel(step_ref, feat_ref, out_ref, all_ref, sems):
+    copies = []
+    for i in range(feat_ref.shape[0]):
+        source = feat_ref.at[step_ref[0] + step_ref[1] * i]
+        copies.append(pltpu.make_async_copy(source, out_ref.at[i], sems.at[2 * i]))
+        copies.append(pltpu.make_async_copy(source, all_ref.at[i], sems.at[2 * i + 1]))
     for copy in copies:
         copy.start()
     for copy in copies:
         copy.wait()
-    whole = pltpu.make_async_copy(out_ref, all_ref, all_sem)
-    whole.start()
-    whole.wait()
+
+
+def numbers_kernel(in_ref, out_ref):
+    for i in range(in_ref.shape[0]):
+        out_ref[i] = in_ref[i]
+
+
+def bias_kernel(sum_ref, out_ref):
+    width = sum_ref.shape[2] // 4
+    for piece in range(PIECES):
+        for gate in range(4):
+            out_ref[piece, gate : gate + 1, :] = jnp.sum(
+                sum_ref[piece, :, gate * width : (gate + 1) * width], axis=0, keepdims=True
+            )
 
 
 def pieces(refs, axis):
@@ -256,7 +268,7 @@
 
 
 def between_kernel(
-    first, last, passed, step_ref, feat_ref, bias_ref, wa_ref, wb_ref, cell_ref, gates_ref, mixed_ref, prev_ref, hidden_ref,
+    first, last, passed, step_ref, feat_ref, ba_ref, bb_ref, wa_ref, wb_ref, cell_ref, gates_ref, mixed_ref, prev_ref, hidden_ref,
     slope_ref, *refs,
 ):
     refs = refs[(0 if first else 6) + passed :]
@@ -275,21 +287,21 @@
     for copy in copies:
         copy.start()
     if not last:
-        inflow_into(feat_ref[step + 1], bias_ref, wa_ref, wb_ref, out_ref)
+        inflow_into(feat_ref[step + 1], ba_ref, bb_ref, wa_ref, wb_ref, out_ref)
     for copy in copies:
         copy.wait()
 
 
-def inflow_into(feat, bias_ref, wa_ref, wb_ref, out_ref):
+def inflow_into(feat, ba_ref, bb_ref, wa_ref, wb_ref, out_ref):
     for piece, quarter, width, cols in pieces((wa_ref, wb_ref), 2):
-        w_ref = (wa_ref, wb_ref)[quarter]
+        w_ref, bias_ref = ((wa_ref, ba_ref), (wb_ref, bb_ref))[quarter]
         for gate in range(4):
             place = slice(gate * width, (gate + 1) * width)
-            out_ref[piece, :, place] = dot(feat, w_ref[gate, :, cols]) + bias_ref[piece, :, place]
-
-
-def inflow_kernel(step_ref, feat_ref, bias_ref, wa_ref, wb_ref, out_ref):
-    inflow_into(feat_ref[0], bias_ref, wa_ref, wb_ref, out_ref)
+            out_ref[piece, :, place] = dot(feat, w_ref[gate, :, cols]) + bias_ref[gate : gate + 1, cols]
+
+
+def inflow_kernel(feat_ref, ba_ref, bb_ref, wa_ref, wb_ref, out_ref):
+    inflow_into(feat_ref[0], ba_ref, bb_ref, wa_ref, wb_ref, out_ref)
 
 
 def backward_kernel(
@@ -423,14 +435,50 @@
     streams, steps, depth = inputs.shape[1:]
     cells = w_in.shape[3]
     width = cells // HALVES
-    rank = lax.axis_index("gate")
-    own = rank % 2
+    n_batch = lax.axis_size("batch")
     gates_size = lax.axis_size("gate")
+    line = n_batch // 2
     swap = [(i, i ^ 1) for i in range(gates_size)]
     across = [(i, i ^ 2) for i in range(gates_size)]
-
-    def pick(stacked, index):
-        return lax.dynamic_index_in_dim(stacked, index, 0, keepdims=False)
+    near_swap = [(i, i ^ 1) for i in range(n_batch)]
+    far_swap = [(i, i ^ 2) for i in range(n_batch)]
+
+    rank, spot = lax.axis_index("gate"), lax.axis_index("batch")
+    half_cols, quarter_cols = depth // 2, depth // 4
+    place_numbers = {
+        "own": rank % 2,
+        "other": 1 - rank % 2,
+        "low": spot % 2,
+        "not_low": 1 - spot % 2,
+        "high": (spot // 2) % 2,
+        "not_high": 1 - (spot // 2) % 2,
+        "spot": spot,
+        "begin": jnp.where(spot // 2 == 0, line - 1, 0),
+        "cols": (rank // 2) * half_cols,
+        "other_cols": (1 - rank // 2) * half_cols,
+    }
+    for stride, count in {(2, line), (4, line // 2)}:
+        here = (spot // stride) % count
+        place_numbers[stride, "here"] = here
+        place_numbers[stride, "not_here"] = jnp.maximum(1 - here, 0)
+        for slot in range(2, count):
+            place_numbers[stride, "rise", slot] = jnp.minimum(here + count - slot, count - 1)
+            place_numbers[stride, "fall", slot] = jnp.maximum(here - count + slot, 0)
+        if count > 2:
+            place_numbers[stride, "begin"] = jnp.where(here == 0, count - 1, 0)
+    names = sorted(place_numbers, key=str)
+    gathered_numbers = pl.pallas_call(
+        numbers_kernel,
+        out_shape=jax.ShapeDtypeStruct((len(names),), jnp.int32),
+        in_specs=[SMEM],
+        out_specs=SMEM,
+        name="numbers",
+    )(jnp.stack([place_numbers[x] for x in names]).astype(jnp.int32))
+    number = {x: gathered_numbers[i] for i, x in enumerate(names)}
+    own, low, high = number["own"], number["low"], number["high"]
+
+    def pick(stacked, index, axis=0):
+        return lax.dynamic_index_in_dim(stacked, index, axis, keepdims=False, allow_negative_indices=False)
 
     def trade(mine, theirs):
         return (mine, lax.ppermute(theirs, "gate", swap))
@@ -460,16 +508,10 @@
             name="layout",
         )(jnp.full((1,), index, jnp.int32), in_hbm(weights))
 
-    win_b, rec_b = (lax.ppermute(by_gate(w, 1 - own, False)[0], "gate", swap) for w in (w_in, w_rec))
+    win_b, rec_b = (lax.ppermute(by_gate(w, number["other"], False)[0], "gate", swap) for w in (w_in, w_rec))
     (win_av, win_a), (rec_av, rec_a) = by_gate(w_in, own), by_gate(w_rec, own)
-    proj_a, proj_b = trade(pick(proj, own), pick(proj, 1 - own))
-    bias_a, bias_b = trade(pick(bias, own), pick(bias, 1 - own))
-
-    def pieces_of(pair):
-        split = [x.reshape(4, HALVES, width) for x in pair]
-        return jnp.transpose(jnp.stack(split), (0, 2, 1, 3)).reshape(PIECES, 1, 4 * width)
-
-    bias_p = pieces_of((bias_a, bias_b)).astype(F32)
+    proj_a, proj_b = trade(pick(proj, own), pick(proj, number["other"]))
+    bias_a, bias_b = trade(pick(bias, own), pick(bias, number["other"]))
 
     def cells_to_pieces(pair):
         both = jnp.stack(pair).reshape(QUARTERS, streams, HALVES, width)
@@ -489,18 +531,12 @@
     docs_c = state_c[stream_doc]
     start_h = pick(jnp.transpose(docs_h, (1, 0, 2)), own).astype(BF16)
     by_dir_c = jnp.transpose(docs_c, (1, 0, 2))
-    start_c = cells_to_pieces(trade(pick(by_dir_c, own), pick(by_dir_c, 1 - own)))
+    start_c = cells_to_pieces(trade(pick(by_dir_c, own), pick(by_dir_c, number["other"])))
 
     def at_step(step):
         near = jnp.array([step, step, max(step - 1, 0), min(step + 1, steps - 1)], jnp.int32)
         turned = jnp.array([step] + [steps - 1 - x for x in (step, max(step - 1, 0), min(step + 1, steps - 1))], jnp.int32)
         return jnp.where(own == 0, near, turned)
-
-    n_batch = lax.axis_size("batch")
-    spot = lax.axis_index("batch")
-    low, high = spot % 2, (spot // 2) % 2
-    near_swap = [(i, i ^ 1) for i in range(n_batch)]
-    far_swap = [(i, i ^ 2) for i in range(n_batch)]
 
     def swapped(array, pairs):
         return lax.ppermute(array, "batch", pairs)
@@ -511,12 +547,12 @@
         out_shape=(vmem(feats.shape, BF16), hbm(feats.shape, BF16)),
         in_specs=[SMEM, ANY],
         out_specs=[VMEM, ANY],
-        scratch_shapes=[pltpu.SemaphoreType.DMA((steps,)), pltpu.SemaphoreType.DMA],
+        scratch_shapes=[pltpu.SemaphoreType.DMA((2 * steps,))],
         compiler_params=params(1),
         name="order",
     )(turn, feats)
     feat_in = (swapped(feat_all, near_swap), swapped(feat_all, far_swap))
-    keep_v, bias_v, win_bv = place(keep, bias_p, win_b)
+    keep_v, bias_av, bias_bv, win_bv = place(keep, bias_a.astype(F32), bias_b.astype(F32), win_b)
     rec_bv, proj_av, proj_bv, start_hv, start_cv = place(rec_b, proj_a, proj_b, start_h, start_c)
 
     gates_shape, cell_shape = (PIECES, streams, 4 * width), (PIECES, streams, width)
@@ -524,11 +560,11 @@
     inflow = pl.pallas_call(
         inflow_kernel,
         out_shape=vmem(gates_shape, F32),
-        in_specs=[SMEM] + [VMEM] * 4,
+        in_specs=[VMEM] * 5,
         out_specs=VMEM,
         compiler_params=params(8),
         name="inflow",
-    )(turn, pinned(feats_v), pinned(bias_v), pinned(win_av), pinned(win_bv))
+    )(pinned(feats_v), pinned(bias_av), pinned(bias_bv), pinned(win_av), pinned(win_bv))
 
     def forward_call(first, step, part, peer, cell, inflow):
         return pl.pallas_call(
@@ -560,12 +596,12 @@
             hbm((steps, streams, depth), BF16),
             hbm((steps, streams, depth), F32),
         )
-        aliases = {11 + i: 1 + i for i in range(len(stacks))}
-        aliases.update({11 + len(stacks) + i: 7 + i for i in range(len(passing))})
+        aliases = {12 + i: 1 + i for i in range(len(stacks))}
+        aliases.update({12 + len(stacks) + i: 7 + i for i in range(len(passing))})
         inflow, *out = pl.pallas_call(
             functools.partial(between_kernel, not stacks, step == steps - 1, len(passing)),
             out_shape=(vmem(gates_shape, F32),) + shapes + tuple(hbm(x.shape, x.dtype) for x in passing),
-            in_specs=[SMEM] + [VMEM] * 10 + [ANY] * (len(stacks) + len(passing)),
+            in_specs=[SMEM] + [VMEM] * 11 + [ANY] * (len(stacks) + len(passing)),
             out_specs=[VMEM] + [ANY] * (6 + len(passing)),
             scratch_shapes=[pltpu.SemaphoreType.DMA((2 * PIECES + 4,))],
             input_output_aliases=aliases,
@@ -573,7 +609,7 @@
             cost_estimate=cost(2 * streams * depth * 8 * cells, 8 * depth * cells * 2),
             name="between",
         )(
-            at_step(step), pinned(feats_v), pinned(bias_v), pinned(win_av), pinned(win_bv),
+            at_step(step), pinned(feats_v), pinned(bias_av), pinned(bias_bv), pinned(win_av), pinned(win_bv),
             *(pinned(x) for x in fresh), *(in_hbm(x) for x in (*stacks, *passing)),
         )
         return inflow, tuple(out[:6]), tuple(out[6:])
@@ -716,32 +752,29 @@
         return jnp.stack([jnp.where(own == 0, mine, theirs), jnp.where(own == 0, theirs, mine)])
 
     def line_sum(chunks, axis, stride, count, first=None, gates={}):
-        here = (spot // stride) % count
-
-        def chunk(index):
-            return lax.dynamic_index_in_dim(chunks, jnp.clip(index, 0, count - 1), axis, keepdims=False)
+        def chunk(*name):
+            return pick(chunks, number[(stride, *name)], axis)
 
         def at(device):
             return (device // stride) % count
 
         if count == 2:
             pairs = [(i, i + stride if at(i) == 0 else i - stride) for i in range(n_batch)]
-            return (chunk(here).astype(F32) + swapped(chunk(1 - here), pairs).astype(F32)).astype(BF16)
+            return (chunk("here").astype(F32) + swapped(chunk("not_here"), pairs).astype(F32)).astype(BF16)
         ends = [(i, i + stride) for i in range(n_batch) if at(i) == 0]
         ends += [(i, i - stride) for i in range(n_batch) if at(i) == count - 1]
-        up = down = swapped(chunk(jnp.where(here == 0, count - 1, 0)) if first is None else first, ends)
+        up = down = swapped(chunk("begin") if first is None else first, ends)
         for slot in range(2, count):
             if slot in gates:
                 up, down = gates[slot](up, down)
-            rise = (chunk(here + count - slot).astype(F32) + up.astype(F32)).astype(BF16)
-            fall = (chunk(here - count + slot).astype(F32) + down.astype(F32)).astype(BF16)
+            rise = (chunk("rise", slot).astype(F32) + up.astype(F32)).astype(BF16)
+            fall = (chunk("fall", slot).astype(F32) + down.astype(F32)).astype(BF16)
             up = swapped(rise, [(i, i + stride) for i in range(n_batch) if at(i) < min(slot, count - 1)])
             down = swapped(fall, [(i, i - stride) for i in range(n_batch) if at(i) > max(count - 1 - slot, 0)])
         if count in gates:
             up, down = gates[count](up, down)
-        return (chunk(here).astype(F32) + up.astype(F32) + down.astype(F32)).astype(BF16)
-
-    line = n_batch // 2
+        return (chunk("here").astype(F32) + up.astype(F32) + down.astype(F32)).astype(BF16)
+
     share_rows = depth // n_batch
 
     def input_grad_of(dz):
@@ -766,21 +799,23 @@
             compiler_params=params(16),
             cost_estimate=cost(0, 0),
             name="input_grad",
-        )(turn, dz, in_hbm(win_a), in_hbm(win_b))
+        )(turn, in_hbm(dz), in_hbm(win_a), in_hbm(win_b))
 
     grad_proj = jnp.einsum("ptnc,tnk->pkc", mixed_all, raw_all, preferred_element_type=F32).astype(BF16)
     grad_proj = grad_proj.reshape(PIECES, line, 2, share_rows, width)
-    own_cells = cells // n_batch
-    bias_rows = jnp.sum(bias_sum, axis=1).reshape(QUARTERS, HALVES, 4, width)
-    bias_rows = jnp.transpose(bias_rows, (0, 2, 1, 3)).reshape(QUARTERS, 4, line, 2, own_cells)
-    bias_rows = jnp.transpose(bias_rows, (2, 3, 0, 1, 4)).reshape(line, 2, -1)
-    bias_rows = jnp.pad(bias_rows, ((0, 0), (0, 0), (0, PIECES * width - bias_rows.shape[2])))
-    bias_rows = jnp.transpose(bias_rows.reshape(line, 2, PIECES, 1, width), (2, 0, 1, 3, 4)).astype(BF16)
+    bias_rows = pl.pallas_call(
+        bias_kernel,
+        out_shape=jax.ShapeDtypeStruct((PIECES, 4, width), F32),
+        in_specs=[VMEM],
+        out_specs=VMEM,
+        compiler_params=params(1),
+        name="bias",
+    )(pinned(bias_sum))
+    bias_rows = jnp.broadcast_to(bias_rows[:, None, None].astype(BF16), (PIECES, line, 2, 4, width))
     grad_proj = jnp.concatenate([grad_proj, bias_rows], axis=3)
 
     def with_partner(grad):
-        mine = lax.dynamic_index_in_dim(grad, low, grad.ndim - 3, keepdims=False)
-        sent = lax.dynamic_index_in_dim(grad, 1 - low, grad.ndim - 3, keepdims=False)
+        mine, sent = (pick(grad, number[x], grad.ndim - 3) for x in ("low", "not_low"))
         taken = swapped(sent, near_swap)
         return sent, taken, (mine.astype(F32) + taken.astype(F32)).astype(BF16)
 
@@ -831,11 +866,10 @@
         )(pinned(left), pinned(right))
 
     near_parts, far_parts = zip(*exchanged)
-    begin = jnp.where(spot // 2 == 0, line - 1, 0)
     chunk_rows = 2 * share_rows if 2 * share_rows % 128 == 0 else 0
     near_left, near_right = gathered(near_all, feat_in[0], prev_in[0], near_parts[:-LATE])
     near_late = after((near_left, proj_sent, *far_parts[-LATE:]), *near_parts[-LATE:])
-    near_right, first = completed(jnp.full((1,), begin, jnp.int32), chunk_rows, near_left, near_right, near_late)
+    near_right, first = completed(jnp.full((1,), number["begin"], jnp.int32), chunk_rows, near_left, near_right, near_late)
     far_all, *far_parts = after((first,), far_all, *far_parts)
     far_left, far_right = gathered(far_all, feat_in[1], prev_in[1], far_parts[:-LATE])
     far_right, _ = completed(jnp.zeros((1,), jnp.int32), 0, far_left, far_right, far_parts[-LATE:])
@@ -859,7 +893,7 @@
     tokens = {}
 
     def second(up, down):
-        up, sent, tokens["dz"], proj_sum = after((), up, far, dz_all, proj_y)
+        up, sent, tokens["dz"], proj_sum = after((), up, far, dz_all, proj_y, free=2 * MIB)
         tokens["in"], tokens["rec"] = (with_partner(sent[i])[2] for i in range(2))
         tokens["proj"] = across_two(proj_sum)
         return up, up
@@ -867,14 +901,14 @@
     def third(up, down):
         dx = input_grad_of(tokens["dz"])
         up, down, tokens["dx"], in_sum, tokens["proj"], hidden, last_cell = after(
-            (), up, down, dx, tokens["in"], tokens["proj"], hidden_all, cell
+            (), up, down, dx, tokens["in"], tokens["proj"], hidden_all, cell, free=2 * MIB
         )
         tokens["in"] = across_two(in_sum)
         tokens["states"] = states_of(hidden, last_cell)
         return up, down
 
     def final(up, down):
-        up, down, tokens["in"], rec_sum = after(tokens["states"], up, down, tokens["in"], tokens["rec"])
+        up, down, tokens["in"], rec_sum = after(tokens["states"], up, down, tokens["in"], tokens["rec"], free=2 * MIB)
         tokens["rec"] = across_two(rec_sum)
         return up, down
 
@@ -884,14 +918,13 @@
     dx_all, (outputs, final_h, final_c) = tokens["dx"], tokens["states"]
     in_two, rec_two, proj_two = tokens["in"], tokens["rec"], tokens["proj"]
 
-    def halves_of(summed, index, pairs):
-        mine = lax.dynamic_index_in_dim(summed, index, 1, keepdims=False)
-        return mine, swapped(lax.dynamic_index_in_dim(summed, 1 - index, 1, keepdims=False), pairs)
-
-    near_pair = halves_of(near, low, near_swap)
-    far_pair = halves_of(jnp.stack([in_two, rec_two]), high, far_swap)
+    def halves_of(summed, name, pairs):
+        return pick(summed, number[name], 1), swapped(pick(summed, number["not_" + name], 1), pairs)
+
+    near_pair = halves_of(near, "low", near_swap)
+    far_pair = halves_of(jnp.stack([in_two, rec_two]), "high", far_swap)
     far_pair = [lax.ppermute(x, "gate", swap) for x in far_pair]
-    proj_mine, proj_theirs = halves_of(proj_two, high, far_swap)
+    proj_mine, proj_theirs = halves_of(proj_two, "high", far_swap)
     grad_proj = proj_mine.astype(F32) + proj_theirs.astype(F32)
     grad_shape = (2, share_rows, 4, cells)
     grad_w_in, grad_w_rec = pl.pallas_call(
@@ -906,23 +939,23 @@
     def home(mine, theirs):
         return by_direction(*trade(mine, theirs)).astype(F32)
 
-    shaped = grad_proj[:, share_rows].reshape(-1)[: QUARTERS * 4 * own_cells].reshape(QUARTERS, 4, own_cells)
+    own_cells = cells // n_batch
+    shaped = jnp.transpose(grad_proj[:, share_rows:].reshape(QUARTERS, HALVES, 4, width), (0, 2, 1, 3))
+    shaped = pick(shaped.reshape(QUARTERS, 4, n_batch, own_cells), number["spot"], 2)
     grad_bias = home(shaped[0], shaped[1])
     grad_proj = grad_proj[:, :share_rows].reshape(QUARTERS, HALVES, share_rows, width)
     grad_proj = jnp.transpose(grad_proj, (0, 1, 3, 2)).reshape(QUARTERS, cells, share_rows).astype(BF16)
     grad_proj = home(grad_proj[0], grad_proj[1])
 
-    half_cols = depth // 2
-    upper = rank // 2
-    keep_cols = lax.dynamic_slice_in_dim(dx_all, upper * half_cols, half_cols, 2)
-    send_cols = lax.dynamic_slice_in_dim(dx_all, (1 - upper) * half_cols, half_cols, 2).astype(BF16)
-    dx_half = keep_cols + lax.ppermute(send_cols, "gate", across).astype(F32)
-    up_half = lax.dynamic_slice_in_dim(ups, upper * half_cols, half_cols, 2).astype(F32)
-    dx_half = (dx_half + up_half).astype(BF16)
-    quarter_cols = half_cols // 2
-    mine = lax.dynamic_slice_in_dim(dx_half, own * quarter_cols, quarter_cols, 2)
-    theirs = lax.dynamic_slice_in_dim(dx_half, (1 - own) * quarter_cols, quarter_cols, 2)
-    dx_dirs = by_direction(*trade(mine, theirs))
+    def columns(array, name, size):
+        return lax.dynamic_slice_in_dim(array, number[name], size, 2, allow_negative_indices=False)
+
+    dx_half = columns(dx_all, "cols", half_cols)
+    dx_sent = columns(dx_all, "other_cols", half_cols).astype(BF16)
+    dx_half = dx_half + lax.ppermute(dx_sent, "gate", across).astype(F32)
+    dx_half = (dx_half + columns(ups, "cols", half_cols).astype(F32)).astype(BF16)
+    dx_half = dx_half.reshape(steps, streams, 2, quarter_cols)
+    dx_dirs = by_direction(*trade(pick(dx_half, own, 2), pick(dx_half, number["other"], 2)))
     input_grad = jnp.transpose(dx_dirs, (0, 2, 1, 3))
     return (outputs, input_grad, grad_w_in, grad_w_rec, grad_bias, grad_proj, final_h, final_c)
 

time: 587 us -> 605 us (1.031)
  other arithmetic: 34.6 us -> 74.8 us
  local copies, waits for them, and re-layouts: 77.8 us -> 61.8 us
  waiting for transfers between devices: 34.1 us -> 22.4 us
    unnamed x312 -> x205, local copies, waits for them, and re-layouts: 48.8 us -> 14.7 us
    concatenate x20, other arithmetic: 1.53 us -> 27.6 us  [aside_call(): jnp.concatenate([at_step(step), jnp.stack([jnp.int32(slot), low, high])])]
    ppermute x28, waiting for transfers between devices: 27.1 us -> 19.8 us  [swapped(): return lax.ppermute(array, 'batch', pairs)]
    squeeze x9 -> x11, local copies, waits for them, and re-layouts: 9.91 us -> 16 us  [the longest x10 15.5 us: pick(): lax.dynamic_index_in_dim(stacked, index, axis, keepdims=False, allow_nega...]
    convert_element_type x7 -> x8, other arithmetic: 12.5 us -> 18.1 us  [the longest x2 8.51 us: line_sum(): fall = (chunk('fall', slot).astype(F32) + down.astype(F32)).astype(BF16)]
  transfers between devices with their start and end apart: 80 -> 80, of which waited for: 34 -> 20; matrix products, arithmetic and copies ran while one was open for 12% -> 21% of each run, Pallas kernels for 53% -> 51%
where the time goes in v9:
time: 605 us; the launch traced here: 594 us
  Pallas kernels  338 us (56%)
  starting transfers between devices  87.9 us (15%)
  other arithmetic  74.8 us (12%)
  local copies, waits for them, and re-layouts  61.8 us (10%)
  waiting for transfers between devices  22.4 us (4%)
    pallas_call x20, Pallas kernels, backward_call(): pl.pallas_call(backward_kernel, out_shape=(vmem((streams, depth), BF16),...  62.6 us
    pallas_call x20, Pallas kernels, between_call(): pl.pallas_call(functools.partial(between_kernel, not stacks, step == step...  59.7 us
    pallas_call x20, Pallas kernels, forward_call(): pl.pallas_call(functools.partial(forward_kernel, first), out_shape=(vmem(...  56.7 us
    pallas_call x20, Pallas kernels, aside_call(): pl.pallas_call(functools.partial(aside_kernel, not stacks, step == 0, not...  55.9 us
    ppermute x28, starting transfers between devices, swapped(): return lax.ppermute(array, 'batch', pairs)  42.5 us
    ppermute x39, starting transfers between devices, body(): peer = lax.ppermute(part, 'gate', across)  42 us
    concatenate x20, other arithmetic, aside_call(): jnp.concatenate([at_step(step), jnp.stack([jnp.int32(slot), low, high])])  27.6 us
    pallas_call x4, Pallas kernels, by_gate(): pl.pallas_call(functools.partial(layout_kernel, keep), out_shape=kept + (...  23.3 us
  transfers between devices with their start and end apart: 80, of which 20 were waited for; matrix products, arithmetic and copies ran while one was open for 21% of the time, Pallas kernels for 51%

profile of v9, /device:TPU:8, one launch (start us, length us, event | category | flops | bytes accessed | tf_op | source)
XLA Modules:
  0.0 594.1 jit_solution(14059910898649412512)
XLA Ops:
  4.6 5.9 layout.4
  10.6 5.8 layout.6
  23.5 4.3 dynamic-slice_bitcast_fusion.2
  32.3 5.8 layout.5
  38.1 5.8 layout.7
  85.5 3.3 between.23
  177.5 3.3 between.36
  205.6 6.0 %turned.1 = (bf16[4,1024,512]{2,1,0:T(8,128)(2,1)S(1)}, bf16[4,1024,512]{2,1,0:T(8,128)(2,1)S(1)}, bf16[512,1024]{1,0:T(8,128)(2,1)S(1)}, bf16[512,1024]{1,0:T(8,128)(2,1)S(1)}) custom-call(bf16[4,512,1024]{2,1,0:T(8,128)(2,1)} %get-tuple-element.963.wa_ref, bf16[4,512,1024]{2,1,0:T(8,128)(2,1)} %collective-permute-done.2.refs_0_.wb_ref, ...), custom_call_target="tpu_custom_call" | custom-call | tf_op jit(solution)/shard_map/turned/pallas_call | solution.py:653
  213.9 3.2 backward_step.20
  264.1 3.3 backward_step.26
  386.1 3.7 backward_step.39
  395.5 3.6 bitcast_convert_fusion
  401.5 4.2 gather.14
  407.2 5.0 late.2
  413.5 4.2 gather.15
  419.5 11.4 %product.3 = bf16[2,512,2048]{2,1,0:T(8,128)(2,1)S(1)} custom-call(bf16[40,48,1024]{2,1,0:T(8,128)(2,1)S(1)} %get-tuple-element.1319.left_ref, bf16[40,48,2048]{2,1,0:T(8,128)(2,1)S(1)} %get-tuple-element.1323.right_ref), custom_call_target="tpu_custom_call" | custom-call | tf_op jit(solution)/shard_map/product/pallas_call | solution.py:858
  432.9 11.2 %product.2 = bf16[2,512,2048]{2,1,0:T(8,128)(2,1)S(1)} custom-call(bf16[40,48,1024]{2,1,0:T(8,128)(2,1)S(1)} %get-tuple-element.1294.refs_0_.left_ref, bf16[40,48,2048]{2,1,0:T(8,128)(2,1)S(1)} %get-tuple-element.1307.right_ref), custom_call_target="tpu_custom_call" | custom-call | tf_op jit(solution)/shard_map/product/pallas_call | solution.py:858
  446.3 4.8 collective-permute-start.63
  451.1 4.1 fusion.71
  457.8 3.4 fusion.3
  470.8 19.2 %input_grad.1.refs_2_ = f32[20,48,512]{2,1,0:T(8,128)S(1)} custom-call(s32[2]{0:T(128)S(1)} %broadcast_select_fusion.21.step_ref, bf16[4,20,48,2048]{3,2,1,0:T(8,128)(2,1)} %get-tuple-element.1326.dz_ref, bf16[4,512,1024]{2,1,0:T(8,128)(2,1)} %get-tuple-element.1327.wa_ref, bf16[4,512,1024]{2,1,0:T(8,128)(2,1)} %collective-permute-done.1.refs_3_.wb_ref), custom_call_target="tpu_custom_call" | custom-call | tf_op jit(solution)/shard_map/input_grad/pallas_call | solution.py:781
  494.9 3.4 collective-permute-start.77
  500.5 5.1 fusion.5
  508.8 3.7 collective-permute-start.69
  518.7 4.2 scatter_fusion.1
  530.4 3.7 select_bitcast_fusion.1
  537.7 3.8 fusion.refs_0_
  547.5 3.2 fusion.18
  552.6 3.6 constant_dynamic-slice_fusion.2
  556.4 11.7 %collective-permute-done.73 = bf16[2,64,2048]{2,1,0:T(8,128)(2,1)} collective-permute-done((bf16[2,64,2048]{2,1,0:T(8,128)(2,1)}, bf16[2,64,2048]{2,1,0:T(8,128)(2,1)}, u32[]{:S(2)}, u32[]{:S(2)}) %collective-permute-start.73) | collective-permute-done | bytes 524320 | tf_op jit(solution)/shard_map/ppermute | solution.py:542
  578.2 7.0 %collective-permute-done.75 = bf16[2,64,2048]{2,1,0:T(8,128)(2,1)S(1)} collective-permute-done((bf16[2,64,2048]{2,1,0:T(8,128)(2,1)S(1)}, bf16[2,64,2048]{2,1,0:T(8,128)(2,1)S(1)}, u32[]{:S(2)}, u32[]{:S(2)}) %collective-permute-start.75) | collective-permute-done | bytes 524320 | tf_op jit(solution)/shard_map/ppermute | solution.py:542
  590.1 3.5 assemble.1
  (562 shorter events, 414.1 us)
Async XLA Ops:
  10.6 40.6 %collective-permute-start.1 = (bf16[4,512,1024]{2,1,0:T(8,128)(2,1)}, bf16[4,512,1024]{2,1,0:T(8,128)(2,1)}, u32[]{:S(2)}, u32[]{:S(2)}) collective-permute-start(bf16[4,512,1024]{2,1,0:T(8,128)(2,1)} %layout.4), channel_id=1, source_target_pairs={{0,1},{1,0},{2,3},{3,2},{4,5},{5,4},{6,7},{7,6},{8,9},{9,8},{10,11... | collective-permute-start | bytes 12582920 | tf_op jit(solution)/shard_map/ppermute | solution.py:511
  16.5 39.6 %collective-permute-start.2 = (bf16[4,512,1024]{2,1,0:T(8,128)(2,1)}, bf16[4,512,1024]{2,1,0:T(8,128)(2,1)}, u32[]{:S(2)}, u32[]{:S(2)}) collective-permute-start(bf16[4,512,1024]{2,1,0:T(8,128)(2,1)} %layout.6), channel_id=1, source_target_pairs={{0,1},{1,0},{2,3},{3,2},{4,5},{5,4},{6,7},{7,6},{8,9},{9,8},{10,11... | collective-permute-start | bytes 12582920 | tf_op jit(solution)/shard_map/ppermute | solution.py:511
  19.0 28.7 %collective-permute-start = (bf16[4,1024]{1,0:T(4,128)(2,1)S(1)}, bf16[4,1024]{1,0:T(4,128)(2,1)S(1)}, u32[]{:S(2)}, u32[]{:S(2)}) collective-permute-start(bf16[4,1024]{1,0:T(4,128)(2,1)S(1)} %get-tuple-element.1398), channel_id=1, source_target_pairs={{0,1},{1,0},{2,3},{3,2},{4,5},{5,4},{6,7},{7,6},{8,9},{9,8},{10,11... | collective-permute-start | bytes 24584 | tf_op jit(solution)/shard_map/ppermute | solution.py:484
  23.0 26.9 %collective-permute-start.4 = (f32[48,1024]{1,0:T(8,128)}, f32[48,1024]{1,0:T(8,128)S(1)}, u32[]{:S(2)}, u32[]{:S(2)}) collective-permute-start(f32[48,1024]{1,0:T(8,128)} %bitcast.238), channel_id=1, source_target_pairs={{0,1},{1,0},{2,3},{3,2},{4,5},{5,4},{6,7},{7,6},{8,9},{9,8},{10,11... | collective-permute-start | bytes 589832 | tf_op jit(solution)/shard_map/ppermute | solution.py:484
  27.8 28.3 %collective-permute-start.3 = (bf16[1024,512]{1,0:T(8,128)(2,1)}, bf16[1024,512]{1,0:T(8,128)(2,1)S(1)}, u32[]{:S(2)}, u32[]{:S(2)}) collective-permute-start(bf16[1024,512]{1,0:T(8,128)(2,1)} %get-tuple-element.1374), channel_id=1, source_target_pairs={{0,1},{1,0},{2,3},{3,2},{4,5},{5,4},{6,7},{7,6},{8,9},{9,8},{10,11... | collective-permute-start | bytes 3145736 | tf_op jit(solution)/shard_map/ppermute | solution.py:484
  47.7 108.3 %collective-permute-start.19 = (bf16[20,48,512]{2,1,0:T(8,128)(2,1)}, bf16[20,48,512]{2,1,0:T(8,128)(2,1)}, u32[]{:S(2)}, u32[]{:S(2)}) collective-permute-start(bf16[20,48,512]{2,1,0:T(8,128)(2,1)} %get-tuple-element.676.refs_0_), channel_id=1, source_target_pairs={{0,4},{4,0},{8,12},{12,8},{16,20},{20,16},{24,28},{28,24},{1,5},{5... | collective-permute-start | bytes 2949128 | tf_op jit(solution)/shard_map/ppermute | solution.py:542
  49.9 106.1 %collective-permute-start.20 = (bf16[20,48,512]{2,1,0:T(8,128)(2,1)}, bf16[20,48,512]{2,1,0:T(8,128)(2,1)}, u32[]{:S(2)}, u32[]{:S(2)}) collective-permute-start(bf16[20,48,512]{2,1,0:T(8,128)(2,1)} %get-tuple-element.676.refs_0_), channel_id=1, source_target_pairs={{0,8},{4,12},{8,0},{12,4},{16,24},{20,28},{24,16},{28,20},{1,9},{5... | collective-permute-start | bytes 2949128 | tf_op jit(solution)/shard_map/ppermute | solution.py:542
  200.7 69.2 %collective-permute-start.33 = (bf16[20,48,512]{2,1,0:T(8,128)(2,1)}, bf16[20,48,512]{2,1,0:T(8,128)(2,1)S(1)}, u32[]{:S(2)}, u32[]{:S(2)}) collective-permute-start(bf16[20,48,512]{2,1,0:T(8,128)(2,1)} %get-tuple-element.961.refs_1_), channel_id=1, source_target_pairs={{0,4},{4,0},{8,12},{12,8},{16,20},{20,16},{24,28},{28,24},{1,5},{5... | collective-permute-start | bytes 2949128 | tf_op jit(solution)/shard_map/ppermute | solution.py:542
  201.3 68.6 %collective-permute-start.34 = (bf16[20,48,512]{2,1,0:T(8,128)(2,1)}, bf16[20,48,512]{2,1,0:T(8,128)(2,1)S(1)}, u32[]{:S(2)}, u32[]{:S(2)}) collective-permute-start(bf16[20,48,512]{2,1,0:T(8,128)(2,1)} %get-tuple-element.961.refs_1_), channel_id=1, source_target_pairs={{0,8},{4,12},{8,0},{12,4},{16,24},{20,28},{24,16},{28,20},{1,9},{5... | collective-permute-start | bytes 2949128 | tf_op jit(solution)/shard_map/ppermute | solution.py:542
  277.2 56.6 %collective-permute-start.43 = (bf16[7,48,2048]{2,1,0:T(8,128)(2,1)}, bf16[7,48,2048]{2,1,0:T(8,128)(2,1)S(1)}, u32[]{:S(2)}, u32[]{:S(2)}) collective-permute-start(bf16[7,48,2048]{2,1,0:T(8,128)(2,1)} %get-tuple-element.1191), channel_id=1, source_target_pairs={{0,4},{4,0},{8,12},{12,8},{16,20},{20,16},{24,28},{28,24},{1,5},{5... | collective-permute-start | bytes 4128776 | tf_op jit(solution)/shard_map/ppermute | solution.py:542
  278.8 55.0 %collective-permute-start.44 = (bf16[7,48,2048]{2,1,0:T(8,128)(2,1)}, bf16[7,48,2048]{2,1,0:T(8,128)(2,1)S(1)}, u32[]{:S(2)}, u32[]{:S(2)}) collective-permute-start(bf16[7,48,2048]{2,1,0:T(8,128)(2,1)} %get-tuple-element.1192), channel_id=1, source_target_pairs={{0,8},{4,12},{8,0},{12,4},{16,24},{20,28},{24,16},{28,20},{1,9},{5... | collective-permute-start | bytes 4128776 | tf_op jit(solution)/shard_map/ppermute | solution.py:542
  329.3 51.2 %collective-permute-start.50 = (bf16[6,48,2048]{2,1,0:T(8,128)(2,1)}, bf16[6,48,2048]{2,1,0:T(8,128)(2,1)S(1)}, u32[]{:S(2)}, u32[]{:S(2)}) collective-permute-start(bf16[6,48,2048]{2,1,0:T(8,128)(2,1)} %get-tuple-element.1271), channel_id=1, source_target_pairs={{0,4},{4,0},{8,12},{12,8},{16,20},{20,16},{24,28},{28,24},{1,5},{5... | collective-permute-start | bytes 3538952 | tf_op jit(solution)/shard_map/ppermute | solution.py:542
  329.9 52.5 %collective-permute-start.51 = (bf16[6,48,2048]{2,1,0:T(8,128)(2,1)}, bf16[6,48,2048]{2,1,0:T(8,128)(2,1)S(1)}, u32[]{:S(2)}, u32[]{:S(2)}) collective-permute-start(bf16[6,48,2048]{2,1,0:T(8,128)(2,1)} %get-tuple-element.1272), channel_id=1, source_target_pairs={{0,8},{4,12},{8,0},{12,4},{16,24},{20,28},{24,16},{28,20},{1,9},{5... | collective-permute-start | bytes 3538952 | tf_op jit(solution)/shard_map/ppermute | solution.py:542
  357.9 32.0 %collective-permute-start.52 = (bf16[3,48,2048]{2,1,0:T(8,128)(2,1)}, bf16[3,48,2048]{2,1,0:T(8,128)(2,1)S(1)}, u32[]{:S(2)}, u32[]{:S(2)}) collective-permute-start(bf16[3,48,2048]{2,1,0:T(8,128)(2,1)} %get-tuple-element.1288), channel_id=1, source_target_pairs={{0,4},{4,0},{8,12},{12,8},{16,20},{20,16},{24,28},{28,24},{1,5},{5... | collective-permute-start | bytes 1769480 | tf_op jit(solution)/shard_map/ppermute | solution.py:542
  359.5 30.4 %collective-permute-start.53 = (bf16[3,48,2048]{2,1,0:T(8,128)(2,1)}, bf16[3,48,2048]{2,1,0:T(8,128)(2,1)S(1)}, u32[]{:S(2)}, u32[]{:S(2)}) collective-permute-start(bf16[3,48,2048]{2,1,0:T(8,128)(2,1)} %get-tuple-element.1289), channel_id=1, source_target_pairs={{0,8},{4,12},{8,0},{12,4},{16,24},{20,28},{24,16},{28,20},{1,9},{5... | collective-permute-start | bytes 1769480 | tf_op jit(solution)/shard_map/ppermute | solution.py:542
  380.5 25.2 %collective-permute-start.54 = (bf16[2,48,2048]{2,1,0:T(8,128)(2,1)}, bf16[2,48,2048]{2,1,0:T(8,128)(2,1)S(1)}, u32[]{:S(2)}, u32[]{:S(2)}) collective-permute-start(bf16[2,48,2048]{2,1,0:T(8,128)(2,1)} %get-tuple-element.1301), channel_id=1, source_target_pairs={{0,8},{4,12},{8,0},{12,4},{16,24},{20,28},{24,16},{28,20},{1,9},{5... | collective-permute-start | bytes 1179656 | tf_op jit(solution)/shard_map/ppermute | solution.py:542
  382.3 23.3 %collective-permute-start.56 = (bf16[2,48,2048]{2,1,0:T(8,128)(2,1)}, bf16[2,48,2048]{2,1,0:T(8,128)(2,1)S(1)}, u32[]{:S(2)}, u32[]{:S(2)}) collective-permute-start(bf16[2,48,2048]{2,1,0:T(8,128)(2,1)} %get-tuple-element.1303), channel_id=1, source_target_pairs={{0,4},{4,0},{8,12},{12,8},{16,20},{20,16},{24,28},{28,24},{1,5},{5... | collective-permute-start | bytes 1179656 | tf_op jit(solution)/shard_map/ppermute | solution.py:542
  400.4 43.7 %collective-permute-start.59 = (bf16[4,4,68,512]{3,1,2,0:T(4,128)(2,1)S(1)}, bf16[4,4,68,512]{3,1,2,0:T(4,128)(2,1)S(1)}, u32[]{:S(2)}, u32[]{:S(2)}) collective-permute-start(bf16[4,4,68,512]{3,1,2,0:T(4,128)(2,1)S(1)} %copy.531), channel_id=1, source_target_pairs={{0,4},{4,0},{8,12},{12,8},{16,20},{20,16},{24,28},{28,24},{1,5},{5... | collective-permute-start | bytes 3342344 | tf_op jit(solution)/shard_map/ppermute | solution.py:542
  412.2 32.9 %collective-permute-start.58 = (bf16[2,2,64,2048]{3,2,1,0:T(8,128)(2,1)S(1)}, bf16[2,2,64,2048]{3,2,1,0:T(8,128)(2,1)S(1)}, u32[]{:S(2)}, u32[]{:S(2)}) collective-permute-start(bf16[2,2,64,2048]{3,2,1,0:T(8,128)(2,1)S(1)} %bitcast.253), channel_id=1, source_target_pairs={{0,8},{4,12},{24,16},{28,20},{1,9},{5,13},{25,17},{29,21},{2,10},{... | collective-permute-start | bytes 3145736 | tf_op jit(solution)/shard_map/ppermute | solution.py:542
  446.3 43.7 %collective-permute-start.63 = (bf16[4,2,68,512]{3,0,2,1:T(4,128)(2,1)S(1)}, bf16[4,2,68,512]{3,0,2,1:T(4,128)(2,1)S(1)}, u32[]{:S(2)}, u32[]{:S(2)}) collective-permute-start(bf16[4,2,68,512]{3,0,2,1:T(4,128)(2,1)S(1)} %copy.536), channel_id=1, source_target_pairs={{0,16},{4,20},{8,24},{12,28},{16,0},{20,4},{24,8},{28,12},{1,17},{... | collective-permute-start | bytes 1671176 | tf_op jit(solution)/shard_map/ppermute | solution.py:542
  457.0 34.0 %collective-permute-start.62 = (bf16[4,64,2048]{2,1,0:T(8,128)(2,1)}, bf16[4,64,2048]{2,1,0:T(8,128)(2,1)}, u32[]{:S(2)}, u32[]{:S(2)}) collective-permute-start(bf16[4,64,2048]{2,1,0:T(8,128)(2,1)} %dynamic-slice_bitcast_fusion.1), channel_id=1, source_target_pairs={{0,4},{4,0},{8,12},{12,8},{16,20},{20,16},{24,28},{28,24},{1,5},{5... | collective-permute-start | bytes 3145736 | tf_op jit(solution)/shard_map/ppermute | solution.py:542
  461.1 32.1 %collective-permute-start.60 = (bf16[2,2,64,2048]{3,2,1,0:T(8,128)(2,1)}, bf16[2,2,64,2048]{3,2,1,0:T(8,128)(2,1)}, u32[]{:S(2)}, u32[]{:S(2)}) collective-permute-start(bf16[2,2,64,2048]{3,2,1,0:T(8,128)(2,1)} %get-tuple-element.1369), channel_id=1, source_target_pairs={{0,8},{4,12},{8,16},{12,20},{1,9},{5,13},{9,17},{13,21},{2,10},{6,... | collective-permute-start | bytes 3145736 | tf_op jit(solution)/shard_map/ppermute | solution.py:542
  463.0 30.2 %collective-permute-start.61 = (bf16[2,2,64,2048]{3,2,1,0:T(8,128)(2,1)}, bf16[2,2,64,2048]{3,2,1,0:T(8,128)(2,1)}, u32[]{:S(2)}, u32[]{:S(2)}) collective-permute-start(bf16[2,2,64,2048]{3,2,1,0:T(8,128)(2,1)} %get-tuple-element.1368), channel_id=1, source_target_pairs={{16,8},{20,12},{24,16},{28,20},{17,9},{21,13},{25,17},{29,21},{18,... | collective-permute-start | bytes 3145736 | tf_op jit(solution)/shard_map/ppermute | solution.py:542
  469.5 43.2 %collective-permute-start.71 = (bf16[4,64,2048]{2,1,0:T(8,128)(2,1)S(1)}, bf16[4,64,2048]{2,1,0:T(8,128)(2,1)S(1)}, u32[]{:S(2)}, u32[]{:S(2)}) collective-permute-start(bf16[4,64,2048]{2,1,0:T(8,128)(2,1)S(1)} %dynamic-slice_bitcast_fusion), channel_id=1, source_target_pairs={{0,4},{4,0},{8,12},{12,8},{16,20},{20,16},{24,28},{28,24},{1,5},{5... | collective-permute-start | bytes 3145736 | tf_op jit(solution)/shard_map/ppermute | solution.py:542
  494.9 28.1 %collective-permute-start.77 = (bf16[4,68,512]{2,1,0:T(8,128)(2,1)}, bf16[4,68,512]{2,1,0:T(8,128)(2,1)}, u32[]{:S(2)}, u32[]{:S(2)}) collective-permute-start(bf16[4,68,512]{2,1,0:T(8,128)(2,1)} %dynamic-slice_bitcast_fusion.11), channel_id=1, source_target_pairs={{0,8},{4,12},{8,0},{12,4},{16,24},{20,28},{24,16},{28,20},{1,9},{5... | collective-permute-start | bytes 835592 | tf_op jit(solution)/shard_map/ppermute | solution.py:542
  499.8 28.1 %collective-permute-start.70 = (bf16[2,64,2048]{2,1,0:T(8,128)(2,1)}, bf16[2,64,2048]{2,1,0:T(8,128)(2,1)}, u32[]{:S(2)}, u32[]{:S(2)}) collective-permute-start(bf16[2,64,2048]{2,1,0:T(8,128)(2,1)} %dynamic-slice_bitcast_fusion.10), channel_id=1, source_target_pairs={{0,16},{4,20},{8,24},{12,28},{16,0},{20,4},{24,8},{28,12},{1,17},{... | collective-permute-start | bytes 1572872 | tf_op jit(solution)/shard_map/ppermute | solution.py:542
  505.7 35.8 %collective-permute-start.68 = (bf16[2,2,64,2048]{3,2,1,0:T(8,128)(2,1)}, bf16[2,2,64,2048]{3,2,1,0:T(8,128)(2,1)}, u32[]{:S(2)}, u32[]{:S(2)}) collective-permute-start(bf16[2,2,64,2048]{3,2,1,0:T(8,128)(2,1)} %get-tuple-element.1373), channel_id=1, source_target_pairs={{0,8},{4,12},{8,16},{12,20},{16,24},{20,28},{1,9},{5,13},{9,17},{1... | collective-permute-start | bytes 3145736 | tf_op jit(solution)/shard_map/ppermute | solution.py:542
  508.8 32.7 %collective-permute-start.69 = (bf16[2,2,64,2048]{3,2,1,0:T(8,128)(2,1)}, bf16[2,2,64,2048]{3,2,1,0:T(8,128)(2,1)}, u32[]{:S(2)}, u32[]{:S(2)}) collective-permute-start(bf16[2,2,64,2048]{3,2,1,0:T(8,128)(2,1)} %get-tuple-element.1372), channel_id=1, source_target_pairs={{8,0},{12,4},{16,8},{20,12},{24,16},{28,20},{9,1},{13,5},{17,9},{2... | collective-permute-start | bytes 3145736 | tf_op jit(solution)/shard_map/ppermute | solution.py:542
  523.0 24.5 %collective-permute-start.65 = (bf16[20,48,256]{2,1,0:T(8,128)(2,1)}, bf16[20,48,256]{2,1,0:T(8,128)(2,1)}, u32[]{:S(2)}, u32[]{:S(2)}) collective-permute-start(bf16[20,48,256]{2,1,0:T(8,128)(2,1)} %dynamic-slice_convert_fusion), channel_id=1, source_target_pairs={{0,2},{1,3},{2,0},{3,1},{4,6},{5,7},{6,4},{7,5},{8,10},{9,11},{10,... | collective-permute-start | bytes 1474568 | tf_op jit(solution)/shard_map/ppermute | solution.py:955
  527.9 57.3 %collective-permute-start.79 = (bf16[1024,64]{0,1:T(8,128)(2,1)}, bf16[1024,64]{0,1:T(8,128)(2,1)}, u32[]{:S(2)}, u32[]{:S(2)}) collective-permute-start(bf16[1024,64]{0,1:T(8,128)(2,1)} %bitcast.160), channel_id=1, source_target_pairs={{0,1},{1,0},{2,3},{3,2},{4,5},{5,4},{6,7},{7,6},{8,9},{9,8},{10,11... | collective-permute-start | bytes 393224 | tf_op jit(solution)/shard_map/ppermute | solution.py:484
  544.0 24.1 %collective-permute-start.73 = (bf16[2,64,2048]{2,1,0:T(8,128)(2,1)}, bf16[2,64,2048]{2,1,0:T(8,128)(2,1)}, u32[]{:S(2)}, u32[]{:S(2)}) collective-permute-start(bf16[2,64,2048]{2,1,0:T(8,128)(2,1)} %dynamic-slice_bitcast_fusion.7), channel_id=1, source_target_pairs={{0,16},{4,20},{8,24},{12,28},{16,0},{20,4},{24,8},{28,12},{1,17},{... | collective-permute-start | bytes 1572872 | tf_op jit(solution)/shard_map/ppermute | solution.py:542
  556.3 30.7 %collective-permute-start.66 = (bf16[20,48,128]{2,1,0:T(8,128)(2,1)S(1)}, bf16[20,48,128]{2,1,0:T(8,128)(2,1)S(1)}, u32[]{:S(2)}, u32[]{:S(2)}) collective-permute-start(bf16[20,48,128]{2,1,0:T(8,128)(2,1)S(1)} %bitcast.268), channel_id=1, source_target_pairs={{0,1},{1,0},{2,3},{3,2},{4,5},{5,4},{6,7},{7,6},{8,9},{9,8},{10,11... | collective-permute-start | bytes 737288 | tf_op jit(solution)/shard_map/ppermute | solution.py:484
  (146 other events, 760.7 us)

commit v10 on v9

--- a/solution.py
+++ b/solution.py
@@ -474,8 +474,9 @@
         out_specs=SMEM,
         name="numbers",
     )(jnp.stack([place_numbers[x] for x in names]).astype(jnp.int32))
-    number = {x: gathered_numbers[i] for i, x in enumerate(names)}
+    number = {x: place_numbers[x].astype(jnp.int32) for x in names}
     own, low, high = number["own"], number["low"], number["high"]
+    which = {x: lax.slice_in_dim(gathered_numbers, names.index(x), names.index(x) + 1) for x in ("own", "other")}
 
     def pick(stacked, index, axis=0):
         return lax.dynamic_index_in_dim(stacked, index, axis, keepdims=False, allow_negative_indices=False)
@@ -506,10 +507,10 @@
             ],
             compiler_params=params(8),
             name="layout",
-        )(jnp.full((1,), index, jnp.int32), in_hbm(weights))
-
-    win_b, rec_b = (lax.ppermute(by_gate(w, number["other"], False)[0], "gate", swap) for w in (w_in, w_rec))
-    (win_av, win_a), (rec_av, rec_a) = by_gate(w_in, own), by_gate(w_rec, own)
+        )(index, in_hbm(weights))
+
+    win_b, rec_b = (lax.ppermute(by_gate(w, which["other"], False)[0], "gate", swap) for w in (w_in, w_rec))
+    (win_av, win_a), (rec_av, rec_a) = by_gate(w_in, which["own"]), by_gate(w_rec, which["own"])
     proj_a, proj_b = trade(pick(proj, own), pick(proj, number["other"]))
     bias_a, bias_b = trade(pick(bias, own), pick(bias, number["other"]))
 
@@ -733,11 +734,13 @@
                 sides = after((part,), *sides) if step else sides
                 pending.append((due, (swapped(sides[0], near_swap), swapped(sides[1], far_swap))))
                 ready = None
-            passing = pending.pop(0)[1] if pending and pending[0][0] >= step else ()
+            passing = ()
+            while pending and pending[0][0] >= step:
+                passing += pending.pop(0)[1]
             saved, stacks, sends, passed = aside_call(
                 step, step - (top - slots), slots, dz, raw, stacks, sends, passing
             )
-            arrived += [passed] if passed else []
+            arrived += [passed[i : i + 2] for i in range(0, len(passed), 2)]
             carry = (part, peer, grad, bias_sum, saved, stacks)
         top -= slots
         ready = (max(top - 1 - (3 * slots + 3) // 4, 0 if slots > 2 else -1), sends)

time: 605 us -> 560 us (0.926)
  other arithmetic: 74.8 us -> 34.5 us
  waiting for transfers between devices: 22.4 us -> 37.1 us
  local copies, waits for them, and re-layouts: 61.8 us -> 49.6 us
    concatenate x20, other arithmetic: 27.6 us -> 1.53 us  [aside_call(): jnp.concatenate([at_step(step), jnp.stack([jnp.int32(slot), low, high])])]
    ppermute x28, waiting for transfers between devices: 19.8 us -> 30.2 us  [swapped(): return lax.ppermute(array, 'batch', pairs)]
    squeeze x10, local copies, waits for them, and re-layouts: 15.5 us -> 9.08 us  [pick(): lax.dynamic_index_in_dim(stacked, index, axis, keepdims=False, allow_nega...]
  transfers between devices with their start and end apart: 80 -> 80, of which waited for: 20 -> 37; matrix products, arithmetic and copies ran while one was open for 21% -> 14% of each run, Pallas kernels for 51% -> 55%
where the time goes in v10:
time: 560 us; the launch traced here: 549 us
  Pallas kernels  337 us (60%)
  starting transfers between devices  84.1 us (15%)
  local copies, waits for them, and re-layouts  49.6 us (9%)
  waiting for transfers between devices  37.1 us (7%)
  other arithmetic  34.5 us (6%)
    pallas_call x20, Pallas kernels, backward_call(): pl.pallas_call(backward_kernel, out_shape=(vmem((streams, depth), BF16),...  62.8 us
    pallas_call x20, Pallas kernels, between_call(): pl.pallas_call(functools.partial(between_kernel, not stacks, step == step...  59.3 us
    pallas_call x20, Pallas kernels, forward_call(): pl.pallas_call(functools.partial(forward_kernel, first), out_shape=(vmem(...  56.9 us
    pallas_call x20, Pallas kernels, aside_call(): pl.pallas_call(functools.partial(aside_kernel, not stacks, step == 0, not...  56 us
    ppermute x39, starting transfers between devices, body(): peer = lax.ppermute(part, 'gate', across)  42.1 us
    ppermute x28, starting transfers between devices, swapped(): return lax.ppermute(array, 'batch', pairs)  38.6 us
    ppermute x28, waiting for transfers between devices, swapped(): return lax.ppermute(array, 'batch', pairs)  30.2 us
    pallas_call x4, Pallas kernels, by_gate(): pl.pallas_call(functools.partial(layout_kernel, keep), out_shape=kept + (...  23.3 us
  transfers between devices with their start and end apart: 80, of which 37 were waited for; matrix products, arithmetic and copies ran while one was open for 14% of the time, Pallas kernels for 55%

profile of v10, /device:TPU:8, one launch (start us, length us, event | category | flops | bytes accessed | tf_op | source)
XLA Modules:
  0.0 549.3 jit_solution(17588526574400840560)
XLA Ops:
  3.9 5.9 %layout.4 = bf16[4,512,1024]{2,1,0:T(8,128)(2,1)} custom-call(s32[1]{0:T(128)} %get-tuple-element.1401.which_ref, bf16[2,512,4,1024]{3,2,1,0:T(4,128)(2,1)} %w_ref.5), custom_call_target="tpu_custom_call" | custom-call | tf_op jit(solution)/shard_map/layout/pallas_call | solution.py:497
  9.9 5.8 %layout.6 = bf16[4,512,1024]{2,1,0:T(8,128)(2,1)} custom-call(s32[1]{0:T(128)} %get-tuple-element.1401.which_ref, bf16[2,512,4,1024]{3,2,1,0:T(4,128)(2,1)} %w_ref.7), custom_call_target="tpu_custom_call" | custom-call | tf_op jit(solution)/shard_map/layout/pallas_call | solution.py:497
  25.7 5.8 %layout.5 = (bf16[4,512,1024]{2,1,0:T(8,128)(2,1)S(1)}, bf16[4,512,1024]{2,1,0:T(8,128)(2,1)}) custom-call(s32[1]{0:T(128)} %get-tuple-element.1400.which_ref, bf16[2,512,4,1024]{3,2,1,0:T(4,128)(2,1)} %w_ref.5), custom_call_target="tpu_custom_call" | custom-call | tf_op jit(solution)/shard_map/layout/pallas_call | solution.py:497
  31.5 5.8 %layout.7 = (bf16[4,512,1024]{2,1,0:T(8,128)(2,1)S(1)}, bf16[4,512,1024]{2,1,0:T(8,128)(2,1)}) custom-call(s32[1]{0:T(128)} %get-tuple-element.1400.which_ref, bf16[2,512,4,1024]{3,2,1,0:T(4,128)(2,1)} %w_ref.7), custom_call_target="tpu_custom_call" | custom-call | tf_op jit(solution)/shard_map/layout/pallas_call | solution.py:497
  78.8 3.1 between.23
  109.9 3.2 forward_step.28
  149.3 3.2 between.33
  170.8 3.1 between.36
  198.2 6.0 %turned.1 = (bf16[4,1024,512]{2,1,0:T(8,128)(2,1)S(1)}, bf16[4,1024,512]{2,1,0:T(8,128)(2,1)S(1)}, bf16[512,1024]{1,0:T(8,128)(2,1)S(1)}, bf16[512,1024]{1,0:T(8,128)(2,1)S(1)}) custom-call(bf16[4,512,1024]{2,1,0:T(8,128)(2,1)} %get-tuple-element.963.wa_ref, bf16[4,512,1024]{2,1,0:T(8,128)(2,1)} %collective-permute-done.2.refs_0_.wb_ref, ...), custom_call_target="tpu_custom_call" | custom-call | tf_op jit(solution)/shard_map/turned/pallas_call | solution.py:654
  206.5 3.4 backward_step.20
  258.9 3.1 backward_step.27
  305.0 3.5 backward_step.33
  316.0 3.1 backward_step.34
  357.0 3.7 backward_step.39
  366.3 3.6 bitcast_convert_fusion
  371.8 4.2 gather.14
  378.0 4.3 late.2
  383.7 4.2 gather.15
  389.6 11.2 %product.3 = bf16[2,512,2048]{2,1,0:T(8,128)(2,1)S(1)} custom-call(bf16[40,48,1024]{2,1,0:T(8,128)(2,1)S(1)} %get-tuple-element.1319.left_ref, bf16[40,48,2048]{2,1,0:T(8,128)(2,1)S(1)} %get-tuple-element.1323.right_ref), custom_call_target="tpu_custom_call" | custom-call | tf_op jit(solution)/shard_map/product/pallas_call | solution.py:861
  402.9 11.2 %product.2 = bf16[2,512,2048]{2,1,0:T(8,128)(2,1)S(1)} custom-call(bf16[40,48,1024]{2,1,0:T(8,128)(2,1)S(1)} %get-tuple-element.1294.refs_0_.left_ref, bf16[40,48,2048]{2,1,0:T(8,128)(2,1)S(1)} %get-tuple-element.1307.right_ref), custom_call_target="tpu_custom_call" | custom-call | tf_op jit(solution)/shard_map/product/pallas_call | solution.py:861
  415.0 4.0 collective-permute-start.63
  418.9 4.1 fusion.71
  433.3 19.2 %input_grad.1.refs_2_ = f32[20,48,512]{2,1,0:T(8,128)S(1)} custom-call(s32[2]{0:T(128)S(1)} %broadcast_select_fusion.21.step_ref, bf16[4,20,48,2048]{3,2,1,0:T(8,128)(2,1)} %get-tuple-element.1326.dz_ref, bf16[4,512,1024]{2,1,0:T(8,128)(2,1)} %get-tuple-element.1327.wa_ref, bf16[4,512,1024]{2,1,0:T(8,128)(2,1)} %collective-permute-done.1.refs_3_.wb_ref), custom_call_target="tpu_custom_call" | custom-call | tf_op jit(solution)/shard_map/input_grad/pallas_call | solution.py:784
  455.7 4.6 collective-permute-done.61.refs_1_
  463.5 3.9 fusion.5
  467.4 3.8 collective-permute-start.68
  479.1 4.2 scatter_fusion.1
  488.8 3.7 select_bitcast_fusion.1
  496.1 3.8 fusion.refs_0_
  510.6 15.5 %collective-permute-done.73 = bf16[2,64,2048]{2,1,0:T(8,128)(2,1)} collective-permute-done((bf16[2,64,2048]{2,1,0:T(8,128)(2,1)}, bf16[2,64,2048]{2,1,0:T(8,128)(2,1)}, u32[]{:S(2)}, u32[]{:S(2)}) %collective-permute-start.73) | collective-permute-done | bytes 524320 | tf_op jit(solution)/shard_map/ppermute | solution.py:543
  533.3 7.6 %collective-permute-done.75 = bf16[2,64,2048]{2,1,0:T(8,128)(2,1)S(1)} collective-permute-done((bf16[2,64,2048]{2,1,0:T(8,128)(2,1)S(1)}, bf16[2,64,2048]{2,1,0:T(8,128)(2,1)S(1)}, u32[]{:S(2)}, u32[]{:S(2)}) %collective-permute-start.75) | collective-permute-done | bytes 524320 | tf_op jit(solution)/shard_map/ppermute | solution.py:543
  545.6 3.5 assemble.1
  (562 shorter events, 370.9 us)
Async XLA Ops:
  9.8 34.7 %collective-permute-start.1 = (bf16[4,512,1024]{2,1,0:T(8,128)(2,1)}, bf16[4,512,1024]{2,1,0:T(8,128)(2,1)}, u32[]{:S(2)}, u32[]{:S(2)}) collective-permute-start(bf16[4,512,1024]{2,1,0:T(8,128)(2,1)} %layout.4), channel_id=1, source_target_pairs={{0,1},{1,0},{2,3},{3,2},{4,5},{5,4},{6,7},{7,6},{8,9},{9,8},{10,11... | collective-permute-start | bytes 12582920 | tf_op jit(solution)/shard_map/ppermute | solution.py:512
  15.7 33.8 %collective-permute-start.2 = (bf16[4,512,1024]{2,1,0:T(8,128)(2,1)}, bf16[4,512,1024]{2,1,0:T(8,128)(2,1)}, u32[]{:S(2)}, u32[]{:S(2)}) collective-permute-start(bf16[4,512,1024]{2,1,0:T(8,128)(2,1)} %layout.6), channel_id=1, source_target_pairs={{0,1},{1,0},{2,3},{3,2},{4,5},{5,4},{6,7},{7,6},{8,9},{9,8},{10,11... | collective-permute-start | bytes 12582920 | tf_op jit(solution)/shard_map/ppermute | solution.py:512
  16.9 24.2 %collective-permute-start = (bf16[4,1024]{1,0:T(4,128)(2,1)S(1)}, bf16[4,1024]{1,0:T(4,128)(2,1)S(1)}, u32[]{:S(2)}, u32[]{:S(2)}) collective-permute-start(bf16[4,1024]{1,0:T(4,128)(2,1)S(1)} %get-tuple-element.1398), channel_id=1, source_target_pairs={{0,1},{1,0},{2,3},{3,2},{4,5},{5,4},{6,7},{7,6},{8,9},{9,8},{10,11... | collective-permute-start | bytes 24584 | tf_op jit(solution)/shard_map/ppermute | solution.py:485
  19.6 23.7 %collective-permute-start.4 = (f32[48,1024]{1,0:T(8,128)}, f32[48,1024]{1,0:T(8,128)S(1)}, u32[]{:S(2)}, u32[]{:S(2)}) collective-permute-start(f32[48,1024]{1,0:T(8,128)} %bitcast.222), channel_id=1, source_target_pairs={{0,1},{1,0},{2,3},{3,2},{4,5},{5,4},{6,7},{7,6},{8,9},{9,8},{10,11... | collective-permute-start | bytes 589832 | tf_op jit(solution)/shard_map/ppermute | solution.py:485
  23.0 26.4 %collective-permute-start.3 = (bf16[1024,512]{1,0:T(8,128)(2,1)}, bf16[1024,512]{1,0:T(8,128)(2,1)S(1)}, u32[]{:S(2)}, u32[]{:S(2)}) collective-permute-start(bf16[1024,512]{1,0:T(8,128)(2,1)} %get-tuple-element.1374), channel_id=1, source_target_pairs={{0,1},{1,0},{2,3},{3,2},{4,5},{5,4},{6,7},{7,6},{8,9},{9,8},{10,11... | collective-permute-start | bytes 3145736 | tf_op jit(solution)/shard_map/ppermute | solution.py:485
  41.0 108.3 %collective-permute-start.19 = (bf16[20,48,512]{2,1,0:T(8,128)(2,1)}, bf16[20,48,512]{2,1,0:T(8,128)(2,1)}, u32[]{:S(2)}, u32[]{:S(2)}) collective-permute-start(bf16[20,48,512]{2,1,0:T(8,128)(2,1)} %get-tuple-element.676.refs_0_), channel_id=1, source_target_pairs={{0,4},{4,0},{8,12},{12,8},{16,20},{20,16},{24,28},{28,24},{1,5},{5... | collective-permute-start | bytes 2949128 | tf_op jit(solution)/shard_map/ppermute | solution.py:543
  43.2 106.1 %collective-permute-start.20 = (bf16[20,48,512]{2,1,0:T(8,128)(2,1)}, bf16[20,48,512]{2,1,0:T(8,128)(2,1)}, u32[]{:S(2)}, u32[]{:S(2)}) collective-permute-start(bf16[20,48,512]{2,1,0:T(8,128)(2,1)} %get-tuple-element.676.refs_0_), channel_id=1, source_target_pairs={{0,8},{4,12},{8,0},{12,4},{16,24},{20,28},{24,16},{28,20},{1,9},{5... | collective-permute-start | bytes 2949128 | tf_op jit(solution)/shard_map/ppermute | solution.py:543
  194.1 60.7 %collective-permute-start.33 = (bf16[20,48,512]{2,1,0:T(8,128)(2,1)}, bf16[20,48,512]{2,1,0:T(8,128)(2,1)S(1)}, u32[]{:S(2)}, u32[]{:S(2)}) collective-permute-start(bf16[20,48,512]{2,1,0:T(8,128)(2,1)} %get-tuple-element.961.refs_1_), channel_id=1, source_target_pairs={{0,4},{4,0},{8,12},{12,8},{16,20},{20,16},{24,28},{28,24},{1,5},{5... | collective-permute-start | bytes 2949128 | tf_op jit(solution)/shard_map/ppermute | solution.py:543
  194.7 60.1 %collective-permute-start.34 = (bf16[20,48,512]{2,1,0:T(8,128)(2,1)}, bf16[20,48,512]{2,1,0:T(8,128)(2,1)S(1)}, u32[]{:S(2)}, u32[]{:S(2)}) collective-permute-start(bf16[20,48,512]{2,1,0:T(8,128)(2,1)} %get-tuple-element.961.refs_1_), channel_id=1, source_target_pairs={{0,8},{4,12},{8,0},{12,4},{16,24},{20,28},{24,16},{28,20},{1,9},{5... | collective-permute-start | bytes 2949128 | tf_op jit(solution)/shard_map/ppermute | solution.py:543
  262.0 49.7 %collective-permute-start.43 = (bf16[7,48,2048]{2,1,0:T(8,128)(2,1)}, bf16[7,48,2048]{2,1,0:T(8,128)(2,1)S(1)}, u32[]{:S(2)}, u32[]{:S(2)}) collective-permute-start(bf16[7,48,2048]{2,1,0:T(8,128)(2,1)} %get-tuple-element.1191), channel_id=1, source_target_pairs={{0,4},{4,0},{8,12},{12,8},{16,20},{20,16},{24,28},{28,24},{1,5},{5... | collective-permute-start | bytes 4128776 | tf_op jit(solution)/shard_map/ppermute | solution.py:543
  263.6 48.1 %collective-permute-start.44 = (bf16[7,48,2048]{2,1,0:T(8,128)(2,1)}, bf16[7,48,2048]{2,1,0:T(8,128)(2,1)S(1)}, u32[]{:S(2)}, u32[]{:S(2)}) collective-permute-start(bf16[7,48,2048]{2,1,0:T(8,128)(2,1)} %get-tuple-element.1192), channel_id=1, source_target_pairs={{0,8},{4,12},{8,0},{12,4},{16,24},{20,28},{24,16},{28,20},{1,9},{5... | collective-permute-start | bytes 4128776 | tf_op jit(solution)/shard_map/ppermute | solution.py:543
  308.5 42.8 %collective-permute-start.50 = (bf16[6,48,2048]{2,1,0:T(8,128)(2,1)}, bf16[6,48,2048]{2,1,0:T(8,128)(2,1)S(1)}, u32[]{:S(2)}, u32[]{:S(2)}) collective-permute-start(bf16[6,48,2048]{2,1,0:T(8,128)(2,1)} %get-tuple-element.1271), channel_id=1, source_target_pairs={{0,4},{4,0},{8,12},{12,8},{16,20},{20,16},{24,28},{28,24},{1,5},{5... | collective-permute-start | bytes 3538952 | tf_op jit(solution)/shard_map/ppermute | solution.py:543
  308.9 44.1 %collective-permute-start.51 = (bf16[6,48,2048]{2,1,0:T(8,128)(2,1)}, bf16[6,48,2048]{2,1,0:T(8,128)(2,1)S(1)}, u32[]{:S(2)}, u32[]{:S(2)}) collective-permute-start(bf16[6,48,2048]{2,1,0:T(8,128)(2,1)} %get-tuple-element.1272), channel_id=1, source_target_pairs={{0,8},{4,12},{8,0},{12,4},{16,24},{20,28},{24,16},{28,20},{1,9},{5... | collective-permute-start | bytes 3538952 | tf_op jit(solution)/shard_map/ppermute | solution.py:543
  333.6 27.2 %collective-permute-start.52 = (bf16[3,48,2048]{2,1,0:T(8,128)(2,1)}, bf16[3,48,2048]{2,1,0:T(8,128)(2,1)S(1)}, u32[]{:S(2)}, u32[]{:S(2)}) collective-permute-start(bf16[3,48,2048]{2,1,0:T(8,128)(2,1)} %get-tuple-element.1288), channel_id=1, source_target_pairs={{0,4},{4,0},{8,12},{12,8},{16,20},{20,16},{24,28},{28,24},{1,5},{5... | collective-permute-start | bytes 1769480 | tf_op jit(solution)/shard_map/ppermute | solution.py:543
  335.1 25.7 %collective-permute-start.53 = (bf16[3,48,2048]{2,1,0:T(8,128)(2,1)}, bf16[3,48,2048]{2,1,0:T(8,128)(2,1)S(1)}, u32[]{:S(2)}, u32[]{:S(2)}) collective-permute-start(bf16[3,48,2048]{2,1,0:T(8,128)(2,1)} %get-tuple-element.1289), channel_id=1, source_target_pairs={{0,8},{4,12},{8,0},{12,4},{16,24},{20,28},{24,16},{28,20},{1,9},{5... | collective-permute-start | bytes 1769480 | tf_op jit(solution)/shard_map/ppermute | solution.py:543
  351.3 24.6 %collective-permute-start.54 = (bf16[2,48,2048]{2,1,0:T(8,128)(2,1)}, bf16[2,48,2048]{2,1,0:T(8,128)(2,1)S(1)}, u32[]{:S(2)}, u32[]{:S(2)}) collective-permute-start(bf16[2,48,2048]{2,1,0:T(8,128)(2,1)} %get-tuple-element.1301), channel_id=1, source_target_pairs={{0,8},{4,12},{8,0},{12,4},{16,24},{20,28},{24,16},{28,20},{1,9},{5... | collective-permute-start | bytes 1179656 | tf_op jit(solution)/shard_map/ppermute | solution.py:543
  353.0 22.9 %collective-permute-start.56 = (bf16[2,48,2048]{2,1,0:T(8,128)(2,1)}, bf16[2,48,2048]{2,1,0:T(8,128)(2,1)S(1)}, u32[]{:S(2)}, u32[]{:S(2)}) collective-permute-start(bf16[2,48,2048]{2,1,0:T(8,128)(2,1)} %get-tuple-element.1303), channel_id=1, source_target_pairs={{0,4},{4,0},{8,12},{12,8},{16,20},{20,16},{24,28},{28,24},{1,5},{5... | collective-permute-start | bytes 1179656 | tf_op jit(solution)/shard_map/ppermute | solution.py:543
  370.7 43.4 %collective-permute-start.59 = (bf16[4,4,68,512]{3,1,2,0:T(4,128)(2,1)S(1)}, bf16[4,4,68,512]{3,1,2,0:T(4,128)(2,1)S(1)}, u32[]{:S(2)}, u32[]{:S(2)}) collective-permute-start(bf16[4,4,68,512]{3,1,2,0:T(4,128)(2,1)S(1)} %copy.531), channel_id=1, source_target_pairs={{0,4},{4,0},{8,12},{12,8},{16,20},{20,16},{24,28},{28,24},{1,5},{5... | collective-permute-start | bytes 3342344 | tf_op jit(solution)/shard_map/ppermute | solution.py:543
  382.4 32.1 %collective-permute-start.58 = (bf16[2,2,64,2048]{3,2,1,0:T(8,128)(2,1)S(1)}, bf16[2,2,64,2048]{3,2,1,0:T(8,128)(2,1)S(1)}, u32[]{:S(2)}, u32[]{:S(2)}) collective-permute-start(bf16[2,2,64,2048]{3,2,1,0:T(8,128)(2,1)S(1)} %bitcast.237), channel_id=1, source_target_pairs={{0,8},{4,12},{24,16},{28,20},{1,9},{5,13},{25,17},{29,21},{2,10},{... | collective-permute-start | bytes 3145736 | tf_op jit(solution)/shard_map/ppermute | solution.py:543
  415.0 37.6 %collective-permute-start.63 = (bf16[4,2,68,512]{3,0,2,1:T(4,128)(2,1)S(1)}, bf16[4,2,68,512]{3,0,2,1:T(4,128)(2,1)S(1)}, u32[]{:S(2)}, u32[]{:S(2)}) collective-permute-start(bf16[4,2,68,512]{3,0,2,1:T(4,128)(2,1)S(1)} %copy.536), channel_id=1, source_target_pairs={{0,16},{4,20},{8,24},{12,28},{16,0},{20,4},{24,8},{28,12},{1,17},{... | collective-permute-start | bytes 1671176 | tf_op jit(solution)/shard_map/ppermute | solution.py:543
  424.3 28.4 %collective-permute-start.62 = (bf16[4,64,2048]{2,1,0:T(8,128)(2,1)}, bf16[4,64,2048]{2,1,0:T(8,128)(2,1)}, u32[]{:S(2)}, u32[]{:S(2)}) collective-permute-start(bf16[4,64,2048]{2,1,0:T(8,128)(2,1)} %dynamic-slice_bitcast_fusion.1), channel_id=1, source_target_pairs={{0,4},{4,0},{8,12},{12,8},{16,20},{20,16},{24,28},{28,24},{1,5},{5... | collective-permute-start | bytes 3145736 | tf_op jit(solution)/shard_map/ppermute | solution.py:543
  427.4 28.3 %collective-permute-start.60 = (bf16[2,2,64,2048]{3,2,1,0:T(8,128)(2,1)}, bf16[2,2,64,2048]{3,2,1,0:T(8,128)(2,1)}, u32[]{:S(2)}, u32[]{:S(2)}) collective-permute-start(bf16[2,2,64,2048]{3,2,1,0:T(8,128)(2,1)} %get-tuple-element.1369), channel_id=1, source_target_pairs={{0,8},{4,12},{8,16},{12,20},{1,9},{5,13},{9,17},{13,21},{2,10},{6,... | collective-permute-start | bytes 3145736 | tf_op jit(solution)/shard_map/ppermute | solution.py:543
  429.6 30.7 %collective-permute-start.61 = (bf16[2,2,64,2048]{3,2,1,0:T(8,128)(2,1)}, bf16[2,2,64,2048]{3,2,1,0:T(8,128)(2,1)}, u32[]{:S(2)}, u32[]{:S(2)}) collective-permute-start(bf16[2,2,64,2048]{3,2,1,0:T(8,128)(2,1)} %get-tuple-element.1368), channel_id=1, source_target_pairs={{16,8},{20,12},{24,16},{28,20},{17,9},{21,13},{25,17},{29,21},{18,... | collective-permute-start | bytes 3145736 | tf_op jit(solution)/shard_map/ppermute | solution.py:543
  432.3 42.1 %collective-permute-start.71 = (bf16[4,64,2048]{2,1,0:T(8,128)(2,1)S(1)}, bf16[4,64,2048]{2,1,0:T(8,128)(2,1)S(1)}, u32[]{:S(2)}, u32[]{:S(2)}) collective-permute-start(bf16[4,64,2048]{2,1,0:T(8,128)(2,1)S(1)} %dynamic-slice_bitcast_fusion), channel_id=1, source_target_pairs={{0,4},{4,0},{8,12},{12,8},{16,20},{20,16},{24,28},{28,24},{1,5},{5... | collective-permute-start | bytes 3145736 | tf_op jit(solution)/shard_map/ppermute | solution.py:543
  461.1 22.2 %collective-permute-start.77 = (bf16[4,68,512]{2,1,0:T(8,128)(2,1)}, bf16[4,68,512]{2,1,0:T(8,128)(2,1)}, u32[]{:S(2)}, u32[]{:S(2)}) collective-permute-start(bf16[4,68,512]{2,1,0:T(8,128)(2,1)} %dynamic-slice_bitcast_fusion.11), channel_id=1, source_target_pairs={{0,8},{4,12},{8,0},{12,4},{16,24},{20,28},{24,16},{28,20},{1,9},{5... | collective-permute-start | bytes 835592 | tf_op jit(solution)/shard_map/ppermute | solution.py:543
  461.9 25.1 %collective-permute-start.70 = (bf16[2,64,2048]{2,1,0:T(8,128)(2,1)}, bf16[2,64,2048]{2,1,0:T(8,128)(2,1)}, u32[]{:S(2)}, u32[]{:S(2)}) collective-permute-start(bf16[2,64,2048]{2,1,0:T(8,128)(2,1)} %dynamic-slice_bitcast_fusion.10), channel_id=1, source_target_pairs={{0,16},{4,20},{8,24},{12,28},{16,0},{20,4},{24,8},{28,12},{1,17},{... | collective-permute-start | bytes 1572872 | tf_op jit(solution)/shard_map/ppermute | solution.py:543
  467.4 32.5 %collective-permute-start.68 = (bf16[2,2,64,2048]{3,2,1,0:T(8,128)(2,1)}, bf16[2,2,64,2048]{3,2,1,0:T(8,128)(2,1)}, u32[]{:S(2)}, u32[]{:S(2)}) collective-permute-start(bf16[2,2,64,2048]{3,2,1,0:T(8,128)(2,1)} %get-tuple-element.1373), channel_id=1, source_target_pairs={{0,8},{4,12},{8,16},{12,20},{16,24},{20,28},{1,9},{5,13},{9,17},{1... | collective-permute-start | bytes 3145736 | tf_op jit(solution)/shard_map/ppermute | solution.py:543
  471.2 28.7 %collective-permute-start.69 = (bf16[2,2,64,2048]{3,2,1,0:T(8,128)(2,1)}, bf16[2,2,64,2048]{3,2,1,0:T(8,128)(2,1)}, u32[]{:S(2)}, u32[]{:S(2)}) collective-permute-start(bf16[2,2,64,2048]{3,2,1,0:T(8,128)(2,1)} %get-tuple-element.1372), channel_id=1, source_target_pairs={{8,0},{12,4},{16,8},{20,12},{24,16},{28,20},{9,1},{13,5},{17,9},{2... | collective-permute-start | bytes 3145736 | tf_op jit(solution)/shard_map/ppermute | solution.py:543
  483.3 20.5 %collective-permute-start.65 = (bf16[20,48,256]{2,1,0:T(8,128)(2,1)}, bf16[20,48,256]{2,1,0:T(8,128)(2,1)}, u32[]{:S(2)}, u32[]{:S(2)}) collective-permute-start(bf16[20,48,256]{2,1,0:T(8,128)(2,1)} %dynamic-slice_convert_fusion), channel_id=1, source_target_pairs={{0,2},{1,3},{2,0},{3,1},{4,6},{5,7},{6,4},{7,5},{8,10},{9,11},{10,... | collective-permute-start | bytes 1474568 | tf_op jit(solution)/shard_map/ppermute | solution.py:958
  487.0 54.0 %collective-permute-start.79 = (bf16[1024,64]{0,1:T(8,128)(2,1)}, bf16[1024,64]{0,1:T(8,128)(2,1)}, u32[]{:S(2)}, u32[]{:S(2)}) collective-permute-start(bf16[1024,64]{0,1:T(8,128)(2,1)} %bitcast.144), channel_id=1, source_target_pairs={{0,1},{1,0},{2,3},{3,2},{4,5},{5,4},{6,7},{7,6},{8,9},{9,8},{10,11... | collective-permute-start | bytes 393224 | tf_op jit(solution)/shard_map/ppermute | solution.py:485
  501.7 24.4 %collective-permute-start.73 = (bf16[2,64,2048]{2,1,0:T(8,128)(2,1)}, bf16[2,64,2048]{2,1,0:T(8,128)(2,1)}, u32[]{:S(2)}, u32[]{:S(2)}) collective-permute-start(bf16[2,64,2048]{2,1,0:T(8,128)(2,1)} %dynamic-slice_bitcast_fusion.7), channel_id=1, source_target_pairs={{0,16},{4,20},{8,24},{12,28},{16,0},{20,4},{24,8},{28,12},{1,17},{... | collective-permute-start | bytes 1572872 | tf_op jit(solution)/shard_map/ppermute | solution.py:543
  510.5 32.2 %collective-permute-start.66 = (bf16[20,48,128]{2,1,0:T(8,128)(2,1)S(1)}, bf16[20,48,128]{2,1,0:T(8,128)(2,1)S(1)}, u32[]{:S(2)}, u32[]{:S(2)}) collective-permute-start(bf16[20,48,128]{2,1,0:T(8,128)(2,1)S(1)} %bitcast.252), channel_id=1, source_target_pairs={{0,1},{1,0},{2,3},{3,2},{4,5},{5,4},{6,7},{7,6},{8,9},{9,8},{10,11... | collective-permute-start | bytes 737288 | tf_op jit(solution)/shard_map/ppermute | solution.py:485
  (146 other events, 719.4 us)

commit v11 on v10

--- a/solution.py
+++ b/solution.py
@@ -32,74 +32,42 @@
     return jnp.dot(left, right, preferred_element_type=F32)
 
 
-def place_kernel(count, *refs):
-    sources, targets, sems = refs[:count], refs[count : 2 * count], refs[2 * count]
-    copies = [pltpu.make_async_copy(a, b, sems.at[i]) for i, (a, b) in enumerate(zip(sources, targets))]
-    for copy in copies:
-        copy.start()
-    for copy in copies:
-        copy.wait()
-
-
-def place(*arrays):
-    count = len(arrays)
-    return pl.pallas_call(
-        functools.partial(place_kernel, count),
-        out_shape=tuple(pltpu.VMEM(x.shape, x.dtype) for x in arrays),
-        in_specs=[ANY] * count,
-        out_specs=[VMEM] * count,
-        scratch_shapes=[pltpu.SemaphoreType.DMA((count,))],
-        compiler_params=params(1),
-        name="place",
-    )(*(in_hbm(x) for x in arrays))
-
-
-def layout_kernel(keep, which_ref, w_ref, first_ref, second_ref, buf, sems, out_sems):
-    out_ref, all_ref = (first_ref, second_ref) if keep else (second_ref, first_ref)
-    depth, part = w_ref.shape[1], buf.shape[1]
+def layout_kernel(keep, spread, which_ref, w_ref, *refs):
+    buf, sems, out_sems = refs[-3:]
+    out_ref = refs[0] if keep else refs[1]
+    all_ref = refs[1] if keep else refs[0]
+    depth, ahead, part = w_ref.shape[1], buf.shape[0], buf.shape[1]
+    count = depth // part
 
     def fetch(i):
-        return pltpu.make_async_copy(w_ref.at[which_ref[0], pl.ds(i * part, part)], buf.at[i % 3], sems.at[i % 3])
+        return pltpu.make_async_copy(w_ref.at[which_ref[0], pl.ds(i * part, part)], buf.at[i % ahead], sems.at[i % ahead])
 
     def store(i):
         rows = pl.ds(i * part, part)
         return pltpu.make_async_copy(out_ref.at[:, rows], all_ref.at[:, rows], out_sems.at[i])
 
-    count = depth // part
-    for i in range(min(2, count)):
+    for i in range(min(ahead - 1, count)):
         fetch(i).start()
     for i in range(count):
-        if i + 2 < count:
-            fetch(i + 2).start()
+        if i + ahead - 1 < count:
+            fetch(i + ahead - 1).start()
         fetch(i).wait()
-        out_ref[:, i * part : (i + 1) * part, :] = jnp.swapaxes(buf[i % 3], 0, 1)
-        store(i).start()
-    for i in range(count):
+        out_ref[:, i * part : (i + 1) * part, :] = jnp.swapaxes(buf[i % ahead], 0, 1)
+        if spread:
+            store(i).start()
+    for i in range(count if spread else 0):
         store(i).wait()
 
 
-def turned_kernel(wa_ref, wb_ref, pa_ref, pb_ref, wat_ref, wbt_ref, pat_ref, pbt_ref, buf, sems, proj_buf, proj_sems):
-    jobs = [(w_ref, out_ref, gate) for w_ref, out_ref in ((wa_ref, wat_ref), (wb_ref, wbt_ref)) for gate in range(4)]
-
-    def fetch(i):
-        return pltpu.make_async_copy(jobs[i][0].at[jobs[i][2]], buf.at[i % 3], sems.at[i % 3])
-
-    proj_fetches = [pltpu.make_async_copy(x, proj_buf.at[i], proj_sems.at[i]) for i, x in enumerate((pa_ref, pb_ref))]
-    fetch(0).start()
-    fetch(1).start()
-    for copy in proj_fetches:
-        copy.start()
-    for i, (_, out_ref, gate) in enumerate(jobs):
-        if i + 2 < len(jobs):
-            fetch(i + 2).start()
-        fetch(i).wait()
-        for half in range(HALVES):
-            width = buf.shape[2] // HALVES
-            cols = slice(half * width, (half + 1) * width)
-            out_ref[gate, cols, :] = buf[i % 3, :, cols].T
-    for i, out_ref in enumerate((pat_ref, pbt_ref)):
-        proj_fetches[i].wait()
-        out_ref[...] = proj_buf[i].T
+def turned_kernel(wa_ref, wb_ref, pa_ref, pb_ref, wat_ref, wbt_ref, pat_ref, pbt_ref):
+    for w_ref, out_ref in ((wa_ref, wat_ref), (wb_ref, wbt_ref)):
+        for gate in range(4):
+            for half in range(HALVES):
+                width = w_ref.shape[2] // HALVES
+                cols = slice(half * width, (half + 1) * width)
+                out_ref[gate, cols, :] = w_ref[gate, :, cols].T
+    pat_ref[...] = pa_ref[...].T
+    pbt_ref[...] = pb_ref[...].T
 
 
 def pass_kernel(*refs):
@@ -300,8 +268,18 @@
             out_ref[piece, :, place] = dot(feat, w_ref[gate, :, cols]) + bias_ref[gate : gate + 1, cols]
 
 
-def inflow_kernel(feat_ref, ba_ref, bb_ref, wa_ref, wb_ref, out_ref):
-    inflow_into(feat_ref[0], ba_ref, bb_ref, wa_ref, wb_ref, out_ref)
+def begin_kernel(which_ref, feat_ref, wa_ref, wb_ref, proj_ref, *refs):
+    sems = refs[-1]
+    out_ref, pa_ref, *placed = refs[-8:-1]
+    copies = [pltpu.make_async_copy(x, y, sems.at[i]) for i, (x, y) in enumerate(zip(refs[:-8], placed))]
+    copies.append(pltpu.make_async_copy(proj_ref.at[which_ref[0]], pa_ref, sems.at[len(copies)]))
+    for copy in copies:
+        copy.start()
+    for copy in copies[:2]:
+        copy.wait()
+    inflow_into(feat_ref[0], *placed[:2], wa_ref, wb_ref, out_ref)
+    for copy in copies[2:]:
+        copy.wait()
 
 
 def backward_kernel(
@@ -345,21 +323,25 @@
 
 
 def finish_kernel(
-    step_ref, p_ref, q_ref, gates_all, cells_all, ups_all, hidden_in, slope_in,
-    gates_ref, cell_ref, prev_ref, slope_ref, up_ref, hidden_all, slope_all,
-    hidden_buf, sems, hidden_sem,
+    step_ref, p_ref, q_ref, mixed_ref, prev_ref, hidden_ref, before_ref, ups_all, mixed_in, prev_in, hidden_in, slope_in,
+    slope_ref, up_ref, mixed_all, prev_all, hidden_all, slope_all, hidden_buf, sems,
 ):
-    copies = fetches(
-        step_ref[0], step_ref[1], (gates_all, cells_all, ups_all), (gates_ref, cell_ref, prev_ref, up_ref), sems
-    )
-    for copy in copies:
+    step, time, time_before = step_ref[0], step_ref[1], step_ref[2]
+    jobs = [(mixed_ref.at[i], mixed_all.at[i, step]) for i in range(PIECES)]
+    jobs += [
+        (ups_all.at[time], up_ref),
+        (prev_ref, prev_all.at[step]),
+        (hidden_ref, hidden_all.at[time_before]),
+        (before_ref, slope_all.at[step - 1]),
+        (hidden_buf, hidden_all.at[time]),
+    ]
+    copies = [pltpu.make_async_copy(x, y, sems.at[i]) for i, (x, y) in enumerate(jobs)]
+    for copy in copies[:-1]:
         copy.start()
     clipped(p_ref, q_ref, hidden_buf, slope_ref)
-    hidden_copy = pltpu.make_async_copy(hidden_buf, hidden_all.at[step_ref[1]], hidden_sem)
-    hidden_copy.start()
+    copies[-1].start()
     for copy in copies:
         copy.wait()
-    hidden_copy.wait()
 
 
 def fetches(step, time, sources, targets, sems):
@@ -476,7 +458,7 @@
     )(jnp.stack([place_numbers[x] for x in names]).astype(jnp.int32))
     number = {x: place_numbers[x].astype(jnp.int32) for x in names}
     own, low, high = number["own"], number["low"], number["high"]
-    which = {x: lax.slice_in_dim(gathered_numbers, names.index(x), names.index(x) + 1) for x in ("own", "other")}
+    which = lax.slice_in_dim(gathered_numbers, names.index("own"), names.index("own") + 1)
 
     def pick(stacked, index, axis=0):
         return lax.dynamic_index_in_dim(stacked, index, axis, keepdims=False, allow_negative_indices=False)
@@ -490,28 +472,29 @@
     def hbm(shape, dtype):
         return pltpu.HBM(shape, dtype)
 
-    def by_gate(weights, index, keep=True):
+    def by_gate(weights, index, keep, spread):
         shape = (4,) + weights.shape[1:2] + weights.shape[3:]
-        kept = (vmem(shape, BF16),) if keep else ()
-        part = weights.shape[1] // 8
+        count = 16
+        kept, spreads = (vmem(shape, BF16),) * keep, (hbm(shape, BF16),) * spread
         return pl.pallas_call(
-            functools.partial(layout_kernel, keep),
-            out_shape=kept + (hbm(shape, BF16),),
+            functools.partial(layout_kernel, keep, spread),
+            out_shape=kept + spreads,
             in_specs=[SMEM, ANY],
-            out_specs=[VMEM] * len(kept) + [ANY],
-            scratch_shapes=([] if kept else [pltpu.VMEM(shape, BF16)])
+            out_specs=[VMEM] * keep + [ANY] * spread,
+            scratch_shapes=[pltpu.VMEM(shape, BF16)] * (1 - keep)
             + [
-                pltpu.VMEM((3, part) + weights.shape[2:], BF16),
-                pltpu.SemaphoreType.DMA((3,)),
-                pltpu.SemaphoreType.DMA((8,)),
+                pltpu.VMEM((4, weights.shape[1] // count) + weights.shape[2:], BF16),
+                pltpu.SemaphoreType.DMA((4,)),
+                pltpu.SemaphoreType.DMA((count,)),
             ],
             compiler_params=params(8),
             name="layout",
         )(index, in_hbm(weights))
 
-    win_b, rec_b = (lax.ppermute(by_gate(w, which["other"], False)[0], "gate", swap) for w in (w_in, w_rec))
-    (win_av, win_a), (rec_av, rec_a) = by_gate(w_in, which["own"]), by_gate(w_rec, which["own"])
-    proj_a, proj_b = trade(pick(proj, own), pick(proj, number["other"]))
+    away = jnp.full((1,), number["other"], jnp.int32)
+    win_b, rec_b = (lax.ppermute(by_gate(w, away, False, True)[0], "gate", swap) for w in (w_in, w_rec))
+    (win_av, win_a), (rec_av,) = by_gate(w_in, which, True, True), by_gate(w_rec, which, True, False)
+    proj_b = lax.ppermute(pick(proj, number["other"]), "gate", swap)
     bias_a, bias_b = trade(pick(bias, own), pick(bias, number["other"]))
 
     def cells_to_pieces(pair):
@@ -552,20 +535,19 @@
         compiler_params=params(1),
         name="order",
     )(turn, feats)
-    feat_in = (swapped(feat_all, near_swap), swapped(feat_all, far_swap))
-    keep_v, bias_av, bias_bv, win_bv = place(keep, bias_a.astype(F32), bias_b.astype(F32), win_b)
-    rec_bv, proj_av, proj_bv, start_hv, start_cv = place(rec_b, proj_a, proj_b, start_h, start_c)
-
     gates_shape, cell_shape = (PIECES, streams, 4 * width), (PIECES, streams, width)
     bias_shape = (PIECES, 8, 4 * width)
-    inflow = pl.pallas_call(
-        inflow_kernel,
-        out_shape=vmem(gates_shape, F32),
-        in_specs=[VMEM] * 5,
-        out_specs=VMEM,
+    win_bv, rec_bv, proj_bv = win_b, rec_b, proj_b
+    sources = (bias_a.astype(F32), bias_b.astype(F32), keep, start_h, start_c)
+    inflow, proj_av, bias_av, bias_bv, keep_v, start_hv, start_cv = pl.pallas_call(
+        begin_kernel,
+        out_shape=(vmem(gates_shape, F32), vmem((cells, depth), BF16)) + tuple(vmem(x.shape, x.dtype) for x in sources),
+        in_specs=[SMEM, VMEM, VMEM, VMEM] + [ANY] * (1 + len(sources)),
+        out_specs=[VMEM] * (2 + len(sources)),
+        scratch_shapes=[pltpu.SemaphoreType.DMA((1 + len(sources),))],
         compiler_params=params(8),
-        name="inflow",
-    )(pinned(feats_v), pinned(bias_av), pinned(bias_bv), pinned(win_av), pinned(win_bv))
+        name="begin",
+    )(which, pinned(feats_v), pinned(win_av), pinned(win_bv), in_hbm(proj), *sources)
 
     def forward_call(first, step, part, peer, cell, inflow):
         return pl.pallas_call(
@@ -618,14 +600,35 @@
     none = jnp.zeros((streams, depth), BF16)
     part, peer, cell, stacks = none, none, start_cv, ()
     for step in range(steps):
+        cell_before = cell
         part, cell, *fresh = forward_call(step == 0, step, part, peer, cell, inflow)
         peer = lax.ppermute(part, "gate", across)
-        due = step == (2 * steps) // 3
+        if step == steps - 1:
+            break
+        if step == 2:
+            (early_feat,) = after((part,), feat_all)
+            feat_in = (swapped(early_feat, near_swap), swapped(early_feat, far_swap))
+        due = step == (3 * steps) // 4
         inflow, stacks, passed = between_call(step, (cell, *fresh), stacks, feat_in if due else ())
-        feat_in = passed if due else feat_in
+        feat_in = passed if due else (feat_in if step >= 2 else None)
+    gates, mixed, prev, hidden, slope = fresh
     gates_all, cells_all, mixed_all, prev_all, hidden_all, slope_all = stacks
-    prev_in = (swapped(prev_all, near_swap), swapped(prev_all, far_swap))
-
+
+    slope_now, up_now, mixed_all, prev_all, hidden_all, slope_all = pl.pallas_call(
+        finish_kernel,
+        out_shape=(vmem((streams, depth), F32), vmem((streams, depth), BF16))
+        + tuple(hbm(x.shape, x.dtype) for x in (mixed_all, prev_all, hidden_all, slope_all)),
+        in_specs=[SMEM] + [VMEM] * 6 + [ANY] * 5,
+        out_specs=[VMEM] * 2 + [ANY] * 4,
+        scratch_shapes=[pltpu.VMEM((streams, depth), BF16), pltpu.SemaphoreType.DMA((PIECES + 5,))],
+        input_output_aliases={8 + i: 2 + i for i in range(4)},
+        compiler_params=params(8),
+        name="finish",
+    )(
+        at_step(steps - 1), pinned(part), pinned(peer), *(pinned(x) for x in (mixed, prev, hidden, slope)), in_hbm(ups),
+        *(in_hbm(x) for x in (mixed_all, prev_all, hidden_all, slope_all)),
+    )
+    saved = (gates, cell, cell_before, slope_now, up_now)
     saved_shapes = (
         vmem(gates_shape, BF16),
         vmem(cell_shape, F32),
@@ -633,38 +636,15 @@
         vmem((streams, depth), F32),
         vmem((streams, depth), BF16),
     )
-    *saved, hidden_all, slope_all = pl.pallas_call(
-        finish_kernel,
-        out_shape=saved_shapes + (hbm((steps, streams, depth), BF16), hbm((steps, streams, depth), F32)),
-        in_specs=[SMEM, VMEM, VMEM] + [ANY] * 5,
-        out_specs=[VMEM] * 5 + [ANY] * 2,
-        scratch_shapes=[
-            pltpu.VMEM((streams, depth), BF16),
-            pltpu.SemaphoreType.DMA((PIECES + 4,)),
-            pltpu.SemaphoreType.DMA,
-        ],
-        input_output_aliases={6: 5, 7: 6},
-        compiler_params=params(8),
-        name="finish",
-    )(
-        at_step(steps - 1), pinned(part), pinned(peer), in_hbm(gates_all), in_hbm(cells_all), in_hbm(ups),
-        in_hbm(hidden_all), in_hbm(slope_all),
-    )
 
     rec_atv, rec_btv, proj_atv, proj_btv = pl.pallas_call(
         turned_kernel,
         out_shape=(vmem((4, cells, depth), BF16),) * 2 + (vmem((depth, cells), BF16),) * 2,
-        in_specs=[ANY] * 4,
+        in_specs=[VMEM] * 4,
         out_specs=[VMEM] * 4,
-        scratch_shapes=[
-            pltpu.VMEM((3, depth, cells), BF16),
-            pltpu.SemaphoreType.DMA((3,)),
-            pltpu.VMEM((2, cells, depth), BF16),
-            pltpu.SemaphoreType.DMA((2,)),
-        ],
         compiler_params=params(8),
         name="turned",
-    )(*(in_hbm(x) for x in (rec_a, rec_b, proj_a, proj_b)))
+    )(pinned(rec_av), pinned(rec_bv), pinned(proj_av), pinned(proj_bv))
 
     def backward_call(step, part, peer, grad, bias, saved):
         return pl.pallas_call(
@@ -721,7 +701,7 @@
         return out[:5], tuple(out[5:9]), tuple(out[9:11]), tuple(out[11:])
 
     carry = (none, none, jnp.zeros(cell_shape, F32), jnp.zeros(bias_shape, F32), saved, ())
-    pending, arrived, ready, top = [(steps - 1 - steps // 3, prev_in)], [], None, steps
+    pending, arrived, ready, top = [], [], None, steps
     for index, share in enumerate(SHARES):
         slots = top if index == len(SHARES) - 1 else round(share * steps)
         sends = ()
@@ -729,6 +709,9 @@
             part, peer, grad, bias_sum, saved, stacks = carry
             part, grad, bias_sum, raw, dz = backward_call(step, part, peer, grad, bias_sum, saved)
             peer = lax.ppermute(part, "gate", across)
+            if step == steps - 1:
+                (early_prev,) = after((part,), prev_all)
+                pending.append((step - steps // 3, (swapped(early_prev, near_swap), swapped(early_prev, far_swap))))
             if ready is not None:
                 due, sides = ready
                 sides = after((part,), *sides) if step else sides

time: 560 us -> 615 us (1.098)
  Pallas kernels: 337 us -> 393 us
    pallas_call x20, Pallas kernels: 56.9 us -> 89.9 us  [forward_call(): pl.pallas_call(functools.partial(forward_kernel, first), out_shape=(vmem(...]
    pallas_call x20 -> x19, Pallas kernels: 59.3 us -> 87.6 us  [between_call(): pl.pallas_call(functools.partial(between_kernel, not stacks, step == step...]
    pallas_call x8 -> x6, Pallas kernels: 32.3 us -> 29.8 us  [the longest x4 23.1 us: by_gate(): pl.pallas_call(functools.partial(layout_kernel, keep, spread), out_shape=...]
    unnamed x205 -> x237, local copies, waits for them, and re-layouts: 15.5 us -> 17.5 us
  transfers between devices with their start and end apart: 80 -> 80, of which waited for: 37 -> 21; matrix products, arithmetic and copies ran while one was open for 14% -> 12% of each run, Pallas kernels for 55% -> 50%
where the time goes in v11:
time: 615 us; the launch traced here: 603 us
  Pallas kernels  393 us (64%)
  starting transfers between devices  84.7 us (14%)
  local copies, waits for them, and re-layouts  51.4 us (8%)
  waiting for transfers between devices  34.7 us (6%)
  other arithmetic  31.8 us (5%)
    pallas_call x20, Pallas kernels, forward_call(): pl.pallas_call(functools.partial(forward_kernel, first), out_shape=(vmem(...  89.9 us
    pallas_call x19, Pallas kernels, between_call(): pl.pallas_call(functools.partial(between_kernel, not stacks, step == step...  87.6 us
    pallas_call x20, Pallas kernels, backward_call(): pl.pallas_call(backward_kernel, out_shape=(vmem((streams, depth), BF16),...  61.7 us
    pallas_call x20, Pallas kernels, aside_call(): pl.pallas_call(functools.partial(aside_kernel, not stacks, step == 0, not...  55.8 us
    ppermute x39, starting transfers between devices, body(): peer = lax.ppermute(part, 'gate', across)  42.4 us
    ppermute x28, starting transfers between devices, swapped(): return lax.ppermute(array, 'batch', pairs)  38.8 us
    ppermute x28, waiting for transfers between devices, swapped(): return lax.ppermute(array, 'batch', pairs)  30.8 us
    pallas_call x4, Pallas kernels, by_gate(): pl.pallas_call(functools.partial(layout_kernel, keep, spread), out_shape=...  23.1 us
  transfers between devices with their start and end apart: 80, of which 21 were waited for; matrix products, arithmetic and copies ran while one was open for 12% of the time, Pallas kernels for 50%

profile of v11, /device:TPU:8, one launch (start us, length us, event | category | flops | bytes accessed | tf_op | source)
XLA Modules:
  0.0 603.4 jit_solution(3129287461168791450)
XLA Ops:
  0.7 5.8 layout.5
  6.6 5.8 layout.7
  24.5 6.4 %layout.4 = (bf16[4,512,1024]{2,1,0:T(8,128)(2,1)S(1)}, bf16[4,512,1024]{2,1,0:T(8,128)(2,1)}) custom-call(s32[1]{0:T(128)} %slice.55.which_ref, bf16[2,512,4,1024]{3,2,1,0:T(4,128)(2,1)} %w_ref.5), custom_call_target="tpu_custom_call" | custom-call | tf_op jit(solution)/shard_map/layout/pallas_call | solution.py:479
  30.9 5.1 layout.6.wa_ref
  39.3 5.2 begin.1
  44.6 4.6 forward_step.20
  60.4 4.6 between.20
  71.1 4.6 between.21
  80.8 4.6 between.22
  91.5 4.6 between.23
  101.3 4.6 between.24
  112.0 4.6 between.25
  121.8 4.6 between.26
  126.4 4.8 forward_step.28
  132.9 4.6 between.27
  142.6 4.6 between.28
  153.4 4.6 between.29
  166.1 4.6 between.30
  170.8 4.6 forward_step.32
  177.0 4.6 between.31
  186.7 4.6 between.32
  197.4 4.6 between.33
  218.9 4.9 between.35
  228.8 4.6 between.36
  239.5 4.6 between.37
  244.2 4.6 forward_step.39
  250.4 5.0 turned.1
  443.0 11.2 %product.3 = bf16[2,512,2048]{2,1,0:T(8,128)(2,1)S(1)} custom-call(bf16[40,48,1024]{2,1,0:T(8,128)(2,1)S(1)} %get-tuple-element.1297.left_ref, bf16[40,48,2048]{2,1,0:T(8,128)(2,1)S(1)} %get-tuple-element.1301.right_ref), custom_call_target="tpu_custom_call" | custom-call | tf_op jit(solution)/shard_map/product/pallas_call | solution.py:844
  456.3 11.2 %product.2 = bf16[2,512,2048]{2,1,0:T(8,128)(2,1)S(1)} custom-call(bf16[40,48,1024]{2,1,0:T(8,128)(2,1)S(1)} %get-tuple-element.1272.refs_0_.left_ref, bf16[40,48,2048]{2,1,0:T(8,128)(2,1)S(1)} %get-tuple-element.1285.right_ref), custom_call_target="tpu_custom_call" | custom-call | tf_op jit(solution)/shard_map/product/pallas_call | solution.py:844
  486.7 19.2 %input_grad.1.refs_2_ = f32[20,48,512]{2,1,0:T(8,128)S(1)} custom-call(s32[2]{0:T(128)S(1)} %copy-done.45, bf16[4,20,48,2048]{3,2,1,0:T(8,128)(2,1)} %get-tuple-element.1304.dz_ref, bf16[4,512,1024]{2,1,0:T(8,128)(2,1)} %get-tuple-element.1305.wa_ref, bf16[4,512,1024]{2,1,0:T(8,128)(2,1)} %collective-permute-done.wb_ref), custom_call_target="tpu_custom_call" | custom-call | tf_op jit(solution)/shard_map/input_grad/pallas_call | solution.py:767
  564.7 15.5 %collective-permute-done.73 = bf16[2,64,2048]{2,1,0:T(8,128)(2,1)} collective-permute-done((bf16[2,64,2048]{2,1,0:T(8,128)(2,1)}, bf16[2,64,2048]{2,1,0:T(8,128)(2,1)}, u32[]{:S(2)}, u32[]{:S(2)}) %collective-permute-start.73) | collective-permute-done | bytes 524320 | tf_op jit(solution)/shard_map/ppermute | solution.py:526
  587.0 8.0 %collective-permute-done.75 = bf16[2,64,2048]{2,1,0:T(8,128)(2,1)S(1)} collective-permute-done((bf16[2,64,2048]{2,1,0:T(8,128)(2,1)S(1)}, bf16[2,64,2048]{2,1,0:T(8,128)(2,1)S(1)}, u32[]{:S(2)}, u32[]{:S(2)}) %collective-permute-start.75) | collective-permute-done | bytes 524320 | tf_op jit(solution)/shard_map/ppermute | solution.py:526
  (593 shorter events, 403.9 us)
Async XLA Ops:
  6.5 32.6 %collective-permute-start = (bf16[4,512,1024]{2,1,0:T(8,128)(2,1)}, bf16[4,512,1024]{2,1,0:T(8,128)(2,1)}, u32[]{:S(2)}, u32[]{:S(2)}) collective-permute-start(bf16[4,512,1024]{2,1,0:T(8,128)(2,1)} %layout.5), channel_id=1, source_target_pairs={{0,1},{1,0},{2,3},{3,2},{4,5},{5,4},{6,7},{7,6},{8,9},{9,8},{10,11... | collective-permute-start | bytes 12582920 | tf_op jit(solution)/shard_map/ppermute | solution.py:495
  12.4 32.1 %collective-permute-start.3 = (bf16[4,512,1024]{2,1,0:T(8,128)(2,1)}, bf16[4,512,1024]{2,1,0:T(8,128)(2,1)}, u32[]{:S(2)}, u32[]{:S(2)}) collective-permute-start(bf16[4,512,1024]{2,1,0:T(8,128)(2,1)} %layout.7), channel_id=1, source_target_pairs={{0,1},{1,0},{2,3},{3,2},{4,5},{5,4},{6,7},{7,6},{8,9},{9,8},{10,11... | collective-permute-start | bytes 12582920 | tf_op jit(solution)/shard_map/ppermute | solution.py:495
  15.0 24.0 %collective-permute-start.2 = (f32[48,1024]{1,0:T(8,128)}, f32[48,1024]{1,0:T(8,128)S(1)}, u32[]{:S(2)}, u32[]{:S(2)}) collective-permute-start(f32[48,1024]{1,0:T(8,128)} %bitcast.220), channel_id=1, source_target_pairs={{0,1},{1,0},{2,3},{3,2},{4,5},{5,4},{6,7},{7,6},{8,9},{9,8},{10,11... | collective-permute-start | bytes 589832 | tf_op jit(solution)/shard_map/ppermute | solution.py:467
  15.1 23.9 %collective-permute-start.1 = (bf16[4,1024]{1,0:T(4,128)(2,1)S(1)}, bf16[4,1024]{1,0:T(4,128)(2,1)S(1)}, u32[]{:S(2)}, u32[]{:S(2)}) collective-permute-start(bf16[4,1024]{1,0:T(4,128)(2,1)S(1)} %get-tuple-element.1374), channel_id=1, source_target_pairs={{0,1},{1,0},{2,3},{3,2},{4,5},{5,4},{6,7},{7,6},{8,9},{9,8},{10,11... | collective-permute-start | bytes 24584 | tf_op jit(solution)/shard_map/ppermute | solution.py:467
  16.9 27.6 %collective-permute-start.4 = (bf16[1024,512]{1,0:T(8,128)(2,1)S(1)}, bf16[1024,512]{1,0:T(8,128)(2,1)S(1)}, u32[]{:S(2)}, u32[]{:S(2)}) collective-permute-start(bf16[1024,512]{1,0:T(8,128)(2,1)S(1)} %dynamic-slice_bitcast_fusion.2), channel_id=1, source_target_pairs={{0,1},{1,0},{2,3},{3,2},{4,5},{5,4},{6,7},{7,6},{8,9},{9,8},{10,11... | collective-permute-start | bytes 3145736 | tf_op jit(solution)/shard_map/ppermute | solution.py:497
  164.1 43.0 %collective-permute-start.21 = (bf16[20,48,512]{2,1,0:T(8,128)(2,1)}, bf16[20,48,512]{2,1,0:T(8,128)(2,1)S(1)}, u32[]{:S(2)}, u32[]{:S(2)}) collective-permute-start(bf16[20,48,512]{2,1,0:T(8,128)(2,1)} %after.11), channel_id=1, source_target_pairs={{0,4},{4,0},{8,12},{12,8},{16,20},{20,16},{24,28},{28,24},{1,5},{5... | collective-permute-start | bytes 2949128 | tf_op jit(solution)/shard_map/ppermute | solution.py:526
  165.7 41.5 %collective-permute-start.22 = (bf16[20,48,512]{2,1,0:T(8,128)(2,1)}, bf16[20,48,512]{2,1,0:T(8,128)(2,1)S(1)}, u32[]{:S(2)}, u32[]{:S(2)}) collective-permute-start(bf16[20,48,512]{2,1,0:T(8,128)(2,1)} %after.11), channel_id=1, source_target_pairs={{0,8},{4,12},{8,0},{12,4},{16,24},{20,28},{24,16},{28,20},{1,9},{5... | collective-permute-start | bytes 2949128 | tf_op jit(solution)/shard_map/ppermute | solution.py:526
  262.3 47.2 %collective-permute-start.33 = (bf16[20,48,512]{2,1,0:T(8,128)(2,1)}, bf16[20,48,512]{2,1,0:T(8,128)(2,1)S(1)}, u32[]{:S(2)}, u32[]{:S(2)}) collective-permute-start(bf16[20,48,512]{2,1,0:T(8,128)(2,1)} %after.12), channel_id=1, source_target_pairs={{0,4},{4,0},{8,12},{12,8},{16,20},{20,16},{24,28},{28,24},{1,5},{5... | collective-permute-start | bytes 2949128 | tf_op jit(solution)/shard_map/ppermute | solution.py:526
  262.9 46.7 %collective-permute-start.34 = (bf16[20,48,512]{2,1,0:T(8,128)(2,1)}, bf16[20,48,512]{2,1,0:T(8,128)(2,1)S(1)}, u32[]{:S(2)}, u32[]{:S(2)}) collective-permute-start(bf16[20,48,512]{2,1,0:T(8,128)(2,1)} %after.12), channel_id=1, source_target_pairs={{0,8},{4,12},{8,0},{12,4},{16,24},{20,28},{24,16},{28,20},{1,9},{5... | collective-permute-start | bytes 2949128 | tf_op jit(solution)/shard_map/ppermute | solution.py:526
  316.9 48.7 %collective-permute-start.43 = (bf16[7,48,2048]{2,1,0:T(8,128)(2,1)}, bf16[7,48,2048]{2,1,0:T(8,128)(2,1)S(1)}, u32[]{:S(2)}, u32[]{:S(2)}) collective-permute-start(bf16[7,48,2048]{2,1,0:T(8,128)(2,1)} %get-tuple-element.1169), channel_id=1, source_target_pairs={{0,4},{4,0},{8,12},{12,8},{16,20},{20,16},{24,28},{28,24},{1,5},{5... | collective-permute-start | bytes 4128776 | tf_op jit(solution)/shard_map/ppermute | solution.py:526
  318.5 47.1 %collective-permute-start.44 = (bf16[7,48,2048]{2,1,0:T(8,128)(2,1)}, bf16[7,48,2048]{2,1,0:T(8,128)(2,1)S(1)}, u32[]{:S(2)}, u32[]{:S(2)}) collective-permute-start(bf16[7,48,2048]{2,1,0:T(8,128)(2,1)} %get-tuple-element.1170), channel_id=1, source_target_pairs={{0,8},{4,12},{8,0},{12,4},{16,24},{20,28},{24,16},{28,20},{1,9},{5... | collective-permute-start | bytes 4128776 | tf_op jit(solution)/shard_map/ppermute | solution.py:526
  362.3 42.9 %collective-permute-start.50 = (bf16[6,48,2048]{2,1,0:T(8,128)(2,1)}, bf16[6,48,2048]{2,1,0:T(8,128)(2,1)S(1)}, u32[]{:S(2)}, u32[]{:S(2)}) collective-permute-start(bf16[6,48,2048]{2,1,0:T(8,128)(2,1)} %get-tuple-element.1249), channel_id=1, source_target_pairs={{0,4},{4,0},{8,12},{12,8},{16,20},{20,16},{24,28},{28,24},{1,5},{5... | collective-permute-start | bytes 3538952 | tf_op jit(solution)/shard_map/ppermute | solution.py:526
  362.9 43.6 %collective-permute-start.51 = (bf16[6,48,2048]{2,1,0:T(8,128)(2,1)}, bf16[6,48,2048]{2,1,0:T(8,128)(2,1)S(1)}, u32[]{:S(2)}, u32[]{:S(2)}) collective-permute-start(bf16[6,48,2048]{2,1,0:T(8,128)(2,1)} %get-tuple-element.1250), channel_id=1, source_target_pairs={{0,8},{4,12},{8,0},{12,4},{16,24},{20,28},{24,16},{28,20},{1,9},{5... | collective-permute-start | bytes 3538952 | tf_op jit(solution)/shard_map/ppermute | solution.py:526
  387.8 26.5 %collective-permute-start.52 = (bf16[3,48,2048]{2,1,0:T(8,128)(2,1)}, bf16[3,48,2048]{2,1,0:T(8,128)(2,1)S(1)}, u32[]{:S(2)}, u32[]{:S(2)}) collective-permute-start(bf16[3,48,2048]{2,1,0:T(8,128)(2,1)} %get-tuple-element.1266), channel_id=1, source_target_pairs={{0,4},{4,0},{8,12},{12,8},{16,20},{20,16},{24,28},{28,24},{1,5},{5... | collective-permute-start | bytes 1769480 | tf_op jit(solution)/shard_map/ppermute | solution.py:526
  388.9 25.5 %collective-permute-start.53 = (bf16[3,48,2048]{2,1,0:T(8,128)(2,1)}, bf16[3,48,2048]{2,1,0:T(8,128)(2,1)S(1)}, u32[]{:S(2)}, u32[]{:S(2)}) collective-permute-start(bf16[3,48,2048]{2,1,0:T(8,128)(2,1)} %get-tuple-element.1267), channel_id=1, source_target_pairs={{0,8},{4,12},{8,0},{12,4},{16,24},{20,28},{24,16},{28,20},{1,9},{5... | collective-permute-start | bytes 1769480 | tf_op jit(solution)/shard_map/ppermute | solution.py:526
  405.2 24.6 %collective-permute-start.54 = (bf16[2,48,2048]{2,1,0:T(8,128)(2,1)}, bf16[2,48,2048]{2,1,0:T(8,128)(2,1)S(1)}, u32[]{:S(2)}, u32[]{:S(2)}) collective-permute-start(bf16[2,48,2048]{2,1,0:T(8,128)(2,1)} %get-tuple-element.1279), channel_id=1, source_target_pairs={{0,8},{4,12},{8,0},{12,4},{16,24},{20,28},{24,16},{28,20},{1,9},{5... | collective-permute-start | bytes 1179656 | tf_op jit(solution)/shard_map/ppermute | solution.py:526
  406.5 23.3 %collective-permute-start.56 = (bf16[2,48,2048]{2,1,0:T(8,128)(2,1)}, bf16[2,48,2048]{2,1,0:T(8,128)(2,1)S(1)}, u32[]{:S(2)}, u32[]{:S(2)}) collective-permute-start(bf16[2,48,2048]{2,1,0:T(8,128)(2,1)} %get-tuple-element.1281), channel_id=1, source_target_pairs={{0,4},{4,0},{8,12},{12,8},{16,20},{20,16},{24,28},{28,24},{1,5},{5... | collective-permute-start | bytes 1179656 | tf_op jit(solution)/shard_map/ppermute | solution.py:526
  424.5 43.0 %collective-permute-start.59 = (bf16[4,4,68,512]{3,1,2,0:T(4,128)(2,1)S(1)}, bf16[4,4,68,512]{3,1,2,0:T(4,128)(2,1)S(1)}, u32[]{:S(2)}, u32[]{:S(2)}) collective-permute-start(bf16[4,4,68,512]{3,1,2,0:T(4,128)(2,1)S(1)} %copy.527), channel_id=1, source_target_pairs={{0,4},{4,0},{8,12},{12,8},{16,20},{20,16},{24,28},{28,24},{1,5},{5... | collective-permute-start | bytes 3342344 | tf_op jit(solution)/shard_map/ppermute | solution.py:526
  435.8 32.1 %collective-permute-start.58 = (bf16[2,2,64,2048]{3,2,1,0:T(8,128)(2,1)S(1)}, bf16[2,2,64,2048]{3,2,1,0:T(8,128)(2,1)S(1)}, u32[]{:S(2)}, u32[]{:S(2)}) collective-permute-start(bf16[2,2,64,2048]{3,2,1,0:T(8,128)(2,1)S(1)} %bitcast.236), channel_id=1, source_target_pairs={{0,8},{4,12},{24,16},{28,20},{1,9},{5,13},{25,17},{29,21},{2,10},{... | collective-permute-start | bytes 3145736 | tf_op jit(solution)/shard_map/ppermute | solution.py:526
  468.4 37.6 %collective-permute-start.63 = (bf16[4,2,68,512]{3,0,2,1:T(4,128)(2,1)S(1)}, bf16[4,2,68,512]{3,0,2,1:T(4,128)(2,1)S(1)}, u32[]{:S(2)}, u32[]{:S(2)}) collective-permute-start(bf16[4,2,68,512]{3,0,2,1:T(4,128)(2,1)S(1)} %copy.532), channel_id=1, source_target_pairs={{0,16},{4,20},{8,24},{12,28},{16,0},{20,4},{24,8},{28,12},{1,17},{... | collective-permute-start | bytes 1671176 | tf_op jit(solution)/shard_map/ppermute | solution.py:526
  477.9 28.2 %collective-permute-start.62 = (bf16[4,64,2048]{2,1,0:T(8,128)(2,1)}, bf16[4,64,2048]{2,1,0:T(8,128)(2,1)}, u32[]{:S(2)}, u32[]{:S(2)}) collective-permute-start(bf16[4,64,2048]{2,1,0:T(8,128)(2,1)} %dynamic-slice_bitcast_fusion.1), channel_id=1, source_target_pairs={{0,4},{4,0},{8,12},{12,8},{16,20},{20,16},{24,28},{28,24},{1,5},{5... | collective-permute-start | bytes 3145736 | tf_op jit(solution)/shard_map/ppermute | solution.py:526
  481.1 30.2 %collective-permute-start.60 = (bf16[2,2,64,2048]{3,2,1,0:T(8,128)(2,1)}, bf16[2,2,64,2048]{3,2,1,0:T(8,128)(2,1)}, u32[]{:S(2)}, u32[]{:S(2)}) collective-permute-start(bf16[2,2,64,2048]{3,2,1,0:T(8,128)(2,1)} %get-tuple-element.1347), channel_id=1, source_target_pairs={{0,8},{4,12},{8,16},{12,20},{1,9},{5,13},{9,17},{13,21},{2,10},{6,... | collective-permute-start | bytes 3145736 | tf_op jit(solution)/shard_map/ppermute | solution.py:526
  483.1 31.3 %collective-permute-start.61 = (bf16[2,2,64,2048]{3,2,1,0:T(8,128)(2,1)}, bf16[2,2,64,2048]{3,2,1,0:T(8,128)(2,1)}, u32[]{:S(2)}, u32[]{:S(2)}) collective-permute-start(bf16[2,2,64,2048]{3,2,1,0:T(8,128)(2,1)} %get-tuple-element.1346), channel_id=1, source_target_pairs={{16,8},{20,12},{24,16},{28,20},{17,9},{21,13},{25,17},{29,21},{18,... | collective-permute-start | bytes 3145736 | tf_op jit(solution)/shard_map/ppermute | solution.py:526
  485.8 42.7 %collective-permute-start.71 = (bf16[4,64,2048]{2,1,0:T(8,128)(2,1)S(1)}, bf16[4,64,2048]{2,1,0:T(8,128)(2,1)S(1)}, u32[]{:S(2)}, u32[]{:S(2)}) collective-permute-start(bf16[4,64,2048]{2,1,0:T(8,128)(2,1)S(1)} %dynamic-slice_bitcast_fusion), channel_id=1, source_target_pairs={{0,4},{4,0},{8,12},{12,8},{16,20},{20,16},{24,28},{28,24},{1,5},{5... | collective-permute-start | bytes 3145736 | tf_op jit(solution)/shard_map/ppermute | solution.py:526
  515.2 22.2 %collective-permute-start.77 = (bf16[4,68,512]{2,1,0:T(8,128)(2,1)}, bf16[4,68,512]{2,1,0:T(8,128)(2,1)}, u32[]{:S(2)}, u32[]{:S(2)}) collective-permute-start(bf16[4,68,512]{2,1,0:T(8,128)(2,1)} %dynamic-slice_bitcast_fusion.10), channel_id=1, source_target_pairs={{0,8},{4,12},{8,0},{12,4},{16,24},{20,28},{24,16},{28,20},{1,9},{5... | collective-permute-start | bytes 835592 | tf_op jit(solution)/shard_map/ppermute | solution.py:526
  516.0 25.1 %collective-permute-start.70 = (bf16[2,64,2048]{2,1,0:T(8,128)(2,1)}, bf16[2,64,2048]{2,1,0:T(8,128)(2,1)}, u32[]{:S(2)}, u32[]{:S(2)}) collective-permute-start(bf16[2,64,2048]{2,1,0:T(8,128)(2,1)} %dynamic-slice_bitcast_fusion.9), channel_id=1, source_target_pairs={{0,16},{4,20},{8,24},{12,28},{16,0},{20,4},{24,8},{28,12},{1,17},{... | collective-permute-start | bytes 1572872 | tf_op jit(solution)/shard_map/ppermute | solution.py:526
  521.5 32.5 %collective-permute-start.68 = (bf16[2,2,64,2048]{3,2,1,0:T(8,128)(2,1)}, bf16[2,2,64,2048]{3,2,1,0:T(8,128)(2,1)}, u32[]{:S(2)}, u32[]{:S(2)}) collective-permute-start(bf16[2,2,64,2048]{3,2,1,0:T(8,128)(2,1)} %get-tuple-element.1351), channel_id=1, source_target_pairs={{0,8},{4,12},{8,16},{12,20},{16,24},{20,28},{1,9},{5,13},{9,17},{1... | collective-permute-start | bytes 3145736 | tf_op jit(solution)/shard_map/ppermute | solution.py:526
  525.3 28.7 %collective-permute-start.69 = (bf16[2,2,64,2048]{3,2,1,0:T(8,128)(2,1)}, bf16[2,2,64,2048]{3,2,1,0:T(8,128)(2,1)}, u32[]{:S(2)}, u32[]{:S(2)}) collective-permute-start(bf16[2,2,64,2048]{3,2,1,0:T(8,128)(2,1)} %get-tuple-element.1350), channel_id=1, source_target_pairs={{8,0},{12,4},{16,8},{20,12},{24,16},{28,20},{9,1},{13,5},{17,9},{2... | collective-permute-start | bytes 3145736 | tf_op jit(solution)/shard_map/ppermute | solution.py:526
  537.4 20.5 %collective-permute-start.65 = (bf16[20,48,256]{2,1,0:T(8,128)(2,1)}, bf16[20,48,256]{2,1,0:T(8,128)(2,1)}, u32[]{:S(2)}, u32[]{:S(2)}) collective-permute-start(bf16[20,48,256]{2,1,0:T(8,128)(2,1)} %dynamic-slice_convert_fusion), channel_id=1, source_target_pairs={{0,2},{1,3},{2,0},{3,1},{4,6},{5,7},{6,4},{7,5},{8,10},{9,11},{10,... | collective-permute-start | bytes 1474568 | tf_op jit(solution)/shard_map/ppermute | solution.py:941
  541.1 53.9 %collective-permute-start.79 = (bf16[1024,64]{0,1:T(8,128)(2,1)}, bf16[1024,64]{0,1:T(8,128)(2,1)}, u32[]{:S(2)}, u32[]{:S(2)}) collective-permute-start(bf16[1024,64]{0,1:T(8,128)(2,1)} %bitcast.143), channel_id=1, source_target_pairs={{0,1},{1,0},{2,3},{3,2},{4,5},{5,4},{6,7},{7,6},{8,9},{9,8},{10,11... | collective-permute-start | bytes 393224 | tf_op jit(solution)/shard_map/ppermute | solution.py:467
  555.9 24.3 %collective-permute-start.73 = (bf16[2,64,2048]{2,1,0:T(8,128)(2,1)}, bf16[2,64,2048]{2,1,0:T(8,128)(2,1)}, u32[]{:S(2)}, u32[]{:S(2)}) collective-permute-start(bf16[2,64,2048]{2,1,0:T(8,128)(2,1)} %dynamic-slice_bitcast_fusion.6), channel_id=1, source_target_pairs={{0,16},{4,20},{8,24},{12,28},{16,0},{20,4},{24,8},{28,12},{1,17},{... | collective-permute-start | bytes 1572872 | tf_op jit(solution)/shard_map/ppermute | solution.py:526
  564.6 32.2 %collective-permute-start.66 = (bf16[20,48,128]{2,1,0:T(8,128)(2,1)S(1)}, bf16[20,48,128]{2,1,0:T(8,128)(2,1)S(1)}, u32[]{:S(2)}, u32[]{:S(2)}) collective-permute-start(bf16[20,48,128]{2,1,0:T(8,128)(2,1)S(1)} %bitcast.251), channel_id=1, source_target_pairs={{0,1},{1,0},{2,3},{3,2},{4,5},{5,4},{6,7},{7,6},{8,9},{9,8},{10,11... | collective-permute-start | bytes 737288 | tf_op jit(solution)/shard_map/ppermute | solution.py:467
  (161 other events, 957.1 us)

commit v12 on v11

--- a/solution.py
+++ b/solution.py
@@ -260,25 +260,30 @@
         copy.wait()
 
 
-def inflow_into(feat, ba_ref, bb_ref, wa_ref, wb_ref, out_ref):
+def inflow_into(feat, ba_ref, bb_ref, wa_ref, wb_ref, out_ref, quarters=(0, 1)):
     for piece, quarter, width, cols in pieces((wa_ref, wb_ref), 2):
+        if quarter not in quarters:
+            continue
         w_ref, bias_ref = ((wa_ref, ba_ref), (wb_ref, bb_ref))[quarter]
         for gate in range(4):
             place = slice(gate * width, (gate + 1) * width)
             out_ref[piece, :, place] = dot(feat, w_ref[gate, :, cols]) + bias_ref[gate : gate + 1, cols]
 
 
-def begin_kernel(which_ref, feat_ref, wa_ref, wb_ref, proj_ref, *refs):
+def begin_kernel(which_ref, feat_ref, wa_ref, proj_ref, *refs):
     sems = refs[-1]
-    out_ref, pa_ref, *placed = refs[-8:-1]
-    copies = [pltpu.make_async_copy(x, y, sems.at[i]) for i, (x, y) in enumerate(zip(refs[:-8], placed))]
+    out_ref, pa_ref, *placed = refs[-11:-1]
+    copies = [pltpu.make_async_copy(x, y, sems.at[i]) for i, (x, y) in enumerate(zip(refs[:-11], placed))]
     copies.append(pltpu.make_async_copy(proj_ref.at[which_ref[0]], pa_ref, sems.at[len(copies)]))
     for copy in copies:
         copy.start()
-    for copy in copies[:2]:
-        copy.wait()
-    inflow_into(feat_ref[0], *placed[:2], wa_ref, wb_ref, out_ref)
-    for copy in copies[2:]:
+    ba_ref, bb_ref, wb_ref = placed[:3]
+    copies[0].wait()
+    inflow_into(feat_ref[0], ba_ref, bb_ref, wa_ref, wb_ref, out_ref, (0,))
+    copies[1].wait()
+    copies[2].wait()
+    inflow_into(feat_ref[0], ba_ref, bb_ref, wa_ref, wb_ref, out_ref, (1,))
+    for copy in copies[3:]:
         copy.wait()
 
 
@@ -537,17 +542,16 @@
     )(turn, feats)
     gates_shape, cell_shape = (PIECES, streams, 4 * width), (PIECES, streams, width)
     bias_shape = (PIECES, 8, 4 * width)
-    win_bv, rec_bv, proj_bv = win_b, rec_b, proj_b
-    sources = (bias_a.astype(F32), bias_b.astype(F32), keep, start_h, start_c)
-    inflow, proj_av, bias_av, bias_bv, keep_v, start_hv, start_cv = pl.pallas_call(
+    sources = (bias_a.astype(F32), bias_b.astype(F32), in_hbm(win_b), in_hbm(rec_b), in_hbm(proj_b), keep, start_h, start_c)
+    inflow, proj_av, bias_av, bias_bv, win_bv, rec_bv, proj_bv, keep_v, start_hv, start_cv = pl.pallas_call(
         begin_kernel,
         out_shape=(vmem(gates_shape, F32), vmem((cells, depth), BF16)) + tuple(vmem(x.shape, x.dtype) for x in sources),
-        in_specs=[SMEM, VMEM, VMEM, VMEM] + [ANY] * (1 + len(sources)),
+        in_specs=[SMEM, VMEM, VMEM] + [ANY] * (1 + len(sources)),
         out_specs=[VMEM] * (2 + len(sources)),
         scratch_shapes=[pltpu.SemaphoreType.DMA((1 + len(sources),))],
         compiler_params=params(8),
         name="begin",
-    )(which, pinned(feats_v), pinned(win_av), pinned(win_bv), in_hbm(proj), *sources)
+    )(which, pinned(feats_v), pinned(win_av), in_hbm(proj), *sources)
 
     def forward_call(first, step, part, peer, cell, inflow):
         return pl.pallas_call(

time: 615 us -> 548 us (0.89)
  Pallas kernels: 393 us -> 326 us
    pallas_call x20, Pallas kernels: 89.9 us -> 56.3 us  [forward_call(): pl.pallas_call(functools.partial(forward_kernel, first), out_shape=(vmem(...]
    pallas_call x19, Pallas kernels: 87.6 us -> 56.5 us  [between_call(): pl.pallas_call(functools.partial(between_kernel, not stacks, step == step...]
    unnamed x237 -> x217, local copies, waits for them, and re-layouts: 17.5 us -> 18.9 us
  transfers between devices with their start and end apart: 80 -> 80, of which waited for: 21 -> 30; matrix products, arithmetic and copies ran while one was open for 12% -> 13% of each run, Pallas kernels for 50% -> 48%
where the time goes in v12:
time: 548 us; the launch traced here: 537 us
  Pallas kernels  326 us (59%)
  starting transfers between devices  84.7 us (15%)
  local copies, waits for them, and re-layouts  51.4 us (9%)
  waiting for transfers between devices  36.1 us (7%)
  other arithmetic  31.9 us (6%)
    pallas_call x20, Pallas kernels, backward_call(): pl.pallas_call(backward_kernel, out_shape=(vmem((streams, depth), BF16),...  61.7 us
    pallas_call x19, Pallas kernels, between_call(): pl.pallas_call(functools.partial(between_kernel, not stacks, step == step...  56.5 us
    pallas_call x20, Pallas kernels, forward_call(): pl.pallas_call(functools.partial(forward_kernel, first), out_shape=(vmem(...  56.3 us
    pallas_call x20, Pallas kernels, aside_call(): pl.pallas_call(functools.partial(aside_kernel, not stacks, step == 0, not...  55.9 us
    ppermute x39, starting transfers between devices, body(): peer = lax.ppermute(part, 'gate', across)  43.1 us
    ppermute x28, starting transfers between devices, swapped(): return lax.ppermute(array, 'batch', pairs)  38 us
    ppermute x28, waiting for transfers between devices, swapped(): return lax.ppermute(array, 'batch', pairs)  31 us
    pallas_call x4, Pallas kernels, by_gate(): pl.pallas_call(functools.partial(layout_kernel, keep, spread), out_shape=...  23.2 us
  transfers between devices with their start and end apart: 80, of which 30 were waited for; matrix products, arithmetic and copies ran while one was open for 13% of the time, Pallas kernels for 48%

profile of v12, /device:TPU:8, one launch (start us, length us, event | category | flops | bytes accessed | tf_op | source)
XLA Modules:
  0.0 537.4 jit_solution(175187627420911198)
XLA Ops:
  0.7 5.8 %layout.5 = bf16[4,512,1024]{2,1,0:T(8,128)(2,1)} custom-call(s32[1]{0:T(128)} %bitcast.17.which_ref, bf16[2,512,4,1024]{3,2,1,0:T(4,128)(2,1)} %w_ref.5), custom_call_target="tpu_custom_call" | custom-call | tf_op jit(solution)/shard_map/layout/pallas_call | solution.py:484
  6.6 5.9 %layout.6 = bf16[4,512,1024]{2,1,0:T(8,128)(2,1)} custom-call(s32[1]{0:T(128)} %bitcast.17.which_ref, bf16[2,512,4,1024]{3,2,1,0:T(4,128)(2,1)} %w_ref.7), custom_call_target="tpu_custom_call" | custom-call | tf_op jit(solution)/shard_map/layout/pallas_call | solution.py:484
  23.2 6.4 %layout.4 = (bf16[4,512,1024]{2,1,0:T(8,128)(2,1)S(1)}, bf16[4,512,1024]{2,1,0:T(8,128)(2,1)}) custom-call(s32[1]{0:T(128)} %slice.55.which_ref, bf16[2,512,4,1024]{3,2,1,0:T(4,128)(2,1)} %w_ref.5), custom_call_target="tpu_custom_call" | custom-call | tf_op jit(solution)/shard_map/layout/pallas_call | solution.py:484
  29.6 5.1 layout.7.wa_ref
  38.7 4.9 begin.1
  99.9 3.2 forward_step.28
  157.4 3.1 between.34
  164.4 3.1 between.35
  193.6 3.0 backward_step.20
  247.1 3.2 backward_step.27
  292.8 3.4 backward_step.33
  303.9 3.0 backward_step.34
  344.6 3.8 backward_step.39
  349.5 3.0 aside.39
  353.7 3.6 bitcast_convert_fusion
  359.4 4.2 gather.14
  365.7 4.3 late.2
  371.4 4.2 gather.15
  377.3 11.2 %product.3 = bf16[2,512,2048]{2,1,0:T(8,128)(2,1)S(1)} custom-call(bf16[40,48,1024]{2,1,0:T(8,128)(2,1)S(1)} %get-tuple-element.1303.left_ref, bf16[40,48,2048]{2,1,0:T(8,128)(2,1)S(1)} %get-tuple-element.1307.right_ref), custom_call_target="tpu_custom_call" | custom-call | tf_op jit(solution)/shard_map/product/pallas_call | solution.py:848
  390.5 11.2 %product.2 = bf16[2,512,2048]{2,1,0:T(8,128)(2,1)S(1)} custom-call(bf16[40,48,1024]{2,1,0:T(8,128)(2,1)S(1)} %get-tuple-element.1278.refs_0_.left_ref, bf16[40,48,2048]{2,1,0:T(8,128)(2,1)S(1)} %get-tuple-element.1291.right_ref), custom_call_target="tpu_custom_call" | custom-call | tf_op jit(solution)/shard_map/product/pallas_call | solution.py:848
  402.6 4.0 collective-permute-start.63
  406.7 4.1 fusion.71
  421.0 19.2 %input_grad.1.refs_2_ = f32[20,48,512]{2,1,0:T(8,128)S(1)} custom-call(s32[2]{0:T(128)S(1)} %copy-done.35, bf16[4,20,48,2048]{3,2,1,0:T(8,128)(2,1)} %get-tuple-element.1310.dz_ref, bf16[4,512,1024]{2,1,0:T(8,128)(2,1)} %get-tuple-element.1311.wa_ref, bf16[4,512,1024]{2,1,0:T(8,128)(2,1)} %collective-permute-done.1.refs_2_.wb_ref), custom_call_target="tpu_custom_call" | custom-call | tf_op jit(solution)/shard_map/input_grad/pallas_call | solution.py:771
  443.6 4.8 collective-permute-done.61.refs_1_
  451.6 3.9 fusion.5
  455.4 3.8 collective-permute-start.68
  467.1 4.2 scatter_fusion.1
  476.9 3.7 select_bitcast_fusion.1
  484.2 3.8 fusion.refs_0_
  498.7 15.5 %collective-permute-done.73 = bf16[2,64,2048]{2,1,0:T(8,128)(2,1)} collective-permute-done((bf16[2,64,2048]{2,1,0:T(8,128)(2,1)}, bf16[2,64,2048]{2,1,0:T(8,128)(2,1)}, u32[]{:S(2)}, u32[]{:S(2)}) %collective-permute-start.73) | collective-permute-done | bytes 524320 | tf_op jit(solution)/shard_map/ppermute | solution.py:531
  521.1 8.0 %collective-permute-done.75 = bf16[2,64,2048]{2,1,0:T(8,128)(2,1)S(1)} collective-permute-done((bf16[2,64,2048]{2,1,0:T(8,128)(2,1)S(1)}, bf16[2,64,2048]{2,1,0:T(8,128)(2,1)S(1)}, u32[]{:S(2)}, u32[]{:S(2)}) %collective-permute-start.75) | collective-permute-done | bytes 524320 | tf_op jit(solution)/shard_map/ppermute | solution.py:531
  533.7 3.5 assemble.1
  (573 shorter events, 359.8 us)
Async XLA Ops:
  6.5 31.3 %collective-permute-start.1 = (bf16[4,512,1024]{2,1,0:T(8,128)(2,1)}, bf16[4,512,1024]{2,1,0:T(8,128)(2,1)}, u32[]{:S(2)}, u32[]{:S(2)}) collective-permute-start(bf16[4,512,1024]{2,1,0:T(8,128)(2,1)} %layout.5), channel_id=1, source_target_pairs={{0,1},{1,0},{2,3},{3,2},{4,5},{5,4},{6,7},{7,6},{8,9},{9,8},{10,11... | collective-permute-start | bytes 12582920 | tf_op jit(solution)/shard_map/ppermute | solution.py:500
  12.5 25.2 %collective-permute-start.2 = (bf16[4,512,1024]{2,1,0:T(8,128)(2,1)}, bf16[4,512,1024]{2,1,0:T(8,128)(2,1)}, u32[]{:S(2)}, u32[]{:S(2)}) collective-permute-start(bf16[4,512,1024]{2,1,0:T(8,128)(2,1)} %layout.6), channel_id=1, source_target_pairs={{0,1},{1,0},{2,3},{3,2},{4,5},{5,4},{6,7},{7,6},{8,9},{9,8},{10,11... | collective-permute-start | bytes 12582920 | tf_op jit(solution)/shard_map/ppermute | solution.py:500
  15.2 22.5 %collective-permute-start.4 = (f32[48,1024]{1,0:T(8,128)}, f32[48,1024]{1,0:T(8,128)S(1)}, u32[]{:S(2)}, u32[]{:S(2)}) collective-permute-start(f32[48,1024]{1,0:T(8,128)} %bitcast.220), channel_id=1, source_target_pairs={{0,1},{1,0},{2,3},{3,2},{4,5},{5,4},{6,7},{7,6},{8,9},{9,8},{10,11... | collective-permute-start | bytes 589832 | tf_op jit(solution)/shard_map/ppermute | solution.py:472
  15.2 22.4 %collective-permute-start = (bf16[4,1024]{1,0:T(4,128)(2,1)S(1)}, bf16[4,1024]{1,0:T(4,128)(2,1)S(1)}, u32[]{:S(2)}, u32[]{:S(2)}) collective-permute-start(bf16[4,1024]{1,0:T(4,128)(2,1)S(1)} %get-tuple-element.1380), channel_id=1, source_target_pairs={{0,1},{1,0},{2,3},{3,2},{4,5},{5,4},{6,7},{7,6},{8,9},{9,8},{10,11... | collective-permute-start | bytes 24584 | tf_op jit(solution)/shard_map/ppermute | solution.py:472
  16.8 20.9 %collective-permute-start.3 = (bf16[1024,512]{1,0:T(8,128)(2,1)}, bf16[1024,512]{1,0:T(8,128)(2,1)S(1)}, u32[]{:S(2)}, u32[]{:S(2)}) collective-permute-start(bf16[1024,512]{1,0:T(8,128)(2,1)} %dynamic-slice_bitcast_fusion.2), channel_id=1, source_target_pairs={{0,1},{1,0},{2,3},{3,2},{4,5},{5,4},{6,7},{7,6},{8,9},{9,8},{10,11... | collective-permute-start | bytes 3145736 | tf_op jit(solution)/shard_map/ppermute | solution.py:502
  126.0 30.0 %collective-permute-start.21 = (bf16[20,48,512]{2,1,0:T(8,128)(2,1)}, bf16[20,48,512]{2,1,0:T(8,128)(2,1)S(1)}, u32[]{:S(2)}, u32[]{:S(2)}) collective-permute-start(bf16[20,48,512]{2,1,0:T(8,128)(2,1)} %after.11), channel_id=1, source_target_pairs={{0,4},{4,0},{8,12},{12,8},{16,20},{20,16},{24,28},{28,24},{1,5},{5... | collective-permute-start | bytes 2949128 | tf_op jit(solution)/shard_map/ppermute | solution.py:531
  127.6 28.5 %collective-permute-start.22 = (bf16[20,48,512]{2,1,0:T(8,128)(2,1)}, bf16[20,48,512]{2,1,0:T(8,128)(2,1)S(1)}, u32[]{:S(2)}, u32[]{:S(2)}) collective-permute-start(bf16[20,48,512]{2,1,0:T(8,128)(2,1)} %after.11), channel_id=1, source_target_pairs={{0,8},{4,12},{8,0},{12,4},{16,24},{20,28},{24,16},{28,20},{1,9},{5... | collective-permute-start | bytes 2949128 | tf_op jit(solution)/shard_map/ppermute | solution.py:531
  196.7 46.3 %collective-permute-start.33 = (bf16[20,48,512]{2,1,0:T(8,128)(2,1)}, bf16[20,48,512]{2,1,0:T(8,128)(2,1)S(1)}, u32[]{:S(2)}, u32[]{:S(2)}) collective-permute-start(bf16[20,48,512]{2,1,0:T(8,128)(2,1)} %after.12), channel_id=1, source_target_pairs={{0,4},{4,0},{8,12},{12,8},{16,20},{20,16},{24,28},{28,24},{1,5},{5... | collective-permute-start | bytes 2949128 | tf_op jit(solution)/shard_map/ppermute | solution.py:531
  197.2 45.7 %collective-permute-start.34 = (bf16[20,48,512]{2,1,0:T(8,128)(2,1)}, bf16[20,48,512]{2,1,0:T(8,128)(2,1)S(1)}, u32[]{:S(2)}, u32[]{:S(2)}) collective-permute-start(bf16[20,48,512]{2,1,0:T(8,128)(2,1)} %after.12), channel_id=1, source_target_pairs={{0,8},{4,12},{8,0},{12,4},{16,24},{20,28},{24,16},{28,20},{1,9},{5... | collective-permute-start | bytes 2949128 | tf_op jit(solution)/shard_map/ppermute | solution.py:531
  250.3 49.3 %collective-permute-start.43 = (bf16[7,48,2048]{2,1,0:T(8,128)(2,1)}, bf16[7,48,2048]{2,1,0:T(8,128)(2,1)S(1)}, u32[]{:S(2)}, u32[]{:S(2)}) collective-permute-start(bf16[7,48,2048]{2,1,0:T(8,128)(2,1)} %get-tuple-element.1175), channel_id=1, source_target_pairs={{0,4},{4,0},{8,12},{12,8},{16,20},{20,16},{24,28},{28,24},{1,5},{5... | collective-permute-start | bytes 4128776 | tf_op jit(solution)/shard_map/ppermute | solution.py:531
  251.9 47.7 %collective-permute-start.44 = (bf16[7,48,2048]{2,1,0:T(8,128)(2,1)}, bf16[7,48,2048]{2,1,0:T(8,128)(2,1)S(1)}, u32[]{:S(2)}, u32[]{:S(2)}) collective-permute-start(bf16[7,48,2048]{2,1,0:T(8,128)(2,1)} %get-tuple-element.1176), channel_id=1, source_target_pairs={{0,8},{4,12},{8,0},{12,4},{16,24},{20,28},{24,16},{28,20},{1,9},{5... | collective-permute-start | bytes 4128776 | tf_op jit(solution)/shard_map/ppermute | solution.py:531
  296.2 42.5 %collective-permute-start.50 = (bf16[6,48,2048]{2,1,0:T(8,128)(2,1)}, bf16[6,48,2048]{2,1,0:T(8,128)(2,1)S(1)}, u32[]{:S(2)}, u32[]{:S(2)}) collective-permute-start(bf16[6,48,2048]{2,1,0:T(8,128)(2,1)} %get-tuple-element.1255), channel_id=1, source_target_pairs={{0,4},{4,0},{8,12},{12,8},{16,20},{20,16},{24,28},{28,24},{1,5},{5... | collective-permute-start | bytes 3538952 | tf_op jit(solution)/shard_map/ppermute | solution.py:531
  296.8 44.0 %collective-permute-start.51 = (bf16[6,48,2048]{2,1,0:T(8,128)(2,1)}, bf16[6,48,2048]{2,1,0:T(8,128)(2,1)S(1)}, u32[]{:S(2)}, u32[]{:S(2)}) collective-permute-start(bf16[6,48,2048]{2,1,0:T(8,128)(2,1)} %get-tuple-element.1256), channel_id=1, source_target_pairs={{0,8},{4,12},{8,0},{12,4},{16,24},{20,28},{24,16},{28,20},{1,9},{5... | collective-permute-start | bytes 3538952 | tf_op jit(solution)/shard_map/ppermute | solution.py:531
  321.3 27.1 %collective-permute-start.52 = (bf16[3,48,2048]{2,1,0:T(8,128)(2,1)}, bf16[3,48,2048]{2,1,0:T(8,128)(2,1)S(1)}, u32[]{:S(2)}, u32[]{:S(2)}) collective-permute-start(bf16[3,48,2048]{2,1,0:T(8,128)(2,1)} %get-tuple-element.1272), channel_id=1, source_target_pairs={{0,4},{4,0},{8,12},{12,8},{16,20},{20,16},{24,28},{28,24},{1,5},{5... | collective-permute-start | bytes 1769480 | tf_op jit(solution)/shard_map/ppermute | solution.py:531
  323.0 25.5 %collective-permute-start.53 = (bf16[3,48,2048]{2,1,0:T(8,128)(2,1)}, bf16[3,48,2048]{2,1,0:T(8,128)(2,1)S(1)}, u32[]{:S(2)}, u32[]{:S(2)}) collective-permute-start(bf16[3,48,2048]{2,1,0:T(8,128)(2,1)} %get-tuple-element.1273), channel_id=1, source_target_pairs={{0,8},{4,12},{8,0},{12,4},{16,24},{20,28},{24,16},{28,20},{1,9},{5... | collective-permute-start | bytes 1769480 | tf_op jit(solution)/shard_map/ppermute | solution.py:531
  338.8 24.8 %collective-permute-start.54 = (bf16[2,48,2048]{2,1,0:T(8,128)(2,1)}, bf16[2,48,2048]{2,1,0:T(8,128)(2,1)S(1)}, u32[]{:S(2)}, u32[]{:S(2)}) collective-permute-start(bf16[2,48,2048]{2,1,0:T(8,128)(2,1)} %get-tuple-element.1285), channel_id=1, source_target_pairs={{0,8},{4,12},{8,0},{12,4},{16,24},{20,28},{24,16},{28,20},{1,9},{5... | collective-permute-start | bytes 1179656 | tf_op jit(solution)/shard_map/ppermute | solution.py:531
  340.8 22.8 %collective-permute-start.56 = (bf16[2,48,2048]{2,1,0:T(8,128)(2,1)}, bf16[2,48,2048]{2,1,0:T(8,128)(2,1)S(1)}, u32[]{:S(2)}, u32[]{:S(2)}) collective-permute-start(bf16[2,48,2048]{2,1,0:T(8,128)(2,1)} %get-tuple-element.1287), channel_id=1, source_target_pairs={{0,4},{4,0},{8,12},{12,8},{16,20},{20,16},{24,28},{28,24},{1,5},{5... | collective-permute-start | bytes 1179656 | tf_op jit(solution)/shard_map/ppermute | solution.py:531
  358.1 43.6 %collective-permute-start.59 = (bf16[4,4,68,512]{3,1,2,0:T(4,128)(2,1)S(1)}, bf16[4,4,68,512]{3,1,2,0:T(4,128)(2,1)S(1)}, u32[]{:S(2)}, u32[]{:S(2)}) collective-permute-start(bf16[4,4,68,512]{3,1,2,0:T(4,128)(2,1)S(1)} %copy.527), channel_id=1, source_target_pairs={{0,4},{4,0},{8,12},{12,8},{16,20},{20,16},{24,28},{28,24},{1,5},{5... | collective-permute-start | bytes 3342344 | tf_op jit(solution)/shard_map/ppermute | solution.py:531
  370.0 32.1 %collective-permute-start.58 = (bf16[2,2,64,2048]{3,2,1,0:T(8,128)(2,1)S(1)}, bf16[2,2,64,2048]{3,2,1,0:T(8,128)(2,1)S(1)}, u32[]{:S(2)}, u32[]{:S(2)}) collective-permute-start(bf16[2,2,64,2048]{3,2,1,0:T(8,128)(2,1)S(1)} %bitcast.236), channel_id=1, source_target_pairs={{0,8},{4,12},{24,16},{28,20},{1,9},{5,13},{25,17},{29,21},{2,10},{... | collective-permute-start | bytes 3145736 | tf_op jit(solution)/shard_map/ppermute | solution.py:531
  402.6 37.6 %collective-permute-start.63 = (bf16[4,2,68,512]{3,0,2,1:T(4,128)(2,1)S(1)}, bf16[4,2,68,512]{3,0,2,1:T(4,128)(2,1)S(1)}, u32[]{:S(2)}, u32[]{:S(2)}) collective-permute-start(bf16[4,2,68,512]{3,0,2,1:T(4,128)(2,1)S(1)} %copy.532), channel_id=1, source_target_pairs={{0,16},{4,20},{8,24},{12,28},{16,0},{20,4},{24,8},{28,12},{1,17},{... | collective-permute-start | bytes 1671176 | tf_op jit(solution)/shard_map/ppermute | solution.py:531
  412.0 28.4 %collective-permute-start.62 = (bf16[4,64,2048]{2,1,0:T(8,128)(2,1)}, bf16[4,64,2048]{2,1,0:T(8,128)(2,1)}, u32[]{:S(2)}, u32[]{:S(2)}) collective-permute-start(bf16[4,64,2048]{2,1,0:T(8,128)(2,1)} %dynamic-slice_bitcast_fusion.1), channel_id=1, source_target_pairs={{0,4},{4,0},{8,12},{12,8},{16,20},{20,16},{24,28},{28,24},{1,5},{5... | collective-permute-start | bytes 3145736 | tf_op jit(solution)/shard_map/ppermute | solution.py:531
  415.1 28.4 %collective-permute-start.60 = (bf16[2,2,64,2048]{3,2,1,0:T(8,128)(2,1)}, bf16[2,2,64,2048]{3,2,1,0:T(8,128)(2,1)}, u32[]{:S(2)}, u32[]{:S(2)}) collective-permute-start(bf16[2,2,64,2048]{3,2,1,0:T(8,128)(2,1)} %get-tuple-element.1353), channel_id=1, source_target_pairs={{0,8},{4,12},{8,16},{12,20},{1,9},{5,13},{9,17},{13,21},{2,10},{6,... | collective-permute-start | bytes 3145736 | tf_op jit(solution)/shard_map/ppermute | solution.py:531
  417.2 31.1 %collective-permute-start.61 = (bf16[2,2,64,2048]{3,2,1,0:T(8,128)(2,1)}, bf16[2,2,64,2048]{3,2,1,0:T(8,128)(2,1)}, u32[]{:S(2)}, u32[]{:S(2)}) collective-permute-start(bf16[2,2,64,2048]{3,2,1,0:T(8,128)(2,1)} %get-tuple-element.1352), channel_id=1, source_target_pairs={{16,8},{20,12},{24,16},{28,20},{17,9},{21,13},{25,17},{29,21},{18,... | collective-permute-start | bytes 3145736 | tf_op jit(solution)/shard_map/ppermute | solution.py:531
  419.9 42.5 %collective-permute-start.71 = (bf16[4,64,2048]{2,1,0:T(8,128)(2,1)S(1)}, bf16[4,64,2048]{2,1,0:T(8,128)(2,1)S(1)}, u32[]{:S(2)}, u32[]{:S(2)}) collective-permute-start(bf16[4,64,2048]{2,1,0:T(8,128)(2,1)S(1)} %dynamic-slice_bitcast_fusion), channel_id=1, source_target_pairs={{0,4},{4,0},{8,12},{12,8},{16,20},{20,16},{24,28},{28,24},{1,5},{5... | collective-permute-start | bytes 3145736 | tf_op jit(solution)/shard_map/ppermute | solution.py:531
  449.1 22.2 %collective-permute-start.77 = (bf16[4,68,512]{2,1,0:T(8,128)(2,1)}, bf16[4,68,512]{2,1,0:T(8,128)(2,1)}, u32[]{:S(2)}, u32[]{:S(2)}) collective-permute-start(bf16[4,68,512]{2,1,0:T(8,128)(2,1)} %dynamic-slice_bitcast_fusion.10), channel_id=1, source_target_pairs={{0,8},{4,12},{8,0},{12,4},{16,24},{20,28},{24,16},{28,20},{1,9},{5... | collective-permute-start | bytes 835592 | tf_op jit(solution)/shard_map/ppermute | solution.py:531
  450.0 25.2 %collective-permute-start.70 = (bf16[2,64,2048]{2,1,0:T(8,128)(2,1)}, bf16[2,64,2048]{2,1,0:T(8,128)(2,1)}, u32[]{:S(2)}, u32[]{:S(2)}) collective-permute-start(bf16[2,64,2048]{2,1,0:T(8,128)(2,1)} %dynamic-slice_bitcast_fusion.9), channel_id=1, source_target_pairs={{0,16},{4,20},{8,24},{12,28},{16,0},{20,4},{24,8},{28,12},{1,17},{... | collective-permute-start | bytes 1572872 | tf_op jit(solution)/shard_map/ppermute | solution.py:531
  455.4 32.6 %collective-permute-start.68 = (bf16[2,2,64,2048]{3,2,1,0:T(8,128)(2,1)}, bf16[2,2,64,2048]{3,2,1,0:T(8,128)(2,1)}, u32[]{:S(2)}, u32[]{:S(2)}) collective-permute-start(bf16[2,2,64,2048]{3,2,1,0:T(8,128)(2,1)} %get-tuple-element.1357), channel_id=1, source_target_pairs={{0,8},{4,12},{8,16},{12,20},{16,24},{20,28},{1,9},{5,13},{9,17},{1... | collective-permute-start | bytes 3145736 | tf_op jit(solution)/shard_map/ppermute | solution.py:531
  459.2 28.8 %collective-permute-start.69 = (bf16[2,2,64,2048]{3,2,1,0:T(8,128)(2,1)}, bf16[2,2,64,2048]{3,2,1,0:T(8,128)(2,1)}, u32[]{:S(2)}, u32[]{:S(2)}) collective-permute-start(bf16[2,2,64,2048]{3,2,1,0:T(8,128)(2,1)} %get-tuple-element.1356), channel_id=1, source_target_pairs={{8,0},{12,4},{16,8},{20,12},{24,16},{28,20},{9,1},{13,5},{17,9},{2... | collective-permute-start | bytes 3145736 | tf_op jit(solution)/shard_map/ppermute | solution.py:531
  471.4 20.6 %collective-permute-start.65 = (bf16[20,48,256]{2,1,0:T(8,128)(2,1)}, bf16[20,48,256]{2,1,0:T(8,128)(2,1)}, u32[]{:S(2)}, u32[]{:S(2)}) collective-permute-start(bf16[20,48,256]{2,1,0:T(8,128)(2,1)} %dynamic-slice_convert_fusion), channel_id=1, source_target_pairs={{0,2},{1,3},{2,0},{3,1},{4,6},{5,7},{6,4},{7,5},{8,10},{9,11},{10,... | collective-permute-start | bytes 1474568 | tf_op jit(solution)/shard_map/ppermute | solution.py:945
  475.1 54.0 %collective-permute-start.79 = (bf16[1024,64]{0,1:T(8,128)(2,1)}, bf16[1024,64]{0,1:T(8,128)(2,1)}, u32[]{:S(2)}, u32[]{:S(2)}) collective-permute-start(bf16[1024,64]{0,1:T(8,128)(2,1)} %bitcast.143), channel_id=1, source_target_pairs={{0,1},{1,0},{2,3},{3,2},{4,5},{5,4},{6,7},{7,6},{8,9},{9,8},{10,11... | collective-permute-start | bytes 393224 | tf_op jit(solution)/shard_map/ppermute | solution.py:472
  489.9 24.4 %collective-permute-start.73 = (bf16[2,64,2048]{2,1,0:T(8,128)(2,1)}, bf16[2,64,2048]{2,1,0:T(8,128)(2,1)}, u32[]{:S(2)}, u32[]{:S(2)}) collective-permute-start(bf16[2,64,2048]{2,1,0:T(8,128)(2,1)} %dynamic-slice_bitcast_fusion.6), channel_id=1, source_target_pairs={{0,16},{4,20},{8,24},{12,28},{16,0},{20,4},{24,8},{28,12},{1,17},{... | collective-permute-start | bytes 1572872 | tf_op jit(solution)/shard_map/ppermute | solution.py:531
  498.6 32.2 %collective-permute-start.66 = (bf16[20,48,128]{2,1,0:T(8,128)(2,1)S(1)}, bf16[20,48,128]{2,1,0:T(8,128)(2,1)S(1)}, u32[]{:S(2)}, u32[]{:S(2)}) collective-permute-start(bf16[20,48,128]{2,1,0:T(8,128)(2,1)S(1)} %bitcast.251), channel_id=1, source_target_pairs={{0,1},{1,0},{2,3},{3,2},{4,5},{5,4},{6,7},{7,6},{8,9},{9,8},{10,11... | collective-permute-start | bytes 737288 | tf_op jit(solution)/shard_map/ppermute | solution.py:472
  (151 other events, 774.4 us)

commit v13 on v12

--- a/solution.py
+++ b/solution.py
@@ -150,6 +150,49 @@
             return 0
 
         lax.fori_loop(0, 4, columns, 0)
+
+
+def whole_product_kernel(lows, *refs):
+    (feat_ref, prev_ref, feat_too, prev_too, kept_ref), refs = refs[:5], refs[5:]
+    groups, (out_ref, left_buf, turned_buf, right_buf, left_sems, sems) = refs[:-6], refs[-6:]
+    steps, streams, depth = feat_ref.shape
+    blocks = right_buf.shape[0]
+    width = right_buf.shape[3]
+    rows = 2 * steps * streams
+
+    def fetches_of(block):
+        cols = slice(block * width, (block + 1) * width)
+        jobs = [(kept_ref.at[:, :, cols], right_buf.at[block, :steps])]
+        jobs += [
+            (x.at[:, :, cols], right_buf.at[block, steps + low : steps + low + x.shape[0]])
+            for x, low in zip(groups, lows)
+        ]
+        return [pltpu.make_async_copy(a, b, sems.at[block, i]) for i, (a, b) in enumerate(jobs)]
+
+    lefts = [(feat_ref, 0, 0), (feat_too, steps, 0), (prev_ref, 0, 1), (prev_too, steps, 1)]
+    lefts = [
+        pltpu.make_async_copy(x, left_buf.at[half, low : low + steps], left_sems.at[i])
+        for i, (x, low, half) in enumerate(lefts)
+    ]
+    for copy in lefts:
+        copy.start()
+    for block in range(blocks):
+        for copy in fetches_of(block):
+            copy.start()
+    for which in range(2):
+        lefts[2 * which].wait()
+        lefts[2 * which + 1].wait()
+        turned_buf[which] = left_buf[which].reshape(rows, depth).T
+    for block in range(blocks):
+        for copy in fetches_of(block):
+            copy.wait()
+
+        def one(which, _):
+            total = dot(turned_buf[which], right_buf[block].reshape(rows, width))
+            out_ref[which, :, block * width : (block + 1) * width] = total.astype(BF16)
+            return 0
+
+        lax.fori_loop(0, 2, one, 0)
 
 
 def assemble_kernel(place_ref, near_a, near_b, far_a, far_b, in_ref, rec_ref):
@@ -741,7 +784,7 @@
     def by_direction(mine, theirs):
         return jnp.stack([jnp.where(own == 0, mine, theirs), jnp.where(own == 0, theirs, mine)])
 
-    def line_sum(chunks, axis, stride, count, first=None, gates={}):
+    def line_sum(chunks, axis, stride, count, first=None, gates={}, hooks={}):
         def chunk(*name):
             return pick(chunks, number[(stride, *name)], axis)
 
@@ -759,6 +802,8 @@
                 up, down = gates[slot](up, down)
             rise = (chunk("rise", slot).astype(F32) + up.astype(F32)).astype(BF16)
             fall = (chunk("fall", slot).astype(F32) + down.astype(F32)).astype(BF16)
+            if slot in hooks:
+                hooks[slot](rise, fall)
             up = swapped(rise, [(i, i + stride) for i in range(n_batch) if at(i) < min(slot, count - 1)])
             down = swapped(fall, [(i, i - stride) for i in range(n_batch) if at(i) > max(count - 1 - slot, 0)])
         if count in gates:
@@ -861,9 +906,24 @@
     near_late = after((near_left, proj_sent, *far_parts[-LATE:]), *near_parts[-LATE:])
     near_right, first = completed(jnp.full((1,), number["begin"], jnp.int32), chunk_rows, near_left, near_right, near_late)
     far_all, *far_parts = after((first,), far_all, *far_parts)
-    far_left, far_right = gathered(far_all, feat_in[1], prev_in[1], far_parts[:-LATE])
-    far_right, _ = completed(jnp.zeros((1,), jnp.int32), 0, far_left, far_right, far_parts[-LATE:])
-    far = multiplied(far_left, far_right).reshape(2, line, 2, share_rows, 4 * width)
+    blocks = 4
+    far = pl.pallas_call(
+        functools.partial(whole_product_kernel, tuple(lows)),
+        out_shape=jax.ShapeDtypeStruct((2, depth, 4 * width), BF16),
+        in_specs=[ANY] * (5 + len(far_parts)),
+        out_specs=VMEM,
+        scratch_shapes=[
+            pltpu.VMEM((2, 2 * steps, streams, depth), BF16),
+            pltpu.VMEM((2, depth, 2 * steps * streams), BF16),
+            pltpu.VMEM((blocks, 2 * steps, streams, 4 * width // blocks), BF16),
+            pltpu.SemaphoreType.DMA((4,)),
+            pltpu.SemaphoreType.DMA((blocks, 1 + len(far_parts))),
+        ],
+        compiler_params=params(28),
+        cost_estimate=cost(0, 0),
+        name="whole_product",
+    )(*(in_hbm(x) for x in (feat_all, prev_all, feat_in[1], prev_in[1], far_all, *far_parts)))
+    far = far.reshape(2, line, 2, share_rows, 4 * width)
     near = multiplied(near_left, near_right).reshape(2, line, 2, share_rows, 4 * width)
 
     def states_of(hidden, cell):
@@ -883,28 +943,36 @@
     tokens = {}
 
     def second(up, down):
-        up, sent, tokens["dz"], proj_sum = after((), up, far, dz_all, proj_y, free=2 * MIB)
+        up, tokens["far"], tokens["dz"], tokens["proj"] = after((), up, far, dz_all, proj_y, free=5 * MIB)
+        return up, up
+
+    def beside_second(rise, fall):
+        (sent,) = after((rise, fall), tokens["far"], free=5 * MIB)
         tokens["in"], tokens["rec"] = (with_partner(sent[i])[2] for i in range(2))
-        tokens["proj"] = across_two(proj_sum)
-        return up, up
+        tokens["proj"] = across_two(tokens["proj"])
 
     def third(up, down):
         dx = input_grad_of(tokens["dz"])
-        up, down, tokens["dx"], in_sum, tokens["proj"], hidden, last_cell = after(
-            (), up, down, dx, tokens["in"], tokens["proj"], hidden_all, cell, free=2 * MIB
+        up, down, tokens["dx"], tokens["in"], tokens["proj"] = after(
+            (), up, down, dx, tokens["in"], tokens["proj"], free=2 * MIB
         )
-        tokens["in"] = across_two(in_sum)
+        return up, down
+
+    def beside_third(rise, fall):
+        in_sum, hidden, last_cell = after((rise, fall), tokens["in"], hidden_all, cell, free=2 * MIB)
+        tokens["in"], tokens["rec"] = across_two(in_sum), across_two(tokens["rec"])
         tokens["states"] = states_of(hidden, last_cell)
+
+    def final(up, down):
+        up, down, tokens["in"], tokens["rec"], tokens["proj"] = after(
+            tokens["states"], up, down, tokens["in"], tokens["rec"], tokens["proj"], free=2 * MIB
+        )
         return up, down
 
-    def final(up, down):
-        up, down, tokens["in"], rec_sum = after(tokens["states"], up, down, tokens["in"], tokens["rec"], free=2 * MIB)
-        tokens["rec"] = across_two(rec_sum)
-        return up, down
-
     gates = {2: second, 3: third, line: final} if line > 3 else {}
+    hooks = {2: beside_second, 3: beside_third} if line > 3 else {}
     first = first.reshape(2, 2, share_rows, 4 * width) if chunk_rows else None
-    near = line_sum(near, 1, 2, line, first, gates)
+    near = line_sum(near, 1, 2, line, first, gates, hooks)
     dx_all, (outputs, final_h, final_c) = tokens["dx"], tokens["states"]
     in_two, rec_two, proj_two = tokens["in"], tokens["rec"], tokens["proj"]
 

time: 548 us -> 562 us (1.026)
  waiting for transfers between devices: 36.1 us -> 53.3 us
  local copies, waits for them, and re-layouts: 51.4 us -> 41.9 us
  starting transfers between devices: 84.7 us -> 91 us
    pallas_call x0 -> x1, Pallas kernels: none -> 16.7 us  [body(): pl.pallas_call(functools.partial(whole_product_kernel, tuple(lows)), out_...]
    pallas_call x2 -> x1, Pallas kernels: 22.4 us -> 11.2 us  [multiplied(): pl.pallas_call(product_kernel, out_shape=jax.ShapeDtypeStruct((2, depth,...]
    ppermute x28, waiting for transfers between devices: 31 us -> 40.5 us  [swapped(): return lax.ppermute(array, 'batch', pairs)]
    ppermute x1, waiting for transfers between devices: 0.01 us -> 7.58 us  [body(): dx_half = dx_half + lax.ppermute(dx_sent, 'gate', across).astype(F32)]
    ppermute x28, starting transfers between devices: 38 us -> 44.1 us  [swapped(): return lax.ppermute(array, 'batch', pairs)]
    unnamed x217 -> x245, local copies, waits for them, and re-layouts: 18.9 us -> 18.4 us
  transfers between devices with their start and end apart: 80 -> 80, of which waited for: 30 -> 33; matrix products, arithmetic and copies ran while one was open for 13% -> 11% of each run, Pallas kernels for 48% -> 47%
where the time goes in v13:
time: 562 us; the launch traced here: 551 us
  Pallas kernels  326 us (58%)
  starting transfers between devices  91 us (16%)
  waiting for transfers between devices  53.3 us (9%)
  local copies, waits for them, and re-layouts  41.9 us (7%)
  other arithmetic  31.5 us (6%)
    pallas_call x20, Pallas kernels, backward_call(): pl.pallas_call(backward_kernel, out_shape=(vmem((streams, depth), BF16),...  61.8 us
    pallas_call x19, Pallas kernels, between_call(): pl.pallas_call(functools.partial(between_kernel, not stacks, step == step...  56.8 us
    pallas_call x20, Pallas kernels, forward_call(): pl.pallas_call(functools.partial(forward_kernel, first), out_shape=(vmem(...  56.1 us
    pallas_call x20, Pallas kernels, aside_call(): pl.pallas_call(functools.partial(aside_kernel, not stacks, step == 0, not...  55.9 us
    ppermute x28, starting transfers between devices, swapped(): return lax.ppermute(array, 'batch', pairs)  44.1 us
    ppermute x39, starting transfers between devices, body(): peer = lax.ppermute(part, 'gate', across)  43.4 us
    ppermute x28, waiting for transfers between devices, swapped(): return lax.ppermute(array, 'batch', pairs)  40.5 us
    pallas_call x4, Pallas kernels, by_gate(): pl.pallas_call(functools.partial(layout_kernel, keep, spread), out_shape=...  23.4 us
  transfers between devices with their start and end apart: 80, of which 33 were waited for; matrix products, arithmetic and copies ran while one was open for 11% of the time, Pallas kernels for 47%

profile of v13, /device:TPU:8, one launch (start us, length us, event | category | flops | bytes accessed | tf_op | source)
XLA Modules:
  0.0 551.0 jit_solution(6426321263460475952)
XLA Ops:
  0.7 5.9 %layout.5 = bf16[4,512,1024]{2,1,0:T(8,128)(2,1)} custom-call(s32[1]{0:T(128)} %bitcast.17.which_ref, bf16[2,512,4,1024]{3,2,1,0:T(4,128)(2,1)} %w_ref.5), custom_call_target="tpu_custom_call" | custom-call | tf_op jit(solution)/shard_map/layout/pallas_call | solution.py:527
  6.6 5.9 %layout.6 = bf16[4,512,1024]{2,1,0:T(8,128)(2,1)} custom-call(s32[1]{0:T(128)} %bitcast.17.which_ref, bf16[2,512,4,1024]{3,2,1,0:T(4,128)(2,1)} %w_ref.7), custom_call_target="tpu_custom_call" | custom-call | tf_op jit(solution)/shard_map/layout/pallas_call | solution.py:527
  24.6 6.4 %layout.4 = (bf16[4,512,1024]{2,1,0:T(8,128)(2,1)S(1)}, bf16[4,512,1024]{2,1,0:T(8,128)(2,1)}) custom-call(s32[1]{0:T(128)} %slice.55.which_ref, bf16[2,512,4,1024]{3,2,1,0:T(4,128)(2,1)} %w_ref.5), custom_call_target="tpu_custom_call" | custom-call | tf_op jit(solution)/shard_map/layout/pallas_call | solution.py:527
  31.1 5.2 layout.7.wa_ref
  42.0 5.0 begin.1
  72.7 3.4 between.22
  160.9 3.2 between.34
  168.1 3.3 between.35
  228.2 3.0 backward_step.24
  242.6 3.0 backward_step.26
  251.0 3.2 backward_step.27
  296.7 3.5 backward_step.33
  322.2 3.0 backward_step.36
  338.6 3.0 backward_step.38
  348.9 3.8 backward_step.39
  353.9 3.0 aside.39
  358.0 3.6 bitcast_convert_fusion
  363.7 4.2 gather.13
  370.1 4.3 late.1
  375.8 11.2 %product.1 = bf16[2,512,2048]{2,1,0:T(8,128)(2,1)S(1)} custom-call(bf16[40,48,1024]{2,1,0:T(8,128)(2,1)S(1)} %get-tuple-element.1277.refs_0_.left_ref, bf16[40,48,2048]{2,1,0:T(8,128)(2,1)S(1)} %get-tuple-element.1290.right_ref), custom_call_target="tpu_custom_call" | custom-call | tf_op jit(solution)/shard_map/product/pallas_call | solution.py:893
  387.0 16.7 %whole_product.1 = bf16[2,512,2048]{2,1,0:T(8,128)(2,1)S(1)} custom-call(bf16[20,48,512]{2,1,0:T(8,128)(2,1)} %get-tuple-element.667.refs_0_, bf16[20,48,512]{2,1,0:T(8,128)(2,1)} %get-tuple-element.949.refs_1_, bf16[20,48,512]{2,1,0:T(8,128)(2,1)} %get-tuple-element.1292.refs_2_, bf16[20,48,512]{2,1,0:T(8,128)(2,1)} %get-tuple-element.1293.refs_3_, ...), custom_call_target="tpu_custom_call" | custom-call | tf_op jit(solution)/shard_map/whole_product/pallas_call | solution.py:910
  408.4 3.9 collective-permute-start.63
  418.1 19.2 %input_grad.1.refs_2_ = f32[20,48,512]{2,1,0:T(8,128)S(1)} custom-call(s32[2]{0:T(128)S(1)} %copy-done.47, bf16[4,20,48,2048]{3,2,1,0:T(8,128)(2,1)} %get-tuple-element.1306.dz_ref, bf16[4,512,1024]{2,1,0:T(8,128)(2,1)} %get-tuple-element.1307.wa_ref, bf16[4,512,1024]{2,1,0:T(8,128)(2,1)} %collective-permute-done.1.refs_2_.wb_ref), custom_call_target="tpu_custom_call" | custom-call | tf_op jit(solution)/shard_map/input_grad/pallas_call | solution.py:816
  445.0 19.0 %collective-permute-done.60.refs_0_ = bf16[2,2,64,2048]{3,2,1,0:T(8,128)(2,1)S(1)} collective-permute-done((bf16[2,2,64,2048]{3,2,1,0:T(8,128)(2,1)}, bf16[2,2,64,2048]{3,2,1,0:T(8,128)(2,1)S(1)}, u32[]{:S(2)}, u32[]{:S(2)}) %collective-permute-start.60) | collective-permute-done | bytes 1048608 | tf_op jit(solution)/shard_map/ppermute | solution.py:574
  466.2 4.3 collective-permute-start.68
  481.0 7.6 %collective-permute-done.65 = bf16[20,48,256]{2,1,0:T(8,128)(2,1)} collective-permute-done((bf16[20,48,256]{2,1,0:T(8,128)(2,1)}, bf16[20,48,256]{2,1,0:T(8,128)(2,1)}, u32[]{:S(2)}, u32[]{:S(2)}) %collective-permute-start.65) | collective-permute-done | bytes 491552 | tf_op jit(solution)/shard_map/ppermute | solution.py:1013
  496.1 9.5 %collective-permute-done.70 = bf16[2,64,2048]{2,1,0:T(8,128)(2,1)} collective-permute-done((bf16[2,64,2048]{2,1,0:T(8,128)(2,1)}, bf16[2,64,2048]{2,1,0:T(8,128)(2,1)}, u32[]{:S(2)}, u32[]{:S(2)}) %collective-permute-start.70) | collective-permute-done | bytes 524320 | tf_op jit(solution)/shard_map/ppermute | solution.py:574
  515.5 3.6 scatter_fusion
  522.9 5.9 %collective-permute-start.77 = (bf16[4,68,512]{2,1,0:T(8,128)(2,1)S(1)}, bf16[4,68,512]{2,1,0:T(8,128)(2,1)S(1)}, u32[]{:S(2)}, u32[]{:S(2)}) collective-permute-start(bf16[4,68,512]{2,1,0:T(8,128)(2,1)S(1)} %dynamic-slice_bitcast_fusion.10), channel_id=1, source_target_pairs={{0,8},{4,12},{8,0},{12,4},{16,24},{20,28},{24,16},{28,20},{1,9},{5... | collective-permute-start | bytes 835592 | tf_op jit(solution)/shard_map/ppermute | solution.py:574
  535.1 4.3 collective-permute-done.75
  540.8 6.3 %collective-permute-done.73.near_b = bf16[2,64,2048]{2,1,0:T(8,128)(2,1)S(1)} collective-permute-done((bf16[2,64,2048]{2,1,0:T(8,128)(2,1)S(1)}, bf16[2,64,2048]{2,1,0:T(8,128)(2,1)S(1)}, u32[]{:S(2)}, u32[]{:S(2)}) %collective-permute-start.73) | collective-permute-done | bytes 524320 | tf_op jit(solution)/shard_map/ppermute | solution.py:574
  547.1 3.5 assemble.1
  (601 shorter events, 356.6 us)
Async XLA Ops:
  6.6 34.5 %collective-permute-start.1 = (bf16[4,512,1024]{2,1,0:T(8,128)(2,1)}, bf16[4,512,1024]{2,1,0:T(8,128)(2,1)}, u32[]{:S(2)}, u32[]{:S(2)}) collective-permute-start(bf16[4,512,1024]{2,1,0:T(8,128)(2,1)} %layout.5), channel_id=1, source_target_pairs={{0,1},{1,0},{2,3},{3,2},{4,5},{5,4},{6,7},{7,6},{8,9},{9,8},{10,11... | collective-permute-start | bytes 12582920 | tf_op jit(solution)/shard_map/ppermute | solution.py:543
  12.6 28.5 %collective-permute-start.2 = (bf16[4,512,1024]{2,1,0:T(8,128)(2,1)}, bf16[4,512,1024]{2,1,0:T(8,128)(2,1)}, u32[]{:S(2)}, u32[]{:S(2)}) collective-permute-start(bf16[4,512,1024]{2,1,0:T(8,128)(2,1)} %layout.6), channel_id=1, source_target_pairs={{0,1},{1,0},{2,3},{3,2},{4,5},{5,4},{6,7},{7,6},{8,9},{9,8},{10,11... | collective-permute-start | bytes 12582920 | tf_op jit(solution)/shard_map/ppermute | solution.py:543
  16.3 22.9 %collective-permute-start.4 = (f32[48,1024]{1,0:T(8,128)}, f32[48,1024]{1,0:T(8,128)}, u32[]{:S(2)}, u32[]{:S(2)}) collective-permute-start(f32[48,1024]{1,0:T(8,128)} %bitcast.223), channel_id=1, source_target_pairs={{0,1},{1,0},{2,3},{3,2},{4,5},{5,4},{6,7},{7,6},{8,9},{9,8},{10,11... | collective-permute-start | bytes 589832 | tf_op jit(solution)/shard_map/ppermute | solution.py:515
  16.4 22.8 %collective-permute-start = (bf16[4,1024]{1,0:T(4,128)(2,1)S(1)}, bf16[4,1024]{1,0:T(4,128)(2,1)S(1)}, u32[]{:S(2)}, u32[]{:S(2)}) collective-permute-start(bf16[4,1024]{1,0:T(4,128)(2,1)S(1)} %get-tuple-element.1378), channel_id=1, source_target_pairs={{0,1},{1,0},{2,3},{3,2},{4,5},{5,4},{6,7},{7,6},{8,9},{9,8},{10,11... | collective-permute-start | bytes 24584 | tf_op jit(solution)/shard_map/ppermute | solution.py:515
  17.0 24.1 %collective-permute-start.3 = (bf16[1024,512]{1,0:T(8,128)(2,1)S(1)}, bf16[1024,512]{1,0:T(8,128)(2,1)S(1)}, u32[]{:S(2)}, u32[]{:S(2)}) collective-permute-start(bf16[1024,512]{1,0:T(8,128)(2,1)S(1)} %dynamic-slice_bitcast_fusion.2), channel_id=1, source_target_pairs={{0,1},{1,0},{2,3},{3,2},{4,5},{5,4},{6,7},{7,6},{8,9},{9,8},{10,11... | collective-permute-start | bytes 3145736 | tf_op jit(solution)/shard_map/ppermute | solution.py:545
  129.8 29.8 %collective-permute-start.21 = (bf16[20,48,512]{2,1,0:T(8,128)(2,1)}, bf16[20,48,512]{2,1,0:T(8,128)(2,1)S(1)}, u32[]{:S(2)}, u32[]{:S(2)}) collective-permute-start(bf16[20,48,512]{2,1,0:T(8,128)(2,1)} %after.13), channel_id=1, source_target_pairs={{0,4},{4,0},{8,12},{12,8},{16,20},{20,16},{24,28},{28,24},{1,5},{5... | collective-permute-start | bytes 2949128 | tf_op jit(solution)/shard_map/ppermute | solution.py:574
  131.3 28.3 %collective-permute-start.22 = (bf16[20,48,512]{2,1,0:T(8,128)(2,1)}, bf16[20,48,512]{2,1,0:T(8,128)(2,1)S(1)}, u32[]{:S(2)}, u32[]{:S(2)}) collective-permute-start(bf16[20,48,512]{2,1,0:T(8,128)(2,1)} %after.13), channel_id=1, source_target_pairs={{0,8},{4,12},{8,0},{12,4},{16,24},{20,28},{24,16},{28,20},{1,9},{5... | collective-permute-start | bytes 2949128 | tf_op jit(solution)/shard_map/ppermute | solution.py:574
  200.3 46.6 %collective-permute-start.33 = (bf16[20,48,512]{2,1,0:T(8,128)(2,1)}, bf16[20,48,512]{2,1,0:T(8,128)(2,1)S(1)}, u32[]{:S(2)}, u32[]{:S(2)}) collective-permute-start(bf16[20,48,512]{2,1,0:T(8,128)(2,1)} %after.14), channel_id=1, source_target_pairs={{0,4},{4,0},{8,12},{12,8},{16,20},{20,16},{24,28},{28,24},{1,5},{5... | collective-permute-start | bytes 2949128 | tf_op jit(solution)/shard_map/ppermute | solution.py:574
  200.8 46.0 %collective-permute-start.34 = (bf16[20,48,512]{2,1,0:T(8,128)(2,1)}, bf16[20,48,512]{2,1,0:T(8,128)(2,1)S(1)}, u32[]{:S(2)}, u32[]{:S(2)}) collective-permute-start(bf16[20,48,512]{2,1,0:T(8,128)(2,1)} %after.14), channel_id=1, source_target_pairs={{0,8},{4,12},{8,0},{12,4},{16,24},{20,28},{24,16},{28,20},{1,9},{5... | collective-permute-start | bytes 2949128 | tf_op jit(solution)/shard_map/ppermute | solution.py:574
  254.3 49.3 %collective-permute-start.43 = (bf16[7,48,2048]{2,1,0:T(8,128)(2,1)}, bf16[7,48,2048]{2,1,0:T(8,128)(2,1)S(1)}, u32[]{:S(2)}, u32[]{:S(2)}) collective-permute-start(bf16[7,48,2048]{2,1,0:T(8,128)(2,1)} %get-tuple-element.1174), channel_id=1, source_target_pairs={{0,4},{4,0},{8,12},{12,8},{16,20},{20,16},{24,28},{28,24},{1,5},{5... | collective-permute-start | bytes 4128776 | tf_op jit(solution)/shard_map/ppermute | solution.py:574
  255.8 47.7 %collective-permute-start.44 = (bf16[7,48,2048]{2,1,0:T(8,128)(2,1)}, bf16[7,48,2048]{2,1,0:T(8,128)(2,1)S(1)}, u32[]{:S(2)}, u32[]{:S(2)}) collective-permute-start(bf16[7,48,2048]{2,1,0:T(8,128)(2,1)} %get-tuple-element.1175), channel_id=1, source_target_pairs={{0,8},{4,12},{8,0},{12,4},{16,24},{20,28},{24,16},{28,20},{1,9},{5... | collective-permute-start | bytes 4128776 | tf_op jit(solution)/shard_map/ppermute | solution.py:574
  300.2 42.8 %collective-permute-start.50 = (bf16[6,48,2048]{2,1,0:T(8,128)(2,1)}, bf16[6,48,2048]{2,1,0:T(8,128)(2,1)S(1)}, u32[]{:S(2)}, u32[]{:S(2)}) collective-permute-start(bf16[6,48,2048]{2,1,0:T(8,128)(2,1)} %get-tuple-element.1254), channel_id=1, source_target_pairs={{0,4},{4,0},{8,12},{12,8},{16,20},{20,16},{24,28},{28,24},{1,5},{5... | collective-permute-start | bytes 3538952 | tf_op jit(solution)/shard_map/ppermute | solution.py:574
  300.7 44.3 %collective-permute-start.51 = (bf16[6,48,2048]{2,1,0:T(8,128)(2,1)}, bf16[6,48,2048]{2,1,0:T(8,128)(2,1)S(1)}, u32[]{:S(2)}, u32[]{:S(2)}) collective-permute-start(bf16[6,48,2048]{2,1,0:T(8,128)(2,1)} %get-tuple-element.1255), channel_id=1, source_target_pairs={{0,8},{4,12},{8,0},{12,4},{16,24},{20,28},{24,16},{28,20},{1,9},{5... | collective-permute-start | bytes 3538952 | tf_op jit(solution)/shard_map/ppermute | solution.py:574
  325.3 27.6 %collective-permute-start.52 = (bf16[3,48,2048]{2,1,0:T(8,128)(2,1)}, bf16[3,48,2048]{2,1,0:T(8,128)(2,1)S(1)}, u32[]{:S(2)}, u32[]{:S(2)}) collective-permute-start(bf16[3,48,2048]{2,1,0:T(8,128)(2,1)} %get-tuple-element.1271), channel_id=1, source_target_pairs={{0,4},{4,0},{8,12},{12,8},{16,20},{20,16},{24,28},{28,24},{1,5},{5... | collective-permute-start | bytes 1769480 | tf_op jit(solution)/shard_map/ppermute | solution.py:574
  327.3 25.6 %collective-permute-start.53 = (bf16[3,48,2048]{2,1,0:T(8,128)(2,1)}, bf16[3,48,2048]{2,1,0:T(8,128)(2,1)S(1)}, u32[]{:S(2)}, u32[]{:S(2)}) collective-permute-start(bf16[3,48,2048]{2,1,0:T(8,128)(2,1)} %get-tuple-element.1272), channel_id=1, source_target_pairs={{0,8},{4,12},{8,0},{12,4},{16,24},{20,28},{24,16},{28,20},{1,9},{5... | collective-permute-start | bytes 1769480 | tf_op jit(solution)/shard_map/ppermute | solution.py:574
  343.0 24.9 %collective-permute-start.54 = (bf16[2,48,2048]{2,1,0:T(8,128)(2,1)}, bf16[2,48,2048]{2,1,0:T(8,128)(2,1)S(1)}, u32[]{:S(2)}, u32[]{:S(2)}) collective-permute-start(bf16[2,48,2048]{2,1,0:T(8,128)(2,1)} %get-tuple-element.1284), channel_id=1, source_target_pairs={{0,8},{4,12},{8,0},{12,4},{16,24},{20,28},{24,16},{28,20},{1,9},{5... | collective-permute-start | bytes 1179656 | tf_op jit(solution)/shard_map/ppermute | solution.py:574
  345.1 22.8 %collective-permute-start.56 = (bf16[2,48,2048]{2,1,0:T(8,128)(2,1)}, bf16[2,48,2048]{2,1,0:T(8,128)(2,1)S(1)}, u32[]{:S(2)}, u32[]{:S(2)}) collective-permute-start(bf16[2,48,2048]{2,1,0:T(8,128)(2,1)} %get-tuple-element.1286), channel_id=1, source_target_pairs={{0,4},{4,0},{8,12},{12,8},{16,20},{20,16},{24,28},{28,24},{1,5},{5... | collective-permute-start | bytes 1179656 | tf_op jit(solution)/shard_map/ppermute | solution.py:574
  362.4 41.3 %collective-permute-start.59 = (bf16[4,4,68,512]{3,1,2,0:T(4,128)(2,1)S(1)}, bf16[4,4,68,512]{3,1,2,0:T(4,128)(2,1)S(1)}, u32[]{:S(2)}, u32[]{:S(2)}) collective-permute-start(bf16[4,4,68,512]{3,1,2,0:T(4,128)(2,1)S(1)} %copy.526), channel_id=1, source_target_pairs={{0,4},{4,0},{8,12},{12,8},{16,20},{20,16},{24,28},{28,24},{1,5},{5... | collective-permute-start | bytes 3342344 | tf_op jit(solution)/shard_map/ppermute | solution.py:574
  374.5 29.7 %collective-permute-start.58 = (bf16[2,2,64,2048]{3,2,1,0:T(8,128)(2,1)S(1)}, bf16[2,2,64,2048]{3,2,1,0:T(8,128)(2,1)S(1)}, u32[]{:S(2)}, u32[]{:S(2)}) collective-permute-start(bf16[2,2,64,2048]{3,2,1,0:T(8,128)(2,1)S(1)} %bitcast.238), channel_id=1, source_target_pairs={{0,8},{4,12},{24,16},{28,20},{1,9},{5,13},{25,17},{29,21},{2,10},{... | collective-permute-start | bytes 3145736 | tf_op jit(solution)/shard_map/ppermute | solution.py:574
  406.9 31.7 %collective-permute-start.71 = (bf16[4,64,2048]{2,1,0:T(8,128)(2,1)S(1)}, bf16[4,64,2048]{2,1,0:T(8,128)(2,1)}, u32[]{:S(2)}, u32[]{:S(2)}) collective-permute-start(bf16[4,64,2048]{2,1,0:T(8,128)(2,1)S(1)} %dynamic-slice_bitcast_fusion), channel_id=1, source_target_pairs={{0,4},{4,0},{8,12},{12,8},{16,20},{20,16},{24,28},{28,24},{1,5},{5... | collective-permute-start | bytes 3145736 | tf_op jit(solution)/shard_map/ppermute | solution.py:574
  408.4 28.9 %collective-permute-start.63 = (bf16[4,2,68,512]{3,0,2,1:T(4,128)(2,1)S(1)}, bf16[4,2,68,512]{3,0,2,1:T(4,128)(2,1)}, u32[]{:S(2)}, u32[]{:S(2)}) collective-permute-start(bf16[4,2,68,512]{3,0,2,1:T(4,128)(2,1)S(1)} %copy.531), channel_id=1, source_target_pairs={{0,16},{4,20},{8,24},{12,28},{16,0},{20,4},{24,8},{28,12},{1,17},{... | collective-permute-start | bytes 1671176 | tf_op jit(solution)/shard_map/ppermute | solution.py:574
  413.4 30.0 %collective-permute-start.62 = (bf16[4,64,2048]{2,1,0:T(8,128)(2,1)}, bf16[4,64,2048]{2,1,0:T(8,128)(2,1)}, u32[]{:S(2)}, u32[]{:S(2)}) collective-permute-start(bf16[4,64,2048]{2,1,0:T(8,128)(2,1)} %dynamic-slice_bitcast_fusion.1), channel_id=1, source_target_pairs={{0,4},{4,0},{8,12},{12,8},{16,20},{20,16},{24,28},{28,24},{1,5},{5... | collective-permute-start | bytes 3145736 | tf_op jit(solution)/shard_map/ppermute | solution.py:574
  414.6 49.5 %collective-permute-start.60 = (bf16[2,2,64,2048]{3,2,1,0:T(8,128)(2,1)}, bf16[2,2,64,2048]{3,2,1,0:T(8,128)(2,1)S(1)}, u32[]{:S(2)}, u32[]{:S(2)}) collective-permute-start(bf16[2,2,64,2048]{3,2,1,0:T(8,128)(2,1)} %get-tuple-element.1351.refs_0_), channel_id=1, source_target_pairs={{0,8},{4,12},{8,16},{12,20},{1,9},{5,13},{9,17},{13,21},{2,10},{6,... | collective-permute-start | bytes 3145736 | tf_op jit(solution)/shard_map/ppermute | solution.py:574
  416.7 47.3 %collective-permute-start.61 = (bf16[2,2,64,2048]{3,2,1,0:T(8,128)(2,1)}, bf16[2,2,64,2048]{3,2,1,0:T(8,128)(2,1)S(1)}, u32[]{:S(2)}, u32[]{:S(2)}) collective-permute-start(bf16[2,2,64,2048]{3,2,1,0:T(8,128)(2,1)} %get-tuple-element.1350.refs_1_), channel_id=1, source_target_pairs={{16,8},{20,12},{24,16},{28,20},{17,9},{21,13},{25,17},{29,21},{18,... | collective-permute-start | bytes 3145736 | tf_op jit(solution)/shard_map/ppermute | solution.py:574
  441.2 52.3 %collective-permute-start.72 = (bf16[2,64,2048]{2,1,0:T(8,128)(2,1)}, bf16[2,64,2048]{2,1,0:T(8,128)(2,1)}, u32[]{:S(2)}, u32[]{:S(2)}) collective-permute-start(bf16[2,64,2048]{2,1,0:T(8,128)(2,1)} %dynamic-slice_bitcast_fusion.8), channel_id=1, source_target_pairs={{0,16},{4,20},{8,24},{12,28},{16,0},{20,4},{24,8},{28,12},{1,17},{... | collective-permute-start | bytes 1572872 | tf_op jit(solution)/shard_map/ppermute | solution.py:574
  466.2 52.9 %collective-permute-start.68 = (bf16[2,2,64,2048]{3,2,1,0:T(8,128)(2,1)}, bf16[2,2,64,2048]{3,2,1,0:T(8,128)(2,1)}, u32[]{:S(2)}, u32[]{:S(2)}) collective-permute-start(bf16[2,2,64,2048]{3,2,1,0:T(8,128)(2,1)} %get-tuple-element.1355.refs_0_), channel_id=1, source_target_pairs={{0,8},{4,12},{8,16},{12,20},{16,24},{20,28},{1,9},{5,13},{9,17},{1... | collective-permute-start | bytes 3145736 | tf_op jit(solution)/shard_map/ppermute | solution.py:574
  470.5 48.7 %collective-permute-start.69 = (bf16[2,2,64,2048]{3,2,1,0:T(8,128)(2,1)}, bf16[2,2,64,2048]{3,2,1,0:T(8,128)(2,1)}, u32[]{:S(2)}, u32[]{:S(2)}) collective-permute-start(bf16[2,2,64,2048]{3,2,1,0:T(8,128)(2,1)} %get-tuple-element.1354.refs_1_), channel_id=1, source_target_pairs={{8,0},{12,4},{16,8},{20,12},{24,16},{28,20},{9,1},{13,5},{17,9},{2... | collective-permute-start | bytes 3145736 | tf_op jit(solution)/shard_map/ppermute | solution.py:574
  474.7 13.9 %collective-permute-start.65 = (bf16[20,48,256]{2,1,0:T(8,128)(2,1)}, bf16[20,48,256]{2,1,0:T(8,128)(2,1)}, u32[]{:S(2)}, u32[]{:S(2)}) collective-permute-start(bf16[20,48,256]{2,1,0:T(8,128)(2,1)} %dynamic-slice_convert_fusion), channel_id=1, source_target_pairs={{0,2},{1,3},{2,0},{3,1},{4,6},{5,7},{6,4},{7,5},{8,10},{9,11},{10,... | collective-permute-start | bytes 1474568 | tf_op jit(solution)/shard_map/ppermute | solution.py:1013
  476.4 29.2 %collective-permute-start.70 = (bf16[2,64,2048]{2,1,0:T(8,128)(2,1)}, bf16[2,64,2048]{2,1,0:T(8,128)(2,1)}, u32[]{:S(2)}, u32[]{:S(2)}) collective-permute-start(bf16[2,64,2048]{2,1,0:T(8,128)(2,1)} %dynamic-slice_bitcast_fusion.9), channel_id=1, source_target_pairs={{0,16},{4,20},{8,24},{12,28},{16,0},{20,4},{24,8},{28,12},{1,17},{... | collective-permute-start | bytes 1572872 | tf_op jit(solution)/shard_map/ppermute | solution.py:574
  488.6 19.8 %collective-permute-start.64 = (bf16[20,48,512]{2,1,0:T(8,128)(2,1)S(1)}, bf16[20,48,512]{2,1,0:T(8,128)(2,1)}, u32[]{:S(2)}, u32[]{:S(2)}) collective-permute-start(bf16[20,48,512]{2,1,0:T(8,128)(2,1)S(1)} %get-tuple-element.1314), channel_id=1, source_target_pairs={{0,1},{1,0},{2,3},{3,2},{4,5},{5,4},{6,7},{7,6},{8,9},{9,8},{10,11... | collective-permute-start | bytes 2949128 | tf_op jit(solution)/shard_map/ppermute | solution.py:515
  493.5 14.0 %collective-permute-start.66 = (bf16[20,48,128]{2,1,0:T(8,128)(2,1)S(1)}, bf16[20,48,128]{2,1,0:T(8,128)(2,1)S(1)}, u32[]{:S(2)}, u32[]{:S(2)}) collective-permute-start(bf16[20,48,128]{2,1,0:T(8,128)(2,1)S(1)} %bitcast.253), channel_id=1, source_target_pairs={{0,1},{1,0},{2,3},{3,2},{4,5},{5,4},{6,7},{7,6},{8,9},{9,8},{10,11... | collective-permute-start | bytes 737288 | tf_op jit(solution)/shard_map/ppermute | solution.py:515
  532.8 14.4 %collective-permute-start.73 = (bf16[2,64,2048]{2,1,0:T(8,128)(2,1)S(1)}, bf16[2,64,2048]{2,1,0:T(8,128)(2,1)S(1)}, u32[]{:S(2)}, u32[]{:S(2)}) collective-permute-start(bf16[2,64,2048]{2,1,0:T(8,128)(2,1)S(1)} %get-tuple-element.1360), channel_id=1, source_target_pairs={{0,4},{4,0},{8,12},{12,8},{16,20},{20,16},{24,28},{28,24},{1,5},{5... | collective-permute-start | bytes 1572872 | tf_op jit(solution)/shard_map/ppermute | solution.py:574
  (165 other events, 878.3 us)

commit v14 on v13

--- a/solution.py
+++ b/solution.py
@@ -959,14 +959,15 @@
         return up, down
 
     def beside_third(rise, fall):
-        in_sum, hidden, last_cell = after((rise, fall), tokens["in"], hidden_all, cell, free=2 * MIB)
-        tokens["in"], tokens["rec"] = across_two(in_sum), across_two(tokens["rec"])
+        (in_sum,) = after((rise, fall), tokens["in"], free=2 * MIB)
+        tokens["in"] = across_two(in_sum)
+
+    def final(up, down):
+        up, down, tokens["in"], rec_sum, tokens["proj"], hidden, last_cell = after(
+            (), up, down, tokens["in"], tokens["rec"], tokens["proj"], hidden_all, cell, free=2 * MIB
+        )
         tokens["states"] = states_of(hidden, last_cell)
-
-    def final(up, down):
-        up, down, tokens["in"], tokens["rec"], tokens["proj"] = after(
-            tokens["states"], up, down, tokens["in"], tokens["rec"], tokens["proj"], free=2 * MIB
-        )
+        (tokens["rec"],) = after(tokens["states"], across_two(rec_sum), free=2 * MIB)
         return up, down
 
     gates = {2: second, 3: third, line: final} if line > 3 else {}

time: 562 us -> 554 us (0.986)
  the two profiles are of different devices: /device:TPU:8 before, /device:TPU:1 now
where the time goes in v14:
time: 554 us; the launch traced here: 546 us
  Pallas kernels  327 us (59%)
  starting transfers between devices  132 us (24%)
  local copies, waits for them, and re-layouts  42.3 us (8%)
  other arithmetic  30.2 us (5%)
  waiting for transfers between devices  6.71 us (1%)
    pallas_call x20, Pallas kernels, backward_call(): pl.pallas_call(backward_kernel, out_shape=(vmem((streams, depth), BF16),...  61.9 us
    pallas_call x19, Pallas kernels, between_call(): pl.pallas_call(functools.partial(between_kernel, not stacks, step == step...  56.7 us
    pallas_call x20, Pallas kernels, forward_call(): pl.pallas_call(functools.partial(forward_kernel, first), out_shape=(vmem(...  56.2 us
    pallas_call x20, Pallas kernels, aside_call(): pl.pallas_call(functools.partial(aside_kernel, not stacks, step == 0, not...  55.9 us
    ppermute x7, starting transfers between devices, trade(): return (mine, lax.ppermute(theirs, 'gate', swap))  54.7 us
    ppermute x28, starting transfers between devices, swapped(): return lax.ppermute(array, 'batch', pairs)  35.4 us
    ppermute x39, starting transfers between devices, body(): peer = lax.ppermute(part, 'gate', across)  32.6 us
    pallas_call x4, Pallas kernels, by_gate(): pl.pallas_call(functools.partial(layout_kernel, keep, spread), out_shape=...  23.3 us
  transfers between devices with their start and end apart: 80, of which 3 were waited for; matrix products, arithmetic and copies ran while one was open for 11% of the time, Pallas kernels for 48%

profile of v14, /device:TPU:1, one launch (start us, length us, event | category | flops | bytes accessed | tf_op | source)
XLA Modules:
  0.0 545.9 jit_solution(5725840998688780574)
XLA Ops:
  0.7 5.8 %layout.5 = bf16[4,512,1024]{2,1,0:T(8,128)(2,1)} custom-call(s32[1]{0:T(128)} %bitcast.17.which_ref, bf16[2,512,4,1024]{3,2,1,0:T(4,128)(2,1)} %w_ref.5), custom_call_target="tpu_custom_call" | custom-call | tf_op jit(solution)/shard_map/layout/pallas_call | solution.py:527
  6.7 5.9 %layout.6 = bf16[4,512,1024]{2,1,0:T(8,128)(2,1)} custom-call(s32[1]{0:T(128)} %bitcast.17.which_ref, bf16[2,512,4,1024]{3,2,1,0:T(4,128)(2,1)} %w_ref.7), custom_call_target="tpu_custom_call" | custom-call | tf_op jit(solution)/shard_map/layout/pallas_call | solution.py:527
  25.3 6.4 %layout.4 = (bf16[4,512,1024]{2,1,0:T(8,128)(2,1)S(1)}, bf16[4,512,1024]{2,1,0:T(8,128)(2,1)}) custom-call(s32[1]{0:T(128)} %slice.55.which_ref, bf16[2,512,4,1024]{3,2,1,0:T(4,128)(2,1)} %w_ref.5), custom_call_target="tpu_custom_call" | custom-call | tf_op jit(solution)/shard_map/layout/pallas_call | solution.py:527
  31.8 5.2 layout.7.wa_ref
  42.7 5.0 begin.1
  73.1 3.3 between.22
  157.8 3.1 between.34
  164.7 3.3 between.35
  219.8 3.0 backward_step.24
  233.2 3.0 backward_step.26
  241.4 3.2 backward_step.27
  284.5 3.5 backward_step.33
  300.3 3.0 backward_step.35
  306.9 3.0 backward_step.36
  316.4 3.0 backward_step.37
  323.2 3.0 backward_step.38
  331.3 3.8 backward_step.39
  340.9 3.6 bitcast_convert_fusion
  346.3 4.2 gather.13
  351.7 4.3 late.1
  358.3 11.2 %product.1 = bf16[2,512,2048]{2,1,0:T(8,128)(2,1)S(1)} custom-call(bf16[40,48,1024]{2,1,0:T(8,128)(2,1)S(1)} %get-tuple-element.1276.refs_0_.left_ref, bf16[40,48,2048]{2,1,0:T(8,128)(2,1)S(1)} %get-tuple-element.1289.right_ref), custom_call_target="tpu_custom_call" | custom-call | tf_op jit(solution)/shard_map/product/pallas_call | solution.py:893
  369.5 16.7 %whole_product.1 = bf16[2,512,2048]{2,1,0:T(8,128)(2,1)S(1)} custom-call(bf16[20,48,512]{2,1,0:T(8,128)(2,1)} %get-tuple-element.666.refs_0_, bf16[20,48,512]{2,1,0:T(8,128)(2,1)} %get-tuple-element.948.refs_1_, bf16[20,48,512]{2,1,0:T(8,128)(2,1)} %get-tuple-element.1291.refs_2_, bf16[20,48,512]{2,1,0:T(8,128)(2,1)} %get-tuple-element.1292.refs_3_, ...), custom_call_target="tpu_custom_call" | custom-call | tf_op jit(solution)/shard_map/whole_product/pallas_call | solution.py:910
  393.0 5.0 collective-permute-start.60
  402.3 19.2 %input_grad.1.refs_2_ = f32[20,48,512]{2,1,0:T(8,128)S(1)} custom-call(s32[2]{0:T(128)S(1)} %copy-done.49, bf16[4,20,48,2048]{3,2,1,0:T(8,128)(2,1)} %get-tuple-element.1305.dz_ref, bf16[4,512,1024]{2,1,0:T(8,128)(2,1)} %get-tuple-element.1306.wa_ref, bf16[4,512,1024]{2,1,0:T(8,128)(2,1)} %collective-permute-done.1.refs_2_.wb_ref), custom_call_target="tpu_custom_call" | custom-call | tf_op jit(solution)/shard_map/input_grad/pallas_call | solution.py:816
  426.8 3.6 fusion.7
  440.4 6.2 %collective-permute-done.69 = bf16[20,48,256]{2,1,0:T(8,128)(2,1)S(1)} collective-permute-done((bf16[20,48,256]{2,1,0:T(8,128)(2,1)S(1)}, bf16[20,48,256]{2,1,0:T(8,128)(2,1)S(1)}, u32[]{:S(2)}, u32[]{:S(2)}) %collective-permute-start.69) | collective-permute-done | bytes 491552 | tf_op jit(solution)/shard_map/ppermute | solution.py:1014
  449.3 29.0 %collective-permute-start.70 = (bf16[20,48,128]{2,1,0:T(8,128)(2,1)S(1)}, bf16[20,48,128]{2,1,0:T(8,128)(2,1)S(1)}, u32[]{:S(2)}, u32[]{:S(2)}) collective-permute-start(bf16[20,48,128]{2,1,0:T(8,128)(2,1)S(1)} %bitcast.257), channel_id=1, source_target_pairs={{0,1},{1,0},{2,3},{3,2},{4,5},{5,4},{6,7},{7,6},{8,9},{9,8},{10,11... | collective-permute-start | bytes 737288 | tf_op jit(solution)/shard_map/ppermute | solution.py:515
  483.8 18.4 %collective-permute-start.72 = (f32[48,1024]{1,0:T(8,128)S(1)}, f32[48,1024]{1,0:T(8,128)S(1)}, u32[]{:S(2)}, u32[]{:S(2)}) collective-permute-start(f32[48,1024]{1,0:T(8,128)S(1)} %bitcast.258), channel_id=1, source_target_pairs={{0,1},{1,0},{2,3},{3,2},{4,5},{5,4},{6,7},{7,6},{8,9},{9,8},{10,11... | collective-permute-start | bytes 589832 | tf_op jit(solution)/shard_map/ppermute | solution.py:515
  515.7 3.6 scatter_fusion
  523.5 6.6 %collective-permute-start.78 = (f32[4,128]{1,0:T(4,128)S(1)}, f32[4,128]{1,0:T(4,128)S(1)}, u32[]{:S(2)}, u32[]{:S(2)}) collective-permute-start(f32[4,128]{1,0:T(4,128)S(1)} %fusion.31), channel_id=1, source_target_pairs={{0,1},{1,0},{2,3},{3,2},{4,5},{5,4},{6,7},{7,6},{8,9},{9,8},{10,11... | collective-permute-start | bytes 6152 | tf_op jit(solution)/shard_map/ppermute | solution.py:515
  531.1 7.0 %collective-permute-start.76 = (bf16[2,64,2048]{2,1,0:T(8,128)(2,1)S(1)}, bf16[2,64,2048]{2,1,0:T(8,128)(2,1)S(1)}, u32[]{:S(2)}, u32[]{:S(2)}) collective-permute-start(bf16[2,64,2048]{2,1,0:T(8,128)(2,1)S(1)} %collective-permute-done.75), channel_id=1, source_target_pairs={{0,1},{1,0},{2,3},{3,2},{4,5},{5,4},{6,7},{7,6},{8,9},{9,8},{10,11... | collective-permute-start | bytes 1572872 | tf_op jit(solution)/shard_map/ppermute | solution.py:985
  541.5 4.0 assemble.1
  (600 shorter events, 332.5 us)
Async XLA Ops:
  6.5 35.2 %collective-permute-start.1 = (bf16[4,512,1024]{2,1,0:T(8,128)(2,1)}, bf16[4,512,1024]{2,1,0:T(8,128)(2,1)}, u32[]{:S(2)}, u32[]{:S(2)}) collective-permute-start(bf16[4,512,1024]{2,1,0:T(8,128)(2,1)} %layout.5), channel_id=1, source_target_pairs={{0,1},{1,0},{2,3},{3,2},{4,5},{5,4},{6,7},{7,6},{8,9},{9,8},{10,11... | collective-permute-start | bytes 12582920 | tf_op jit(solution)/shard_map/ppermute | solution.py:543
  12.6 29.2 %collective-permute-start.2 = (bf16[4,512,1024]{2,1,0:T(8,128)(2,1)}, bf16[4,512,1024]{2,1,0:T(8,128)(2,1)}, u32[]{:S(2)}, u32[]{:S(2)}) collective-permute-start(bf16[4,512,1024]{2,1,0:T(8,128)(2,1)} %layout.6), channel_id=1, source_target_pairs={{0,1},{1,0},{2,3},{3,2},{4,5},{5,4},{6,7},{7,6},{8,9},{9,8},{10,11... | collective-permute-start | bytes 12582920 | tf_op jit(solution)/shard_map/ppermute | solution.py:543
  16.4 23.5 %collective-permute-start.4 = (f32[48,1024]{1,0:T(8,128)}, f32[48,1024]{1,0:T(8,128)}, u32[]{:S(2)}, u32[]{:S(2)}) collective-permute-start(f32[48,1024]{1,0:T(8,128)} %bitcast.227), channel_id=1, source_target_pairs={{0,1},{1,0},{2,3},{3,2},{4,5},{5,4},{6,7},{7,6},{8,9},{9,8},{10,11... | collective-permute-start | bytes 589832 | tf_op jit(solution)/shard_map/ppermute | solution.py:515
  16.5 23.4 %collective-permute-start = (bf16[4,1024]{1,0:T(4,128)(2,1)S(1)}, bf16[4,1024]{1,0:T(4,128)(2,1)S(1)}, u32[]{:S(2)}, u32[]{:S(2)}) collective-permute-start(bf16[4,1024]{1,0:T(4,128)(2,1)S(1)} %get-tuple-element.1376), channel_id=1, source_target_pairs={{0,1},{1,0},{2,3},{3,2},{4,5},{5,4},{6,7},{7,6},{8,9},{9,8},{10,11... | collective-permute-start | bytes 24584 | tf_op jit(solution)/shard_map/ppermute | solution.py:515
  17.1 24.7 %collective-permute-start.3 = (bf16[1024,512]{1,0:T(8,128)(2,1)S(1)}, bf16[1024,512]{1,0:T(8,128)(2,1)S(1)}, u32[]{:S(2)}, u32[]{:S(2)}) collective-permute-start(bf16[1024,512]{1,0:T(8,128)(2,1)S(1)} %dynamic-slice_bitcast_fusion.2), channel_id=1, source_target_pairs={{0,1},{1,0},{2,3},{3,2},{4,5},{5,4},{6,7},{7,6},{8,9},{9,8},{10,11... | collective-permute-start | bytes 3145736 | tf_op jit(solution)/shard_map/ppermute | solution.py:545
  127.4 29.1 %collective-permute-start.21 = (bf16[20,48,512]{2,1,0:T(8,128)(2,1)}, bf16[20,48,512]{2,1,0:T(8,128)(2,1)S(1)}, u32[]{:S(2)}, u32[]{:S(2)}) collective-permute-start(bf16[20,48,512]{2,1,0:T(8,128)(2,1)} %after.14), channel_id=1, source_target_pairs={{0,4},{4,0},{8,12},{12,8},{16,20},{20,16},{24,28},{28,24},{1,5},{5... | collective-permute-start | bytes 2949128 | tf_op jit(solution)/shard_map/ppermute | solution.py:574
  128.7 27.9 %collective-permute-start.22 = (bf16[20,48,512]{2,1,0:T(8,128)(2,1)}, bf16[20,48,512]{2,1,0:T(8,128)(2,1)S(1)}, u32[]{:S(2)}, u32[]{:S(2)}) collective-permute-start(bf16[20,48,512]{2,1,0:T(8,128)(2,1)} %after.14), channel_id=1, source_target_pairs={{0,8},{4,12},{8,0},{12,4},{16,24},{20,28},{24,16},{28,20},{1,9},{5... | collective-permute-start | bytes 2949128 | tf_op jit(solution)/shard_map/ppermute | solution.py:574
  195.5 41.8 %collective-permute-start.33 = (bf16[20,48,512]{2,1,0:T(8,128)(2,1)}, bf16[20,48,512]{2,1,0:T(8,128)(2,1)S(1)}, u32[]{:S(2)}, u32[]{:S(2)}) collective-permute-start(bf16[20,48,512]{2,1,0:T(8,128)(2,1)} %after.15), channel_id=1, source_target_pairs={{0,4},{4,0},{8,12},{12,8},{16,20},{20,16},{24,28},{28,24},{1,5},{5... | collective-permute-start | bytes 2949128 | tf_op jit(solution)/shard_map/ppermute | solution.py:574
  195.8 41.5 %collective-permute-start.34 = (bf16[20,48,512]{2,1,0:T(8,128)(2,1)}, bf16[20,48,512]{2,1,0:T(8,128)(2,1)S(1)}, u32[]{:S(2)}, u32[]{:S(2)}) collective-permute-start(bf16[20,48,512]{2,1,0:T(8,128)(2,1)} %after.15), channel_id=1, source_target_pairs={{0,8},{4,12},{8,0},{12,4},{16,24},{20,28},{24,16},{28,20},{1,9},{5... | collective-permute-start | bytes 2949128 | tf_op jit(solution)/shard_map/ppermute | solution.py:574
  244.7 44.4 %collective-permute-start.43 = (bf16[7,48,2048]{2,1,0:T(8,128)(2,1)}, bf16[7,48,2048]{2,1,0:T(8,128)(2,1)S(1)}, u32[]{:S(2)}, u32[]{:S(2)}) collective-permute-start(bf16[7,48,2048]{2,1,0:T(8,128)(2,1)} %get-tuple-element.1173), channel_id=1, source_target_pairs={{0,4},{4,0},{8,12},{12,8},{16,20},{20,16},{24,28},{28,24},{1,5},{5... | collective-permute-start | bytes 4128776 | tf_op jit(solution)/shard_map/ppermute | solution.py:574
  246.0 43.1 %collective-permute-start.44 = (bf16[7,48,2048]{2,1,0:T(8,128)(2,1)}, bf16[7,48,2048]{2,1,0:T(8,128)(2,1)S(1)}, u32[]{:S(2)}, u32[]{:S(2)}) collective-permute-start(bf16[7,48,2048]{2,1,0:T(8,128)(2,1)} %get-tuple-element.1174), channel_id=1, source_target_pairs={{0,8},{4,12},{8,0},{12,4},{16,24},{20,28},{24,16},{28,20},{1,9},{5... | collective-permute-start | bytes 4128776 | tf_op jit(solution)/shard_map/ppermute | solution.py:574
  288.0 39.1 %collective-permute-start.50 = (bf16[6,48,2048]{2,1,0:T(8,128)(2,1)}, bf16[6,48,2048]{2,1,0:T(8,128)(2,1)S(1)}, u32[]{:S(2)}, u32[]{:S(2)}) collective-permute-start(bf16[6,48,2048]{2,1,0:T(8,128)(2,1)} %get-tuple-element.1253), channel_id=1, source_target_pairs={{0,4},{4,0},{8,12},{12,8},{16,20},{20,16},{24,28},{28,24},{1,5},{5... | collective-permute-start | bytes 3538952 | tf_op jit(solution)/shard_map/ppermute | solution.py:574
  288.3 39.0 %collective-permute-start.51 = (bf16[6,48,2048]{2,1,0:T(8,128)(2,1)}, bf16[6,48,2048]{2,1,0:T(8,128)(2,1)S(1)}, u32[]{:S(2)}, u32[]{:S(2)}) collective-permute-start(bf16[6,48,2048]{2,1,0:T(8,128)(2,1)} %get-tuple-element.1254), channel_id=1, source_target_pairs={{0,8},{4,12},{8,0},{12,4},{16,24},{20,28},{24,16},{28,20},{1,9},{5... | collective-permute-start | bytes 3538952 | tf_op jit(solution)/shard_map/ppermute | solution.py:574
  310.0 25.2 %collective-permute-start.52 = (bf16[3,48,2048]{2,1,0:T(8,128)(2,1)}, bf16[3,48,2048]{2,1,0:T(8,128)(2,1)S(1)}, u32[]{:S(2)}, u32[]{:S(2)}) collective-permute-start(bf16[3,48,2048]{2,1,0:T(8,128)(2,1)} %get-tuple-element.1270), channel_id=1, source_target_pairs={{0,4},{4,0},{8,12},{12,8},{16,20},{20,16},{24,28},{28,24},{1,5},{5... | collective-permute-start | bytes 1769480 | tf_op jit(solution)/shard_map/ppermute | solution.py:574
  311.3 23.9 %collective-permute-start.53 = (bf16[3,48,2048]{2,1,0:T(8,128)(2,1)}, bf16[3,48,2048]{2,1,0:T(8,128)(2,1)S(1)}, u32[]{:S(2)}, u32[]{:S(2)}) collective-permute-start(bf16[3,48,2048]{2,1,0:T(8,128)(2,1)} %get-tuple-element.1271), channel_id=1, source_target_pairs={{0,8},{4,12},{8,0},{12,4},{16,24},{20,28},{24,16},{28,20},{1,9},{5... | collective-permute-start | bytes 1769480 | tf_op jit(solution)/shard_map/ppermute | solution.py:574
  327.0 23.5 %collective-permute-start.54 = (bf16[2,48,2048]{2,1,0:T(8,128)(2,1)}, bf16[2,48,2048]{2,1,0:T(8,128)(2,1)S(1)}, u32[]{:S(2)}, u32[]{:S(2)}) collective-permute-start(bf16[2,48,2048]{2,1,0:T(8,128)(2,1)} %get-tuple-element.1283), channel_id=1, source_target_pairs={{0,8},{4,12},{8,0},{12,4},{16,24},{20,28},{24,16},{28,20},{1,9},{5... | collective-permute-start | bytes 1179656 | tf_op jit(solution)/shard_map/ppermute | solution.py:574
  327.3 23.3 %collective-permute-start.56 = (bf16[2,48,2048]{2,1,0:T(8,128)(2,1)}, bf16[2,48,2048]{2,1,0:T(8,128)(2,1)S(1)}, u32[]{:S(2)}, u32[]{:S(2)}) collective-permute-start(bf16[2,48,2048]{2,1,0:T(8,128)(2,1)} %get-tuple-element.1285), channel_id=1, source_target_pairs={{0,4},{4,0},{8,12},{12,8},{16,20},{20,16},{24,28},{28,24},{1,5},{5... | collective-permute-start | bytes 1179656 | tf_op jit(solution)/shard_map/ppermute | solution.py:574
  345.2 41.0 %collective-permute-start.59 = (bf16[4,4,68,512]{3,1,2,0:T(4,128)(2,1)S(1)}, bf16[4,4,68,512]{3,1,2,0:T(4,128)(2,1)S(1)}, u32[]{:S(2)}, u32[]{:S(2)}) collective-permute-start(bf16[4,4,68,512]{3,1,2,0:T(4,128)(2,1)S(1)} %copy.531), channel_id=1, source_target_pairs={{0,4},{4,0},{8,12},{12,8},{16,20},{20,16},{24,28},{28,24},{1,5},{5... | collective-permute-start | bytes 3342344 | tf_op jit(solution)/shard_map/ppermute | solution.py:574
  356.0 30.6 %collective-permute-start.58 = (bf16[2,2,64,2048]{3,2,1,0:T(8,128)(2,1)S(1)}, bf16[2,2,64,2048]{3,2,1,0:T(8,128)(2,1)S(1)}, u32[]{:S(2)}, u32[]{:S(2)}) collective-permute-start(bf16[2,2,64,2048]{3,2,1,0:T(8,128)(2,1)S(1)} %bitcast.244), channel_id=1, source_target_pairs={{0,8},{4,12},{24,16},{28,20},{1,9},{5,13},{25,17},{29,21},{2,10},{... | collective-permute-start | bytes 3145736 | tf_op jit(solution)/shard_map/ppermute | solution.py:574
  390.7 32.1 %collective-permute-start.62 = (bf16[4,64,2048]{2,1,0:T(8,128)(2,1)S(1)}, bf16[4,64,2048]{2,1,0:T(8,128)(2,1)}, u32[]{:S(2)}, u32[]{:S(2)}) collective-permute-start(bf16[4,64,2048]{2,1,0:T(8,128)(2,1)S(1)} %dynamic-slice_bitcast_fusion.1), channel_id=1, source_target_pairs={{0,4},{4,0},{8,12},{12,8},{16,20},{20,16},{24,28},{28,24},{1,5},{5... | collective-permute-start | bytes 3145736 | tf_op jit(solution)/shard_map/ppermute | solution.py:574
  391.5 30.0 %collective-permute-start.63 = (bf16[4,2,68,512]{3,0,2,1:T(4,128)(2,1)S(1)}, bf16[4,2,68,512]{3,0,2,1:T(4,128)(2,1)}, u32[]{:S(2)}, u32[]{:S(2)}) collective-permute-start(bf16[4,2,68,512]{3,0,2,1:T(4,128)(2,1)S(1)} %copy.536), channel_id=1, source_target_pairs={{0,16},{4,20},{8,24},{12,28},{16,0},{20,4},{24,8},{28,12},{1,17},{... | collective-permute-start | bytes 1671176 | tf_op jit(solution)/shard_map/ppermute | solution.py:574
  393.0 31.4 %collective-permute-start.60 = (bf16[2,2,64,2048]{3,2,1,0:T(8,128)(2,1)}, bf16[2,2,64,2048]{3,2,1,0:T(8,128)(2,1)}, u32[]{:S(2)}, u32[]{:S(2)}) collective-permute-start(bf16[2,2,64,2048]{3,2,1,0:T(8,128)(2,1)} %get-tuple-element.1349.refs_0_), channel_id=1, source_target_pairs={{0,8},{4,12},{8,16},{12,20},{1,9},{5,13},{9,17},{13,21},{2,10},{6,... | collective-permute-start | bytes 3145736 | tf_op jit(solution)/shard_map/ppermute | solution.py:574
  398.1 26.3 %collective-permute-start.61 = (bf16[2,2,64,2048]{3,2,1,0:T(8,128)(2,1)}, bf16[2,2,64,2048]{3,2,1,0:T(8,128)(2,1)}, u32[]{:S(2)}, u32[]{:S(2)}) collective-permute-start(bf16[2,2,64,2048]{3,2,1,0:T(8,128)(2,1)} %get-tuple-element.1348.refs_1_), channel_id=1, source_target_pairs={{16,8},{20,12},{24,16},{28,20},{17,9},{21,13},{25,17},{29,21},{18,... | collective-permute-start | bytes 3145736 | tf_op jit(solution)/shard_map/ppermute | solution.py:574
  401.1 38.8 %collective-permute-start.67 = (bf16[4,64,2048]{2,1,0:T(8,128)(2,1)S(1)}, bf16[4,64,2048]{2,1,0:T(8,128)(2,1)S(1)}, u32[]{:S(2)}, u32[]{:S(2)}) collective-permute-start(bf16[4,64,2048]{2,1,0:T(8,128)(2,1)S(1)} %dynamic-slice_bitcast_fusion), channel_id=1, source_target_pairs={{0,4},{4,0},{8,12},{12,8},{16,20},{20,16},{24,28},{28,24},{1,5},{5... | collective-permute-start | bytes 3145736 | tf_op jit(solution)/shard_map/ppermute | solution.py:574
  430.4 49.9 %collective-permute-start.64 = (bf16[2,2,64,2048]{3,2,1,0:T(8,128)(2,1)}, bf16[2,2,64,2048]{3,2,1,0:T(8,128)(2,1)}, u32[]{:S(2)}, u32[]{:S(2)}) collective-permute-start(bf16[2,2,64,2048]{3,2,1,0:T(8,128)(2,1)} %get-tuple-element.1353.refs_0_), channel_id=1, source_target_pairs={{0,8},{4,12},{8,16},{12,20},{16,24},{20,28},{1,9},{5,13},{9,17},{1... | collective-permute-start | bytes 3145736 | tf_op jit(solution)/shard_map/ppermute | solution.py:574
  433.3 47.0 %collective-permute-start.65 = (bf16[2,2,64,2048]{3,2,1,0:T(8,128)(2,1)}, bf16[2,2,64,2048]{3,2,1,0:T(8,128)(2,1)}, u32[]{:S(2)}, u32[]{:S(2)}) collective-permute-start(bf16[2,2,64,2048]{3,2,1,0:T(8,128)(2,1)} %get-tuple-element.1352.refs_1_), channel_id=1, source_target_pairs={{8,0},{12,4},{16,8},{20,12},{24,16},{28,20},{9,1},{13,5},{17,9},{2... | collective-permute-start | bytes 3145736 | tf_op jit(solution)/shard_map/ppermute | solution.py:574
  435.7 42.6 %collective-permute-start.66 = (bf16[2,64,2048]{2,1,0:T(8,128)(2,1)}, bf16[2,64,2048]{2,1,0:T(8,128)(2,1)}, u32[]{:S(2)}, u32[]{:S(2)}) collective-permute-start(bf16[2,64,2048]{2,1,0:T(8,128)(2,1)} %dynamic-slice_bitcast_fusion.9), channel_id=1, source_target_pairs={{0,16},{4,20},{8,24},{12,28},{16,0},{20,4},{24,8},{28,12},{1,17},{... | collective-permute-start | bytes 1572872 | tf_op jit(solution)/shard_map/ppermute | solution.py:574
  449.3 30.2 %collective-permute-start.70 = (bf16[20,48,128]{2,1,0:T(8,128)(2,1)S(1)}, bf16[20,48,128]{2,1,0:T(8,128)(2,1)S(1)}, u32[]{:S(2)}, u32[]{:S(2)}) collective-permute-start(bf16[20,48,128]{2,1,0:T(8,128)(2,1)S(1)} %bitcast.257), channel_id=1, source_target_pairs={{0,1},{1,0},{2,3},{3,2},{4,5},{5,4},{6,7},{7,6},{8,9},{9,8},{10,11... | collective-permute-start | bytes 737288 | tf_op jit(solution)/shard_map/ppermute | solution.py:515
  481.2 41.1 %collective-permute-start.77 = (bf16[4,68,512]{2,1,0:T(8,128)(2,1)}, bf16[4,68,512]{2,1,0:T(8,128)(2,1)}, u32[]{:S(2)}, u32[]{:S(2)}) collective-permute-start(bf16[4,68,512]{2,1,0:T(8,128)(2,1)} %dynamic-slice_bitcast_fusion.10), channel_id=1, source_target_pairs={{0,8},{4,12},{8,0},{12,4},{16,24},{20,28},{24,16},{28,20},{1,9},{5... | collective-permute-start | bytes 835592 | tf_op jit(solution)/shard_map/ppermute | solution.py:574
  482.8 26.8 %collective-permute-start.73 = (bf16[2,64,2048]{2,1,0:T(8,128)(2,1)}, bf16[2,64,2048]{2,1,0:T(8,128)(2,1)S(1)}, u32[]{:S(2)}, u32[]{:S(2)}) collective-permute-start(bf16[2,64,2048]{2,1,0:T(8,128)(2,1)} %dynamic-slice_bitcast_fusion.6), channel_id=1, source_target_pairs={{0,16},{4,20},{8,24},{12,28},{16,0},{20,4},{24,8},{28,12},{1,17},{... | collective-permute-start | bytes 1572872 | tf_op jit(solution)/shard_map/ppermute | solution.py:574
  483.8 23.0 %collective-permute-start.72 = (f32[48,1024]{1,0:T(8,128)S(1)}, f32[48,1024]{1,0:T(8,128)S(1)}, u32[]{:S(2)}, u32[]{:S(2)}) collective-permute-start(f32[48,1024]{1,0:T(8,128)S(1)} %bitcast.258), channel_id=1, source_target_pairs={{0,1},{1,0},{2,3},{3,2},{4,5},{5,4},{6,7},{7,6},{8,9},{9,8},{10,11... | collective-permute-start | bytes 589832 | tf_op jit(solution)/shard_map/ppermute | solution.py:515
  505.9 35.6 %collective-permute-start.71 = (bf16[2,64,2048]{2,1,0:T(8,128)(2,1)}, bf16[2,64,2048]{2,1,0:T(8,128)(2,1)}, u32[]{:S(2)}, u32[]{:S(2)}) collective-permute-start(bf16[2,64,2048]{2,1,0:T(8,128)(2,1)} %get-tuple-element.1358), channel_id=1, source_target_pairs={{0,4},{4,0},{8,12},{12,8},{16,20},{20,16},{24,28},{28,24},{1,5},{5... | collective-permute-start | bytes 1572872 | tf_op jit(solution)/shard_map/ppermute | solution.py:574
  (164 other events, 889.7 us)

commit v15 on v13

--- a/solution.py
+++ b/solution.py
@@ -219,9 +219,8 @@
         copy.wait()
 
 
-def numbers_kernel(in_ref, out_ref):
-    for i in range(in_ref.shape[0]):
-        out_ref[i] = in_ref[i]
+def numbers_kernel(index, in_ref, out_ref):
+    out_ref[0] = in_ref[index]
 
 
 def bias_kernel(sum_ref, out_ref):
@@ -497,16 +496,15 @@
         if count > 2:
             place_numbers[stride, "begin"] = jnp.where(here == 0, count - 1, 0)
     names = sorted(place_numbers, key=str)
-    gathered_numbers = pl.pallas_call(
-        numbers_kernel,
-        out_shape=jax.ShapeDtypeStruct((len(names),), jnp.int32),
+    which = pl.pallas_call(
+        functools.partial(numbers_kernel, names.index("own")),
+        out_shape=jax.ShapeDtypeStruct((1,), jnp.int32),
         in_specs=[SMEM],
         out_specs=SMEM,
         name="numbers",
     )(jnp.stack([place_numbers[x] for x in names]).astype(jnp.int32))
     number = {x: place_numbers[x].astype(jnp.int32) for x in names}
     own, low, high = number["own"], number["low"], number["high"]
-    which = lax.slice_in_dim(gathered_numbers, names.index("own"), names.index("own") + 1)
 
     def pick(stacked, index, axis=0):
         return lax.dynamic_index_in_dim(stacked, index, axis, keepdims=False, allow_negative_indices=False)
@@ -653,8 +651,8 @@
         if step == steps - 1:
             break
         if step == 2:
-            (early_feat,) = after((part,), feat_all)
-            feat_in = (swapped(early_feat, near_swap), swapped(early_feat, far_swap))
+            (feat_all,) = after((part,), feat_all)
+            feat_in = (swapped(feat_all, near_swap), swapped(feat_all, far_swap))
         due = step == (3 * steps) // 4
         inflow, stacks, passed = between_call(step, (cell, *fresh), stacks, feat_in if due else ())
         feat_in = passed if due else (feat_in if step >= 2 else None)
@@ -757,8 +755,8 @@
             part, grad, bias_sum, raw, dz = backward_call(step, part, peer, grad, bias_sum, saved)
             peer = lax.ppermute(part, "gate", across)
             if step == steps - 1:
-                (early_prev,) = after((part,), prev_all)
-                pending.append((step - steps // 3, (swapped(early_prev, near_swap), swapped(early_prev, far_swap))))
+                (prev_all,) = after((part,), prev_all)
+                pending.append((step - steps // 3, (swapped(prev_all, near_swap), swapped(prev_all, far_swap))))
             if ready is not None:
                 due, sides = ready
                 sides = after((part,), *sides) if step else sides
@@ -953,24 +951,22 @@
 
     def third(up, down):
         dx = input_grad_of(tokens["dz"])
-        up, down, tokens["dx"], tokens["in"], tokens["proj"] = after(
-            (), up, down, dx, tokens["in"], tokens["proj"], free=2 * MIB
+        up, down, tokens["dx"], in_sum, tokens["proj"], hidden, last_cell = after(
+            (), up, down, dx, tokens["in"], tokens["proj"], hidden_all, cell, free=2 * MIB
         )
+        tokens["in"] = across_two(in_sum)
+        tokens["states"] = states_of(hidden, last_cell)
         return up, down
 
-    def beside_third(rise, fall):
-        in_sum, hidden, last_cell = after((rise, fall), tokens["in"], hidden_all, cell, free=2 * MIB)
-        tokens["in"], tokens["rec"] = across_two(in_sum), across_two(tokens["rec"])
-        tokens["states"] = states_of(hidden, last_cell)
-
     def final(up, down):
-        up, down, tokens["in"], tokens["rec"], tokens["proj"] = after(
-            tokens["states"], up, down, tokens["in"], tokens["rec"], tokens["proj"], free=2 * MIB
+        up, down, tokens["in"], rec_sum = after(
+            tokens["states"], up, down, tokens["in"], tokens["rec"], free=2 * MIB
         )
+        tokens["rec"] = across_two(rec_sum)
         return up, down
 
     gates = {2: second, 3: third, line: final} if line > 3 else {}
-    hooks = {2: beside_second, 3: beside_third} if line > 3 else {}
+    hooks = {2: beside_second} if line > 3 else {}
     first = first.reshape(2, 2, share_rows, 4 * width) if chunk_rows else None
     near = line_sum(near, 1, 2, line, first, gates, hooks)
     dx_all, (outputs, final_h, final_c) = tokens["dx"], tokens["states"]

time: 562 us -> 548 us (0.975)
  waiting for transfers between devices: 53.3 us -> 44.7 us
    ppermute x1, waiting for transfers between devices: 7.58 us -> 0.01 us  [body(): dx_half = dx_half + lax.ppermute(dx_sent, 'gate', across).astype(F32)]
    unnamed x245 -> x213, local copies, waits for them, and re-layouts: 18.4 us -> 13 us
  transfers between devices with their start and end apart: 80 -> 80, of which waited for: 33 -> 33; matrix products, arithmetic and copies ran while one was open for 11% -> 12% of each run, Pallas kernels for 47% -> 48%
where the time goes in v15:
time: 548 us; the launch traced here: 537 us
  Pallas kernels  326 us (59%)
  starting transfers between devices  85.5 us (16%)
  waiting for transfers between devices  44.7 us (8%)
  local copies, waits for them, and re-layouts  41.9 us (8%)
  other arithmetic  31.5 us (6%)
    pallas_call x20, Pallas kernels, backward_call(): pl.pallas_call(backward_kernel, out_shape=(vmem((streams, depth), BF16),...  62.1 us
    pallas_call x19, Pallas kernels, between_call(): pl.pallas_call(functools.partial(between_kernel, not stacks, step == step...  56.5 us
    pallas_call x20, Pallas kernels, forward_call(): pl.pallas_call(functools.partial(forward_kernel, first), out_shape=(vmem(...  56.3 us
    pallas_call x20, Pallas kernels, aside_call(): pl.pallas_call(functools.partial(aside_kernel, not stacks, step == 0, not...  55.9 us
    ppermute x39, starting transfers between devices, body(): peer = lax.ppermute(part, 'gate', across)  43 us
    ppermute x28, waiting for transfers between devices, swapped(): return lax.ppermute(array, 'batch', pairs)  39.4 us
    ppermute x28, starting transfers between devices, swapped(): return lax.ppermute(array, 'batch', pairs)  39.1 us
    pallas_call x4, Pallas kernels, by_gate(): pl.pallas_call(functools.partial(layout_kernel, keep, spread), out_shape=...  23.2 us
  transfers between devices with their start and end apart: 80, of which 33 were waited for; matrix products, arithmetic and copies ran while one was open for 12% of the time, Pallas kernels for 48%

profile of v15, /device:TPU:8, one launch (start us, length us, event | category | flops | bytes accessed | tf_op | source)
XLA Modules:
  0.0 537.0 jit_solution(17310566591578529482)
XLA Ops:
  0.7 5.8 %layout.5 = bf16[4,512,1024]{2,1,0:T(8,128)(2,1)} custom-call(s32[1]{0:T(128)} %bitcast.15.which_ref, bf16[2,512,4,1024]{3,2,1,0:T(4,128)(2,1)} %w_ref.5), custom_call_target="tpu_custom_call" | custom-call | tf_op jit(solution)/shard_map/layout/pallas_call | solution.py:525
  6.6 5.9 %layout.6 = bf16[4,512,1024]{2,1,0:T(8,128)(2,1)} custom-call(s32[1]{0:T(128)} %bitcast.15.which_ref, bf16[2,512,4,1024]{3,2,1,0:T(4,128)(2,1)} %w_ref.7), custom_call_target="tpu_custom_call" | custom-call | tf_op jit(solution)/shard_map/layout/pallas_call | solution.py:525
  22.0 6.4 %layout.4 = (bf16[4,512,1024]{2,1,0:T(8,128)(2,1)S(1)}, bf16[4,512,1024]{2,1,0:T(8,128)(2,1)}) custom-call(s32[1]{0:T(128)} %numbers.1.which_ref, bf16[2,512,4,1024]{3,2,1,0:T(4,128)(2,1)} %w_ref.5), custom_call_target="tpu_custom_call" | custom-call | tf_op jit(solution)/shard_map/layout/pallas_call | solution.py:525
  28.4 5.1 layout.7.wa_ref
  37.5 4.9 begin.1
  98.7 3.2 forward_step.28
  155.1 3.2 between.34
  162.2 3.1 between.35
  189.2 3.0 backward_step.20
  198.5 3.4 backward_step.21
  243.1 3.2 backward_step.27
  288.8 3.4 backward_step.33
  299.9 3.0 backward_step.34
  314.2 3.0 backward_step.36
  340.5 3.8 backward_step.39
  345.4 3.0 aside.39
  349.7 3.6 bitcast_convert_fusion
  355.4 4.2 gather.13
  361.7 4.3 late.1
  367.3 11.2 %product.1 = bf16[2,512,2048]{2,1,0:T(8,128)(2,1)S(1)} custom-call(bf16[40,48,1024]{2,1,0:T(8,128)(2,1)S(1)} %get-tuple-element.1275.refs_0_.left_ref, bf16[40,48,2048]{2,1,0:T(8,128)(2,1)S(1)} %get-tuple-element.1288.right_ref), custom_call_target="tpu_custom_call" | custom-call | tf_op jit(solution)/shard_map/product/pallas_call | solution.py:891
  378.5 16.7 %whole_product.1 = bf16[2,512,2048]{2,1,0:T(8,128)(2,1)S(1)} custom-call(bf16[20,48,512]{2,1,0:T(8,128)(2,1)} %after.12.refs_0_, bf16[20,48,512]{2,1,0:T(8,128)(2,1)} %after.13.refs_1_, bf16[20,48,512]{2,1,0:T(8,128)(2,1)} %get-tuple-element.1290.refs_2_, bf16[20,48,512]{2,1,0:T(8,128)(2,1)} %get-tuple-element.1291.refs_3_, ...), custom_call_target="tpu_custom_call" | custom-call | tf_op jit(solution)/shard_map/whole_product/pallas_call | solution.py:908
  402.4 4.0 collective-permute-start.63
  412.3 19.2 %input_grad.1.refs_2_ = f32[20,48,512]{2,1,0:T(8,128)S(1)} custom-call(s32[2]{0:T(128)S(1)} %copy-done.34, bf16[4,20,48,2048]{3,2,1,0:T(8,128)(2,1)} %get-tuple-element.1304.dz_ref, bf16[4,512,1024]{2,1,0:T(8,128)(2,1)} %get-tuple-element.1305.wa_ref, bf16[4,512,1024]{2,1,0:T(8,128)(2,1)} %collective-permute-done.1.refs_2_.wb_ref), custom_call_target="tpu_custom_call" | custom-call | tf_op jit(solution)/shard_map/input_grad/pallas_call | solution.py:814
  433.4 13.2 %collective-permute-done.60.refs_0_ = bf16[2,2,64,2048]{3,2,1,0:T(8,128)(2,1)} collective-permute-done((bf16[2,2,64,2048]{3,2,1,0:T(8,128)(2,1)}, bf16[2,2,64,2048]{3,2,1,0:T(8,128)(2,1)}, u32[]{:S(2)}, u32[]{:S(2)}) %collective-permute-start.60) | collective-permute-done | bytes 1048608 | tf_op jit(solution)/shard_map/ppermute | solution.py:572
  452.2 3.9 fusion.5
  459.1 4.0 collective-permute-start.69
  468.0 4.0 scatter_fusion.1
  477.5 3.3 select_bitcast_fusion.1
  484.6 3.8 fusion.refs_0_
  498.3 15.5 %collective-permute-done.73 = bf16[2,64,2048]{2,1,0:T(8,128)(2,1)} collective-permute-done((bf16[2,64,2048]{2,1,0:T(8,128)(2,1)}, bf16[2,64,2048]{2,1,0:T(8,128)(2,1)}, u32[]{:S(2)}, u32[]{:S(2)}) %collective-permute-start.73) | collective-permute-done | bytes 524320 | tf_op jit(solution)/shard_map/ppermute | solution.py:572
  520.8 7.8 %collective-permute-done.75 = bf16[2,64,2048]{2,1,0:T(8,128)(2,1)S(1)} collective-permute-done((bf16[2,64,2048]{2,1,0:T(8,128)(2,1)S(1)}, bf16[2,64,2048]{2,1,0:T(8,128)(2,1)S(1)}, u32[]{:S(2)}, u32[]{:S(2)}) %collective-permute-start.75) | collective-permute-done | bytes 524320 | tf_op jit(solution)/shard_map/ppermute | solution.py:572
  533.2 3.5 assemble.1
  (567 shorter events, 347.9 us)
Async XLA Ops:
  6.5 30.0 %collective-permute-start.1 = (bf16[4,512,1024]{2,1,0:T(8,128)(2,1)}, bf16[4,512,1024]{2,1,0:T(8,128)(2,1)}, u32[]{:S(2)}, u32[]{:S(2)}) collective-permute-start(bf16[4,512,1024]{2,1,0:T(8,128)(2,1)} %layout.5), channel_id=1, source_target_pairs={{0,1},{1,0},{2,3},{3,2},{4,5},{5,4},{6,7},{7,6},{8,9},{9,8},{10,11... | collective-permute-start | bytes 12582920 | tf_op jit(solution)/shard_map/ppermute | solution.py:541
  12.6 24.0 %collective-permute-start.2 = (bf16[4,512,1024]{2,1,0:T(8,128)(2,1)}, bf16[4,512,1024]{2,1,0:T(8,128)(2,1)}, u32[]{:S(2)}, u32[]{:S(2)}) collective-permute-start(bf16[4,512,1024]{2,1,0:T(8,128)(2,1)} %layout.6), channel_id=1, source_target_pairs={{0,1},{1,0},{2,3},{3,2},{4,5},{5,4},{6,7},{7,6},{8,9},{9,8},{10,11... | collective-permute-start | bytes 12582920 | tf_op jit(solution)/shard_map/ppermute | solution.py:541
  15.2 21.3 %collective-permute-start.4 = (f32[48,1024]{1,0:T(8,128)}, f32[48,1024]{1,0:T(8,128)S(1)}, u32[]{:S(2)}, u32[]{:S(2)}) collective-permute-start(f32[48,1024]{1,0:T(8,128)} %bitcast.228), channel_id=1, source_target_pairs={{0,1},{1,0},{2,3},{3,2},{4,5},{5,4},{6,7},{7,6},{8,9},{9,8},{10,11... | collective-permute-start | bytes 589832 | tf_op jit(solution)/shard_map/ppermute | solution.py:513
  15.2 21.2 %collective-permute-start = (bf16[4,1024]{1,0:T(4,128)(2,1)S(1)}, bf16[4,1024]{1,0:T(4,128)(2,1)S(1)}, u32[]{:S(2)}, u32[]{:S(2)}) collective-permute-start(bf16[4,1024]{1,0:T(4,128)(2,1)S(1)} %get-tuple-element.1374), channel_id=1, source_target_pairs={{0,1},{1,0},{2,3},{3,2},{4,5},{5,4},{6,7},{7,6},{8,9},{9,8},{10,11... | collective-permute-start | bytes 24584 | tf_op jit(solution)/shard_map/ppermute | solution.py:513
  16.8 19.7 %collective-permute-start.3 = (bf16[1024,512]{1,0:T(8,128)(2,1)}, bf16[1024,512]{1,0:T(8,128)(2,1)S(1)}, u32[]{:S(2)}, u32[]{:S(2)}) collective-permute-start(bf16[1024,512]{1,0:T(8,128)(2,1)} %dynamic-slice_bitcast_fusion.2), channel_id=1, source_target_pairs={{0,1},{1,0},{2,3},{3,2},{4,5},{5,4},{6,7},{7,6},{8,9},{9,8},{10,11... | collective-permute-start | bytes 3145736 | tf_op jit(solution)/shard_map/ppermute | solution.py:543
  123.9 29.9 %collective-permute-start.21 = (bf16[20,48,512]{2,1,0:T(8,128)(2,1)}, bf16[20,48,512]{2,1,0:T(8,128)(2,1)S(1)}, u32[]{:S(2)}, u32[]{:S(2)}) collective-permute-start(bf16[20,48,512]{2,1,0:T(8,128)(2,1)} %after.12.refs_0_), channel_id=1, source_target_pairs={{0,4},{4,0},{8,12},{12,8},{16,20},{20,16},{24,28},{28,24},{1,5},{5... | collective-permute-start | bytes 2949128 | tf_op jit(solution)/shard_map/ppermute | solution.py:572
  125.5 28.4 %collective-permute-start.22 = (bf16[20,48,512]{2,1,0:T(8,128)(2,1)}, bf16[20,48,512]{2,1,0:T(8,128)(2,1)S(1)}, u32[]{:S(2)}, u32[]{:S(2)}) collective-permute-start(bf16[20,48,512]{2,1,0:T(8,128)(2,1)} %after.12.refs_0_), channel_id=1, source_target_pairs={{0,8},{4,12},{8,0},{12,4},{16,24},{20,28},{24,16},{28,20},{1,9},{5... | collective-permute-start | bytes 2949128 | tf_op jit(solution)/shard_map/ppermute | solution.py:572
  192.3 46.7 %collective-permute-start.33 = (bf16[20,48,512]{2,1,0:T(8,128)(2,1)}, bf16[20,48,512]{2,1,0:T(8,128)(2,1)S(1)}, u32[]{:S(2)}, u32[]{:S(2)}) collective-permute-start(bf16[20,48,512]{2,1,0:T(8,128)(2,1)} %after.13.refs_1_), channel_id=1, source_target_pairs={{0,4},{4,0},{8,12},{12,8},{16,20},{20,16},{24,28},{28,24},{1,5},{5... | collective-permute-start | bytes 2949128 | tf_op jit(solution)/shard_map/ppermute | solution.py:572
  192.8 46.1 %collective-permute-start.34 = (bf16[20,48,512]{2,1,0:T(8,128)(2,1)}, bf16[20,48,512]{2,1,0:T(8,128)(2,1)S(1)}, u32[]{:S(2)}, u32[]{:S(2)}) collective-permute-start(bf16[20,48,512]{2,1,0:T(8,128)(2,1)} %after.13.refs_1_), channel_id=1, source_target_pairs={{0,8},{4,12},{8,0},{12,4},{16,24},{20,28},{24,16},{28,20},{1,9},{5... | collective-permute-start | bytes 2949128 | tf_op jit(solution)/shard_map/ppermute | solution.py:572
  246.3 49.2 %collective-permute-start.43 = (bf16[7,48,2048]{2,1,0:T(8,128)(2,1)}, bf16[7,48,2048]{2,1,0:T(8,128)(2,1)S(1)}, u32[]{:S(2)}, u32[]{:S(2)}) collective-permute-start(bf16[7,48,2048]{2,1,0:T(8,128)(2,1)} %get-tuple-element.1172), channel_id=1, source_target_pairs={{0,4},{4,0},{8,12},{12,8},{16,20},{20,16},{24,28},{28,24},{1,5},{5... | collective-permute-start | bytes 4128776 | tf_op jit(solution)/shard_map/ppermute | solution.py:572
  247.9 47.7 %collective-permute-start.44 = (bf16[7,48,2048]{2,1,0:T(8,128)(2,1)}, bf16[7,48,2048]{2,1,0:T(8,128)(2,1)S(1)}, u32[]{:S(2)}, u32[]{:S(2)}) collective-permute-start(bf16[7,48,2048]{2,1,0:T(8,128)(2,1)} %get-tuple-element.1173), channel_id=1, source_target_pairs={{0,8},{4,12},{8,0},{12,4},{16,24},{20,28},{24,16},{28,20},{1,9},{5... | collective-permute-start | bytes 4128776 | tf_op jit(solution)/shard_map/ppermute | solution.py:572
  292.2 42.5 %collective-permute-start.50 = (bf16[6,48,2048]{2,1,0:T(8,128)(2,1)}, bf16[6,48,2048]{2,1,0:T(8,128)(2,1)S(1)}, u32[]{:S(2)}, u32[]{:S(2)}) collective-permute-start(bf16[6,48,2048]{2,1,0:T(8,128)(2,1)} %get-tuple-element.1252), channel_id=1, source_target_pairs={{0,4},{4,0},{8,12},{12,8},{16,20},{20,16},{24,28},{28,24},{1,5},{5... | collective-permute-start | bytes 3538952 | tf_op jit(solution)/shard_map/ppermute | solution.py:572
  292.8 43.9 %collective-permute-start.51 = (bf16[6,48,2048]{2,1,0:T(8,128)(2,1)}, bf16[6,48,2048]{2,1,0:T(8,128)(2,1)S(1)}, u32[]{:S(2)}, u32[]{:S(2)}) collective-permute-start(bf16[6,48,2048]{2,1,0:T(8,128)(2,1)} %get-tuple-element.1253), channel_id=1, source_target_pairs={{0,8},{4,12},{8,0},{12,4},{16,24},{20,28},{24,16},{28,20},{1,9},{5... | collective-permute-start | bytes 3538952 | tf_op jit(solution)/shard_map/ppermute | solution.py:572
  317.3 27.1 %collective-permute-start.52 = (bf16[3,48,2048]{2,1,0:T(8,128)(2,1)}, bf16[3,48,2048]{2,1,0:T(8,128)(2,1)S(1)}, u32[]{:S(2)}, u32[]{:S(2)}) collective-permute-start(bf16[3,48,2048]{2,1,0:T(8,128)(2,1)} %get-tuple-element.1269), channel_id=1, source_target_pairs={{0,4},{4,0},{8,12},{12,8},{16,20},{20,16},{24,28},{28,24},{1,5},{5... | collective-permute-start | bytes 1769480 | tf_op jit(solution)/shard_map/ppermute | solution.py:572
  318.9 25.5 %collective-permute-start.53 = (bf16[3,48,2048]{2,1,0:T(8,128)(2,1)}, bf16[3,48,2048]{2,1,0:T(8,128)(2,1)S(1)}, u32[]{:S(2)}, u32[]{:S(2)}) collective-permute-start(bf16[3,48,2048]{2,1,0:T(8,128)(2,1)} %get-tuple-element.1270), channel_id=1, source_target_pairs={{0,8},{4,12},{8,0},{12,4},{16,24},{20,28},{24,16},{28,20},{1,9},{5... | collective-permute-start | bytes 1769480 | tf_op jit(solution)/shard_map/ppermute | solution.py:572
  334.7 24.8 %collective-permute-start.54 = (bf16[2,48,2048]{2,1,0:T(8,128)(2,1)}, bf16[2,48,2048]{2,1,0:T(8,128)(2,1)S(1)}, u32[]{:S(2)}, u32[]{:S(2)}) collective-permute-start(bf16[2,48,2048]{2,1,0:T(8,128)(2,1)} %get-tuple-element.1282), channel_id=1, source_target_pairs={{0,8},{4,12},{8,0},{12,4},{16,24},{20,28},{24,16},{28,20},{1,9},{5... | collective-permute-start | bytes 1179656 | tf_op jit(solution)/shard_map/ppermute | solution.py:572
  336.7 22.9 %collective-permute-start.56 = (bf16[2,48,2048]{2,1,0:T(8,128)(2,1)}, bf16[2,48,2048]{2,1,0:T(8,128)(2,1)S(1)}, u32[]{:S(2)}, u32[]{:S(2)}) collective-permute-start(bf16[2,48,2048]{2,1,0:T(8,128)(2,1)} %get-tuple-element.1284), channel_id=1, source_target_pairs={{0,4},{4,0},{8,12},{12,8},{16,20},{20,16},{24,28},{28,24},{1,5},{5... | collective-permute-start | bytes 1179656 | tf_op jit(solution)/shard_map/ppermute | solution.py:572
  354.1 41.2 %collective-permute-start.59 = (bf16[4,4,68,512]{3,1,2,0:T(4,128)(2,1)S(1)}, bf16[4,4,68,512]{3,1,2,0:T(4,128)(2,1)S(1)}, u32[]{:S(2)}, u32[]{:S(2)}) collective-permute-start(bf16[4,4,68,512]{3,1,2,0:T(4,128)(2,1)S(1)} %copy.527), channel_id=1, source_target_pairs={{0,4},{4,0},{8,12},{12,8},{16,20},{20,16},{24,28},{28,24},{1,5},{5... | collective-permute-start | bytes 3342344 | tf_op jit(solution)/shard_map/ppermute | solution.py:572
  366.0 29.7 %collective-permute-start.58 = (bf16[2,2,64,2048]{3,2,1,0:T(8,128)(2,1)S(1)}, bf16[2,2,64,2048]{3,2,1,0:T(8,128)(2,1)S(1)}, u32[]{:S(2)}, u32[]{:S(2)}) collective-permute-start(bf16[2,2,64,2048]{3,2,1,0:T(8,128)(2,1)S(1)} %bitcast.244), channel_id=1, source_target_pairs={{0,8},{4,12},{24,16},{28,20},{1,9},{5,13},{25,17},{29,21},{2,10},{... | collective-permute-start | bytes 3145736 | tf_op jit(solution)/shard_map/ppermute | solution.py:572
  400.9 30.8 %collective-permute-start.62 = (bf16[4,64,2048]{2,1,0:T(8,128)(2,1)}, bf16[4,64,2048]{2,1,0:T(8,128)(2,1)}, u32[]{:S(2)}, u32[]{:S(2)}) collective-permute-start(bf16[4,64,2048]{2,1,0:T(8,128)(2,1)} %dynamic-slice_bitcast_fusion.1), channel_id=1, source_target_pairs={{0,4},{4,0},{8,12},{12,8},{16,20},{20,16},{24,28},{28,24},{1,5},{5... | collective-permute-start | bytes 3145736 | tf_op jit(solution)/shard_map/ppermute | solution.py:572
  402.4 29.1 %collective-permute-start.63 = (bf16[4,2,68,512]{3,0,2,1:T(4,128)(2,1)S(1)}, bf16[4,2,68,512]{3,0,2,1:T(4,128)(2,1)S(1)}, u32[]{:S(2)}, u32[]{:S(2)}) collective-permute-start(bf16[4,2,68,512]{3,0,2,1:T(4,128)(2,1)S(1)} %copy.532), channel_id=1, source_target_pairs={{0,16},{4,20},{8,24},{12,28},{16,0},{20,4},{24,8},{28,12},{1,17},{... | collective-permute-start | bytes 1671176 | tf_op jit(solution)/shard_map/ppermute | solution.py:572
  406.4 40.2 %collective-permute-start.60 = (bf16[2,2,64,2048]{3,2,1,0:T(8,128)(2,1)}, bf16[2,2,64,2048]{3,2,1,0:T(8,128)(2,1)}, u32[]{:S(2)}, u32[]{:S(2)}) collective-permute-start(bf16[2,2,64,2048]{3,2,1,0:T(8,128)(2,1)} %get-tuple-element.1347.refs_0_), channel_id=1, source_target_pairs={{0,8},{4,12},{8,16},{12,20},{1,9},{5,13},{9,17},{13,21},{2,10},{6,... | collective-permute-start | bytes 3145736 | tf_op jit(solution)/shard_map/ppermute | solution.py:572
  408.5 39.7 %collective-permute-start.61 = (bf16[2,2,64,2048]{3,2,1,0:T(8,128)(2,1)}, bf16[2,2,64,2048]{3,2,1,0:T(8,128)(2,1)}, u32[]{:S(2)}, u32[]{:S(2)}) collective-permute-start(bf16[2,2,64,2048]{3,2,1,0:T(8,128)(2,1)} %get-tuple-element.1346.refs_1_), channel_id=1, source_target_pairs={{16,8},{20,12},{24,16},{28,20},{17,9},{21,13},{25,17},{29,21},{18,... | collective-permute-start | bytes 3145736 | tf_op jit(solution)/shard_map/ppermute | solution.py:572
  411.2 52.1 %collective-permute-start.71 = (bf16[4,64,2048]{2,1,0:T(8,128)(2,1)S(1)}, bf16[4,64,2048]{2,1,0:T(8,128)(2,1)S(1)}, u32[]{:S(2)}, u32[]{:S(2)}) collective-permute-start(bf16[4,64,2048]{2,1,0:T(8,128)(2,1)S(1)} %dynamic-slice_bitcast_fusion), channel_id=1, source_target_pairs={{0,4},{4,0},{8,12},{12,8},{16,20},{20,16},{24,28},{28,24},{1,5},{5... | collective-permute-start | bytes 3145736 | tf_op jit(solution)/shard_map/ppermute | solution.py:572
  449.0 23.0 %collective-permute-start.77 = (bf16[4,68,512]{2,1,0:T(8,128)(2,1)}, bf16[4,68,512]{2,1,0:T(8,128)(2,1)}, u32[]{:S(2)}, u32[]{:S(2)}) collective-permute-start(bf16[4,68,512]{2,1,0:T(8,128)(2,1)} %dynamic-slice_bitcast_fusion.10), channel_id=1, source_target_pairs={{0,8},{4,12},{8,0},{12,4},{16,24},{20,28},{24,16},{28,20},{1,9},{5... | collective-permute-start | bytes 835592 | tf_op jit(solution)/shard_map/ppermute | solution.py:572
  449.8 25.9 %collective-permute-start.70 = (bf16[2,64,2048]{2,1,0:T(8,128)(2,1)}, bf16[2,64,2048]{2,1,0:T(8,128)(2,1)}, u32[]{:S(2)}, u32[]{:S(2)}) collective-permute-start(bf16[2,64,2048]{2,1,0:T(8,128)(2,1)} %dynamic-slice_bitcast_fusion.9), channel_id=1, source_target_pairs={{0,16},{4,20},{8,24},{12,28},{16,0},{20,4},{24,8},{28,12},{1,17},{... | collective-permute-start | bytes 1572872 | tf_op jit(solution)/shard_map/ppermute | solution.py:572
  456.0 32.3 %collective-permute-start.68 = (bf16[2,2,64,2048]{3,2,1,0:T(8,128)(2,1)}, bf16[2,2,64,2048]{3,2,1,0:T(8,128)(2,1)}, u32[]{:S(2)}, u32[]{:S(2)}) collective-permute-start(bf16[2,2,64,2048]{3,2,1,0:T(8,128)(2,1)} %get-tuple-element.1351), channel_id=1, source_target_pairs={{0,8},{4,12},{8,16},{12,20},{16,24},{20,28},{1,9},{5,13},{9,17},{1... | collective-permute-start | bytes 3145736 | tf_op jit(solution)/shard_map/ppermute | solution.py:572
  459.1 29.3 %collective-permute-start.69 = (bf16[2,2,64,2048]{3,2,1,0:T(8,128)(2,1)}, bf16[2,2,64,2048]{3,2,1,0:T(8,128)(2,1)}, u32[]{:S(2)}, u32[]{:S(2)}) collective-permute-start(bf16[2,2,64,2048]{3,2,1,0:T(8,128)(2,1)} %get-tuple-element.1350), channel_id=1, source_target_pairs={{8,0},{12,4},{16,8},{20,12},{24,16},{28,20},{9,1},{13,5},{17,9},{2... | collective-permute-start | bytes 3145736 | tf_op jit(solution)/shard_map/ppermute | solution.py:572
  472.0 19.5 %collective-permute-start.65 = (bf16[20,48,256]{2,1,0:T(8,128)(2,1)}, bf16[20,48,256]{2,1,0:T(8,128)(2,1)}, u32[]{:S(2)}, u32[]{:S(2)}) collective-permute-start(bf16[20,48,256]{2,1,0:T(8,128)(2,1)} %dynamic-slice_convert_fusion), channel_id=1, source_target_pairs={{0,2},{1,3},{2,0},{3,1},{4,6},{5,7},{6,4},{7,5},{8,10},{9,11},{10,... | collective-permute-start | bytes 1474568 | tf_op jit(solution)/shard_map/ppermute | solution.py:1009
  475.7 52.9 %collective-permute-start.79 = (bf16[1024,64]{0,1:T(8,128)(2,1)}, bf16[1024,64]{0,1:T(8,128)(2,1)}, u32[]{:S(2)}, u32[]{:S(2)}) collective-permute-start(bf16[1024,64]{0,1:T(8,128)(2,1)} %bitcast.151), channel_id=1, source_target_pairs={{0,1},{1,0},{2,3},{3,2},{4,5},{5,4},{6,7},{7,6},{8,9},{9,8},{10,11... | collective-permute-start | bytes 393224 | tf_op jit(solution)/shard_map/ppermute | solution.py:513
  490.2 23.6 %collective-permute-start.73 = (bf16[2,64,2048]{2,1,0:T(8,128)(2,1)}, bf16[2,64,2048]{2,1,0:T(8,128)(2,1)}, u32[]{:S(2)}, u32[]{:S(2)}) collective-permute-start(bf16[2,64,2048]{2,1,0:T(8,128)(2,1)} %dynamic-slice_bitcast_fusion.6), channel_id=1, source_target_pairs={{0,16},{4,20},{8,24},{12,28},{16,0},{20,4},{24,8},{28,12},{1,17},{... | collective-permute-start | bytes 1572872 | tf_op jit(solution)/shard_map/ppermute | solution.py:572
  498.2 32.2 %collective-permute-start.66 = (bf16[20,48,128]{2,1,0:T(8,128)(2,1)S(1)}, bf16[20,48,128]{2,1,0:T(8,128)(2,1)S(1)}, u32[]{:S(2)}, u32[]{:S(2)}) collective-permute-start(bf16[20,48,128]{2,1,0:T(8,128)(2,1)S(1)} %bitcast.259), channel_id=1, source_target_pairs={{0,1},{1,0},{2,3},{3,2},{4,5},{5,4},{6,7},{7,6},{8,9},{9,8},{10,11... | collective-permute-start | bytes 737288 | tf_op jit(solution)/shard_map/ppermute | solution.py:513
  (150 other events, 793.0 us)

commit v16 on v15

--- a/solution.py
+++ b/solution.py
@@ -152,10 +152,9 @@
         lax.fori_loop(0, 4, columns, 0)
 
 
-def whole_product_kernel(lows, *refs):
-    (feat_ref, prev_ref, feat_too, prev_too, kept_ref), refs = refs[:5], refs[5:]
+def whole_product_kernel(lows, mine_ref, theirs_ref, kept_ref, *refs):
     groups, (out_ref, left_buf, turned_buf, right_buf, left_sems, sems) = refs[:-6], refs[-6:]
-    steps, streams, depth = feat_ref.shape
+    steps, streams, depth = mine_ref.shape
     blocks = right_buf.shape[0]
     width = right_buf.shape[3]
     rows = 2 * steps * streams
@@ -169,42 +168,40 @@
         ]
         return [pltpu.make_async_copy(a, b, sems.at[block, i]) for i, (a, b) in enumerate(jobs)]
 
-    lefts = [(feat_ref, 0, 0), (feat_too, steps, 0), (prev_ref, 0, 1), (prev_too, steps, 1)]
     lefts = [
-        pltpu.make_async_copy(x, left_buf.at[half, low : low + steps], left_sems.at[i])
-        for i, (x, low, half) in enumerate(lefts)
+        pltpu.make_async_copy(mine_ref, left_buf.at[:steps], left_sems.at[0]),
+        pltpu.make_async_copy(theirs_ref, left_buf.at[steps:], left_sems.at[1]),
     ]
     for copy in lefts:
         copy.start()
     for block in range(blocks):
         for copy in fetches_of(block):
             copy.start()
-    for which in range(2):
-        lefts[2 * which].wait()
-        lefts[2 * which + 1].wait()
-        turned_buf[which] = left_buf[which].reshape(rows, depth).T
+    for copy in lefts:
+        copy.wait()
+    turned_buf[...] = left_buf[...].reshape(rows, depth).T
     for block in range(blocks):
         for copy in fetches_of(block):
             copy.wait()
-
-        def one(which, _):
-            total = dot(turned_buf[which], right_buf[block].reshape(rows, width))
-            out_ref[which, :, block * width : (block + 1) * width] = total.astype(BF16)
-            return 0
-
-        lax.fori_loop(0, 2, one, 0)
-
-
-def assemble_kernel(place_ref, near_a, near_b, far_a, far_b, in_ref, rec_ref):
+        total = dot(turned_buf[...], right_buf[block].reshape(rows, width))
+        out_ref[:, block * width : (block + 1) * width] = total.astype(BF16)
+
+
+def assemble_kernel(place_ref, near_a, near_b, in_a, in_b, rec_a, rec_b, in_ref, rec_ref):
     own, low, high = place_ref[0], place_ref[1], place_ref[2]
     width = in_ref.shape[3] // HALVES
-    for direction, mine_ref, theirs_ref, index in ((own, near_a, near_b, low), (1 - own, far_a, far_b, high)):
-        for which, out_ref in ((0, in_ref), (1, rec_ref)):
-            mine, theirs = mine_ref[which].astype(F32), theirs_ref[which].astype(F32)
-            for half in range(HALVES):
-                whole = jnp.where(index == half, mine, theirs)
-                gates = jnp.stack([whole[:, gate * width : (gate + 1) * width] for gate in range(4)])
-                out_ref[direction, :, :, half * width : (half + 1) * width] = jnp.swapaxes(gates, 0, 1)
+    jobs = [
+        (own, near_a, near_b, 0, low, in_ref),
+        (own, near_a, near_b, 1, low, rec_ref),
+        (1 - own, in_a, in_b, 0, high, in_ref),
+        (1 - own, rec_a, rec_b, 0, high, rec_ref),
+    ]
+    for direction, mine_ref, theirs_ref, which, index, out_ref in jobs:
+        mine, theirs = mine_ref[which].astype(F32), theirs_ref[which].astype(F32)
+        for half in range(HALVES):
+            whole = jnp.where(index == half, mine, theirs)
+            gates = jnp.stack([whole[:, gate * width : (gate + 1) * width] for gate in range(4)])
+            out_ref[direction, :, :, half * width : (half + 1) * width] = jnp.swapaxes(gates, 0, 1)
 
 
 def order_kernel(step_ref, feat_ref, out_ref, all_ref, sems):
@@ -905,23 +902,27 @@
     near_right, first = completed(jnp.full((1,), number["begin"], jnp.int32), chunk_rows, near_left, near_right, near_late)
     far_all, *far_parts = after((first,), far_all, *far_parts)
     blocks = 4
-    far = pl.pallas_call(
-        functools.partial(whole_product_kernel, tuple(lows)),
-        out_shape=jax.ShapeDtypeStruct((2, depth, 4 * width), BF16),
-        in_specs=[ANY] * (5 + len(far_parts)),
-        out_specs=VMEM,
-        scratch_shapes=[
-            pltpu.VMEM((2, 2 * steps, streams, depth), BF16),
-            pltpu.VMEM((2, depth, 2 * steps * streams), BF16),
-            pltpu.VMEM((blocks, 2 * steps, streams, 4 * width // blocks), BF16),
-            pltpu.SemaphoreType.DMA((4,)),
-            pltpu.SemaphoreType.DMA((blocks, 1 + len(far_parts))),
-        ],
-        compiler_params=params(28),
-        cost_estimate=cost(0, 0),
-        name="whole_product",
-    )(*(in_hbm(x) for x in (feat_all, prev_all, feat_in[1], prev_in[1], far_all, *far_parts)))
-    far = far.reshape(2, line, 2, share_rows, 4 * width)
+
+    def far_product(mine, theirs):
+        grad = pl.pallas_call(
+            functools.partial(whole_product_kernel, tuple(lows)),
+            out_shape=jax.ShapeDtypeStruct((depth, 4 * width), BF16),
+            in_specs=[ANY] * (3 + len(far_parts)),
+            out_specs=VMEM,
+            scratch_shapes=[
+                pltpu.VMEM((2 * steps, streams, depth), BF16),
+                pltpu.VMEM((depth, 2 * steps * streams), BF16),
+                pltpu.VMEM((blocks, 2 * steps, streams, 4 * width // blocks), BF16),
+                pltpu.SemaphoreType.DMA((2,)),
+                pltpu.SemaphoreType.DMA((blocks, 1 + len(far_parts))),
+            ],
+            compiler_params=params(24),
+            cost_estimate=cost(0, 0),
+            name="whole_product",
+        )(*(in_hbm(x) for x in (mine, theirs, far_all, *far_parts)))
+        return grad.reshape(line, 2, share_rows, 4 * width)
+
+    far_in = far_product(feat_all, feat_in[1])
     near = multiplied(near_left, near_right).reshape(2, line, 2, share_rows, 4 * width)
 
     def states_of(hidden, cell):
@@ -941,12 +942,15 @@
     tokens = {}
 
     def second(up, down):
-        up, tokens["far"], tokens["dz"], tokens["proj"] = after((), up, far, dz_all, proj_y, free=5 * MIB)
+        up, tokens["far"], tokens["dz"], tokens["proj"], tokens["prev"] = after(
+            (), up, far_in, dz_all, proj_y, prev_in[1], free=5 * MIB
+        )
         return up, up
 
     def beside_second(rise, fall):
         (sent,) = after((rise, fall), tokens["far"], free=5 * MIB)
-        tokens["in"], tokens["rec"] = (with_partner(sent[i])[2] for i in range(2))
+        tokens["in"] = with_partner(sent)[2]
+        tokens["rec"] = with_partner(far_product(prev_all, tokens["prev"]))[2]
         tokens["proj"] = across_two(tokens["proj"])
 
     def third(up, down):
@@ -976,19 +980,20 @@
         return pick(summed, number[name], 1), swapped(pick(summed, number["not_" + name], 1), pairs)
 
     near_pair = halves_of(near, "low", near_swap)
-    far_pair = halves_of(jnp.stack([in_two, rec_two]), "high", far_swap)
-    far_pair = [lax.ppermute(x, "gate", swap) for x in far_pair]
+    in_pair, rec_pair = (
+        [lax.ppermute(y, "gate", swap) for y in halves_of(x[None], "high", far_swap)] for x in (in_two, rec_two)
+    )
     proj_mine, proj_theirs = halves_of(proj_two, "high", far_swap)
     grad_proj = proj_mine.astype(F32) + proj_theirs.astype(F32)
     grad_shape = (2, share_rows, 4, cells)
     grad_w_in, grad_w_rec = pl.pallas_call(
         assemble_kernel,
         out_shape=(jax.ShapeDtypeStruct(grad_shape, F32),) * 2,
-        in_specs=[SMEM] + [VMEM] * 4,
+        in_specs=[SMEM] + [VMEM] * 6,
         out_specs=[VMEM] * 2,
         compiler_params=params(14),
         name="assemble",
-    )(jnp.stack([own, low, high]), *near_pair, *far_pair)
+    )(jnp.stack([own, low, high]), *near_pair, *in_pair, *rec_pair)
 
     def home(mine, theirs):
         return by_direction(*trade(mine, theirs)).astype(F32)

time: 548 us -> 536 us (0.978)
  waiting for transfers between devices: 44.7 us -> 28.1 us
    ppermute x28 -> x29, waiting for transfers between devices: 39.4 us -> 22.8 us  [swapped(): return lax.ppermute(array, 'batch', pairs)]
    pallas_call x1 -> x2, Pallas kernels: 16.7 us -> 20.8 us  [far_product(): pl.pallas_call(functools.partial(whole_product_kernel, tuple(lows)), out_...]
    ppermute x28 -> x29, starting transfers between devices: 39.1 us -> 42.1 us  [swapped(): return lax.ppermute(array, 'batch', pairs)]
    unnamed x213 -> x217, local copies, waits for them, and re-layouts: 13 us -> 13.7 us
  transfers between devices with their start and end apart: 80 -> 83, of which waited for: 33 -> 33; matrix products, arithmetic and copies ran while one was open for 12% -> 12% of each run, Pallas kernels for 48% -> 50%
where the time goes in v16:
time: 536 us; the launch traced here: 526 us
  Pallas kernels  331 us (62%)
  starting transfers between devices  89.3 us (17%)
  local copies, waits for them, and re-layouts  39.3 us (7%)
  other arithmetic  31.4 us (6%)
  waiting for transfers between devices  28.1 us (5%)
    pallas_call x20, Pallas kernels, backward_call(): pl.pallas_call(backward_kernel, out_shape=(vmem((streams, depth), BF16),...  62 us
    pallas_call x19, Pallas kernels, between_call(): pl.pallas_call(functools.partial(between_kernel, not stacks, step == step...  56.8 us
    pallas_call x20, Pallas kernels, forward_call(): pl.pallas_call(functools.partial(forward_kernel, first), out_shape=(vmem(...  56.1 us
    pallas_call x20, Pallas kernels, aside_call(): pl.pallas_call(functools.partial(aside_kernel, not stacks, step == 0, not...  55.9 us
    ppermute x39, starting transfers between devices, body(): peer = lax.ppermute(part, 'gate', across)  43.4 us
    ppermute x29, starting transfers between devices, swapped(): return lax.ppermute(array, 'batch', pairs)  42.1 us
    pallas_call x4, Pallas kernels, by_gate(): pl.pallas_call(functools.partial(layout_kernel, keep, spread), out_shape=...  23.2 us
    ppermute x29, waiting for transfers between devices, swapped(): return lax.ppermute(array, 'batch', pairs)  22.8 us
  transfers between devices with their start and end apart: 83, of which 33 were waited for; matrix products, arithmetic and copies ran while one was open for 12% of the time, Pallas kernels for 50%

profile of v16, /device:TPU:8, one launch (start us, length us, event | category | flops | bytes accessed | tf_op | source)
XLA Modules:
  0.0 525.8 jit_solution(12237497490968471070)
XLA Ops:
  0.7 5.8 %layout.5 = bf16[4,512,1024]{2,1,0:T(8,128)(2,1)} custom-call(s32[1]{0:T(128)} %bitcast.15.which_ref, bf16[2,512,4,1024]{3,2,1,0:T(4,128)(2,1)} %w_ref.5), custom_call_target="tpu_custom_call" | custom-call | tf_op jit(solution)/shard_map/layout/pallas_call | solution.py:522
  6.6 5.9 %layout.6 = bf16[4,512,1024]{2,1,0:T(8,128)(2,1)} custom-call(s32[1]{0:T(128)} %bitcast.15.which_ref, bf16[2,512,4,1024]{3,2,1,0:T(4,128)(2,1)} %w_ref.7), custom_call_target="tpu_custom_call" | custom-call | tf_op jit(solution)/shard_map/layout/pallas_call | solution.py:522
  21.9 6.4 %layout.4 = (bf16[4,512,1024]{2,1,0:T(8,128)(2,1)S(1)}, bf16[4,512,1024]{2,1,0:T(8,128)(2,1)}) custom-call(s32[1]{0:T(128)} %numbers.1.which_ref, bf16[2,512,4,1024]{3,2,1,0:T(4,128)(2,1)} %w_ref.5), custom_call_target="tpu_custom_call" | custom-call | tf_op jit(solution)/shard_map/layout/pallas_call | solution.py:522
  28.3 5.1 layout.7.wa_ref
  37.5 5.0 begin.1
  155.0 3.2 between.34
  162.1 3.3 between.35
  189.2 3.0 backward_step.20
  198.5 3.2 backward_step.21
  205.8 3.0 backward_step.22
  242.8 3.2 backward_step.27
  288.4 3.5 backward_step.33
  299.5 3.0 backward_step.34
  340.4 3.8 backward_step.39
  345.4 3.0 aside.39
  349.6 3.6 bitcast_convert_fusion
  355.3 4.2 gather.13
  361.6 4.3 late.1
  367.2 11.2 %product.1 = bf16[2,512,2048]{2,1,0:T(8,128)(2,1)S(1)} custom-call(bf16[40,48,1024]{2,1,0:T(8,128)(2,1)S(1)} %get-tuple-element.1276.refs_0_.left_ref, bf16[40,48,2048]{2,1,0:T(8,128)(2,1)S(1)} %get-tuple-element.1289.right_ref), custom_call_target="tpu_custom_call" | custom-call | tf_op jit(solution)/shard_map/product/pallas_call | solution.py:888
  378.5 11.2 %whole_product.2 = bf16[512,2048]{1,0:T(8,128)(2,1)S(1)} custom-call(bf16[20,48,512]{2,1,0:T(8,128)(2,1)} %after.12.refs_0_.mine_ref, bf16[20,48,512]{2,1,0:T(8,128)(2,1)} %get-tuple-element.1291.theirs_ref, bf16[20,48,2048]{2,1,0:T(8,128)(2,1)} %get-tuple-element.1296.kept_ref, bf16[7,48,2048]{2,1,0:T(8,128)(2,1)} %get-tuple-element.1297.refs_0_, ...), custom_call_target="tpu_custom_call" | custom-call | tf_op jit(solution)/shard_map/whole_product/pallas_call | solution.py:907
  396.3 4.0 collective-permute-start.63
  403.7 9.7 %whole_product.3 = bf16[512,2048]{1,0:T(8,128)(2,1)S(1)} custom-call(bf16[20,48,512]{2,1,0:T(8,128)(2,1)} %after.13.refs_1_.mine_ref, bf16[20,48,512]{2,1,0:T(8,128)(2,1)} %copy-done.14, bf16[20,48,2048]{2,1,0:T(8,128)(2,1)} %get-tuple-element.1296.kept_ref, bf16[7,48,2048]{2,1,0:T(8,128)(2,1)} %get-tuple-element.1297.refs_0_, ...), custom_call_target="tpu_custom_call" | custom-call | tf_op jit(solution)/shard_map/whole_product/pallas_call | solution.py:907
  414.6 19.4 %input_grad.1.refs_2_ = f32[20,48,512]{2,1,0:T(8,128)S(1)} custom-call(s32[2]{0:T(128)S(1)} %copy-done.40, bf16[4,20,48,2048]{3,2,1,0:T(8,128)(2,1)} %get-tuple-element.1305.dz_ref, bf16[4,512,1024]{2,1,0:T(8,128)(2,1)} %get-tuple-element.1306.wa_ref, bf16[4,512,1024]{2,1,0:T(8,128)(2,1)} %collective-permute-done.1.refs_2_.wb_ref), custom_call_target="tpu_custom_call" | custom-call | tf_op jit(solution)/shard_map/input_grad/pallas_call | solution.py:811
  437.8 3.1 collective-permute-start.80
  442.7 3.7 fusion.5
  449.1 4.1 collective-permute-start.69
  459.4 6.2 %scatter_fusion.1 = f32[48,2,1024]{2,1,0:T(2,128)} fusion(f32[48,2,1024]{2,1,0:T(2,128)} %broadcast_in_dim.45, s32[48]{0:T(128)S(1)} %copy-done.61, f32[48,2,1024]{2,1,0:T(2,128)} %maximum_bitcast_fusion.1), kind=kCustom, calls=%fused_computation.3 | custom fusion | bytes 1179840 | tf_op jit(solution)/shard_map/scatter | solution.py:939
  475.3 3.3 select_bitcast_fusion.1
  482.3 3.8 fusion.refs_0_
  491.9 17.7 %collective-permute-done.76 = bf16[2,64,2048]{2,1,0:T(8,128)(2,1)S(1)} collective-permute-done((bf16[2,64,2048]{2,1,0:T(8,128)(2,1)S(1)}, bf16[2,64,2048]{2,1,0:T(8,128)(2,1)S(1)}, u32[]{:S(2)}, u32[]{:S(2)}) %collective-permute-start.76) | collective-permute-done | bytes 524320 | tf_op jit(solution)/shard_map/ppermute | solution.py:569
  514.2 3.8 collective-permute-done.78
  521.9 3.5 assemble.1
  (578 shorter events, 345.2 us)
Async XLA Ops:
  6.5 30.0 %collective-permute-start.1 = (bf16[4,512,1024]{2,1,0:T(8,128)(2,1)}, bf16[4,512,1024]{2,1,0:T(8,128)(2,1)}, u32[]{:S(2)}, u32[]{:S(2)}) collective-permute-start(bf16[4,512,1024]{2,1,0:T(8,128)(2,1)} %layout.5), channel_id=1, source_target_pairs={{0,1},{1,0},{2,3},{3,2},{4,5},{5,4},{6,7},{7,6},{8,9},{9,8},{10,11... | collective-permute-start | bytes 12582920 | tf_op jit(solution)/shard_map/ppermute | solution.py:538
  12.5 24.0 %collective-permute-start.2 = (bf16[4,512,1024]{2,1,0:T(8,128)(2,1)}, bf16[4,512,1024]{2,1,0:T(8,128)(2,1)}, u32[]{:S(2)}, u32[]{:S(2)}) collective-permute-start(bf16[4,512,1024]{2,1,0:T(8,128)(2,1)} %layout.6), channel_id=1, source_target_pairs={{0,1},{1,0},{2,3},{3,2},{4,5},{5,4},{6,7},{7,6},{8,9},{9,8},{10,11... | collective-permute-start | bytes 12582920 | tf_op jit(solution)/shard_map/ppermute | solution.py:538
  15.2 21.3 %collective-permute-start.4 = (f32[48,1024]{1,0:T(8,128)}, f32[48,1024]{1,0:T(8,128)S(1)}, u32[]{:S(2)}, u32[]{:S(2)}) collective-permute-start(f32[48,1024]{1,0:T(8,128)} %bitcast.218), channel_id=1, source_target_pairs={{0,1},{1,0},{2,3},{3,2},{4,5},{5,4},{6,7},{7,6},{8,9},{9,8},{10,11... | collective-permute-start | bytes 589832 | tf_op jit(solution)/shard_map/ppermute | solution.py:510
  15.2 21.2 %collective-permute-start = (bf16[4,1024]{1,0:T(4,128)(2,1)S(1)}, bf16[4,1024]{1,0:T(4,128)(2,1)S(1)}, u32[]{:S(2)}, u32[]{:S(2)}) collective-permute-start(bf16[4,1024]{1,0:T(4,128)(2,1)S(1)} %get-tuple-element.1376), channel_id=1, source_target_pairs={{0,1},{1,0},{2,3},{3,2},{4,5},{5,4},{6,7},{7,6},{8,9},{9,8},{10,11... | collective-permute-start | bytes 24584 | tf_op jit(solution)/shard_map/ppermute | solution.py:510
  123.6 30.1 %collective-permute-start.21 = (bf16[20,48,512]{2,1,0:T(8,128)(2,1)}, bf16[20,48,512]{2,1,0:T(8,128)(2,1)S(1)}, u32[]{:S(2)}, u32[]{:S(2)}) collective-permute-start(bf16[20,48,512]{2,1,0:T(8,128)(2,1)} %after.12.refs_0_.mine_ref), channel_id=1, source_target_pairs={{0,4},{4,0},{8,12},{12,8},{16,20},{20,16},{24,28},{28,24},{1,5},{5... | collective-permute-start | bytes 2949128 | tf_op jit(solution)/shard_map/ppermute | solution.py:569
  125.2 28.5 %collective-permute-start.22 = (bf16[20,48,512]{2,1,0:T(8,128)(2,1)}, bf16[20,48,512]{2,1,0:T(8,128)(2,1)S(1)}, u32[]{:S(2)}, u32[]{:S(2)}) collective-permute-start(bf16[20,48,512]{2,1,0:T(8,128)(2,1)} %after.12.refs_0_.mine_ref), channel_id=1, source_target_pairs={{0,8},{4,12},{8,0},{12,4},{16,24},{20,28},{24,16},{28,20},{1,9},{5... | collective-permute-start | bytes 2949128 | tf_op jit(solution)/shard_map/ppermute | solution.py:569
  192.2 46.4 %collective-permute-start.33 = (bf16[20,48,512]{2,1,0:T(8,128)(2,1)}, bf16[20,48,512]{2,1,0:T(8,128)(2,1)S(1)}, u32[]{:S(2)}, u32[]{:S(2)}) collective-permute-start(bf16[20,48,512]{2,1,0:T(8,128)(2,1)} %after.13.refs_1_.mine_ref), channel_id=1, source_target_pairs={{0,4},{4,0},{8,12},{12,8},{16,20},{20,16},{24,28},{28,24},{1,5},{5... | collective-permute-start | bytes 2949128 | tf_op jit(solution)/shard_map/ppermute | solution.py:569
  192.8 45.9 %collective-permute-start.34 = (bf16[20,48,512]{2,1,0:T(8,128)(2,1)}, bf16[20,48,512]{2,1,0:T(8,128)(2,1)S(1)}, u32[]{:S(2)}, u32[]{:S(2)}) collective-permute-start(bf16[20,48,512]{2,1,0:T(8,128)(2,1)} %after.13.refs_1_.mine_ref), channel_id=1, source_target_pairs={{0,8},{4,12},{8,0},{12,4},{16,24},{20,28},{24,16},{28,20},{1,9},{5... | collective-permute-start | bytes 2949128 | tf_op jit(solution)/shard_map/ppermute | solution.py:569
  246.1 49.1 %collective-permute-start.43 = (bf16[7,48,2048]{2,1,0:T(8,128)(2,1)}, bf16[7,48,2048]{2,1,0:T(8,128)(2,1)S(1)}, u32[]{:S(2)}, u32[]{:S(2)}) collective-permute-start(bf16[7,48,2048]{2,1,0:T(8,128)(2,1)} %get-tuple-element.1173), channel_id=1, source_target_pairs={{0,4},{4,0},{8,12},{12,8},{16,20},{20,16},{24,28},{28,24},{1,5},{5... | collective-permute-start | bytes 4128776 | tf_op jit(solution)/shard_map/ppermute | solution.py:569
  247.6 47.6 %collective-permute-start.44 = (bf16[7,48,2048]{2,1,0:T(8,128)(2,1)}, bf16[7,48,2048]{2,1,0:T(8,128)(2,1)S(1)}, u32[]{:S(2)}, u32[]{:S(2)}) collective-permute-start(bf16[7,48,2048]{2,1,0:T(8,128)(2,1)} %get-tuple-element.1174), channel_id=1, source_target_pairs={{0,8},{4,12},{8,0},{12,4},{16,24},{20,28},{24,16},{28,20},{1,9},{5... | collective-permute-start | bytes 4128776 | tf_op jit(solution)/shard_map/ppermute | solution.py:569
  291.9 42.6 %collective-permute-start.50 = (bf16[6,48,2048]{2,1,0:T(8,128)(2,1)}, bf16[6,48,2048]{2,1,0:T(8,128)(2,1)S(1)}, u32[]{:S(2)}, u32[]{:S(2)}) collective-permute-start(bf16[6,48,2048]{2,1,0:T(8,128)(2,1)} %get-tuple-element.1253), channel_id=1, source_target_pairs={{0,4},{4,0},{8,12},{12,8},{16,20},{20,16},{24,28},{28,24},{1,5},{5... | collective-permute-start | bytes 3538952 | tf_op jit(solution)/shard_map/ppermute | solution.py:569
  292.5 44.1 %collective-permute-start.51 = (bf16[6,48,2048]{2,1,0:T(8,128)(2,1)}, bf16[6,48,2048]{2,1,0:T(8,128)(2,1)S(1)}, u32[]{:S(2)}, u32[]{:S(2)}) collective-permute-start(bf16[6,48,2048]{2,1,0:T(8,128)(2,1)} %get-tuple-element.1254), channel_id=1, source_target_pairs={{0,8},{4,12},{8,0},{12,4},{16,24},{20,28},{24,16},{28,20},{1,9},{5... | collective-permute-start | bytes 3538952 | tf_op jit(solution)/shard_map/ppermute | solution.py:569
  316.9 27.4 %collective-permute-start.52 = (bf16[3,48,2048]{2,1,0:T(8,128)(2,1)}, bf16[3,48,2048]{2,1,0:T(8,128)(2,1)S(1)}, u32[]{:S(2)}, u32[]{:S(2)}) collective-permute-start(bf16[3,48,2048]{2,1,0:T(8,128)(2,1)} %get-tuple-element.1270), channel_id=1, source_target_pairs={{0,4},{4,0},{8,12},{12,8},{16,20},{20,16},{24,28},{28,24},{1,5},{5... | collective-permute-start | bytes 1769480 | tf_op jit(solution)/shard_map/ppermute | solution.py:569
  318.8 25.5 %collective-permute-start.53 = (bf16[3,48,2048]{2,1,0:T(8,128)(2,1)}, bf16[3,48,2048]{2,1,0:T(8,128)(2,1)S(1)}, u32[]{:S(2)}, u32[]{:S(2)}) collective-permute-start(bf16[3,48,2048]{2,1,0:T(8,128)(2,1)} %get-tuple-element.1271), channel_id=1, source_target_pairs={{0,8},{4,12},{8,0},{12,4},{16,24},{20,28},{24,16},{28,20},{1,9},{5... | collective-permute-start | bytes 1769480 | tf_op jit(solution)/shard_map/ppermute | solution.py:569
  334.5 24.9 %collective-permute-start.54 = (bf16[2,48,2048]{2,1,0:T(8,128)(2,1)}, bf16[2,48,2048]{2,1,0:T(8,128)(2,1)S(1)}, u32[]{:S(2)}, u32[]{:S(2)}) collective-permute-start(bf16[2,48,2048]{2,1,0:T(8,128)(2,1)} %get-tuple-element.1283), channel_id=1, source_target_pairs={{0,8},{4,12},{8,0},{12,4},{16,24},{20,28},{24,16},{28,20},{1,9},{5... | collective-permute-start | bytes 1179656 | tf_op jit(solution)/shard_map/ppermute | solution.py:569
  336.6 22.8 %collective-permute-start.56 = (bf16[2,48,2048]{2,1,0:T(8,128)(2,1)}, bf16[2,48,2048]{2,1,0:T(8,128)(2,1)S(1)}, u32[]{:S(2)}, u32[]{:S(2)}) collective-permute-start(bf16[2,48,2048]{2,1,0:T(8,128)(2,1)} %get-tuple-element.1285), channel_id=1, source_target_pairs={{0,4},{4,0},{8,12},{12,8},{16,20},{20,16},{24,28},{28,24},{1,5},{5... | collective-permute-start | bytes 1179656 | tf_op jit(solution)/shard_map/ppermute | solution.py:569
  354.0 35.7 %collective-permute-start.59 = (bf16[4,4,68,512]{3,1,2,0:T(4,128)(2,1)S(1)}, bf16[4,4,68,512]{3,1,2,0:T(4,128)(2,1)S(1)}, u32[]{:S(2)}, u32[]{:S(2)}) collective-permute-start(bf16[4,4,68,512]{3,1,2,0:T(4,128)(2,1)S(1)} %copy.527), channel_id=1, source_target_pairs={{0,4},{4,0},{8,12},{12,8},{16,20},{20,16},{24,28},{28,24},{1,5},{5... | collective-permute-start | bytes 3342344 | tf_op jit(solution)/shard_map/ppermute | solution.py:569
  365.9 24.1 %collective-permute-start.58 = (bf16[2,2,64,2048]{3,2,1,0:T(8,128)(2,1)S(1)}, bf16[2,2,64,2048]{3,2,1,0:T(8,128)(2,1)S(1)}, u32[]{:S(2)}, u32[]{:S(2)}) collective-permute-start(bf16[2,2,64,2048]{3,2,1,0:T(8,128)(2,1)S(1)} %bitcast.235), channel_id=1, source_target_pairs={{0,8},{4,12},{24,16},{28,20},{1,9},{5,13},{25,17},{29,21},{2,10},{... | collective-permute-start | bytes 3145736 | tf_op jit(solution)/shard_map/ppermute | solution.py:569
  394.0 41.4 %collective-permute-start.62 = (bf16[4,64,2048]{2,1,0:T(8,128)(2,1)}, bf16[4,64,2048]{2,1,0:T(8,128)(2,1)}, u32[]{:S(2)}, u32[]{:S(2)}) collective-permute-start(bf16[4,64,2048]{2,1,0:T(8,128)(2,1)} %dynamic-slice_bitcast_fusion.1), channel_id=1, source_target_pairs={{0,4},{4,0},{8,12},{12,8},{16,20},{20,16},{24,28},{28,24},{1,5},{5... | collective-permute-start | bytes 3145736 | tf_op jit(solution)/shard_map/ppermute | solution.py:569
  396.3 37.7 %collective-permute-start.63 = (bf16[4,2,68,512]{3,0,2,1:T(4,128)(2,1)}, bf16[4,2,68,512]{3,0,2,1:T(4,128)(2,1)}, u32[]{:S(2)}, u32[]{:S(2)}) collective-permute-start(bf16[4,2,68,512]{3,0,2,1:T(4,128)(2,1)} %copy.532), channel_id=1, source_target_pairs={{0,16},{4,20},{8,24},{12,28},{16,0},{20,4},{24,8},{28,12},{1,17},{... | collective-permute-start | bytes 1671176 | tf_op jit(solution)/shard_map/ppermute | solution.py:569
  400.2 36.7 %collective-permute-start.60 = (bf16[2,2,64,2048]{3,2,1,0:T(8,128)(2,1)}, bf16[2,2,64,2048]{3,2,1,0:T(8,128)(2,1)}, u32[]{:S(2)}, u32[]{:S(2)}) collective-permute-start(bf16[2,2,64,2048]{3,2,1,0:T(8,128)(2,1)} %get-tuple-element.1349.refs_0_), channel_id=1, source_target_pairs={{0,8},{4,12},{8,16},{12,20},{1,9},{5,13},{9,17},{13,21},{2,10},{6,... | collective-permute-start | bytes 3145736 | tf_op jit(solution)/shard_map/ppermute | solution.py:569
  402.3 34.6 %collective-permute-start.61 = (bf16[2,2,64,2048]{3,2,1,0:T(8,128)(2,1)}, bf16[2,2,64,2048]{3,2,1,0:T(8,128)(2,1)}, u32[]{:S(2)}, u32[]{:S(2)}) collective-permute-start(bf16[2,2,64,2048]{3,2,1,0:T(8,128)(2,1)} %get-tuple-element.1348.refs_1_), channel_id=1, source_target_pairs={{16,8},{20,12},{24,16},{28,20},{17,9},{21,13},{25,17},{29,21},{18,... | collective-permute-start | bytes 3145736 | tf_op jit(solution)/shard_map/ppermute | solution.py:569
  413.5 40.0 %collective-permute-start.71 = (bf16[4,64,2048]{2,1,0:T(8,128)(2,1)S(1)}, bf16[4,64,2048]{2,1,0:T(8,128)(2,1)S(1)}, u32[]{:S(2)}, u32[]{:S(2)}) collective-permute-start(bf16[4,64,2048]{2,1,0:T(8,128)(2,1)S(1)} %dynamic-slice_bitcast_fusion), channel_id=1, source_target_pairs={{0,4},{4,0},{8,12},{12,8},{16,20},{20,16},{24,28},{28,24},{1,5},{5... | collective-permute-start | bytes 3145736 | tf_op jit(solution)/shard_map/ppermute | solution.py:569
  437.8 27.7 %collective-permute-start.80 = (bf16[4,68,512]{2,1,0:T(8,128)(2,1)}, bf16[4,68,512]{2,1,0:T(8,128)(2,1)}, u32[]{:S(2)}, u32[]{:S(2)}) collective-permute-start(bf16[4,68,512]{2,1,0:T(8,128)(2,1)} %dynamic-slice_bitcast_fusion.10), channel_id=1, source_target_pairs={{0,8},{4,12},{8,0},{12,4},{16,24},{20,28},{24,16},{28,20},{1,9},{5... | collective-permute-start | bytes 835592 | tf_op jit(solution)/shard_map/ppermute | solution.py:569
  441.8 31.8 %collective-permute-start.70 = (bf16[2,64,2048]{2,1,0:T(8,128)(2,1)}, bf16[2,64,2048]{2,1,0:T(8,128)(2,1)}, u32[]{:S(2)}, u32[]{:S(2)}) collective-permute-start(bf16[2,64,2048]{2,1,0:T(8,128)(2,1)} %dynamic-slice_bitcast_fusion.9), channel_id=1, source_target_pairs={{0,16},{4,20},{8,24},{12,28},{16,0},{20,4},{24,8},{28,12},{1,17},{... | collective-permute-start | bytes 1572872 | tf_op jit(solution)/shard_map/ppermute | solution.py:569
  446.4 39.7 %collective-permute-start.68 = (bf16[2,2,64,2048]{3,2,1,0:T(8,128)(2,1)}, bf16[2,2,64,2048]{3,2,1,0:T(8,128)(2,1)}, u32[]{:S(2)}, u32[]{:S(2)}) collective-permute-start(bf16[2,2,64,2048]{3,2,1,0:T(8,128)(2,1)} %get-tuple-element.1351), channel_id=1, source_target_pairs={{0,8},{4,12},{8,16},{12,20},{16,24},{20,28},{1,9},{5,13},{9,17},{1... | collective-permute-start | bytes 3145736 | tf_op jit(solution)/shard_map/ppermute | solution.py:569
  449.1 37.0 %collective-permute-start.69 = (bf16[2,2,64,2048]{3,2,1,0:T(8,128)(2,1)}, bf16[2,2,64,2048]{3,2,1,0:T(8,128)(2,1)}, u32[]{:S(2)}, u32[]{:S(2)}) collective-permute-start(bf16[2,2,64,2048]{3,2,1,0:T(8,128)(2,1)} %get-tuple-element.1350), channel_id=1, source_target_pairs={{8,0},{12,4},{16,8},{20,12},{24,16},{28,20},{9,1},{13,5},{17,9},{2... | collective-permute-start | bytes 3145736 | tf_op jit(solution)/shard_map/ppermute | solution.py:569
  470.1 41.8 %collective-permute-start.82 = (bf16[1024,64]{0,1:T(8,128)(2,1)}, bf16[1024,64]{0,1:T(8,128)(2,1)}, u32[]{:S(2)}, u32[]{:S(2)}) collective-permute-start(bf16[1024,64]{0,1:T(8,128)(2,1)} %bitcast.144), channel_id=1, source_target_pairs={{0,1},{1,0},{2,3},{3,2},{4,5},{5,4},{6,7},{7,6},{8,9},{9,8},{10,11... | collective-permute-start | bytes 393224 | tf_op jit(solution)/shard_map/ppermute | solution.py:510
  473.6 40.6 %collective-permute-start.66 = (bf16[20,48,128]{2,1,0:T(8,128)(2,1)}, bf16[20,48,128]{2,1,0:T(8,128)(2,1)}, u32[]{:S(2)}, u32[]{:S(2)}) collective-permute-start(bf16[20,48,128]{2,1,0:T(8,128)(2,1)} %bitcast.217), channel_id=1, source_target_pairs={{0,1},{1,0},{2,3},{3,2},{4,5},{5,4},{6,7},{7,6},{8,9},{9,8},{10,11... | collective-permute-start | bytes 737288 | tf_op jit(solution)/shard_map/ppermute | solution.py:510
  486.2 23.4 %collective-permute-start.76 = (bf16[2,64,2048]{2,1,0:T(8,128)(2,1)S(1)}, bf16[2,64,2048]{2,1,0:T(8,128)(2,1)S(1)}, u32[]{:S(2)}, u32[]{:S(2)}) collective-permute-start(bf16[2,64,2048]{2,1,0:T(8,128)(2,1)S(1)} %dynamic-slice_bitcast_fusion.6), channel_id=1, source_target_pairs={{0,16},{4,20},{8,24},{12,28},{16,0},{20,4},{24,8},{28,12},{1,17},{... | collective-permute-start | bytes 1572872 | tf_op jit(solution)/shard_map/ppermute | solution.py:569
  490.7 31.1 %collective-permute-start.72 = (bf16[2,64,2048]{2,1,0:T(8,128)(2,1)S(1)}, bf16[2,64,2048]{2,1,0:T(8,128)(2,1)S(1)}, u32[]{:S(2)}, u32[]{:S(2)}) collective-permute-start(bf16[2,64,2048]{2,1,0:T(8,128)(2,1)S(1)} %get-tuple-element.1354), channel_id=1, source_target_pairs={{0,4},{4,0},{8,12},{12,8},{16,20},{20,16},{24,28},{28,24},{1,5},{5... | collective-permute-start | bytes 1572872 | tf_op jit(solution)/shard_map/ppermute | solution.py:569
  491.8 21.8 %collective-permute-start.74 = (bf16[1,64,2048]{2,1,0:T(8,128)(2,1)S(1)}, bf16[1,64,2048]{2,1,0:T(8,128)(2,1)S(1)}, u32[]{:S(2)}, u32[]{:S(2)}) collective-permute-start(bf16[1,64,2048]{2,1,0:T(8,128)(2,1)S(1)} %get-tuple-element.1360), channel_id=1, source_target_pairs={{0,8},{4,12},{8,0},{12,4},{16,24},{20,28},{24,16},{28,20},{1,9},{5... | collective-permute-start | bytes 786440 | tf_op jit(solution)/shard_map/ppermute | solution.py:569
  (155 other events, 778.1 us)

commit v17 on v16

--- a/solution.py
+++ b/solution.py
@@ -964,7 +964,7 @@
 
     def final(up, down):
         up, down, tokens["in"], rec_sum = after(
-            tokens["states"], up, down, tokens["in"], tokens["rec"], free=2 * MIB
+            tokens["states"][1:], up, down, tokens["in"], tokens["rec"], free=2 * MIB
         )
         tokens["rec"] = across_two(rec_sum)
         return up, down

time: 536 us -> 538 us (level)
  waiting for transfers between devices: 28.1 us -> 35 us
    unnamed x217 -> x222, local copies, waits for them, and re-layouts: 13.7 us -> 12.4 us
  transfers between devices with their start and end apart: 83 -> 83, of which waited for: 33 -> 31; matrix products, arithmetic and copies ran while one was open for 12% -> 10% of each run, Pallas kernels for 50% -> 50%
where the time goes in v17:
time: 538 us; the launch traced here: 527 us
  Pallas kernels  331 us (62%)
  starting transfers between devices  88.9 us (17%)
  local copies, waits for them, and re-layouts  36.1 us (7%)
  waiting for transfers between devices  35 us (7%)
  other arithmetic  29.2 us (5%)
    pallas_call x20, Pallas kernels, backward_call(): pl.pallas_call(backward_kernel, out_shape=(vmem((streams, depth), BF16),...  62.5 us
    pallas_call x19, Pallas kernels, between_call(): pl.pallas_call(functools.partial(between_kernel, not stacks, step == step...  56.4 us
    pallas_call x20, Pallas kernels, forward_call(): pl.pallas_call(functools.partial(forward_kernel, first), out_shape=(vmem(...  56.1 us
    pallas_call x20, Pallas kernels, aside_call(): pl.pallas_call(functools.partial(aside_kernel, not stacks, step == 0, not...  55.9 us
    ppermute x39, starting transfers between devices, body(): peer = lax.ppermute(part, 'gate', across)  43.6 us
    ppermute x29, starting transfers between devices, swapped(): return lax.ppermute(array, 'batch', pairs)  41.9 us
    ppermute x29, waiting for transfers between devices, swapped(): return lax.ppermute(array, 'batch', pairs)  23.6 us
    pallas_call x4, Pallas kernels, by_gate(): pl.pallas_call(functools.partial(layout_kernel, keep, spread), out_shape=...  23.3 us
  transfers between devices with their start and end apart: 83, of which 31 were waited for; matrix products, arithmetic and copies ran while one was open for 10% of the time, Pallas kernels for 50%

profile of v17, /device:TPU:8, one launch (start us, length us, event | category | flops | bytes accessed | tf_op | source)
XLA Modules:
  0.0 527.0 jit_solution(79219585718392502)
XLA Ops:
  0.7 5.8 %layout.5 = bf16[4,512,1024]{2,1,0:T(8,128)(2,1)} custom-call(s32[1]{0:T(128)} %bitcast.15.which_ref, bf16[2,512,4,1024]{3,2,1,0:T(4,128)(2,1)} %w_ref.5), custom_call_target="tpu_custom_call" | custom-call | tf_op jit(solution)/shard_map/layout/pallas_call | solution.py:522
  6.6 5.9 %layout.6 = bf16[4,512,1024]{2,1,0:T(8,128)(2,1)} custom-call(s32[1]{0:T(128)} %bitcast.15.which_ref, bf16[2,512,4,1024]{3,2,1,0:T(4,128)(2,1)} %w_ref.7), custom_call_target="tpu_custom_call" | custom-call | tf_op jit(solution)/shard_map/layout/pallas_call | solution.py:522
  23.4 6.4 %layout.4 = (bf16[4,512,1024]{2,1,0:T(8,128)(2,1)S(1)}, bf16[4,512,1024]{2,1,0:T(8,128)(2,1)}) custom-call(s32[1]{0:T(128)} %numbers.1.which_ref, bf16[2,512,4,1024]{3,2,1,0:T(4,128)(2,1)} %w_ref.5), custom_call_target="tpu_custom_call" | custom-call | tf_op jit(solution)/shard_map/layout/pallas_call | solution.py:522
  29.9 5.2 layout.7.wa_ref
  40.8 4.9 begin.1
  102.3 3.2 forward_step.28
  158.6 3.2 between.34
  165.8 3.1 between.35
  192.5 3.0 backward_step.20
  201.8 3.4 backward_step.21
  216.6 3.0 backward_step.23
  231.0 3.0 backward_step.25
  246.6 3.2 backward_step.27
  270.4 3.0 backward_step.30
  292.5 3.4 backward_step.33
  303.3 3.1 backward_step.34
  310.7 3.0 backward_step.35
  344.7 3.9 backward_step.39
  353.8 3.6 bitcast_convert_fusion
  359.5 4.2 gather.13
  365.9 4.3 late.1
  371.6 11.2 %product.1 = bf16[2,512,2048]{2,1,0:T(8,128)(2,1)S(1)} custom-call(bf16[40,48,1024]{2,1,0:T(8,128)(2,1)S(1)} %get-tuple-element.1276.refs_0_.left_ref, bf16[40,48,2048]{2,1,0:T(8,128)(2,1)S(1)} %get-tuple-element.1289.right_ref), custom_call_target="tpu_custom_call" | custom-call | tf_op jit(solution)/shard_map/product/pallas_call | solution.py:888
  382.8 11.2 %whole_product.2 = bf16[512,2048]{1,0:T(8,128)(2,1)S(1)} custom-call(bf16[20,48,512]{2,1,0:T(8,128)(2,1)} %after.12.refs_0_.mine_ref, bf16[20,48,512]{2,1,0:T(8,128)(2,1)} %get-tuple-element.1291.theirs_ref, bf16[20,48,2048]{2,1,0:T(8,128)(2,1)} %get-tuple-element.1296.kept_ref, bf16[7,48,2048]{2,1,0:T(8,128)(2,1)} %get-tuple-element.1297.refs_0_, ...), custom_call_target="tpu_custom_call" | custom-call | tf_op jit(solution)/shard_map/whole_product/pallas_call | solution.py:907
  400.6 3.7 collective-permute-start.63
  408.0 9.7 %whole_product.3 = bf16[512,2048]{1,0:T(8,128)(2,1)S(1)} custom-call(bf16[20,48,512]{2,1,0:T(8,128)(2,1)} %after.13.refs_1_.mine_ref, bf16[20,48,512]{2,1,0:T(8,128)(2,1)} %copy-done.13, bf16[20,48,2048]{2,1,0:T(8,128)(2,1)} %get-tuple-element.1296.kept_ref, bf16[7,48,2048]{2,1,0:T(8,128)(2,1)} %get-tuple-element.1297.refs_0_, ...), custom_call_target="tpu_custom_call" | custom-call | tf_op jit(solution)/shard_map/whole_product/pallas_call | solution.py:907
  418.9 19.3 %input_grad.1.refs_2_ = f32[20,48,512]{2,1,0:T(8,128)S(1)} custom-call(s32[2]{0:T(128)S(1)} %copy-done.40, bf16[4,20,48,2048]{3,2,1,0:T(8,128)(2,1)} %get-tuple-element.1305.dz_ref, bf16[4,512,1024]{2,1,0:T(8,128)(2,1)} %get-tuple-element.1306.wa_ref, bf16[4,512,1024]{2,1,0:T(8,128)(2,1)} %collective-permute-done.1.refs_2_.wb_ref), custom_call_target="tpu_custom_call" | custom-call | tf_op jit(solution)/shard_map/input_grad/pallas_call | solution.py:811
  447.1 3.6 fusion.5
  453.3 4.2 collective-permute-start.69
  468.0 5.3 %collective-permute-done.65 = bf16[20,48,256]{2,1,0:T(8,128)(2,1)} collective-permute-done((bf16[20,48,256]{2,1,0:T(8,128)(2,1)}, bf16[20,48,256]{2,1,0:T(8,128)(2,1)}, u32[]{:S(2)}, u32[]{:S(2)}) %collective-permute-start.65) | collective-permute-done | bytes 491552 | tf_op jit(solution)/shard_map/ppermute | solution.py:1014
  494.2 18.3 %collective-permute-done.76 = bf16[2,64,2048]{2,1,0:T(8,128)(2,1)S(1)} collective-permute-done((bf16[2,64,2048]{2,1,0:T(8,128)(2,1)S(1)}, bf16[2,64,2048]{2,1,0:T(8,128)(2,1)S(1)}, u32[]{:S(2)}, u32[]{:S(2)}) %collective-permute-start.76) | collective-permute-done | bytes 524320 | tf_op jit(solution)/shard_map/ppermute | solution.py:569
  517.3 3.8 collective-permute-done.78
  523.2 3.5 assemble.1
  (585 shorter events, 347.8 us)
Async XLA Ops:
  6.5 33.4 %collective-permute-start.1 = (bf16[4,512,1024]{2,1,0:T(8,128)(2,1)}, bf16[4,512,1024]{2,1,0:T(8,128)(2,1)}, u32[]{:S(2)}, u32[]{:S(2)}) collective-permute-start(bf16[4,512,1024]{2,1,0:T(8,128)(2,1)} %layout.5), channel_id=1, source_target_pairs={{0,1},{1,0},{2,3},{3,2},{4,5},{5,4},{6,7},{7,6},{8,9},{9,8},{10,11... | collective-permute-start | bytes 12582920 | tf_op jit(solution)/shard_map/ppermute | solution.py:538
  12.5 27.3 %collective-permute-start.2 = (bf16[4,512,1024]{2,1,0:T(8,128)(2,1)}, bf16[4,512,1024]{2,1,0:T(8,128)(2,1)}, u32[]{:S(2)}, u32[]{:S(2)}) collective-permute-start(bf16[4,512,1024]{2,1,0:T(8,128)(2,1)} %layout.6), channel_id=1, source_target_pairs={{0,1},{1,0},{2,3},{3,2},{4,5},{5,4},{6,7},{7,6},{8,9},{9,8},{10,11... | collective-permute-start | bytes 12582920 | tf_op jit(solution)/shard_map/ppermute | solution.py:538
  16.4 21.6 %collective-permute-start.4 = (f32[48,1024]{1,0:T(8,128)}, f32[48,1024]{1,0:T(8,128)}, u32[]{:S(2)}, u32[]{:S(2)}) collective-permute-start(f32[48,1024]{1,0:T(8,128)} %bitcast.218), channel_id=1, source_target_pairs={{0,1},{1,0},{2,3},{3,2},{4,5},{5,4},{6,7},{7,6},{8,9},{9,8},{10,11... | collective-permute-start | bytes 589832 | tf_op jit(solution)/shard_map/ppermute | solution.py:510
  16.4 21.6 %collective-permute-start = (bf16[4,1024]{1,0:T(4,128)(2,1)S(1)}, bf16[4,1024]{1,0:T(4,128)(2,1)S(1)}, u32[]{:S(2)}, u32[]{:S(2)}) collective-permute-start(bf16[4,1024]{1,0:T(4,128)(2,1)S(1)} %get-tuple-element.1352), channel_id=1, source_target_pairs={{0,1},{1,0},{2,3},{3,2},{4,5},{5,4},{6,7},{7,6},{8,9},{9,8},{10,11... | collective-permute-start | bytes 24584 | tf_op jit(solution)/shard_map/ppermute | solution.py:510
  17.0 22.8 %collective-permute-start.3 = (bf16[1024,512]{1,0:T(8,128)(2,1)S(1)}, bf16[1024,512]{1,0:T(8,128)(2,1)S(1)}, u32[]{:S(2)}, u32[]{:S(2)}) collective-permute-start(bf16[1024,512]{1,0:T(8,128)(2,1)S(1)} %dynamic-slice_bitcast_fusion.2), channel_id=1, source_target_pairs={{0,1},{1,0},{2,3},{3,2},{4,5},{5,4},{6,7},{7,6},{8,9},{9,8},{10,11... | collective-permute-start | bytes 3145736 | tf_op jit(solution)/shard_map/ppermute | solution.py:540
  127.5 29.9 %collective-permute-start.21 = (bf16[20,48,512]{2,1,0:T(8,128)(2,1)}, bf16[20,48,512]{2,1,0:T(8,128)(2,1)S(1)}, u32[]{:S(2)}, u32[]{:S(2)}) collective-permute-start(bf16[20,48,512]{2,1,0:T(8,128)(2,1)} %after.12.refs_0_.mine_ref), channel_id=1, source_target_pairs={{0,4},{4,0},{8,12},{12,8},{16,20},{20,16},{24,28},{28,24},{1,5},{5... | collective-permute-start | bytes 2949128 | tf_op jit(solution)/shard_map/ppermute | solution.py:569
  129.0 28.3 %collective-permute-start.22 = (bf16[20,48,512]{2,1,0:T(8,128)(2,1)}, bf16[20,48,512]{2,1,0:T(8,128)(2,1)S(1)}, u32[]{:S(2)}, u32[]{:S(2)}) collective-permute-start(bf16[20,48,512]{2,1,0:T(8,128)(2,1)} %after.12.refs_0_.mine_ref), channel_id=1, source_target_pairs={{0,8},{4,12},{8,0},{12,4},{16,24},{20,28},{24,16},{28,20},{1,9},{5... | collective-permute-start | bytes 2949128 | tf_op jit(solution)/shard_map/ppermute | solution.py:569
  195.6 46.9 %collective-permute-start.33 = (bf16[20,48,512]{2,1,0:T(8,128)(2,1)}, bf16[20,48,512]{2,1,0:T(8,128)(2,1)S(1)}, u32[]{:S(2)}, u32[]{:S(2)}) collective-permute-start(bf16[20,48,512]{2,1,0:T(8,128)(2,1)} %after.13.refs_1_.mine_ref), channel_id=1, source_target_pairs={{0,4},{4,0},{8,12},{12,8},{16,20},{20,16},{24,28},{28,24},{1,5},{5... | collective-permute-start | bytes 2949128 | tf_op jit(solution)/shard_map/ppermute | solution.py:569
  196.1 46.4 %collective-permute-start.34 = (bf16[20,48,512]{2,1,0:T(8,128)(2,1)}, bf16[20,48,512]{2,1,0:T(8,128)(2,1)S(1)}, u32[]{:S(2)}, u32[]{:S(2)}) collective-permute-start(bf16[20,48,512]{2,1,0:T(8,128)(2,1)} %after.13.refs_1_.mine_ref), channel_id=1, source_target_pairs={{0,8},{4,12},{8,0},{12,4},{16,24},{20,28},{24,16},{28,20},{1,9},{5... | collective-permute-start | bytes 2949128 | tf_op jit(solution)/shard_map/ppermute | solution.py:569
  249.8 49.2 %collective-permute-start.43 = (bf16[7,48,2048]{2,1,0:T(8,128)(2,1)}, bf16[7,48,2048]{2,1,0:T(8,128)(2,1)S(1)}, u32[]{:S(2)}, u32[]{:S(2)}) collective-permute-start(bf16[7,48,2048]{2,1,0:T(8,128)(2,1)} %get-tuple-element.1173), channel_id=1, source_target_pairs={{0,4},{4,0},{8,12},{12,8},{16,20},{20,16},{24,28},{28,24},{1,5},{5... | collective-permute-start | bytes 4128776 | tf_op jit(solution)/shard_map/ppermute | solution.py:569
  251.4 47.6 %collective-permute-start.44 = (bf16[7,48,2048]{2,1,0:T(8,128)(2,1)}, bf16[7,48,2048]{2,1,0:T(8,128)(2,1)S(1)}, u32[]{:S(2)}, u32[]{:S(2)}) collective-permute-start(bf16[7,48,2048]{2,1,0:T(8,128)(2,1)} %get-tuple-element.1174), channel_id=1, source_target_pairs={{0,8},{4,12},{8,0},{12,4},{16,24},{20,28},{24,16},{28,20},{1,9},{5... | collective-permute-start | bytes 4128776 | tf_op jit(solution)/shard_map/ppermute | solution.py:569
  295.9 42.9 %collective-permute-start.50 = (bf16[6,48,2048]{2,1,0:T(8,128)(2,1)}, bf16[6,48,2048]{2,1,0:T(8,128)(2,1)S(1)}, u32[]{:S(2)}, u32[]{:S(2)}) collective-permute-start(bf16[6,48,2048]{2,1,0:T(8,128)(2,1)} %get-tuple-element.1253), channel_id=1, source_target_pairs={{0,4},{4,0},{8,12},{12,8},{16,20},{20,16},{24,28},{28,24},{1,5},{5... | collective-permute-start | bytes 3538952 | tf_op jit(solution)/shard_map/ppermute | solution.py:569
  296.5 44.4 %collective-permute-start.51 = (bf16[6,48,2048]{2,1,0:T(8,128)(2,1)}, bf16[6,48,2048]{2,1,0:T(8,128)(2,1)S(1)}, u32[]{:S(2)}, u32[]{:S(2)}) collective-permute-start(bf16[6,48,2048]{2,1,0:T(8,128)(2,1)} %get-tuple-element.1254), channel_id=1, source_target_pairs={{0,8},{4,12},{8,0},{12,4},{16,24},{20,28},{24,16},{28,20},{1,9},{5... | collective-permute-start | bytes 3538952 | tf_op jit(solution)/shard_map/ppermute | solution.py:569
  321.0 27.6 %collective-permute-start.52 = (bf16[3,48,2048]{2,1,0:T(8,128)(2,1)}, bf16[3,48,2048]{2,1,0:T(8,128)(2,1)S(1)}, u32[]{:S(2)}, u32[]{:S(2)}) collective-permute-start(bf16[3,48,2048]{2,1,0:T(8,128)(2,1)} %get-tuple-element.1270), channel_id=1, source_target_pairs={{0,4},{4,0},{8,12},{12,8},{16,20},{20,16},{24,28},{28,24},{1,5},{5... | collective-permute-start | bytes 1769480 | tf_op jit(solution)/shard_map/ppermute | solution.py:569
  323.0 25.6 %collective-permute-start.53 = (bf16[3,48,2048]{2,1,0:T(8,128)(2,1)}, bf16[3,48,2048]{2,1,0:T(8,128)(2,1)S(1)}, u32[]{:S(2)}, u32[]{:S(2)}) collective-permute-start(bf16[3,48,2048]{2,1,0:T(8,128)(2,1)} %get-tuple-element.1271), channel_id=1, source_target_pairs={{0,8},{4,12},{8,0},{12,4},{16,24},{20,28},{24,16},{28,20},{1,9},{5... | collective-permute-start | bytes 1769480 | tf_op jit(solution)/shard_map/ppermute | solution.py:569
  338.8 24.9 %collective-permute-start.54 = (bf16[2,48,2048]{2,1,0:T(8,128)(2,1)}, bf16[2,48,2048]{2,1,0:T(8,128)(2,1)S(1)}, u32[]{:S(2)}, u32[]{:S(2)}) collective-permute-start(bf16[2,48,2048]{2,1,0:T(8,128)(2,1)} %get-tuple-element.1283), channel_id=1, source_target_pairs={{0,8},{4,12},{8,0},{12,4},{16,24},{20,28},{24,16},{28,20},{1,9},{5... | collective-permute-start | bytes 1179656 | tf_op jit(solution)/shard_map/ppermute | solution.py:569
  340.9 22.8 %collective-permute-start.56 = (bf16[2,48,2048]{2,1,0:T(8,128)(2,1)}, bf16[2,48,2048]{2,1,0:T(8,128)(2,1)S(1)}, u32[]{:S(2)}, u32[]{:S(2)}) collective-permute-start(bf16[2,48,2048]{2,1,0:T(8,128)(2,1)} %get-tuple-element.1285), channel_id=1, source_target_pairs={{0,4},{4,0},{8,12},{12,8},{16,20},{20,16},{24,28},{28,24},{1,5},{5... | collective-permute-start | bytes 1179656 | tf_op jit(solution)/shard_map/ppermute | solution.py:569
  358.2 35.8 %collective-permute-start.59 = (bf16[4,4,68,512]{3,1,2,0:T(4,128)(2,1)S(1)}, bf16[4,4,68,512]{3,1,2,0:T(4,128)(2,1)S(1)}, u32[]{:S(2)}, u32[]{:S(2)}) collective-permute-start(bf16[4,4,68,512]{3,1,2,0:T(4,128)(2,1)S(1)} %copy.513), channel_id=1, source_target_pairs={{0,4},{4,0},{8,12},{12,8},{16,20},{20,16},{24,28},{28,24},{1,5},{5... | collective-permute-start | bytes 3342344 | tf_op jit(solution)/shard_map/ppermute | solution.py:569
  370.3 24.1 %collective-permute-start.58 = (bf16[2,2,64,2048]{3,2,1,0:T(8,128)(2,1)S(1)}, bf16[2,2,64,2048]{3,2,1,0:T(8,128)(2,1)S(1)}, u32[]{:S(2)}, u32[]{:S(2)}) collective-permute-start(bf16[2,2,64,2048]{3,2,1,0:T(8,128)(2,1)S(1)} %bitcast.235), channel_id=1, source_target_pairs={{0,8},{4,12},{24,16},{28,20},{1,9},{5,13},{25,17},{29,21},{2,10},{... | collective-permute-start | bytes 3145736 | tf_op jit(solution)/shard_map/ppermute | solution.py:569
  398.3 41.4 %collective-permute-start.62 = (bf16[4,64,2048]{2,1,0:T(8,128)(2,1)}, bf16[4,64,2048]{2,1,0:T(8,128)(2,1)}, u32[]{:S(2)}, u32[]{:S(2)}) collective-permute-start(bf16[4,64,2048]{2,1,0:T(8,128)(2,1)} %dynamic-slice_bitcast_fusion.1), channel_id=1, source_target_pairs={{0,4},{4,0},{8,12},{12,8},{16,20},{20,16},{24,28},{28,24},{1,5},{5... | collective-permute-start | bytes 3145736 | tf_op jit(solution)/shard_map/ppermute | solution.py:569
  400.6 37.7 %collective-permute-start.63 = (bf16[4,2,68,512]{3,0,2,1:T(4,128)(2,1)}, bf16[4,2,68,512]{3,0,2,1:T(4,128)(2,1)}, u32[]{:S(2)}, u32[]{:S(2)}) collective-permute-start(bf16[4,2,68,512]{3,0,2,1:T(4,128)(2,1)} %copy.518), channel_id=1, source_target_pairs={{0,16},{4,20},{8,24},{12,28},{16,0},{20,4},{24,8},{28,12},{1,17},{... | collective-permute-start | bytes 1671176 | tf_op jit(solution)/shard_map/ppermute | solution.py:569
  404.3 37.0 %collective-permute-start.60 = (bf16[2,2,64,2048]{3,2,1,0:T(8,128)(2,1)}, bf16[2,2,64,2048]{3,2,1,0:T(8,128)(2,1)}, u32[]{:S(2)}, u32[]{:S(2)}) collective-permute-start(bf16[2,2,64,2048]{3,2,1,0:T(8,128)(2,1)} %get-tuple-element.1325.refs_0_), channel_id=1, source_target_pairs={{0,8},{4,12},{8,16},{12,20},{1,9},{5,13},{9,17},{13,21},{2,10},{6,... | collective-permute-start | bytes 3145736 | tf_op jit(solution)/shard_map/ppermute | solution.py:569
  406.7 34.6 %collective-permute-start.61 = (bf16[2,2,64,2048]{3,2,1,0:T(8,128)(2,1)}, bf16[2,2,64,2048]{3,2,1,0:T(8,128)(2,1)}, u32[]{:S(2)}, u32[]{:S(2)}) collective-permute-start(bf16[2,2,64,2048]{3,2,1,0:T(8,128)(2,1)} %get-tuple-element.1324.refs_1_), channel_id=1, source_target_pairs={{16,8},{20,12},{24,16},{28,20},{17,9},{21,13},{25,17},{29,21},{18,... | collective-permute-start | bytes 3145736 | tf_op jit(solution)/shard_map/ppermute | solution.py:569
  417.8 40.0 %collective-permute-start.71 = (bf16[4,64,2048]{2,1,0:T(8,128)(2,1)S(1)}, bf16[4,64,2048]{2,1,0:T(8,128)(2,1)S(1)}, u32[]{:S(2)}, u32[]{:S(2)}) collective-permute-start(bf16[4,64,2048]{2,1,0:T(8,128)(2,1)S(1)} %dynamic-slice_bitcast_fusion), channel_id=1, source_target_pairs={{0,4},{4,0},{8,12},{12,8},{16,20},{20,16},{24,28},{28,24},{1,5},{5... | collective-permute-start | bytes 3145736 | tf_op jit(solution)/shard_map/ppermute | solution.py:569
  442.1 21.0 %collective-permute-start.80 = (bf16[4,68,512]{2,1,0:T(8,128)(2,1)}, bf16[4,68,512]{2,1,0:T(8,128)(2,1)}, u32[]{:S(2)}, u32[]{:S(2)}) collective-permute-start(bf16[4,68,512]{2,1,0:T(8,128)(2,1)} %dynamic-slice_bitcast_fusion.10), channel_id=1, source_target_pairs={{0,8},{4,12},{8,0},{12,4},{16,24},{20,28},{24,16},{28,20},{1,9},{5... | collective-permute-start | bytes 835592 | tf_op jit(solution)/shard_map/ppermute | solution.py:569
  445.9 35.6 %collective-permute-start.70 = (bf16[2,64,2048]{2,1,0:T(8,128)(2,1)}, bf16[2,64,2048]{2,1,0:T(8,128)(2,1)}, u32[]{:S(2)}, u32[]{:S(2)}) collective-permute-start(bf16[2,64,2048]{2,1,0:T(8,128)(2,1)} %dynamic-slice_bitcast_fusion.9), channel_id=1, source_target_pairs={{0,16},{4,20},{8,24},{12,28},{16,0},{20,4},{24,8},{28,12},{1,17},{... | collective-permute-start | bytes 1572872 | tf_op jit(solution)/shard_map/ppermute | solution.py:569
  450.7 37.4 %collective-permute-start.68 = (bf16[2,2,64,2048]{3,2,1,0:T(8,128)(2,1)}, bf16[2,2,64,2048]{3,2,1,0:T(8,128)(2,1)}, u32[]{:S(2)}, u32[]{:S(2)}) collective-permute-start(bf16[2,2,64,2048]{3,2,1,0:T(8,128)(2,1)} %get-tuple-element.1327), channel_id=1, source_target_pairs={{0,8},{4,12},{8,16},{12,20},{16,24},{20,28},{1,9},{5,13},{9,17},{1... | collective-permute-start | bytes 3145736 | tf_op jit(solution)/shard_map/ppermute | solution.py:569
  453.3 34.9 %collective-permute-start.69 = (bf16[2,2,64,2048]{3,2,1,0:T(8,128)(2,1)}, bf16[2,2,64,2048]{3,2,1,0:T(8,128)(2,1)}, u32[]{:S(2)}, u32[]{:S(2)}) collective-permute-start(bf16[2,2,64,2048]{3,2,1,0:T(8,128)(2,1)} %get-tuple-element.1326), channel_id=1, source_target_pairs={{8,0},{12,4},{16,8},{20,12},{24,16},{28,20},{9,1},{13,5},{17,9},{2... | collective-permute-start | bytes 3145736 | tf_op jit(solution)/shard_map/ppermute | solution.py:569
  481.5 33.5 %collective-permute-start.66 = (bf16[20,48,128]{2,1,0:T(8,128)(2,1)}, bf16[20,48,128]{2,1,0:T(8,128)(2,1)}, u32[]{:S(2)}, u32[]{:S(2)}) collective-permute-start(bf16[20,48,128]{2,1,0:T(8,128)(2,1)} %bitcast.217), channel_id=1, source_target_pairs={{0,1},{1,0},{2,3},{3,2},{4,5},{5,4},{6,7},{7,6},{8,9},{9,8},{10,11... | collective-permute-start | bytes 737288 | tf_op jit(solution)/shard_map/ppermute | solution.py:510
  488.8 23.7 %collective-permute-start.76 = (bf16[2,64,2048]{2,1,0:T(8,128)(2,1)S(1)}, bf16[2,64,2048]{2,1,0:T(8,128)(2,1)S(1)}, u32[]{:S(2)}, u32[]{:S(2)}) collective-permute-start(bf16[2,64,2048]{2,1,0:T(8,128)(2,1)S(1)} %dynamic-slice_bitcast_fusion.6), channel_id=1, source_target_pairs={{0,16},{4,20},{8,24},{12,28},{16,0},{20,4},{24,8},{28,12},{1,17},{... | collective-permute-start | bytes 1572872 | tf_op jit(solution)/shard_map/ppermute | solution.py:569
  493.0 30.2 %collective-permute-start.72 = (bf16[2,64,2048]{2,1,0:T(8,128)(2,1)S(1)}, bf16[2,64,2048]{2,1,0:T(8,128)(2,1)S(1)}, u32[]{:S(2)}, u32[]{:S(2)}) collective-permute-start(bf16[2,64,2048]{2,1,0:T(8,128)(2,1)S(1)} %get-tuple-element.1330), channel_id=1, source_target_pairs={{0,4},{4,0},{8,12},{12,8},{16,20},{20,16},{24,28},{28,24},{1,5},{5... | collective-permute-start | bytes 1572872 | tf_op jit(solution)/shard_map/ppermute | solution.py:569
  494.1 22.6 %collective-permute-start.74 = (bf16[1,64,2048]{2,1,0:T(8,128)(2,1)S(1)}, bf16[1,64,2048]{2,1,0:T(8,128)(2,1)S(1)}, u32[]{:S(2)}, u32[]{:S(2)}) collective-permute-start(bf16[1,64,2048]{2,1,0:T(8,128)(2,1)S(1)} %get-tuple-element.1336), channel_id=1, source_target_pairs={{0,8},{4,12},{8,0},{12,4},{16,24},{20,28},{24,16},{28,20},{1,9},{5... | collective-permute-start | bytes 786440 | tf_op jit(solution)/shard_map/ppermute | solution.py:569
  (158 other events, 851.0 us)
